TPU v7x, 128 devices: a whole 4x4x4 slice. The times are simulated.
128 devices in a mesh: wide: 64 (over y_hi, z, x, core), narrow: 2 (over y_lo).
Axes of the slice: x: 4, y: 4 (y_hi: 2, y_lo: 2; y = y_hi * 2 + y_lo), z: 4, core: 2. Of those that a mesh axis runs over, the one named last changes fastest.
Arguments:
- x_first: bfloat16 [8192, 1024], P('wide', 'narrow'), may hold values from -6 to 6
- x_second: bfloat16 [8192, 1024], P('wide', 'narrow'), may hold values from -6 to 6
- grad_first: bfloat16 [8192, 1024], P('wide', 'narrow'), may hold values from -6 to 6
- grad_second: bfloat16 [8192, 1024], P('wide', 'narrow'), may hold values from -6 to 6
- sort_target: int32 [2, 2, 8192], replicated, may hold values from 0 to 8191, as said below
- owner: int32 [176], replicated, may hold values from 0 to 319, as said below
- master: float32 [320, 128, 1024], P('wide', None, 'narrow')
- moment_first: float32 [320, 128, 1024], P('wide', None, 'narrow')
- moment_second: float32 [320, 128, 1024], P('wide', None, 'narrow')
- gains: float32 [2, 2, 1024], P(None, None, 'narrow'), may hold values from 0.5 to 1.5
- gain_first: float32 [2, 2, 1024], P(None, None, 'narrow')
- gain_second: float32 [2, 2, 1024], P(None, None, 'narrow')
Outputs:
- y_first: float32 [8192, 1024], P('wide', 'narrow')
- y_second: float32 [8192, 1024], P('wide', 'narrow')
- dx_first: float32 [8192, 1024], P('wide', 'narrow')
- dx_second: float32 [8192, 1024], P('wide', 'narrow')
- slot_grad: float32 [320, 128, 1024], P('wide', None, 'narrow')
- slot_first: float32 [320, 128, 1024], P('wide', None, 'narrow')
- slot_second: float32 [320, 128, 1024], P('wide', None, 'narrow')
- slot_new: float32 [320, 128, 1024], P('wide', None, 'narrow')
- gain_grad: float32 [2, 2, 1024], P(None, None, 'narrow')
- gain_first_new: float32 [2, 2, 1024], P(None, None, 'narrow')
- gain_second_new: float32 [2, 2, 1024], P(None, None, 'narrow')
- gain_new: float32 [2, 2, 1024], P(None, None, 'narrow')
Inputs may be any that keep to these rules, and one draw needn't show every extreme that they name: For each layer and round, sort_target is a permutation of the 8192 positions in which the 128 positions of every aligned block of 128 go to exactly 128 // 64 places in every aligned block of 128 places. owner holds 176 different slots; slots k * 5 to k * 5 + 4 belong to index k of wide; the slots of some index are all used; in each aligned group of 3 tile numbers at most 1 tiles belong to one index of wide.
All inputs are finite; a program needn't handle non-finite values.
Results may differ from a plain program's by a relative error of at most 0.024.
Values may be sent and summed in bfloat16 or wider, within the bound.
No kernel may reach another device: no remote copies, remote signals or barrier semaphores. Data moves between devices by JAX's collectives and lax.ppermute only.
A program may use at most 320 MiB of HBM per device.

v0:
```python
import jax
import jax.numpy as jnp
from jax import lax
from jax.sharding import PartitionSpec as P

DH = 128
FF = 4096
SPAN = 64
ROUNDS = 2
LAYERS = 2
STEP = 5
TR = 128


MASK_FILL = -1000000000.0
NORM_EPS = 1e-05
BETA_ONE = 0.5
BETA_TWO = 0.5
RATE_WEIGHT = 0.05
RATE_GAIN = 0.2
DECAY = 0.01
EPSILON = 1e-08


def shifted(block, axis, distance):
    devices = range(lax.axis_size(axis))
    route = [((i - distance) % len(devices), i) for i in devices]
    return lax.ppermute(block, axis, route)


def rounded(values):
    return lax.optimization_barrier(values.astype(jnp.bfloat16)).astype(jnp.float32)


def smooth(values):
    return jax.nn.gelu(values, approximate=False)


def narrow_sums(first, second):
    return lax.psum((jnp.sum(first, axis=1), jnp.sum(second, axis=1)), "narrow")


def norm_forward(values, width):
    total, squares = narrow_sums(values, values * values)
    mean = total / width
    rstd = lax.rsqrt(squares / width - mean * mean + NORM_EPS)
    return ((values - mean[:, None]) * rstd[:, None], rstd)


def norm_backward(upstream, gain, normed, rstd, width):
    scaled = upstream * gain
    total, cross = narrow_sums(scaled, scaled * normed)
    grad_in = rstd[:, None] * (scaled - total[:, None] / width - normed * (cross[:, None] / width))
    return (grad_in, jnp.sum(upstream * normed, axis=0))


def gather_features(hidden):
    return lax.all_gather(hidden, "narrow", axis=1, tiled=True)


def branch_sum(partial_rows):
    return lax.psum_scatter(partial_rows, "narrow", scatter_dimension=1, tiled=True)


def unpack(tiles, width, part_width):
    rows = tiles.reshape(LAYERS, -1, part_width)
    layers = []
    for layer in range(LAYERS):
        block = rows[layer]
        layers.append(
            {
                "qk": block[:width],
                "value": block[width : 2 * width],
                "out": block[2 * width : 3 * width],
                "up": block[3 * width : 3 * width + FF].reshape(width, -1),
                "down": block[3 * width + FF :].reshape(width, -1),
            }
        )
    return layers


def sort_plan(target, me, tok):
    mine = lax.dynamic_slice_in_dim(target, me * tok, tok)
    send_order = jnp.argsort(mine, stable=True)
    source_pos = jnp.argsort(send_order, stable=True)
    inverse = jnp.argsort(target, stable=True)
    anchor = lax.dynamic_slice_in_dim(inverse, me * tok, tok)
    keyed = anchor // tok * tok + jnp.arange(tok, dtype=jnp.int32)
    slot_order = jnp.argsort(keyed, stable=True)
    slot_pos = jnp.argsort(slot_order, stable=True)
    return (send_order, source_pos, slot_order, slot_pos)


def to_sorted(mixed, values, plan, nwide):
    tok = mixed.shape[0]
    share = tok // nwide
    moved_q, moved_v = (
        lax.all_to_all(
            mixed[plan[0]].reshape(nwide, share, -1),
            "wide",
            split_axis=0,
            concat_axis=0,
            tiled=True,
        ),
        lax.all_to_all(
            values[plan[0]].reshape(nwide, share, -1),
            "wide",
            split_axis=0,
            concat_axis=0,
            tiled=True,
        ),
    )
    return (moved_q.reshape(tok, -1)[plan[3]], moved_v.reshape(tok, -1)[plan[3]])


def to_initial(attended, total, plan, nwide):
    tok = attended.shape[0]
    share = tok // nwide
    back_o, back_t = (
        lax.all_to_all(
            attended[plan[2]].reshape(nwide, share, -1),
            "wide",
            split_axis=0,
            concat_axis=0,
            tiled=True,
        ),
        lax.all_to_all(
            total[plan[2]].reshape(nwide, share, -1),
            "wide",
            split_axis=0,
            concat_axis=0,
            tiled=True,
        ),
    )
    return (back_o.reshape(tok, -1)[plan[1]], back_t.reshape(tok, -1)[plan[1]])


def grad_sorted(d_out, d_total, plan, nwide):
    tok = d_out.shape[0]
    share = tok // nwide
    moved_o, moved_t = (
        lax.all_to_all(
            d_out[plan[0]].reshape(nwide, share, -1),
            "wide",
            split_axis=0,
            concat_axis=0,
            tiled=True,
        ),
        lax.all_to_all(
            d_total[plan[0]].reshape(nwide, share, -1),
            "wide",
            split_axis=0,
            concat_axis=0,
            tiled=True,
        ),
    )
    return (moved_o.reshape(tok, -1)[plan[3]], moved_t.reshape(tok, -1)[plan[3]])


def grad_initial(d_query, d_value, plan, nwide):
    tok = d_query.shape[0]
    share = tok // nwide
    back_q, back_v = (
        lax.all_to_all(
            d_query[plan[2]].reshape(nwide, share, -1),
            "wide",
            split_axis=0,
            concat_axis=0,
            tiled=True,
        ),
        lax.all_to_all(
            d_value[plan[2]].reshape(nwide, share, -1),
            "wide",
            split_axis=0,
            concat_axis=0,
            tiled=True,
        ),
    )
    return (back_q.reshape(tok, -1)[plan[1]], back_v.reshape(tok, -1)[plan[1]])


def attend_parts(queries, values, prev_queries, prev_values):
    count = queries.shape[0] // SPAN
    heads = queries.shape[1]
    cur_q = queries.reshape(count, SPAN, heads, DH)
    cur_v = values.reshape(count, SPAN, heads, DH)
    keys = jnp.concatenate([jnp.concatenate([prev_queries[None], cur_q[:-1]], 0), cur_q], 1)
    vals = jnp.concatenate([jnp.concatenate([prev_values[None], cur_v[:-1]], 0), cur_v], 1)
    inv_len = lax.rsqrt(jnp.sum(keys * keys, axis=-1, keepdims=True) + 1e-06)
    unit = rounded(keys * inv_len)
    scores = jnp.einsum("cqhd,ckhd->chqk", cur_q, unit)
    own = jnp.arange(2 * SPAN)[None, :] == jnp.arange(SPAN)[:, None] + SPAN
    scores = jnp.where(own, MASK_FILL, scores)
    peak = jnp.max(scores, axis=-1, keepdims=True)
    total = peak + jnp.log(jnp.sum(jnp.exp(scores - peak), axis=-1, keepdims=True))
    exact = jnp.exp(scores - total)
    return (cur_q, keys, vals, inv_len, unit, own, total, exact)


def attend(queries, values, prev_queries, prev_values):
    count = queries.shape[0] // SPAN
    heads = queries.shape[1]
    cur_q, keys, vals, inv_len, unit, own, total, exact = attend_parts(
        queries, values, prev_queries, prev_values
    )
    probs = rounded(exact)
    out = jnp.einsum("chqk,ckhd->cqhd", probs, vals)
    lse = jnp.transpose(total[..., 0], (0, 2, 1)).reshape(count * SPAN, heads)
    return (out.reshape(count * SPAN, heads, DH), lse)


def attend_backward(queries, values, prev_queries, prev_values, d_out, d_total):
    count = queries.shape[0] // SPAN
    heads = queries.shape[1]
    cur_q, keys, vals, inv_len, unit, own, total, exact = attend_parts(
        queries, values, prev_queries, prev_values
    )
    probs = rounded(exact)
    g_out = rounded(d_out).reshape(count, SPAN, heads, DH)
    g_probs = jnp.einsum("cqhd,ckhd->chqk", g_out, vals)
    g_vals = jnp.einsum("chqk,cqhd->ckhd", probs, g_out)
    g_lse = jnp.transpose(d_total.reshape(count, SPAN, heads), (0, 2, 1))[..., None]
    inner = jnp.sum(g_probs * exact, axis=-1, keepdims=True)
    g_scores = exact * (g_probs - inner + g_lse)
    g_scores = rounded(jnp.where(own, 0.0, g_scores))
    g_query = jnp.einsum("chqk,ckhd->cqhd", g_scores, unit)
    g_unit = jnp.einsum("chqk,cqhd->ckhd", g_scores, cur_q)
    along = jnp.sum(g_unit * keys, axis=-1, keepdims=True)
    g_keys = inv_len * g_unit - keys * (inv_len * inv_len * inv_len) * along
    g_query = g_query + g_keys[:, SPAN:]
    g_value = g_vals[:, SPAN:]
    lent_q = g_keys[:, :SPAN]
    lent_v = g_vals[:, :SPAN]
    g_query = g_query.at[:-1].add(lent_q[1:])
    g_value = g_value.at[:-1].add(lent_v[1:])
    return (
        g_query.reshape(count * SPAN, heads, DH),
        g_value.reshape(count * SPAN, heads, DH),
        lent_q[0],
        lent_v[0],
    )


def combine(outs, totals):
    stacked = jnp.stack(outs)
    logits = jnp.stack(totals)
    top = jnp.max(logits, axis=0, keepdims=True)
    expo = jnp.exp(logits - top)
    share = expo / jnp.sum(expo, axis=0, keepdims=True)
    return jnp.sum(share[..., None] * stacked, axis=0)


def widen(piece, heads):
    return piece.astype(jnp.float32).reshape(piece.shape[0], heads, DH)


def attention_branch(x_two, gain, weights, plans, nwide, width):
    tok, part_width = x_two.shape
    heads = part_width // DH
    normed, rstd = norm_forward(x_two, width)
    full = gather_features((normed * gain).astype(jnp.bfloat16))
    mixed = jnp.dot(full, weights["qk"], preferred_element_type=jnp.float32).astype(jnp.bfloat16)
    values = jnp.dot(full, weights["value"], preferred_element_type=jnp.float32).astype(
        jnp.bfloat16
    )
    rows = []
    outs = []
    totals = []
    for rnd in range(ROUNDS):
        sorted_q, sorted_v = to_sorted(mixed, values, plans[rnd], nwide)
        prev_q, prev_v = shifted((sorted_q[-SPAN:], sorted_v[-SPAN:]), "wide", 1)
        rows.append((sorted_q, sorted_v, prev_q, prev_v))
        current = rows[rnd]
        attended, total = attend(
            widen(current[0], heads),
            widen(current[1], heads),
            widen(current[2], heads),
            widen(current[3], heads),
        )
        back_o, back_t = to_initial(attended.reshape(tok, part_width), total, plans[rnd], nwide)
        outs.append(back_o.reshape(tok, heads, DH))
        totals.append(back_t)
    merged = combine(tuple(outs), tuple(totals)).reshape(tok, part_width).astype(jnp.bfloat16)
    partial_rows = jnp.einsum(
        "tk,dk->td", merged, weights["out"], preferred_element_type=jnp.float32
    )
    saved = {
        "normed": normed,
        "rstd": rstd,
        "full": full,
        "rows": rows,
        "outs": outs,
        "totals": totals,
        "merged": merged,
    }
    return (branch_sum(partial_rows), saved)


def attention_backward(grad_out, gain, saved, weights, plans, nwide, width):
    tok, part_width = grad_out.shape
    heads = part_width // DH
    back = gather_features(grad_out.astype(jnp.bfloat16))
    d_merged = jnp.dot(back, weights["out"], preferred_element_type=jnp.float32)
    grad_out_w = jnp.einsum("td,tk->dk", back, saved["merged"], preferred_element_type=jnp.float32)
    unused, pull = jax.vjp(combine, tuple(saved["outs"]), tuple(saved["totals"]))
    d_outs, d_totals = pull(d_merged.reshape(tok, heads, DH))
    sum_query = jnp.zeros((tok, part_width), jnp.float32)
    sum_value = jnp.zeros((tok, part_width), jnp.float32)
    for rnd in range(ROUNDS):
        d_out, d_total = grad_sorted(
            d_outs[rnd].reshape(tok, part_width), d_totals[rnd], plans[rnd], nwide
        )
        current = saved["rows"][rnd]
        g_query, g_value, g_prev_q, g_prev_v = attend_backward(
            widen(current[0], heads),
            widen(current[1], heads),
            widen(current[2], heads),
            widen(current[3], heads),
            d_out.reshape(tok, heads, DH),
            d_total,
        )
        next_q, next_v = shifted(
            (g_prev_q.reshape(SPAN, part_width), g_prev_v.reshape(SPAN, part_width)), "wide", -1
        )
        g_query = g_query.reshape(tok, part_width).at[tok - SPAN :].add(next_q)
        g_value = g_value.reshape(tok, part_width).at[tok - SPAN :].add(next_v)
        orig_q, orig_v = grad_initial(g_query, g_value, plans[rnd], nwide)
        sum_query = sum_query + orig_q
        sum_value = sum_value + orig_v
    d_query = sum_query.astype(jnp.bfloat16)
    d_value = sum_value.astype(jnp.bfloat16)
    grad_qk_w = jnp.einsum("td,tk->dk", saved["full"], d_query, preferred_element_type=jnp.float32)
    grad_value_w = jnp.einsum(
        "td,tk->dk", saved["full"], d_value, preferred_element_type=jnp.float32
    )
    d_full = jnp.einsum("tk,dk->td", d_query, weights["qk"], preferred_element_type=jnp.float32)
    d_full = d_full + jnp.einsum(
        "tk,dk->td", d_value, weights["value"], preferred_element_type=jnp.float32
    )
    d_normed = branch_sum(d_full)
    d_in, d_gain = norm_backward(d_normed, gain, saved["normed"], saved["rstd"], width)
    return (d_in, (grad_qk_w, grad_value_w, grad_out_w), d_gain)


def ffn_branch(y_one, gain, weights, width):
    normed, rstd = norm_forward(y_one, width)
    full = gather_features((normed * gain).astype(jnp.bfloat16))
    pre = jnp.dot(full, weights["up"], preferred_element_type=jnp.float32)
    act = smooth(pre).astype(jnp.bfloat16)
    partial_rows = jnp.einsum("tf,df->td", act, weights["down"], preferred_element_type=jnp.float32)
    saved = {"normed": normed, "rstd": rstd, "full": full, "pre": pre, "act": act}
    return (branch_sum(partial_rows), saved)


def ffn_backward(grad_out, gain, saved, weights, width):
    back = gather_features(grad_out.astype(jnp.bfloat16))
    d_act = jnp.dot(back, weights["down"], preferred_element_type=jnp.float32)
    grad_down = jnp.einsum("td,tf->df", back, saved["act"], preferred_element_type=jnp.float32)
    unused, pull = jax.vjp(smooth, saved["pre"])
    d_pre = pull(d_act)[0].astype(jnp.bfloat16)
    grad_up = jnp.einsum("td,tf->df", saved["full"], d_pre, preferred_element_type=jnp.float32)
    d_full = jnp.einsum("tf,df->td", d_pre, weights["up"], preferred_element_type=jnp.float32)
    d_normed = branch_sum(d_full)
    d_in, d_gain = norm_backward(d_normed, gain, saved["normed"], saved["rstd"], width)
    return (d_in, (grad_up, grad_down), d_gain)


def adam(grad, first, second, weight, rate):
    first_new = BETA_ONE * first + (1.0 - BETA_ONE) * grad
    second_new = BETA_TWO * second + (1.0 - BETA_TWO) * grad * grad
    step = (
        first_new
        / (1.0 - BETA_ONE**STEP)
        / (jnp.sqrt(second_new / (1.0 - BETA_TWO**STEP)) + EPSILON)
    )
    return (first_new, second_new, weight - rate * (step + DECAY * weight))


def on_device(
    x_first,
    x_second,
    grad_first,
    grad_second,
    sort_target,
    owner,
    master,
    moment_first,
    moment_second,
    gains,
    gain_first,
    gain_second,
):
    nwide = lax.axis_size("wide")
    nnar = lax.axis_size("narrow")
    me = lax.axis_index("wide")
    tok = x_first.shape[0]
    part_width = x_first.shape[1]
    width = part_width * nnar
    slots_here = master.shape[0]
    pooled = lax.all_gather(master.astype(jnp.bfloat16), "wide", axis=0, tiled=True)
    layers = unpack(pooled[owner], width, part_width)
    plans = [
        [sort_plan(sort_target[layer, rnd], me, tok) for rnd in range(ROUNDS)]
        for layer in range(LAYERS)
    ]
    x_one = x_first.astype(jnp.float32)
    x_two = x_second.astype(jnp.float32)
    kept_rows = []
    for layer in range(LAYERS):
        attn_value, attn_saved = attention_branch(
            x_two, gains[layer, 0], layers[layer], plans[layer], nwide, width
        )
        x_one = x_one + attn_value
        ffn_value, unused_saved = ffn_branch(x_one, gains[layer, 1], layers[layer], width)
        x_two = x_two + ffn_value
        kept_rows.append(attn_saved["rows"])
    grad_one = grad_first.astype(jnp.float32)
    grad_two = grad_second.astype(jnp.float32)
    top_one = x_one
    top_two = x_two
    weight_grads = [None] * LAYERS
    gain_grads = [None] * LAYERS
    for layer in reversed(range(LAYERS)):
        ffn_value, ffn_saved = ffn_branch(top_one, gains[layer, 1], layers[layer], width)
        below_two = top_two - ffn_value
        extra_one, ffn_grads, ffn_gain = ffn_backward(
            grad_two, gains[layer, 1], ffn_saved, layers[layer], width
        )
        grad_one = grad_one + extra_one
        attn_value, attn_saved = attention_branch(
            below_two, gains[layer, 0], layers[layer], plans[layer], nwide, width
        )
        below_one = top_one - attn_value
        extra_two, attn_grads, attn_gain = attention_backward(
            grad_one, gains[layer, 0], attn_saved, layers[layer], plans[layer], nwide, width
        )
        grad_two = grad_two + extra_two
        top_one = below_one
        top_two = below_two
        weight_grads[layer] = jnp.concatenate(
            [
                attn_grads[0],
                attn_grads[1],
                attn_grads[2],
                ffn_grads[0].reshape(-1, part_width),
                ffn_grads[1].reshape(-1, part_width),
            ],
            0,
        )
        gain_grads[layer] = jnp.stack([attn_gain, ffn_gain])
    tile_grads = jnp.stack(weight_grads).reshape(-1, TR, part_width)
    tile_count = tile_grads.shape[0]
    tile_of_slot = (
        jnp.full((nwide * slots_here,), -1, jnp.int32)
        .at[owner]
        .set(jnp.arange(tile_count, dtype=jnp.int32))
    )
    picked = tile_grads[jnp.maximum(tile_of_slot, 0)]
    slot_grad = lax.psum_scatter(
        jnp.where((tile_of_slot >= 0)[:, None, None], picked, 0.0),
        "wide",
        scatter_dimension=0,
        tiled=True,
    )
    slot_first, slot_second, slot_new = adam(
        slot_grad, moment_first, moment_second, master, RATE_WEIGHT
    )
    gain_grad = lax.psum(jnp.stack(gain_grads), "wide")
    gain_first_new, gain_second_new, gain_new = adam(
        gain_grad, gain_first, gain_second, gains, RATE_GAIN
    )
    return (
        x_one,
        x_two,
        grad_one,
        grad_two,
        slot_grad,
        slot_first,
        slot_second,
        slot_new,
        gain_grad,
        gain_first_new,
        gain_second_new,
        gain_new,
    )


def solution(mesh):
    in_specs = (
        P("wide", "narrow"),
        P("wide", "narrow"),
        P("wide", "narrow"),
        P("wide", "narrow"),
        P(),
        P(),
        P("wide", None, "narrow"),
        P("wide", None, "narrow"),
        P("wide", None, "narrow"),
        P(None, None, "narrow"),
        P(None, None, "narrow"),
        P(None, None, "narrow"),
    )
    out_specs = (
        P("wide", "narrow"),
        P("wide", "narrow"),
        P("wide", "narrow"),
        P("wide", "narrow"),
        P("wide", None, "narrow"),
        P("wide", None, "narrow"),
        P("wide", None, "narrow"),
        P("wide", None, "narrow"),
        P(None, None, "narrow"),
        P(None, None, "narrow"),
        P(None, None, "narrow"),
        P(None, None, "narrow"),
    )
    return jax.shard_map(
        on_device, mesh=mesh, in_specs=in_specs, out_specs=out_specs, check_vma=False
    )
```

profile of v0, /device:TPU:1, one launch (start us, length us, event | category | flops | bytes accessed | tf_op | source)
XLA Modules:
  0.0 2173.0 jit_solution(18417918101717372451)
XLA Ops:
  93.5 111.0 %all-gather.2.cloned.1.call-done = bf16[320,128,512]{2,1,0:T(8,128)(2,1)} async-done(((bf16[5,128,512]{2,1,0:T(8,128)(2,1)}), bf16[320,128,512]{2,1,0:T(8,128)(2,1)}) %all-gather.2.cloned.1.call-update) | async-done | bytes 41943056 | tf_op jit(solution)/shard_map/all_gather | solution.py:400
  204.5 16.9 gather_fusion
  244.8 8.2 all-to-all-start.6
  269.4 8.5 all-to-all-done
  284.1 8.5 all-to-all-done.4
  304.8 9.9 all-to-all-start.1
  379.8 12.4 fusion.281
  392.2 7.5 reshape.1355
  399.7 7.6 reshape.1354
  417.8 8.6 fusion.51
  433.9 7.6 reduce-scatter.17.cloned.1.call-done
  454.0 12.6 all-to-all-start.10
  498.3 8.6 all-to-all-done.8
  512.9 8.6 all-to-all-done.12
  531.8 10.2 all-to-all-start.9
  612.8 7.6 reshape.1374
  620.4 7.5 reshape.1375
  667.7 18.5 reduce-scatter.23.cloned.1.call-done
  698.4 12.7 all-to-all-start.16
  725.7 11.3 all-to-all-start.20
  753.5 8.4 all-to-all-done.18
  768.1 8.3 all-to-all-done.22
  793.3 9.9 all-to-all-start.17
  855.8 8.3 all-to-all-done.27
  959.8 10.9 all-to-all-start.30
  999.0 10.3 all-to-all-start.26
  1048.7 9.9 reshape.1462
  1063.1 9.1 copy.916
  1072.3 9.9 reshape.1463
  1108.5 12.9 reduce-scatter.31.cloned.1.call-done
  1136.4 7.7 constant_dynamic-update-slice_fusion.7
  1144.1 7.7 constant_dynamic-update-slice_fusion.6
  1168.9 12.7 all-to-all-start.32
  1196.4 11.3 all-to-all-start.34
  1224.0 8.4 all-to-all-done.37
  1239.0 8.5 all-to-all-done.39
  1263.1 9.9 all-to-all-start.33
  1328.3 7.7 all-to-all-done.43
  1430.9 11.3 all-to-all-start.46
  1470.1 7.8 all-to-all-start.42
  1501.9 9.8 reshape.1460
  1511.8 9.8 reshape.1461
  1536.9 8.0 constant_dynamic-update-slice_fusion.5
  1549.1 33.2 %pad_maximum_fusion = f32[2,11264,512]{2,1,0:T(8,128)} fusion(f32[1,11264,512]{2,1,0:T(8,128)} %bitcast.111, f32[1,11264,512]{2,1,0:T(8,128)} %bitcast.499), kind=kLoop, calls=%fused_computation.103 | loop fusion | flops 11534336 | bytes 92274688 | tf_op jit(solution)/shard_map/stack | solution.py:451
  1582.3 53.2 %gather_fusion.97 = f32[320,128,512]{2,1,0:T(8,128)} fusion(f32[176,128,512]{2,1,0:T(8,128)} %bitcast.496, s32[1024]{0:T(1024)S(1)} %copy-done.143), kind=kCustom, calls=%fused_computation.97 | custom fusion | bytes 167773440 | tf_op jit(solution)/shard_map/gather | solution.py:458
  1635.5 54.4 %broadcast_select_fusion = f32[320,128,512]{2,1,0:T(8,128)} fusion(f32[320,128,512]{2,1,0:T(8,128)} %gather_fusion.97, pred[320]{0:T(512)(128)(4,1)S(1)} %copy-done.170), kind=kLoop, calls=%fused_computation.104 | loop fusion | flops 20971520 | bytes 167772480 | tf_op jit(solution)/shard_map/jit(_where)/select_n | solution.py:460
  1695.9 169.3 %psum.189 = f32[2,2,512]{2,1,0:T(2,128)S(1)} all-reduce(f32[2,2,512]{2,1,0:T(2,128)S(1)} %pad_maximum_fusion.21), channel_id=1, replica_groups=mesh['wide'=64,'narrow'=2] {'wide'}, use_global_device_ids=true, to_apply=%region_128.129 | all-reduce | flops 2048 | bytes 16384 | tf_op jit(solution)/shard_map/psum | solution.py:468
  1867.7 293.7 %reduce-scatter.35.cloned.1.call-done = f32[5,128,512]{2,1,0:T(8,128)} async-done(((f32[320,128,512]{2,1,0:T(8,128)}), f32[5,128,512]{2,1,0:T(8,128)}) %reduce-scatter.35.cloned.1.call-update) | async-done | bytes 1310736
  (1247 shorter events, 1027.5 us)
Async XLA Ops:
  7.2 197.3 %all-gather.2.cloned.1.call-start = ((), (), s32[]{:S(2)}) async-start(), calls=%async_computation.59 | async-start | bytes 42598400 | tf_op jit(solution)/shard_map/all_gather | solution.py:400
  255.6 44.7 %collective-permute-start.1 = (bf16[64,512]{1,0:T(8,128)(2,1)}, bf16[64,512]{1,0:T(8,128)(2,1)}, u32[]{:S(2)}, u32[]{:S(2)}) collective-permute-start(bf16[64,512]{1,0:T(8,128)(2,1)} %get-tuple-element.389), channel_id=1, source_target_pairs={{126,0},{0,2},{2,4},{4,6},{6,8},{8,10},{10,12},{12,14},{14,16},{16... | collective-permute-start | bytes 196616 | tf_op jit(solution)/shard_map/ppermute | solution.py:28
  295.8 19.4 collective-permute-start.3
  299.7 44.5 %collective-permute-start.2 = (bf16[64,512]{1,0:T(8,128)(2,1)}, bf16[64,512]{1,0:T(8,128)(2,1)}, u32[]{:S(2)}, u32[]{:S(2)}) collective-permute-start(bf16[64,512]{1,0:T(8,128)(2,1)} %get-tuple-element.383), channel_id=1, source_target_pairs={{126,0},{0,2},{2,4},{4,6},{6,8},{8,10},{10,12},{12,14},{14,16},{16... | collective-permute-start | bytes 196616 | tf_op jit(solution)/shard_map/ppermute | solution.py:28
  304.8 19.6 all-to-all-start.1
  360.7 46.6 %reduce-scatter.15.cloned.1.call-start = ((), (), s32[]{:S(2)}) async-start(), calls=%async_computation.60 | async-start | bytes 786432 | tf_op jit(solution)/shard_map/reduce_scatter | solution.py:62
  378.4 63.2 %reduce-scatter.17.cloned.1.call-start = ((), (), s32[]{:S(2)}) async-start(), calls=%async_computation.61 | async-start | bytes 786432 | tf_op jit(solution)/shard_map/reduce_scatter | solution.py:62
  454.0 22.7 %all-to-all-start.10 = ((bf16[64,2,512]{2,1,0:T(2,128)(2,1)}), bf16[64,2,512]{2,1,0:T(2,128)(2,1)S(1)}, u32[]{:S(2)}, u32[]{:S(2)}) async-start(bf16[64,2,512]{2,1,0:T(2,128)(2,1)} %reshape.1361), calls=%async_computation.12 | async-start | bytes 262144 | tf_op jit(solution)/shard_map/all_to_all | solution.py:98
  483.7 43.8 %collective-permute-start.5 = (bf16[64,512]{1,0:T(8,128)(2,1)}, bf16[64,512]{1,0:T(8,128)(2,1)}, u32[]{:S(2)}, u32[]{:S(2)}) collective-permute-start(bf16[64,512]{1,0:T(8,128)(2,1)} %get-tuple-element.381), channel_id=1, source_target_pairs={{126,0},{0,2},{2,4},{4,6},{6,8},{8,10},{10,12},{12,14},{14,16},{16... | collective-permute-start | bytes 196616 | tf_op jit(solution)/shard_map/ppermute | solution.py:28
  526.8 45.1 %collective-permute-start.6 = (bf16[64,512]{1,0:T(8,128)(2,1)}, bf16[64,512]{1,0:T(8,128)(2,1)}, u32[]{:S(2)}, u32[]{:S(2)}) collective-permute-start(bf16[64,512]{1,0:T(8,128)(2,1)} %get-tuple-element.371), channel_id=1, source_target_pairs={{126,0},{0,2},{2,4},{4,6},{6,8},{8,10},{10,12},{12,14},{14,16},{16... | collective-permute-start | bytes 196616 | tf_op jit(solution)/shard_map/ppermute | solution.py:28
  531.8 20.1 all-to-all-start.9
  588.5 39.4 %reduce-scatter.19.cloned.1.call-start = ((), (), s32[]{:S(2)}) async-start(), calls=%async_computation.62 | async-start | bytes 786432 | tf_op jit(solution)/shard_map/reduce_scatter | solution.py:62
  606.2 59.7 %reduce-scatter.21.cloned.1.call-start = ((), (), s32[]{:S(2)}) async-start(), calls=%async_computation.63 | async-start | bytes 786432 | tf_op jit(solution)/shard_map/reduce_scatter | solution.py:62
  650.1 36.1 %reduce-scatter.23.cloned.1.call-start = ((), (), s32[]{:S(2)}) async-start(), calls=%async_computation.64 | async-start | bytes 786432 | tf_op jit(solution)/shard_map/reduce_scatter | solution.py:62
  698.4 27.3 %all-to-all-start.16 = ((bf16[64,2,512]{2,1,0:T(2,128)(2,1)}), bf16[64,2,512]{2,1,0:T(2,128)(2,1)}, u32[]{:S(2)}, u32[]{:S(2)}) async-start(bf16[64,2,512]{2,1,0:T(2,128)(2,1)} %reshape.1376), calls=%async_computation.21 | async-start | bytes 262144 | tf_op jit(solution)/shard_map/all_to_all | solution.py:98
  725.7 21.4 all-to-all-start.20
  739.6 44.7 %collective-permute-start.8 = (bf16[64,512]{1,0:T(8,128)(2,1)}, bf16[64,512]{1,0:T(8,128)(2,1)}, u32[]{:S(2)}, u32[]{:S(2)}) collective-permute-start(bf16[64,512]{1,0:T(8,128)(2,1)} %get-tuple-element.369), channel_id=1, source_target_pairs={{126,0},{0,2},{2,4},{4,6},{6,8},{8,10},{10,12},{12,14},{14,16},{16... | collective-permute-start | bytes 196616 | tf_op jit(solution)/shard_map/ppermute | solution.py:28
  779.8 25.9 %collective-permute-start.10 = (bf16[64,512]{1,0:T(8,128)(2,1)}, bf16[64,512]{1,0:T(8,128)(2,1)S(1)}, u32[]{:S(2)}, u32[]{:S(2)}) collective-permute-start(bf16[64,512]{1,0:T(8,128)(2,1)} %get-tuple-element.365), channel_id=1, source_target_pairs={{126,0},{0,2},{2,4},{4,6},{6,8},{8,10},{10,12},{12,14},{14,16},{16... | collective-permute-start | bytes 196616 | tf_op jit(solution)/shard_map/ppermute | solution.py:28
  783.6 37.7 %collective-permute-start.11 = (bf16[64,512]{1,0:T(8,128)(2,1)}, bf16[64,512]{1,0:T(8,128)(2,1)}, u32[]{:S(2)}, u32[]{:S(2)}) collective-permute-start(bf16[64,512]{1,0:T(8,128)(2,1)} %get-tuple-element.363), channel_id=1, source_target_pairs={{126,0},{0,2},{2,4},{4,6},{6,8},{8,10},{10,12},{12,14},{14,16},{16... | collective-permute-start | bytes 196616 | tf_op jit(solution)/shard_map/ppermute | solution.py:28
  793.3 19.6 all-to-all-start.17
  908.4 22.6 %all-to-all-start.25 = ((f32[64,2,4]{2,1,0:T(2,128)}), f32[64,2,4]{2,1,0:T(2,128)S(1)}, u32[]{:S(2)}, u32[]{:S(2)}) async-start(f32[64,2,4]{2,1,0:T(2,128)} %bitcast.60), calls=%async_computation.31 | async-start | bytes 131072 | tf_op jit(solution)/shard_map/all_to_all | solution.py:149
  919.4 36.1 %collective-permute-start.14 = (f32[64,512]{1,0:T(8,128)}, f32[64,512]{1,0:T(8,128)}, u32[]{:S(2)}, u32[]{:S(2)}) collective-permute-start(f32[64,512]{1,0:T(8,128)} %bitcast.469), channel_id=1, source_target_pairs={{2,0},{4,2},{6,4},{8,6},{10,8},{12,10},{14,12},{16,14},{18,16},{20... | collective-permute-start | bytes 393224 | tf_op jit(solution)/shard_map/ppermute | solution.py:28
  921.4 51.2 %collective-permute-start.15 = (f32[64,512]{1,0:T(8,128)}, f32[64,512]{1,0:T(8,128)}, u32[]{:S(2)}, u32[]{:S(2)}) collective-permute-start(f32[64,512]{1,0:T(8,128)} %bitcast.468), channel_id=1, source_target_pairs={{2,0},{4,2},{6,4},{8,6},{10,8},{12,10},{14,12},{16,14},{18,16},{20... | collective-permute-start | bytes 393224 | tf_op jit(solution)/shard_map/ppermute | solution.py:28
  943.8 49.1 %collective-permute-start.12 = (f32[64,512]{1,0:T(8,128)}, f32[64,512]{1,0:T(8,128)}, u32[]{:S(2)}, u32[]{:S(2)}) collective-permute-start(f32[64,512]{1,0:T(8,128)} %bitcast.471), channel_id=1, source_target_pairs={{2,0},{4,2},{6,4},{8,6},{10,8},{12,10},{14,12},{16,14},{18,16},{20... | collective-permute-start | bytes 393224 | tf_op jit(solution)/shard_map/ppermute | solution.py:28
  959.8 22.2 %all-to-all-start.30 = ((f32[64,2,512]{2,1,0:T(2,128)}), f32[64,2,512]{2,1,0:T(2,128)}, u32[]{:S(2)}, u32[]{:S(2)}) async-start(f32[64,2,512]{2,1,0:T(2,128)} %reshape.1413), calls=%async_computation.36 | async-start | bytes 524288 | tf_op jit(solution)/shard_map/all_to_all | solution.py:171
  992.3 20.6 collective-permute-start.13
  999.0 21.7 all-to-all-start.26
  1009.3 72.9 %reduce-scatter.25.cloned.1.call-start = ((), (), s32[]{:S(2)}) async-start(), calls=%async_computation.65 | async-start | bytes 786432 | tf_op jit(solution)/shard_map/reduce_scatter | solution.py:62
  1028.0 55.3 %reduce-scatter.27.cloned.1.call-start = ((), (), s32[]{:S(2)}) async-start(), calls=%async_computation.66 | async-start | bytes 786432 | tf_op jit(solution)/shard_map/reduce_scatter | solution.py:62
  1043.2 78.2 %reduce-scatter.31.cloned.1.call-start = ((), (), s32[]{:S(2)}) async-start(), calls=%async_computation.68 | async-start | bytes 786432 | tf_op jit(solution)/shard_map/reduce_scatter | solution.py:62
  1103.0 52.5 %reduce-scatter.29.cloned.1.call-start = ((), (), s32[]{:S(2)}) async-start(), calls=%async_computation.67 | async-start | bytes 786432 | tf_op jit(solution)/shard_map/reduce_scatter | solution.py:62
  1168.9 27.6 %all-to-all-start.32 = ((bf16[64,2,512]{2,1,0:T(2,128)(2,1)}), bf16[64,2,512]{2,1,0:T(2,128)(2,1)}, u32[]{:S(2)}, u32[]{:S(2)}) async-start(bf16[64,2,512]{2,1,0:T(2,128)(2,1)} %reshape.1418), calls=%async_computation.41 | async-start | bytes 262144 | tf_op jit(solution)/shard_map/all_to_all | solution.py:98
  1196.4 21.4 all-to-all-start.34
  1210.3 48.3 %collective-permute-start.16 = (bf16[64,512]{1,0:T(8,128)(2,1)}, bf16[64,512]{1,0:T(8,128)(2,1)}, u32[]{:S(2)}, u32[]{:S(2)}) collective-permute-start(bf16[64,512]{1,0:T(8,128)(2,1)} %get-tuple-element.361), channel_id=1, source_target_pairs={{126,0},{0,2},{2,4},{4,6},{6,8},{8,10},{10,12},{12,14},{14,16},{16... | collective-permute-start | bytes 196616 | tf_op jit(solution)/shard_map/ppermute | solution.py:28
  1251.9 21.1 collective-permute-start.17
  1255.6 22.3 %collective-permute-start.18 = (bf16[64,512]{1,0:T(8,128)(2,1)}, bf16[64,512]{1,0:T(8,128)(2,1)}, u32[]{:S(2)}, u32[]{:S(2)}) collective-permute-start(bf16[64,512]{1,0:T(8,128)(2,1)} %get-tuple-element.357), channel_id=1, source_target_pairs={{126,0},{0,2},{2,4},{4,6},{6,8},{8,10},{10,12},{12,14},{14,16},{16... | collective-permute-start | bytes 196616 | tf_op jit(solution)/shard_map/ppermute | solution.py:28
  1257.9 35.2 %collective-permute-start.19 = (bf16[64,512]{1,0:T(8,128)(2,1)}, bf16[64,512]{1,0:T(8,128)(2,1)}, u32[]{:S(2)}, u32[]{:S(2)}) collective-permute-start(bf16[64,512]{1,0:T(8,128)(2,1)} %get-tuple-element.355), channel_id=1, source_target_pairs={{126,0},{0,2},{2,4},{4,6},{6,8},{8,10},{10,12},{12,14},{14,16},{16... | collective-permute-start | bytes 196616 | tf_op jit(solution)/shard_map/ppermute | solution.py:28
  1263.1 19.6 all-to-all-start.33
  1379.7 22.7 %all-to-all-start.41 = ((f32[64,2,4]{2,1,0:T(2,128)}), f32[64,2,4]{2,1,0:T(2,128)S(1)}, u32[]{:S(2)}, u32[]{:S(2)}) async-start(f32[64,2,4]{2,1,0:T(2,128)} %bitcast.93), calls=%async_computation.50 | async-start | bytes 131072 | tf_op jit(solution)/shard_map/all_to_all | solution.py:149
  1390.8 35.7 %collective-permute-start.22 = (f32[64,512]{1,0:T(8,128)}, f32[64,512]{1,0:T(8,128)}, u32[]{:S(2)}, u32[]{:S(2)}) collective-permute-start(f32[64,512]{1,0:T(8,128)} %bitcast.465), channel_id=1, source_target_pairs={{2,0},{4,2},{6,4},{8,6},{10,8},{12,10},{14,12},{16,14},{18,16},{20... | collective-permute-start | bytes 393224 | tf_op jit(solution)/shard_map/ppermute | solution.py:28
  1392.9 50.5 %collective-permute-start.23 = (f32[64,512]{1,0:T(8,128)}, f32[64,512]{1,0:T(8,128)}, u32[]{:S(2)}, u32[]{:S(2)}) collective-permute-start(f32[64,512]{1,0:T(8,128)} %bitcast.464), channel_id=1, source_target_pairs={{2,0},{4,2},{6,4},{8,6},{10,8},{12,10},{14,12},{16,14},{18,16},{20... | collective-permute-start | bytes 393224 | tf_op jit(solution)/shard_map/ppermute | solution.py:28
  1415.0 46.5 %collective-permute-start.20 = (f32[64,512]{1,0:T(8,128)}, f32[64,512]{1,0:T(8,128)}, u32[]{:S(2)}, u32[]{:S(2)}) collective-permute-start(f32[64,512]{1,0:T(8,128)} %bitcast.467), channel_id=1, source_target_pairs={{2,0},{4,2},{6,4},{8,6},{10,8},{12,10},{14,12},{16,14},{18,16},{20... | collective-permute-start | bytes 393224 | tf_op jit(solution)/shard_map/ppermute | solution.py:28
  1430.9 22.6 %all-to-all-start.46 = ((f32[64,2,512]{2,1,0:T(2,128)}), f32[64,2,512]{2,1,0:T(2,128)}, u32[]{:S(2)}, u32[]{:S(2)}) async-start(f32[64,2,512]{2,1,0:T(2,128)} %reshape.1455), calls=%async_computation.55 | async-start | bytes 524288 | tf_op jit(solution)/shard_map/all_to_all | solution.py:171
  1460.8 22.8 %collective-permute-start.21 = (f32[64,512]{1,0:T(8,128)}, f32[64,512]{1,0:T(8,128)S(1)}, u32[]{:S(2)}, u32[]{:S(2)}) collective-permute-start(f32[64,512]{1,0:T(8,128)} %bitcast.466), channel_id=1, source_target_pairs={{2,0},{4,2},{6,4},{8,6},{10,8},{12,10},{14,12},{16,14},{18,16},{20... | collective-permute-start | bytes 393224 | tf_op jit(solution)/shard_map/ppermute | solution.py:28
  1470.1 19.2 all-to-all-start.42
  1489.3 38.4 %all-to-all-start.45 = ((f32[64,2,512]{2,1,0:T(2,128)}), f32[64,2,512]{2,1,0:T(2,128)}, u32[]{:S(2)}, u32[]{:S(2)}) async-start(f32[64,2,512]{2,1,0:T(2,128)} %reshape.1452), calls=%async_computation.54 | async-start | bytes 524288 | tf_op jit(solution)/shard_map/all_to_all | solution.py:164
  1496.2 194.4 %reduce-scatter.33.cloned.1.call-start = ((), (), s32[]{:S(2)}) async-start(), calls=%async_computation.69 | async-start | bytes 786432 | tf_op jit(solution)/shard_map/reduce_scatter | solution.py:62
  1533.3 628.1 %reduce-scatter.35.cloned.1.call-start = ((), (), s32[]{:S(2)}) async-start(), calls=%async_computation.70 | async-start | bytes 85196800
  (215 other events, 5914.8 us)
Sparse Core Ops, SparseCore 0:
  11.7 192.7 all-gather.1
  378.5 12.8 reduce-scatter.14
  426.5 14.9 reduce-scatter.16
  606.3 12.8 reduce-scatter.18
  650.2 15.6 reduce-scatter.20
  668.1 18.0 reduce-scatter.22
  1013.2 20.5 reduce-scatter.24
  1043.3 15.9 reduce-scatter.26
  1103.1 18.2 reduce-scatter.30
  1136.6 18.9 reduce-scatter.28
  1533.4 18.2 reduce-scatter.32
  1690.2 471.1 reduce-scatter.34
where the time goes:
time: 2200 us; the launch traced here: 2170 us
  waiting for transfers between devices  690 us (31%)
  local copies, waits for them, and re-layouts  465 us (21%)
  starting transfers between devices  364 us (17%)
  other arithmetic  261 us (12%)
  blocking collectives  256 us (12%)
  matrix products  118 us (5%)
    unnamed x13, waiting for transfers between devices  294 us
    psum x1, blocking collectives, on_device(): gain_grad = lax.psum(jnp.stack(gain_grads), 'wide')  169 us
    all_gather x1, waiting for transfers between devices, on_device(): lax.all_gather(master.astype(jnp.bfloat16), 'wide', axis=0, tiled=True)  111 us
    all_to_all x8, starting transfers between devices, to_sorted(): lax.all_to_all(mixed[plan[0]].reshape(nwide, share, -1), 'wide', split_ax...  69.1 us
    all_to_all x8, starting transfers between devices, to_initial(): lax.all_to_all(total[plan[2]].reshape(nwide, share, -1), 'wide', split_ax...  61.3 us
    all_to_all x8, waiting for transfers between devices, to_sorted(): lax.all_to_all(values[plan[0]].reshape(nwide, share, -1), 'wide', split_a...  60.9 us
    all_gather x11, blocking collectives, gather_features(): return lax.all_gather(hidden, 'narrow', axis=1, tiled=True)  54.8 us
    select_n x1, other arithmetic, on_device(): jnp.where((tile_of_slot >= 0)[:, None, None], picked, 0.0)  54.4 us
  transfers between devices with their start and end apart: 84, of which 50 were waited for; matrix products, arithmetic and copies ran while one was open for 32% of the time, Pallas kernels for 0%

commit v1 on v0

v1 whole, which is shorter than its diff:
```python
import functools

import jax
import jax.numpy as jnp
import numpy as np
from jax import lax
from jax.experimental import pallas as pl
from jax.experimental.pallas import tpu as pltpu
from jax.sharding import PartitionSpec as P

D = 1024
PART = 512
DH = 128
HN = 4
SPAN = 64
TR = 128
CAP = 5
TOK = 128
NW = 64
LAYERS = 2
ROUNDS = 2
STEP = 5
GROUPS = 8
SEND_ROWS = 18
QV_LANES = SEND_ROWS * 2 * DH
O_LANES = 17 * DH
QUAD = 4
UP, DOWN = 0, 1
OUT, QK, VALUE = 8, 9, 10
LAYER_ROWS = 176
REST_ROWS = 144

MASK_FILL = -1000000000.0
NORM_EPS = 1e-05
BETA_ONE = 0.5
BETA_TWO = 0.5
RATE_WEIGHT = 0.05
RATE_GAIN = 0.2
DECAY = 0.01
EPSILON = 1e-08

F32 = jnp.float32
BF16 = jnp.bfloat16
I32 = jnp.int32
VMEM_BYTES = 56 * 1024 * 1024


def feature_of(p):
    c0 = p >> 9
    j3 = (p >> 6) & 7
    tau = (p >> 4) & 3
    t = (p >> 1) & 7
    e = p & 1
    return t * 128 + tau * 32 + c0 * 16 + j3 * 2 + e


def tile_rows():
    tiles, parity = [], []
    for base in (24, 56):
        for tau in range(4):
            for t in range(8):
                for e in range(2):
                    tiles.append(base + t * 4 + tau)
                    parity.append(e)
    for base in (16, 0, 8):
        for t in range(8):
            for e in range(2):
                tiles.append(base + t)
                parity.append(e)
    return np.array(tiles, np.int32), np.array(parity, np.int32)


def iota(shape, dim):
    return lax.broadcasted_iota(I32, shape, dim)


def hot(mask):
    return jnp.where(mask, 1.0, 0.0).astype(BF16)


def dot(a, b, ca, cb):
    return lax.dot_general(a, b, (((ca,), (cb,)), ((), ())), preferred_element_type=F32)


def call(kernel, args, outs, grid=(1,), specs=None, out_specs=None, scratch=(), prefetch=0, name=None):
    specs = specs or {}
    out_specs = out_specs or {}
    def whole(shape):
        zeros = (0,) * len(shape)
        return pl.BlockSpec(shape, lambda *_: zeros)
    in_list = [specs.get(i, whole(a.shape)) for i, a in enumerate(args[prefetch:])]
    out_list = [out_specs.get(i, whole(o.shape)) for i, o in enumerate(outs)]
    return pl.pallas_call(
        kernel,
        out_shape=outs,
        grid_spec=pltpu.PrefetchScalarGridSpec(
            num_scalar_prefetch=prefetch,
            grid=grid,
            in_specs=in_list,
            out_specs=out_list,
            scratch_shapes=list(scratch),
        ),
        compiler_params=pltpu.CompilerParams(vmem_limit_bytes=VMEM_BYTES),
        name=name,
    )(*args)


def sds(shape, dtype):
    return jax.ShapeDtypeStruct(shape, dtype)


def norm_parts(values):
    mean = jnp.mean(values, axis=-1, keepdims=True)
    var = jnp.mean(values * values, axis=-1, keepdims=True) - mean * mean
    rstd = lax.rsqrt(var + NORM_EPS)
    return (values - mean) * rstd, rstd


def norm_back(upstream, gain, xhat, rstd):
    gh = upstream * gain
    m1 = jnp.mean(gh, axis=-1, keepdims=True)
    m2 = jnp.mean(gh * xhat, axis=-1, keepdims=True)
    return rstd * (gh - m1 - xhat * m2), jnp.sum(upstream * xhat, axis=0, keepdims=True)


def weight(ref):
    return jnp.concatenate([ref[:, 0].reshape(PART, PART), ref[:, 1].reshape(PART, PART)], 0)


def send_select(rank_row, rows):
    r = iota((rows, 1), 0)
    i = r >> 3
    g = r & 7
    want = jnp.where(i < 16, 16 * g + i, (16 * g - 18 + i) & 127)
    return hot(want == rank_row)


def place_select(place_ref, b):
    col = jnp.concatenate([place_ref[:, 2 * b : 2 * b + 1], place_ref[:, 2 * b + 1 : 2 * b + 2]], 0)
    return hot(col == iota((TOK, TOK), 1))


def pieces(col):
    hi = col.astype(BF16).astype(F32)
    rest = col - hi
    mid = rest.astype(BF16).astype(F32)
    return hi, mid, rest - mid


def spread(col, lanes):
    hi, mid, lo = pieces(col)
    k = lanes & 7
    return jnp.where(k == 0, hi, jnp.where(k == 1, mid, jnp.where(k == 2, lo, 0.0)))


def slot_rows(kind):
    r = iota((TR, 1), 0)
    e = r >> 6
    j = r & 63
    c0 = j & 1
    tau = (j >> 1) & 3
    j3 = j >> 3
    low = c0 * 16 + j3 * 2 + e
    row = jnp.where(kind == 1, low * 4 + tau, tau * 32 + low)
    return hot(row == iota((TR, TR), 1))


def route_out_kernel(kind_ref, master_ref, out_ref):
    picked = slot_rows(kind_ref[pl.program_id(0)])
    rows = dot(picked, master_ref[0].astype(BF16), 1, 0).astype(BF16)
    out_ref[:, :PART] = rows[:NW]
    out_ref[:, PART:] = rows[NW:]


def route_out(kind, master):
    return call(
        route_out_kernel,
        (kind, master),
        [sds((NW, CAP * 2 * PART), BF16)],
        grid=(CAP,),
        specs={0: pl.BlockSpec((1, TR, PART), lambda s, k: (s, 0, 0))},
        out_specs={0: pl.BlockSpec((NW, 2 * PART), lambda s, k: (0, s))},
        prefetch=1,
        name="route_out",
    )[0]


def slot_code(rows, dim):
    shape = (rows, 1) if dim == 0 else (1, rows)
    m = iota(shape, dim)
    k = m & 63
    e = (m >> 6) & 1
    s = m >> 7
    return (k * CAP + s) * 2 + e


def pick_kernel(code_ref, moved_ref, first_ref, rest_ref, last_ref):
    all_rows = jnp.concatenate([moved_ref[:, m * PART : (m + 1) * PART] for m in range(2 * CAP)], 0)
    picked = hot(code_ref[...] == slot_code(2 * CAP * NW, 1))
    rows = dot(picked, all_rows, 1, 0).astype(BF16)
    rest_ref[...] = rows[:REST_ROWS]
    first_ref[...] = rows[REST_ROWS:LAYER_ROWS]
    last_ref[...] = rows[LAYER_ROWS:]


def pick(code_col, moved):
    return call(
        pick_kernel,
        (code_col, moved),
        [sds((32, PART), BF16), sds((REST_ROWS, PART), BF16), sds((LAYER_ROWS, PART), BF16)],
        name="pick",
    )


def route_back_kernel(code_ref, rows_ref, out_ref):
    placed = hot(slot_code(2 * CAP * NW, 0) == code_ref[...])
    rows = dot(placed, rows_ref[...].astype(BF16), 1, 0).astype(BF16)
    for m in range(2 * CAP):
        out_ref[:, m * PART : (m + 1) * PART] = rows[m * NW : (m + 1) * NW]


def route_back(code_row, rows):
    return call(
        route_back_kernel, (code_row, rows), [sds((NW, CAP * 2 * PART), BF16)], name="route_back"
    )[0]


def adam(grad, first, second, weights, rate):
    first_new = BETA_ONE * first + (1.0 - BETA_ONE) * grad
    second_new = BETA_TWO * second + (1.0 - BETA_TWO) * grad * grad
    step = (
        first_new
        / (1.0 - BETA_ONE**STEP)
        / (jnp.sqrt(second_new / (1.0 - BETA_TWO**STEP)) + EPSILON)
    )
    return first_new, second_new, weights - rate * (step + DECAY * weights)


def slots_kernel(kind_ref, moved_ref, m_ref, a_ref, b_ref, grad_ref, first_ref, second_ref, new_ref):
    placed = slot_rows(kind_ref[pl.program_id(0)])
    rows = jnp.concatenate([moved_ref[:, :PART], moved_ref[:, PART:]], 0)
    grad = dot(placed, rows, 0, 0)
    grad_ref[0] = grad
    first_ref[0], second_ref[0], new_ref[0] = adam(grad, a_ref[0], b_ref[0], m_ref[0], RATE_WEIGHT)


def slots_update(kind, moved, master, first, second):
    tile = pl.BlockSpec((1, TR, PART), lambda s, k: (s, 0, 0))
    return call(
        slots_kernel,
        (kind, moved, master, first, second),
        [sds((CAP, TR, PART), F32)] * 4,
        grid=(CAP,),
        specs={0: pl.BlockSpec((NW, 2 * PART), lambda s, k: (0, s)), 1: tile, 2: tile, 3: tile},
        out_specs={i: tile for i in range(4)},
        prefetch=1,
        name="slots_update",
    )


def inner_kernel(half_ref, *refs):
    count = len(refs) // 3
    n = half_ref[0]
    feature = feature_of(iota((1, D), 1))
    mine = hot(feature == iota((PART, 1), 0) + n * PART)
    theirs = hot(feature == iota((PART, 1), 0) + (1 - n) * PART)
    for i in range(count):
        own, other, out = refs[2 * i], refs[2 * i + 1], refs[2 * count + i]
        if own.dtype == BF16:
            out[...] = dot(own[...], mine, 1, 0) + dot(other[...], theirs, 1, 0)
        else:
            total = jnp.zeros(out.shape, F32)
            for a, b in zip(pieces(own[...]), pieces(other[...])):
                total = total + (dot(a.astype(BF16), mine, 1, 0) + dot(b.astype(BF16), theirs, 1, 0))
            out[...] = total


def inner(half, pairs, name):
    flat = [a for pair in pairs for a in pair]
    outs = [sds((own.shape[0], D), F32) for own, _ in pairs]
    return call(inner_kernel, (half, *flat), outs, prefetch=1, name=name)


def outer_kernel(count, half_ref, *refs):
    n = half_ref[0]
    feature = feature_of(iota((1, D), 1))
    back = hot(feature == iota((PART, 1), 0) + n * PART)
    for i in range(count):
        total = jnp.zeros(refs[count + i].shape, F32)
        for part in pieces(refs[i][...]):
            total = total + dot(part.astype(BF16), back, 1, 1)
        refs[count + i][...] = total


def outer(half, arrays, name):
    outs = [sds((a.shape[0], PART), F32) for a in arrays]
    return call(
        functools.partial(outer_kernel, len(arrays)), (half, *arrays), outs, prefetch=1, name=name
    )


def attn_spec(index):
    return pl.BlockSpec((32, 2, 16, PART), lambda *_: (0, 0, index, 0))


def project_kernel(pending, *refs):
    if pending:
        x_ref, own_ref, other_ref, gain_ref, wq_ref, wv_ref, rank_ref, x_out, hn_out, send_out = refs
        x = x_ref[...] + (own_ref[...] + other_ref[...].astype(F32))
    else:
        x_ref, gain_ref, wq_ref, wv_ref, rank_ref, x_out, hn_out, send_out = refs
        x = x_ref[...]
    x_out[...] = x
    xhat, _ = norm_parts(x)
    hn = (xhat * gain_ref[...]).astype(BF16)
    hn_out[0] = hn[:, :PART]
    hn_out[1] = hn[:, PART:]
    q = dot(hn, weight(wq_ref), 1, 0).astype(BF16)
    v = dot(hn, weight(wv_ref), 1, 0).astype(BF16)
    qv = jnp.concatenate(
        [m[:, h * DH : (h + 1) * DH] for h in range(HN) for m in (q, v)], 1
    )
    rows = []
    for r in range(ROUNDS):
        moved = dot(send_select(rank_ref[r : r + 1, :], SEND_ROWS * GROUPS), qv, 1, 0)
        for h in range(HN):
            cols = slice(h * 2 * DH, (h + 1) * 2 * DH)
            rows.append(
                jnp.concatenate([moved[i * 8 : i * 8 + 8, cols] for i in range(SEND_ROWS)], 1)
            )
    send_out[...] = jnp.concatenate(rows, 0).astype(BF16)


def project(x, pending, gain, wq, wv, rank_row):
    args = [x, *(pending or ()), gain, wq[0], wv[0], rank_row]
    at = len(args) - 3
    return call(
        functools.partial(project_kernel, pending is not None),
        args,
        [sds((TOK, D), F32), sds((2, TOK, PART), BF16), sds((NW, QV_LANES), BF16)],
        specs={at: attn_spec(wq[1]), at + 1: attn_spec(wv[1])},
        name="project",
    )


def sorted_rows(moved, place_ref, width):
    blocks = []
    for b in range(9):
        pair = jnp.concatenate(
            [
                moved[:, (2 * b) * width : (2 * b + 1) * width],
                moved[:, (2 * b + 1) * width : (2 * b + 2) * width],
            ],
            0,
        )
        blocks.append(dot(place_select(place_ref, b), pair, 0, 0).astype(BF16))
    return blocks


def scores_of(rows):
    keys = rows[:, :DH].astype(F32)
    inv = lax.rsqrt(jnp.sum(keys * keys, axis=-1, keepdims=True) + 1e-06)
    unit = (keys * inv).astype(BF16)
    scores = jnp.concatenate(
        [
            dot(
                rows[(c + 1) * SPAN : (c + 2) * SPAN, :DH],
                unit[c * SPAN : (c + 2) * SPAN],
                1,
                1,
            )
            for c in range(16)
        ],
        0,
    )
    own = iota((1024, TOK), 1) == (iota((1024, TOK), 0) & (SPAN - 1)) + SPAN
    scores = jnp.where(own, MASK_FILL, scores)
    peak = jnp.max(scores, axis=-1, keepdims=True)
    total = peak + jnp.log(jnp.sum(jnp.exp(scores - peak), axis=-1, keepdims=True))
    exact = jnp.exp(scores - total)
    return keys, inv, unit, own, total, exact


def attend_kernel(moved_ref, place_ref, sorted_out, send_out):
    blocks = sorted_rows(moved_ref[...], place_ref, 2 * DH)
    rows = jnp.concatenate([blocks[8][SPAN:]] + blocks[:8], 0)
    sorted_out[...] = rows
    _, _, _, _, total, exact = scores_of(rows)
    probs = exact.astype(BF16)
    lanes = iota((NW, TOK), 1)
    extra = jnp.zeros((NW, TOK), F32)
    for b in range(8):
        outs = jnp.concatenate(
            [
                dot(
                    probs[c * SPAN : (c + 1) * SPAN],
                    rows[c * SPAN : (c + 2) * SPAN, DH:],
                    1,
                    0,
                )
                for c in (2 * b, 2 * b + 1)
            ],
            0,
        )
        aux = spread(total[b * TOK : (b + 1) * TOK], iota((TOK, TOK), 1))
        back = dot(
            place_select(place_ref, b), jnp.concatenate([outs, aux], 1).astype(BF16), 1, 0
        )
        for j in range(2):
            i = 2 * b + j
            part = back[j * NW : (j + 1) * NW]
            send_out[:, i * DH : (i + 1) * DH] = part[:, :DH].astype(BF16)
            extra = extra + jnp.where(lanes >> 3 == i, part[:, DH:], 0.0)
    send_out[:, 16 * DH :] = extra.astype(BF16)


def attend(moved, place):
    return call(
        attend_kernel,
        (moved, place),
        [sds((1088, 2 * DH), BF16), sds((NW, O_LANES), BF16)],
        name="attend",
    )


def merge_kernel(moved_ref, rank_row_ref, rank_col_ref, wo_ref, part_out, send_out, o_out, share_out, merged_out):
    moved = moved_ref[...]
    wide = moved.astype(F32)
    lanes = iota((TOK, TOK), 1)
    outs, logs = [], []
    for r in range(ROUNDS):
        rows = jnp.concatenate(
            [
                jnp.concatenate(
                    [
                        wide[r * 32 + h * 8 : r * 32 + h * 8 + 8, i * DH : (i + 1) * DH]
                        for h in range(HN)
                    ],
                    1,
                )
                for i in range(16)
            ],
            0,
        ).astype(BF16)
        back = dot(send_select(rank_row_ref[r : r + 1, :], TOK), rows, 0, 0)
        o_out[r] = back.astype(BF16)
        outs.append(back)
        rank = rank_col_ref[:, r : r + 1]
        logs_r = []
        for h in range(HN):
            at = hot(iota((TOK, NW), 1) == r * 32 + h * 8 + (rank >> 4))
            aux = dot(at, moved[:, 16 * DH :], 1, 0)
            logs_r.append(
                jnp.sum(jnp.where(lanes >> 3 == (rank & 15), aux, 0.0), axis=-1, keepdims=True)
            )
        logs.append(logs_r)
    merged = []
    share_all = jnp.zeros((TOK, TOK), F32)
    for h in range(HN):
        top = jnp.maximum(logs[0][h], logs[1][h])
        e0 = jnp.exp(logs[0][h] - top)
        e1 = jnp.exp(logs[1][h] - top)
        total = e0 + e1
        cols = slice(h * DH, (h + 1) * DH)
        s0, s1 = e0 / total, e1 / total
        merged.append(s0 * outs[0][:, cols] + s1 * outs[1][:, cols])
        share_all = jnp.where(lanes == h, s0, jnp.where(lanes == HN + h, s1, share_all))
    share_out[...] = share_all
    merged = jnp.concatenate(merged, 1).astype(BF16)
    merged_out[...] = merged
    partial = dot(merged, weight(wo_ref), 1, 1)
    part_out[...] = partial
    send_out[...] = partial.astype(BF16)


def merge(moved, rank_row, rank_col, wo):
    return call(
        merge_kernel,
        (moved, rank_row, rank_col, wo[0]),
        [
            sds((TOK, D), F32),
            sds((TOK, D), BF16),
            sds((ROUNDS, TOK, PART), BF16),
            sds((TOK, TOK), F32),
            sds((TOK, PART), BF16),
        ],
        specs={3: attn_spec(wo[1])},
        name="merge",
    )


def ffn_specs(rows):
    def block(index):
        return pl.BlockSpec((8, 1, 2, 64, PART), lambda c: (0, c, 0, index, 0))

    return block


def ffn_weight(ref):
    return jnp.concatenate([ref[:, 0, 0].reshape(PART, PART), ref[:, 0, 1].reshape(PART, PART)], 0)


def ffn_kernel(
    x_ref, own_ref, other_ref, gain_ref, up_ref, down_ref, y_out, hf_out, pre_out, act_out, part_out, send_out, hf_ref, acc_ref
):
    c = pl.program_id(0)

    @pl.when(c == 0)
    def _():
        y = x_ref[...] + (own_ref[...] + other_ref[...].astype(F32))
        y_out[...] = y
        xhat, _ = norm_parts(y)
        hf = (xhat * gain_ref[...]).astype(BF16)
        hf_ref[...] = hf
        hf_out[0] = hf[:, :PART]
        hf_out[1] = hf[:, PART:]
        acc_ref[...] = jnp.zeros_like(acc_ref)

    pre = dot(hf_ref[...], ffn_weight(up_ref), 1, 0)
    pre_out[...] = pre
    act = (0.5 * pre * (1.0 + lax.erf(pre * (0.5**0.5)))).astype(BF16)
    act_out[...] = act
    acc_ref[...] += dot(act, ffn_weight(down_ref), 1, 1)

    @pl.when(c == QUAD - 1)
    def _():
        part_out[...] = acc_ref[...]
        send_out[...] = acc_ref[...].astype(BF16)


def ffn(x, own, other, gain, w):
    block = ffn_specs(0)
    cols = pl.BlockSpec((TOK, PART), lambda c: (0, c))
    return call(
        ffn_kernel,
        (x, own, other, gain, w, w),
        [
            sds((TOK, D), F32),
            sds((2, TOK, PART), BF16),
            sds((TOK, QUAD * PART), F32),
            sds((TOK, QUAD * PART), BF16),
            sds((TOK, D), F32),
            sds((TOK, D), BF16),
        ],
        grid=(QUAD,),
        specs={4: block(UP), 5: block(DOWN)},
        out_specs={2: cols, 3: cols},
        scratch=[pltpu.VMEM((TOK, D), BF16), pltpu.VMEM((TOK, D), F32)],
        name="ffn",
    )


def ffn_back_kernel(pending, *refs):
    if pending:
        g_ref, own_ref, other_ref, x_ref, gain_ref = refs[:5]
        rest = refs[5:]
    else:
        g_ref = refs[0]
        rest = refs[1:]
    pre_ref, up_ref, down_ref, g_out, back_out, da_out, part_out, send_out, dgain_out, back_ref, acc_ref = rest
    c = pl.program_id(0)

    @pl.when(c == 0)
    def _():
        g = g_ref[...]
        if pending:
            xhat, rstd = norm_parts(x_ref[...])
            add, dgain = norm_back(
                own_ref[...] + other_ref[...].astype(F32), gain_ref[...], xhat, rstd
            )
            g = g + add
            dgain_out[...] = dgain
        else:
            dgain_out[...] = jnp.zeros_like(dgain_out)
        g_out[...] = g
        back = g.astype(BF16)
        back_ref[...] = back
        back_out[0] = back[:, :PART]
        back_out[1] = back[:, PART:]
        acc_ref[...] = jnp.zeros_like(acc_ref)

    d_act = dot(back_ref[...], ffn_weight(down_ref), 1, 0)
    pre = pre_ref[...]
    slope = 0.5 * (1.0 + lax.erf(pre * (0.5**0.5))) + pre * (
        jnp.exp(-0.5 * pre * pre) * np.float32(1.0 / np.sqrt(2.0 * np.pi))
    )
    d_pre = (d_act * slope).astype(BF16)
    da_out[...] = d_pre
    acc_ref[...] += dot(d_pre, ffn_weight(up_ref), 1, 1)

    @pl.when(c == QUAD - 1)
    def _():
        part_out[...] = acc_ref[...]
        send_out[...] = acc_ref[...].astype(BF16)


def ffn_back(g, pending, pre, w):
    block = ffn_specs(0)
    cols = pl.BlockSpec((TOK, PART), lambda c: (0, c))
    args = [g, *(pending or ()), pre, w, w]
    at = len(args) - 3
    return call(
        functools.partial(ffn_back_kernel, pending is not None),
        args,
        [
            sds((TOK, D), F32),
            sds((2, TOK, PART), BF16),
            sds((TOK, QUAD * PART), BF16),
            sds((TOK, D), F32),
            sds((TOK, D), BF16),
            sds((1, D), F32),
        ],
        grid=(QUAD,),
        specs={at: cols, at + 1: block(UP), at + 2: block(DOWN)},
        out_specs={2: cols},
        scratch=[pltpu.VMEM((TOK, D), BF16), pltpu.VMEM((TOK, D), F32)],
        name="ffn_back",
    )


def merge_back_kernel(
    g_ref, own_ref, other_ref, y_ref, gain_ref, wo_ref, o_ref, share_ref, rank_row_ref, rank_col_ref, g_out, back_out, send_out, dgain_out
):
    xhat, rstd = norm_parts(y_ref[...])
    add, dgain = norm_back(own_ref[...] + other_ref[...].astype(F32), gain_ref[...], xhat, rstd)
    dgain_out[...] = dgain
    g = g_ref[...] + add
    g_out[...] = g
    back = g.astype(BF16)
    back_out[0] = back[:, :PART]
    back_out[1] = back[:, PART:]
    dout = dot(back, weight(wo_ref), 1, 0)
    share = share_ref[...]
    o0 = o_ref[0].astype(F32)
    o1 = o_ref[1].astype(F32)
    lanes = iota((TOK, TOK), 1)
    parts = [[], []]
    logs = [[], []]
    for h in range(HN):
        cols = slice(h * DH, (h + 1) * DH)
        s0 = share[:, h : h + 1]
        s1 = share[:, HN + h : HN + h + 1]
        dh = dout[:, cols]
        t0 = jnp.sum(dh * o0[:, cols], axis=-1, keepdims=True)
        t1 = jnp.sum(dh * o1[:, cols], axis=-1, keepdims=True)
        mean = s0 * t0 + s1 * t1
        parts[0].append(s0 * dh)
        parts[1].append(s1 * dh)
        logs[0].append(s0 * (t0 - mean))
        logs[1].append(s1 * (t1 - mean))
    rows = []
    for r in range(ROUNDS):
        rank = rank_col_ref[:, r : r + 1]
        moved = dot(
            send_select(rank_row_ref[r : r + 1, :], TOK),
            jnp.concatenate(parts[r], 1).astype(BF16),
            1,
            0,
        )
        group = hot(iota((TOK, 8), 1) == (rank >> 4))
        for h in range(HN):
            aux = jnp.where(lanes >> 3 == (rank & 15), spread(logs[r][h], lanes), 0.0).astype(BF16)
            extra = dot(group, aux, 0, 0)
            rows.append(
                jnp.concatenate(
                    [moved[i * 8 : i * 8 + 8, h * DH : (h + 1) * DH] for i in range(16)] + [extra],
                    1,
                )
            )
    send_out[...] = jnp.concatenate(rows, 0).astype(BF16)


def merge_back(g, own, other, y, gain, wo, o, share, rank_row, rank_col):
    return call(
        merge_back_kernel,
        (g, own, other, y, gain, wo[0], o, share, rank_row, rank_col),
        [
            sds((TOK, D), F32),
            sds((2, TOK, PART), BF16),
            sds((NW, O_LANES), BF16),
            sds((1, D), F32),
        ],
        specs={5: attn_spec(wo[1])},
        name="merge_back",
    )


def attend_back_kernel(moved_ref, sorted_ref, place_ref, send_out):
    moved = moved_ref[...]
    extra = moved[:, 16 * DH :]
    lanes = iota((NW, TOK), 1)
    d_outs, d_logs = [], []
    for b in range(8):
        pair = jnp.concatenate(
            [
                jnp.concatenate(
                    [
                        moved[:, i * DH : (i + 1) * DH],
                        jnp.where(lanes >> 3 == i, extra.astype(F32), 0.0).astype(BF16),
                    ],
                    1,
                )
                for i in (2 * b, 2 * b + 1)
            ],
            0,
        )
        got = dot(place_select(place_ref, b), pair, 0, 0)
        d_outs.append(got[:, :DH].astype(BF16))
        d_logs.append(jnp.sum(got[:, DH:], axis=-1, keepdims=True))
    d_out = jnp.concatenate(d_outs, 0)
    d_log = jnp.concatenate(d_logs, 0)
    rows = sorted_ref[...]
    keys, inv, unit, own, total, exact = scores_of(rows)
    probs = exact.astype(BF16)
    g_probs = jnp.concatenate(
        [
            dot(
                d_out[c * SPAN : (c + 1) * SPAN],
                rows[c * SPAN : (c + 2) * SPAN, DH:],
                1,
                1,
            )
            for c in range(16)
        ],
        0,
    )
    inner_sum = jnp.sum(g_probs * exact, axis=-1, keepdims=True)
    g_scores = exact * (g_probs - inner_sum + d_log)
    g_scores = jnp.where(own, 0.0, g_scores).astype(BF16)
    d_query, d_unit, d_value = [], [], []
    for c in range(16):
        here = slice(c * SPAN, (c + 1) * SPAN)
        both = slice(c * SPAN, (c + 2) * SPAN)
        after = slice((c + 1) * SPAN, (c + 2) * SPAN)
        d_query.append(dot(g_scores[here], unit[both], 1, 0))
        d_unit.append(dot(g_scores[here], rows[after, :DH], 0, 0))
        d_value.append(dot(probs[here], d_out[here], 0, 0))

    def overlap(parts):
        out = [parts[0][:SPAN]]
        for c in range(15):
            out.append(parts[c][SPAN:] + parts[c + 1][:SPAN])
        out.append(parts[15][SPAN:])
        return jnp.concatenate(out, 0)

    g_unit = overlap(d_unit)
    along = jnp.sum(g_unit * keys, axis=-1, keepdims=True)
    g_keys = inv * g_unit - keys * (inv * inv * inv) * along
    g_query = jnp.concatenate([jnp.zeros((SPAN, DH), F32)] + d_query, 0) + g_keys
    grads = jnp.concatenate([g_query, overlap(d_value)], 1).astype(BF16)
    for b in range(9):
        picked = place_select(place_ref, b)
        if b < 8:
            back = dot(picked, grads[SPAN + b * TOK : SPAN + (b + 1) * TOK], 1, 0)
        else:
            lent = jnp.concatenate([jnp.zeros((SPAN, 2 * DH), BF16), grads[:SPAN]], 0)
            back = dot(picked, lent, 1, 0)
        for j in range(2):
            i = 2 * b + j
            send_out[:, i * 2 * DH : (i + 1) * 2 * DH] = back[j * NW : (j + 1) * NW].astype(BF16)


def attend_back(moved, rows, place):
    return call(
        attend_back_kernel, (moved, rows, place), [sds((NW, QV_LANES), BF16)], name="attend_back"
    )[0]


def project_back_kernel(moved_ref, rank_ref, wq_ref, wv_ref, part_out, send_out, dq_out, dv_out):
    wide = moved_ref[...].astype(F32)
    total = jnp.zeros((TOK, HN * 2 * DH), F32)
    for r in range(ROUNDS):
        rows = jnp.concatenate(
            [
                jnp.concatenate(
                    [
                        wide[r * 32 + h * 8 : r * 32 + h * 8 + 8, i * 2 * DH : (i + 1) * 2 * DH]
                        for h in range(HN)
                    ],
                    1,
                )
                for i in range(SEND_ROWS)
            ],
            0,
        ).astype(BF16)
        total = total + dot(send_select(rank_ref[r : r + 1, :], SEND_ROWS * GROUPS), rows, 0, 0)
    total = total.astype(BF16)
    d_q = jnp.concatenate([total[:, h * 2 * DH : h * 2 * DH + DH] for h in range(HN)], 1)
    d_v = jnp.concatenate([total[:, h * 2 * DH + DH : (h + 1) * 2 * DH] for h in range(HN)], 1)
    dq_out[...] = d_q
    dv_out[...] = d_v
    partial = dot(d_q, weight(wq_ref), 1, 1) + dot(d_v, weight(wv_ref), 1, 1)
    part_out[...] = partial
    send_out[...] = partial.astype(BF16)


def project_back(moved, rank_row, wq, wv):
    return call(
        project_back_kernel,
        (moved, rank_row, wq[0], wv[0]),
        [
            sds((TOK, D), F32),
            sds((TOK, D), BF16),
            sds((TOK, PART), BF16),
            sds((TOK, PART), BF16),
        ],
        specs={2: attn_spec(wq[1]), 3: attn_spec(wv[1])},
        name="project_back",
    )


def last_kernel(g_ref, own_ref, other_ref, x_ref, gain_ref, g_out, dgain_out):
    xhat, rstd = norm_parts(x_ref[...])
    add, dgain = norm_back(own_ref[...] + other_ref[...].astype(F32), gain_ref[...], xhat, rstd)
    g_out[...] = g_ref[...] + add
    dgain_out[...] = dgain


def last(g, own, other, x, gain):
    return call(
        last_kernel, (g, own, other, x, gain), [sds((TOK, D), F32), sds((1, D), F32)], name="last"
    )


def pair_dot(left_a, left_b, right_a, right_b):
    left = jnp.concatenate([left_a, left_b], 0)
    right = jnp.concatenate([right_a, right_b], 0)
    return dot(left, right, 0, 0).astype(BF16)


def ffn_grad_kernel(core_ref, hf_a, hf_b, back_a, back_b, da_a, da_b, u_a, u_b, out_ref):
    up = pair_dot(hf_a[0], hf_b[0], da_a[...], da_b[...])
    down = pair_dot(back_a[0], back_b[0], u_a[...], u_b[...])
    out_ref[:, 0, :64] = up.reshape(8, 64, PART)
    out_ref[:, 0, 64:] = down.reshape(8, 64, PART)


def ffn_grad(core, hf, back, da, act):
    half = pl.BlockSpec((1, TOK, PART), lambda c, core: (core[0], 0, 0))
    cols = pl.BlockSpec((TOK, PART), lambda c, core: (0, c))
    return call(
        ffn_grad_kernel,
        (core, *hf, *back, *da, *act),
        [sds((8, QUAD, 128, PART), BF16)],
        grid=(QUAD,),
        specs={0: half, 1: half, 2: half, 3: half, 4: cols, 5: cols, 6: cols, 7: cols},
        out_specs={0: pl.BlockSpec((8, 1, 128, PART), lambda c, core: (0, c, 0, 0))},
        prefetch=1,
        name="ffn_grad",
    )[0].reshape(32, 128, PART)


def attn_grad_kernel(count, core_ref, *refs):
    out_ref = refs[-1]
    for i in range(count):
        la, lb, ra, rb = refs[4 * i : 4 * i + 4]
        got = pair_dot(la[0], lb[0], ra[...], rb[...])
        out_ref[:, i * 16 : (i + 1) * 16] = got.reshape(32, 16, PART)


def attn_grad(core, pairs):
    half = pl.BlockSpec((1, TOK, PART), lambda i, core: (core[0], 0, 0))
    args = [a for left, right in pairs for a in (*left, *right)]
    specs = {4 * i + j: half for i in range(len(pairs)) for j in range(2)}
    return call(
        functools.partial(attn_grad_kernel, len(pairs)),
        (core, *args),
        [sds((32, 16 * len(pairs), PART), BF16)],
        specs=specs,
        prefetch=1,
        name="attn_grad",
    )[0]


def swap_narrow(values):
    return lax.ppermute(values, "narrow", [(0, 1), (1, 0)])


def with_core(values):
    other = lax.ppermute(values, "wide", [(i, i ^ 1) for i in range(NW)])
    return values, other


def to_all(values):
    return lax.all_to_all(values, "wide", split_axis=0, concat_axis=0, tiled=True)


SAME_CORE = [[2 * k + c for k in range(NW // 2)] for c in range(2)]


def summed(values):
    moved = lax.all_to_all(
        values, "wide", split_axis=0, concat_axis=0, tiled=True, axis_index_groups=SAME_CORE
    )
    return jnp.sum(moved.astype(F32), axis=0)


def gathered(rows):
    got = lax.all_gather(rows, "wide", axis=0, tiled=True)
    return got.reshape(32, 2, rows.shape[0], PART)


def on_device(
    x_first,
    x_second,
    grad_first,
    grad_second,
    sort_target,
    owner,
    master,
    moment_first,
    moment_second,
    gains,
    gain_first,
    gain_second,
):
    me = lax.axis_index("wide").astype(I32)
    half = lax.axis_index("narrow").astype(I32).reshape(1)
    core = (me & 1).reshape(1)

    tiles, parity = tile_rows()
    tile_of_row = np.concatenate([tiles, tiles + 88])
    code = owner[tile_of_row] * 2 + np.concatenate([parity, parity])
    code_col = code.reshape(-1, 1)
    code_row = code.reshape(1, -1)
    is_ffn = (np.arange(176) % 88 >= 24)[None, :]
    slots = me * CAP + jnp.arange(CAP, dtype=I32)
    kind = jnp.any((owner[None, :] == slots[:, None]) & is_ffn, axis=1).astype(I32)
    mine = lax.dynamic_slice_in_dim(sort_target, me * TOK, TOK, axis=2)
    ranks = jnp.sum((mine[:, :, None, :] < mine[:, :, :, None]).astype(I32), axis=3)
    rank_rows = [ranks[l] for l in range(LAYERS)]
    rank_cols = [ranks[l].T for l in range(LAYERS)]
    rnd, group = me >> 5, me & 7
    by_source = lax.dynamic_slice_in_dim(sort_target, rnd, 1, axis=1).reshape(LAYERS, NW, 1, TOK)
    wanted = jnp.concatenate([group * 8 + jnp.arange(8, dtype=I32), ((group * 8 - 1) & 63).reshape(1)])
    inside = (by_source >> 7) == wanted[None, None, :, None]
    low = jnp.min(jnp.where(inside, by_source & 127, TOK), axis=3)
    high = jnp.max(jnp.where(inside, by_source & 127, -1), axis=3)
    places = jnp.stack([low, high], axis=3).reshape(LAYERS, NW, SEND_ROWS)

    moved = to_all(route_out(kind, master))
    first_rows, rest_rows, last_rows = pick(code_col, moved)
    first_w = to_all(jnp.broadcast_to(first_rows[None], (NW, 32, PART))).reshape(32, 2, 32, PART)
    rest_w = gathered(rest_rows)
    last_w = gathered(last_rows)
    attn_w = [
        {"qk": (first_w, 0), "value": (first_w, 1), "out": (rest_w, OUT)},
        {"qk": (last_w, QK), "value": (last_w, VALUE), "out": (last_w, OUT)},
    ]
    ffn_w = [
        rest_w.reshape(8, QUAD, 2, REST_ROWS, PART),
        last_w.reshape(8, QUAD, 2, LAYER_ROWS, PART),
    ]

    flat_gains = gains.reshape(LAYERS * 2, PART)
    x_two, gain_rows = inner(
        half, [(x_second, swap_narrow(x_second)), (flat_gains, swap_narrow(flat_gains))], "inner_a"
    )
    x_one, g_one, g_two = inner(
        half, [(a, swap_narrow(a)) for a in (x_first, grad_first, grad_second)], "inner_b"
    )
    gain = [[gain_rows[2 * l + i].reshape(1, D) for i in range(2)] for l in range(LAYERS)]

    saved = []
    pending = None
    for l in range(LAYERS):
        w = attn_w[l]
        x_two, hn, send = project(x_two, pending, gain[l][0], w["qk"], w["value"], rank_rows[l])
        rows, send = attend(to_all(send), places[l])
        own, send, o, share, merged = merge(to_all(send), rank_rows[l], rank_cols[l], w["out"])
        x_one, hf, pre, act, own_f, send_f = ffn(x_one, own, swap_narrow(send), gain[l][1], ffn_w[l])
        pending = (own_f, swap_narrow(send_f))
        saved.append((x_two, x_one, hn, rows, o, share, merged, hf, pre, act))
    y_two = x_two + (pending[0] + pending[1].astype(F32))
    y_first, y_second = outer(half, (x_one, y_two), "outer_y")

    pending = None
    reduced = [None] * LAYERS
    dgains = [[None, None], [None, None]]
    for l in reversed(range(LAYERS)):
        w = attn_w[l]
        x_in, y_mid, hn, rows, o, share, merged, hf, pre, act = saved[l]
        g_two, back, da, own, send, dgain = ffn_back(g_two, pending, pre, ffn_w[l])
        if pending is not None:
            dgains[l + 1][0] = dgain
        other = swap_narrow(send)
        ffn_rows = summed(
            ffn_grad(core, with_core(hf), with_core(back), with_core(da), with_core(act))
        )
        g_one, back, send, dgains[l][1] = merge_back(
            g_one, own, other, y_mid, gain[l][1], w["out"], o, share, rank_rows[l], rank_cols[l]
        )
        send = attend_back(to_all(send), rows, places[l])
        own, send, dq, dv = project_back(to_all(send), rank_rows[l], w["qk"], w["value"])
        pending = (own, swap_narrow(send), x_in, gain[l][0])
        hn2 = with_core(hn)
        out_pair = (with_core(back), with_core(merged))
        in_pairs = [(hn2, with_core(dq)), (hn2, with_core(dv))]
        if l > 0:
            attn_rows = summed(attn_grad(core, [out_pair] + in_pairs))
        else:
            attn_rows = jnp.concatenate(
                [summed(attn_grad(core, [out_pair])), summed(attn_grad(core, in_pairs))], 0
            )
        reduced[l] = jnp.concatenate([ffn_rows, attn_rows], 0)
    g_two, dgains[0][0] = last(g_two, *pending)
    dx_first, dx_second = outer(half, (g_one, g_two), "outer_dx")

    back_rows = to_all(route_back(code_row, jnp.concatenate(reduced, 0).astype(BF16)))
    slot_grad, slot_first, slot_second, slot_new = slots_update(
        kind, back_rows, master, moment_first, moment_second
    )
    gain_sum = lax.psum(jnp.concatenate([d for pair in dgains for d in pair], 0), "wide")
    gain_grad = outer(half, (gain_sum,), "outer_gain")[0].reshape(LAYERS, 2, PART)
    gain_first_new, gain_second_new, gain_new = adam(
        gain_grad, gain_first, gain_second, gains, RATE_GAIN
    )
    return (
        y_first,
        y_second,
        dx_first,
        dx_second,
        slot_grad,
        slot_first,
        slot_second,
        slot_new,
        gain_grad,
        gain_first_new,
        gain_second_new,
        gain_new,
    )


def solution(mesh):
    rows = P("wide", "narrow")
    tiles = P("wide", None, "narrow")
    gains = P(None, None, "narrow")
    return jax.shard_map(
        on_device,
        mesh=mesh,
        in_specs=(rows,) * 4 + (P(), P()) + (tiles,) * 3 + (gains,) * 3,
        out_specs=(rows,) * 4 + (tiles,) * 4 + (gains,) * 4,
        check_vma=False,
    )
```

time: 2200 us -> 1050 us (0.48)
  local copies, waits for them, and re-layouts: 465 us -> 48.4 us
  waiting for transfers between devices: 690 us -> 327 us
  starting transfers between devices: 364 us -> 116 us
  other arithmetic: 261 us -> 30.3 us
  Pallas kernels: 0 us -> 133 us
  matrix products: 118 us -> 0 us
  blocking collectives: 256 us -> 360 us
    unnamed x13 -> x2, waiting for transfers between devices: 294 us -> 0.71 us
    all_to_all x48 -> x14, starting transfers between devices: 332 us -> 95.3 us  [the longest x9 68.4 us: to_all(): lax.all_to_all(values, 'wide', split_axis=0, concat_axis=0, tiled=True)]
    gather x100 -> x1, local copies, waits for them, and re-layouts: 174 us -> 2.81 us  [on_device(): code = owner[tile_of_row] * 2 + np.concatenate([parity, parity])]
    pallas_call x0 -> x31, Pallas kernels: none -> 133 us  [call(): pl.pallas_call(kernel, out_shape=outs, grid_spec=pltpu.PrefetchScalarGrid...]
    reshape x84 -> x4, local copies, waits for them, and re-layouts: 128 us -> 2.08 us  [the longest x1 0.78 us: on_device(): code_col = code.reshape(-1, 1)]
    psum x9 -> x1, blocking collectives: 202 us -> 324 us  [on_device(): lax.psum(jnp.concatenate([d for pair in dgains for d in pair], 0), 'wide')]
    dot_general x68 -> x0, matrix products: 118 us -> none  [the longest x3 13.2 us: ffn_branch(): jnp.einsum('tf,df->td', act, weights['down'], preferred_element_type=jnp....]
    ppermute x24 -> x31, waiting for transfers between devices: 0.06 us -> 93.6 us  [the longest x13 84.9 us: swap_narrow(): return lax.ppermute(values, 'narrow', [(0, 1), (1, 0)])]
  transfers between devices with their start and end apart: 84 -> 47, of which waited for: 50 -> 34; matrix products, arithmetic and copies ran while one was open for 32% -> 4% of each run, Pallas kernels for 0% -> 7%
where the time goes in v1:
time: 1050 us; the launch traced here: 1030 us
  blocking collectives  360 us (34%)
  waiting for transfers between devices  327 us (31%)
  Pallas kernels  133 us (13%)
  starting transfers between devices  116 us (11%)
  local copies, waits for them, and re-layouts  48.4 us (5%)
  other arithmetic  30.3 us (3%)
  between operations  15.2 us (1%)
    psum x1, blocking collectives, on_device(): lax.psum(jnp.concatenate([d for pair in dgains for d in pair], 0), 'wide')  324 us
    pallas_call x31, Pallas kernels, call(): pl.pallas_call(kernel, out_shape=outs, grid_spec=pltpu.PrefetchScalarGrid...  133 us
    all_to_all x5, waiting for transfers between devices, summed(): lax.all_to_all(values, 'wide', split_axis=0, concat_axis=0, tiled=True, a...  106 us
    ppermute x13, waiting for transfers between devices, swap_narrow(): return lax.ppermute(values, 'narrow', [(0, 1), (1, 0)])  84.9 us
    all_to_all x9, waiting for transfers between devices, to_all(): lax.all_to_all(values, 'wide', split_axis=0, concat_axis=0, tiled=True)  76.5 us
    all_to_all x9, starting transfers between devices, to_all(): lax.all_to_all(values, 'wide', split_axis=0, concat_axis=0, tiled=True)  68.4 us
    all_gather x2, waiting for transfers between devices, gathered(): got = lax.all_gather(rows, 'wide', axis=0, tiled=True)  50.9 us
    all_to_all x2, blocking collectives, to_all(): lax.all_to_all(values, 'wide', split_axis=0, concat_axis=0, tiled=True)  36.4 us
  transfers between devices with their start and end apart: 47, of which 34 were waited for; matrix products, arithmetic and copies ran while one was open for 4% of the time, Pallas kernels for 7%

profile of v1, /device:TPU:1, one launch (start us, length us, event | category | flops | bytes accessed | tf_op | source)
XLA Modules:
  0.0 1030.7 jit_solution(5724771734352495225)
XLA Ops:
  8.6 4.8 route_out.1
  17.5 12.5 %all-to-all-start = ((bf16[64,2,2560]{2,1,0:T(2,128)(2,1)}), bf16[64,2,2560]{2,1,0:T(2,128)(2,1)S(1)}, u32[]{:S(2)}, u32[]{:S(2)}) async-start(bf16[64,2,2560]{2,1,0:T(2,128)(2,1)} %reshape.134), calls=%async_computation | async-start | bytes 1310720 | tf_op jit(solution)/shard_map/all_to_all | solution.py:885
  33.7 11.4 %all-to-all-done = bf16[64,2,2560]{2,1,0:T(2,128)(2,1)S(1)} async-done(((bf16[64,2,2560]{2,1,0:T(2,128)(2,1)}), bf16[64,2,2560]{2,1,0:T(2,128)(2,1)S(1)}, u32[]{:S(2)}, u32[]{:S(2)}) %all-to-all-start) | async-done | bytes 655392 | tf_op jit(solution)/shard_map/all_to_all | solution.py:885
  52.1 4.6 all-to-all-start.1
  59.2 25.4 %collective-permute-done.4.refs_3_ = f32[4,512]{1,0:T(4,128)S(1)} collective-permute-done((f32[4,512]{1,0:T(4,128)S(1)}, f32[4,512]{1,0:T(4,128)S(1)}, u32[]{:S(2)}, u32[]{:S(2)}) %collective-permute-start.4) | collective-permute-done | bytes 8224 | tf_op jit(solution)/shard_map/ppermute | solution.py:876
  97.3 11.3 %all-to-all-start.2 = ((bf16[64,2,2304]{2,1,0:T(2,128)(2,1)}), bf16[64,2,2304]{2,1,0:T(2,128)(2,1)S(1)}, u32[]{:S(2)}, u32[]{:S(2)}) async-start(bf16[64,2,2304]{2,1,0:T(2,128)(2,1)} %reshape.136), calls=%async_computation.2 | async-start | bytes 1179648 | tf_op jit(solution)/shard_map/all_to_all | solution.py:885
  110.3 12.8 %all-to-all-done.2 = bf16[64,2,2304]{2,1,0:T(2,128)(2,1)S(1)} async-done(((bf16[64,2,2304]{2,1,0:T(2,128)(2,1)}), bf16[64,2,2304]{2,1,0:T(2,128)(2,1)S(1)}, u32[]{:S(2)}, u32[]{:S(2)}) %all-to-all-start.2) | async-done | bytes 589856 | tf_op jit(solution)/shard_map/all_to_all | solution.py:885
  130.9 4.6 all-to-all-start.3
  136.3 13.4 %all-to-all-done.3 = bf16[64,2,1088]{2,1,0:T(2,128)(2,1)S(1)} async-done(((bf16[64,2,1088]{2,1,0:T(2,128)(2,1)}), bf16[64,2,1088]{2,1,0:T(2,128)(2,1)S(1)}, u32[]{:S(2)}, u32[]{:S(2)}) %all-to-all-start.3) | async-done | bytes 278560 | tf_op jit(solution)/shard_map/all_to_all | solution.py:885
  157.0 8.3 collective-permute-done.refs_1_
  176.1 7.5 ffn.2
  184.0 11.2 %collective-permute-done.6.refs_2_ = bf16[128,1024]{1,0:T(8,128)(2,1)S(1)} collective-permute-done((bf16[128,1024]{1,0:T(8,128)(2,1)}, bf16[128,1024]{1,0:T(8,128)(2,1)S(1)}, u32[]{:S(2)}, u32[]{:S(2)}) %collective-permute-start.6) | collective-permute-done | bytes 262176 | tf_op jit(solution)/shard_map/ppermute | solution.py:876
  195.2 50.9 %all-gather.5.cloned.1.call-done = bf16[11264,512]{1,0:T(8,128)(2,1)} async-done(((bf16[176,512]{1,0:T(8,128)(2,1)}), bf16[11264,512]{1,0:T(8,128)(2,1)}) %all-gather.5.cloned.1.call-update) | async-done | bytes 11534352 | tf_op jit(solution)/shard_map/all_gather | solution.py:899
  252.7 5.9 all-to-all-start.4
  259.4 13.7 %all-to-all-done.4 = bf16[64,2,2304]{2,1,0:T(2,128)(2,1)S(1)} async-done(((bf16[64,2,2304]{2,1,0:T(2,128)(2,1)}), bf16[64,2,2304]{2,1,0:T(2,128)(2,1)S(1)}, u32[]{:S(2)}, u32[]{:S(2)}) %all-to-all-start.4) | async-done | bytes 589856 | tf_op jit(solution)/shard_map/all_to_all | solution.py:885
  280.9 4.4 all-to-all-start.5
  286.1 11.0 %all-to-all-done.5 = bf16[64,2,1088]{2,1,0:T(2,128)(2,1)S(1)} async-done(((bf16[64,2,1088]{2,1,0:T(2,128)(2,1)}), bf16[64,2,1088]{2,1,0:T(2,128)(2,1)S(1)}, u32[]{:S(2)}, u32[]{:S(2)}) %all-to-all-start.5) | async-done | bytes 278560 | tf_op jit(solution)/shard_map/all_to_all | solution.py:885
  303.0 6.5 collective-permute-done.7.other_ref
  310.2 7.5 ffn.3
  317.7 7.1 ffn_back.2
  326.1 5.6 collective-permute-done.9.other_ref
  332.4 4.1 merge_back.2
  338.5 18.0 %all_to_all.140 = bf16[64,2,1088]{2,1,0:T(2,128)(2,1)S(1)} all-to-all(bf16[64,2,1088]{2,1,0:T(2,128)(2,1)S(1)} %reshape.144), channel_id=1, replica_groups=mesh['wide'=64,'narrow'=2] {'wide'}, dimensions={0} | all-to-all | bytes 557056 | tf_op jit(solution)/shard_map/all_to_all | solution.py:885
  357.6 5.5 attend_back.2
  365.3 18.4 %all_to_all.141 = bf16[64,2,2304]{2,1,0:T(2,128)(2,1)S(1)} all-to-all(bf16[64,2,2304]{2,1,0:T(2,128)(2,1)S(1)} %reshape.146), channel_id=1, replica_groups=mesh['wide'=64,'narrow'=2] {'wide'}, dimensions={0} | all-to-all | bytes 1179648 | tf_op jit(solution)/shard_map/all_to_all | solution.py:885
  389.4 7.2 collective-permute-done.10.refs_2_
  397.3 7.9 ffn_back.3
  406.0 6.3 collective-permute-done.11.other_ref
  419.8 6.2 all-to-all-start.8
  430.9 6.8 all-to-all-done.8
  442.7 5.5 attend_back.3
  453.6 8.2 all-to-all-start.9
  468.7 7.5 all-to-all-done.9
  491.4 12.1 %all-to-all-done.14 = bf16[32,48,512]{2,1,0:T(8,128)(2,1)S(1)} async-done(((bf16[32,48,512]{2,1,0:T(8,128)(2,1)}), bf16[32,48,512]{2,1,0:T(8,128)(2,1)S(1)}, u32[]{:S(2)}, u32[]{:S(2)}) %all-to-all-start.14) | async-done | bytes 1572896 | tf_op jit(solution)/shard_map/all_to_all | solution.py:892
  503.5 5.3 all-to-all-start.12
  514.6 5.6 ffn_grad.3
  520.2 5.6 all-to-all-done.12
  525.7 5.1 all-to-all-start.13
  537.8 5.5 ffn_grad.2
  543.3 39.4 %all-to-all-done.13 = bf16[32,128,512]{2,1,0:T(8,128)(2,1)} async-done(((bf16[32,128,512]{2,1,0:T(8,128)(2,1)}), bf16[32,128,512]{2,1,0:T(8,128)(2,1)}, u32[]{:S(2)}, u32[]{:S(2)}) %all-to-all-start.13) | async-done | bytes 4194336 | tf_op jit(solution)/shard_map/all_to_all | solution.py:892
  582.8 8.6 all-to-all-start.10
  596.9 46.4 %all-to-all-done.10 = bf16[32,128,512]{2,1,0:T(8,128)(2,1)} async-done(((bf16[32,128,512]{2,1,0:T(8,128)(2,1)}), bf16[32,128,512]{2,1,0:T(8,128)(2,1)}, u32[]{:S(2)}, u32[]{:S(2)}) %all-to-all-start.10) | async-done | bytes 4194336 | tf_op jit(solution)/shard_map/all_to_all | solution.py:892
  652.7 10.8 %all-to-all-start.15 = ((bf16[64,2,2560]{2,1,0:T(2,128)(2,1)}), bf16[64,2,2560]{2,1,0:T(2,128)(2,1)S(1)}, u32[]{:S(2)}, u32[]{:S(2)}) async-start(bf16[64,2,2560]{2,1,0:T(2,128)(2,1)} %reshape.152), calls=%async_computation.15 | async-start | bytes 1310720 | tf_op jit(solution)/shard_map/all_to_all | solution.py:885
  666.4 4.1 outer_y.1
  670.5 8.2 collective-permute-done.12.other_ref
  682.7 323.8 %psum.7.refs_0_ = f32[4,1024]{1,0:T(4,128)} all-reduce(f32[4,1024]{1,0:T(4,128)S(1)} %pad_maximum_fusion), channel_id=1, replica_groups=mesh['wide'=64,'narrow'=2] {'wide'}, use_global_device_ids=true, to_apply=%region_9.10 | all-reduce | flops 4096 | bytes 32768 | tf_op jit(solution)/shard_map/psum | solution.py:1013
  1009.5 4.1 outer_dx.1
  1015.8 7.6 slots_update.1
  (291 shorter events, 181.4 us)
Async XLA Ops:
  17.5 27.5 %all-to-all-start = ((bf16[64,2,2560]{2,1,0:T(2,128)(2,1)}), bf16[64,2,2560]{2,1,0:T(2,128)(2,1)S(1)}, u32[]{:S(2)}, u32[]{:S(2)}) async-start(bf16[64,2,2560]{2,1,0:T(2,128)(2,1)} %reshape.134), calls=%async_computation | async-start | bytes 1310720 | tf_op jit(solution)/shard_map/all_to_all | solution.py:885
  30.0 120.8 %all-gather.3.cloned.1.call-start = ((), (), s32[]{:S(2)}) async-start(), calls=%async_computation.16 | async-start | bytes 9584640 | tf_op jit(solution)/shard_map/all_gather | solution.py:899
  49.0 197.0 %all-gather.5.cloned.1.call-start = ((), (), s32[]{:S(2)}) async-start(), calls=%async_computation.17 | async-start | bytes 11714560 | tf_op jit(solution)/shard_map/all_gather | solution.py:899
  52.1 37.5 %all-to-all-start.1 = ((bf16[64,32,512]{2,1,0:T(8,128)(2,1)}), bf16[64,32,512]{2,1,0:T(8,128)(2,1)S(1)}, u32[]{:S(2)}, u32[]{:S(2)}) async-start(bf16[64,32,512]{2,1,0:T(8,128)(2,1)} %broadcast_in_dim.33), calls=%async_computation.1 | async-start | bytes 4194304 | tf_op jit(solution)/shard_map/all_to_all | solution.py:885
  56.7 28.0 %collective-permute-start.3 = (bf16[128,512]{1,0:T(8,128)(2,1)S(1)}, bf16[128,512]{1,0:T(8,128)(2,1)S(1)}, u32[]{:S(2)}, u32[]{:S(2)}) collective-permute-start(bf16[128,512]{1,0:T(8,128)(2,1)S(1)} %copy-done.42), channel_id=1, source_target_pairs={{0,1},{1,0},{2,3},{3,2},{4,5},{5,4},{6,7},{7,6},{8,9},{9,8},{10,11... | collective-permute-start | bytes 393224 | tf_op jit(solution)/shard_map/ppermute | solution.py:876
  57.2 27.4 %collective-permute-start.4 = (f32[4,512]{1,0:T(4,128)S(1)}, f32[4,512]{1,0:T(4,128)S(1)}, u32[]{:S(2)}, u32[]{:S(2)}) collective-permute-start(f32[4,512]{1,0:T(4,128)S(1)} %reshape.114.refs_2_), channel_id=1, source_target_pairs={{0,1},{1,0},{2,3},{3,2},{4,5},{5,4},{6,7},{7,6},{8,9},{9,8},{10,11... | collective-permute-start | bytes 24584 | tf_op jit(solution)/shard_map/ppermute | solution.py:876
  97.3 25.7 %all-to-all-start.2 = ((bf16[64,2,2304]{2,1,0:T(2,128)(2,1)}), bf16[64,2,2304]{2,1,0:T(2,128)(2,1)S(1)}, u32[]{:S(2)}, u32[]{:S(2)}) async-start(bf16[64,2,2304]{2,1,0:T(2,128)(2,1)} %reshape.136), calls=%async_computation.2 | async-start | bytes 1179648 | tf_op jit(solution)/shard_map/all_to_all | solution.py:885
  130.9 18.8 %all-to-all-start.3 = ((bf16[64,2,1088]{2,1,0:T(2,128)(2,1)}), bf16[64,2,1088]{2,1,0:T(2,128)(2,1)S(1)}, u32[]{:S(2)}, u32[]{:S(2)}) async-start(bf16[64,2,1088]{2,1,0:T(2,128)(2,1)} %reshape.138), calls=%async_computation.3 | async-start | bytes 589824 | tf_op jit(solution)/shard_map/all_to_all | solution.py:885
  154.1 21.3 %collective-permute-start.5 = (bf16[128,1024]{1,0:T(8,128)(2,1)}, bf16[128,1024]{1,0:T(8,128)(2,1)S(1)}, u32[]{:S(2)}, u32[]{:S(2)}) collective-permute-start(bf16[128,1024]{1,0:T(8,128)(2,1)} %get-tuple-element.97), channel_id=1, source_target_pairs={{0,1},{1,0},{2,3},{3,2},{4,5},{5,4},{6,7},{7,6},{8,9},{9,8},{10,11... | collective-permute-start | bytes 786440 | tf_op jit(solution)/shard_map/ppermute | solution.py:876
  154.1 11.2 %collective-permute-start = (bf16[128,512]{1,0:T(8,128)(2,1)S(1)}, bf16[128,512]{1,0:T(8,128)(2,1)S(1)}, u32[]{:S(2)}, u32[]{:S(2)}) collective-permute-start(bf16[128,512]{1,0:T(8,128)(2,1)S(1)} %copy-done.44), channel_id=1, source_target_pairs={{0,1},{1,0},{2,3},{3,2},{4,5},{5,4},{6,7},{7,6},{8,9},{9,8},{10,11... | collective-permute-start | bytes 393224 | tf_op jit(solution)/shard_map/ppermute | solution.py:876
  155.5 13.1 %collective-permute-start.1 = (bf16[128,512]{1,0:T(8,128)(2,1)S(1)}, bf16[128,512]{1,0:T(8,128)(2,1)S(1)}, u32[]{:S(2)}, u32[]{:S(2)}) collective-permute-start(bf16[128,512]{1,0:T(8,128)(2,1)S(1)} %copy-done.45), channel_id=1, source_target_pairs={{0,1},{1,0},{2,3},{3,2},{4,5},{5,4},{6,7},{7,6},{8,9},{9,8},{10,11... | collective-permute-start | bytes 393224 | tf_op jit(solution)/shard_map/ppermute | solution.py:876
  155.6 16.0 %collective-permute-start.2 = (bf16[128,512]{1,0:T(8,128)(2,1)S(1)}, bf16[128,512]{1,0:T(8,128)(2,1)S(1)}, u32[]{:S(2)}, u32[]{:S(2)}) collective-permute-start(bf16[128,512]{1,0:T(8,128)(2,1)S(1)} %copy-done.46), channel_id=1, source_target_pairs={{0,1},{1,0},{2,3},{3,2},{4,5},{5,4},{6,7},{7,6},{8,9},{9,8},{10,11... | collective-permute-start | bytes 393224 | tf_op jit(solution)/shard_map/ppermute | solution.py:876
  183.6 11.6 %collective-permute-start.6 = (bf16[128,1024]{1,0:T(8,128)(2,1)}, bf16[128,1024]{1,0:T(8,128)(2,1)S(1)}, u32[]{:S(2)}, u32[]{:S(2)}) collective-permute-start(bf16[128,1024]{1,0:T(8,128)(2,1)} %get-tuple-element.101), channel_id=1, source_target_pairs={{0,1},{1,0},{2,3},{3,2},{4,5},{5,4},{6,7},{7,6},{8,9},{9,8},{10,11... | collective-permute-start | bytes 786440 | tf_op jit(solution)/shard_map/ppermute | solution.py:876
  252.7 20.3 %all-to-all-start.4 = ((bf16[64,2,2304]{2,1,0:T(2,128)(2,1)}), bf16[64,2,2304]{2,1,0:T(2,128)(2,1)S(1)}, u32[]{:S(2)}, u32[]{:S(2)}) async-start(bf16[64,2,2304]{2,1,0:T(2,128)(2,1)} %reshape.140), calls=%async_computation.4 | async-start | bytes 1179648 | tf_op jit(solution)/shard_map/all_to_all | solution.py:885
  280.9 16.2 %all-to-all-start.5 = ((bf16[64,2,1088]{2,1,0:T(2,128)(2,1)}), bf16[64,2,1088]{2,1,0:T(2,128)(2,1)S(1)}, u32[]{:S(2)}, u32[]{:S(2)}) async-start(bf16[64,2,1088]{2,1,0:T(2,128)(2,1)} %reshape.142), calls=%async_computation.5 | async-start | bytes 589824 | tf_op jit(solution)/shard_map/all_to_all | solution.py:885
  301.4 8.1 collective-permute-start.7
  324.9 6.9 collective-permute-start.9
  388.9 7.7 collective-permute-start.10
  405.2 7.1 collective-permute-start.11
  419.8 18.0 %all-to-all-start.8 = ((bf16[64,2,1088]{2,1,0:T(2,128)(2,1)}), bf16[64,2,1088]{2,1,0:T(2,128)(2,1)S(1)}, u32[]{:S(2)}, u32[]{:S(2)}) async-start(bf16[64,2,1088]{2,1,0:T(2,128)(2,1)} %reshape.148), calls=%async_computation.8 | async-start | bytes 589824 | tf_op jit(solution)/shard_map/all_to_all | solution.py:885
  426.0 2.0 collective-permute-start.17
  426.6 1.3 collective-permute-start.18
  437.7 15.8 %all-to-all-start.11 = ((bf16[32,16,512]{2,1,0:T(8,128)(2,1)}), bf16[32,16,512]{2,1,0:T(8,128)(2,1)S(1)}, u32[]{:S(2)}, u32[]{:S(2)}) async-start(bf16[32,16,512]{2,1,0:T(8,128)(2,1)} %attn_grad.3), calls=%async_computation.11 | async-start | bytes 1048576 | tf_op jit(solution)/shard_map/all_to_all | solution.py:892
  453.6 22.6 %all-to-all-start.9 = ((bf16[64,2,2304]{2,1,0:T(2,128)(2,1)}), bf16[64,2,2304]{2,1,0:T(2,128)(2,1)S(1)}, u32[]{:S(2)}, u32[]{:S(2)}) async-start(bf16[64,2,2304]{2,1,0:T(2,128)(2,1)} %reshape.150), calls=%async_computation.9 | async-start | bytes 1179648 | tf_op jit(solution)/shard_map/all_to_all | solution.py:885
  461.7 1.7 collective-permute-start.28
  462.3 1.7 collective-permute-start.26
  462.4 1.6 collective-permute-start.27
  462.8 1.4 collective-permute-start.29
  462.9 1.5 collective-permute-start.30
  476.1 27.3 %all-to-all-start.14 = ((bf16[32,48,512]{2,1,0:T(8,128)(2,1)}), bf16[32,48,512]{2,1,0:T(8,128)(2,1)S(1)}, u32[]{:S(2)}, u32[]{:S(2)}) async-start(bf16[32,48,512]{2,1,0:T(8,128)(2,1)} %attn_grad.5), calls=%async_computation.14 | async-start | bytes 3145728 | tf_op jit(solution)/shard_map/all_to_all | solution.py:892
  480.1 6.2 collective-permute-start.19
  485.6 1.7 collective-permute-start.20
  486.0 1.6 collective-permute-start.21
  503.5 22.3 %all-to-all-start.12 = ((bf16[32,32,512]{2,1,0:T(8,128)(2,1)}), bf16[32,32,512]{2,1,0:T(8,128)(2,1)S(1)}, u32[]{:S(2)}, u32[]{:S(2)}) async-start(bf16[32,32,512]{2,1,0:T(8,128)(2,1)} %attn_grad.4), calls=%async_computation.12 | async-start | bytes 2097152 | tf_op jit(solution)/shard_map/all_to_all | solution.py:892
  508.8 4.1 collective-permute-start.24
  509.8 3.1 collective-permute-start.25
  509.9 2.9 collective-permute-start.22
  510.3 2.6 collective-permute-start.23
  525.7 57.0 %all-to-all-start.13 = ((bf16[32,128,512]{2,1,0:T(8,128)(2,1)}), bf16[32,128,512]{2,1,0:T(8,128)(2,1)}, u32[]{:S(2)}, u32[]{:S(2)}) async-start(bf16[32,128,512]{2,1,0:T(8,128)(2,1)} %bitcast.90), calls=%async_computation.13 | async-start | bytes 8388608 | tf_op jit(solution)/shard_map/all_to_all | solution.py:892
  530.9 4.5 collective-permute-start.16
  533.1 3.3 collective-permute-start.15
  533.2 2.2 collective-permute-start.13
  533.6 2.7 collective-permute-start.14
  582.8 60.5 %all-to-all-start.10 = ((bf16[32,128,512]{2,1,0:T(8,128)(2,1)}), bf16[32,128,512]{2,1,0:T(8,128)(2,1)}, u32[]{:S(2)}, u32[]{:S(2)}) async-start(bf16[32,128,512]{2,1,0:T(8,128)(2,1)} %bitcast.91), calls=%async_computation.10 | async-start | bytes 8388608 | tf_op jit(solution)/shard_map/all_to_all | solution.py:892
  591.9 73.5 %collective-permute-start.8 = (bf16[128,1024]{1,0:T(8,128)(2,1)}, bf16[128,1024]{1,0:T(8,128)(2,1)S(1)}, u32[]{:S(2)}, u32[]{:S(2)}) collective-permute-start(bf16[128,1024]{1,0:T(8,128)(2,1)} %get-tuple-element.110), channel_id=1, source_target_pairs={{0,1},{1,0},{2,3},{3,2},{4,5},{5,4},{6,7},{7,6},{8,9},{9,8},{10,11... | collective-permute-start | bytes 786440 | tf_op jit(solution)/shard_map/ppermute | solution.py:876
  652.7 361.5 %all-to-all-start.15 = ((bf16[64,2,2560]{2,1,0:T(2,128)(2,1)}), bf16[64,2,2560]{2,1,0:T(2,128)(2,1)S(1)}, u32[]{:S(2)}, u32[]{:S(2)}) async-start(bf16[64,2,2560]{2,1,0:T(2,128)(2,1)} %reshape.152), calls=%async_computation.15 | async-start | bytes 1310720 | tf_op jit(solution)/shard_map/all_to_all | solution.py:885
  663.5 15.1 %collective-permute-start.12 = (bf16[128,1024]{1,0:T(8,128)(2,1)S(1)}, bf16[128,1024]{1,0:T(8,128)(2,1)S(1)}, u32[]{:S(2)}, u32[]{:S(2)}) collective-permute-start(bf16[128,1024]{1,0:T(8,128)(2,1)S(1)} %copy-done.62), channel_id=1, source_target_pairs={{0,1},{1,0},{2,3},{3,2},{4,5},{5,4},{6,7},{7,6},{8,9},{9,8},{10,11... | collective-permute-start | bytes 786440 | tf_op jit(solution)/shard_map/ppermute | solution.py:876
  679.4 334.2 %copy-start.55 = (f32[2,2,512]{2,1,0:T(2,128)S(1)}, f32[2,2,512]{2,1,0:T(2,128)}, u32[]{:S(2)}) copy-start(f32[2,2,512]{2,1,0:T(2,128)} %param.26) | copy-start | bytes 24580
  (62 other events, 748.8 us)
Sparse Core Ops, SparseCore 0:
  49.1 101.1 all-gather.2
  153.5 92.5 all-gather.4

commit v2 on v1

v2 whole, which is shorter than its diff:
```python
import functools

import jax
import jax.numpy as jnp
import numpy as np
from jax import lax
from jax.experimental import pallas as pl
from jax.experimental.pallas import tpu as pltpu
from jax.sharding import PartitionSpec as P

D = 1024
PART = 512
DH = 128
HN = 4
SPAN = 64
TR = 128
CAP = 5
TOK = 128
NW = 64
LAYERS = 2
ROUNDS = 2
STEP = 5
GROUPS = 8
QV_LANES = 5 * DH
O_LANES = 3 * DH
ROWS = NW * 8
QUAD = 4
UP, DOWN = 0, 1
LAYER_ROWS = 176
REST_ROWS = 144
EARLY_ROWS = 192
FFN_ROWS = 128

MASK_FILL = -1000000000.0
NORM_EPS = 1e-05
BETA_ONE = 0.5
BETA_TWO = 0.5
RATE_WEIGHT = 0.05
RATE_GAIN = 0.2
DECAY = 0.01
EPSILON = 1e-08

F32 = jnp.float32
BF16 = jnp.bfloat16
I32 = jnp.int32
VMEM_BYTES = 56 * 1024 * 1024


def feature_of(p):
    c0 = p >> 9
    j3 = (p >> 6) & 7
    tau = (p >> 4) & 3
    t = (p >> 1) & 7
    e = p & 1
    return t * 128 + tau * 32 + c0 * 16 + j3 * 2 + e


def tile_rows():
    tiles, parity = [], []
    for base in (24, 56):
        for tau in range(4):
            for t in range(8):
                for e in range(2):
                    tiles.append(base + t * 4 + tau)
                    parity.append(e)
    for base in (16, 0, 8):
        for t in range(8):
            for e in range(2):
                tiles.append(base + t)
                parity.append(e)
    return np.array(tiles, np.int32), np.array(parity, np.int32)


def iota(shape, dim):
    return lax.broadcasted_iota(I32, shape, dim)


def hot(mask):
    return jnp.where(mask, 1.0, 0.0).astype(BF16)


def dot(a, b, ca, cb):
    return lax.dot_general(a, b, (((ca,), (cb,)), ((), ())), preferred_element_type=F32)


def call(kernel, args, outs, grid=(1,), specs=None, out_specs=None, scratch=(), prefetch=0, name=None):
    specs = specs or {}
    out_specs = out_specs or {}
    def whole(shape):
        zeros = (0,) * len(shape)
        return pl.BlockSpec(shape, lambda *_: zeros)
    in_list = [specs.get(i, whole(a.shape)) for i, a in enumerate(args[prefetch:])]
    out_list = [out_specs.get(i, whole(o.shape)) for i, o in enumerate(outs)]
    return pl.pallas_call(
        kernel,
        out_shape=outs,
        grid_spec=pltpu.PrefetchScalarGridSpec(
            num_scalar_prefetch=prefetch,
            grid=grid,
            in_specs=in_list,
            out_specs=out_list,
            scratch_shapes=list(scratch),
        ),
        compiler_params=pltpu.CompilerParams(vmem_limit_bytes=VMEM_BYTES),
        name=name,
    )(*args)


def sds(shape, dtype):
    return jax.ShapeDtypeStruct(shape, dtype)


def norm_parts(values):
    mean = jnp.mean(values, axis=-1, keepdims=True)
    var = jnp.mean(values * values, axis=-1, keepdims=True) - mean * mean
    rstd = lax.rsqrt(var + NORM_EPS)
    return (values - mean) * rstd, rstd


def norm_back(upstream, gain, xhat, rstd):
    gh = upstream * gain
    m1 = jnp.mean(gh, axis=-1, keepdims=True)
    m2 = jnp.mean(gh * xhat, axis=-1, keepdims=True)
    return rstd * (gh - m1 - xhat * m2), jnp.sum(upstream * xhat, axis=0, keepdims=True)


def flat(ref):
    return ref[...].reshape(PART, PART)


def halves(core, first, second):
    mine = core == 0
    return jnp.where(mine, first, second), jnp.where(mine, second, first)


def into(core, full, weights):
    own, other = halves(core, full[:, :PART], full[:, PART:])
    return dot(own.astype(BF16), weights[0], 1, 0) + dot(other.astype(BF16), weights[1], 1, 0)


def out_of(core, part, weights):
    return halves(core, dot(part, weights[0], 1, 1), dot(part, weights[1], 1, 1))


def wanted(shape, dim):
    m = iota(shape, dim)
    g16 = (m >> 3) * 16
    b = m & 7
    before = (g16 - 2) & 127
    lent = before + (b >> 1)
    return (
        g16 + 2 * b,
        g16 + 2 * b + 1,
        jnp.where((b == 0) | (b == 2), lent, -1),
        jnp.where((b == 1) | (b == 3), lent, -1),
    )


def send_hots(rank_row, count=4):
    return hot(jnp.concatenate(wanted((NW, 1), 0)[:count], 0) == rank_row)


def return_hots(rank_col, count=4):
    return hot(rank_col == jnp.concatenate(wanted((1, NW), 1)[:count], 1))


def spread(col, lanes):
    hi, mid, lo = pieces(col)
    k = lanes & 7
    return jnp.where(k == 0, hi, jnp.where(k == 1, mid, jnp.where(k == 2, lo, 0.0)))


def pieces(col):
    hi = col.astype(BF16).astype(F32)
    rest = col - hi
    mid = rest.astype(BF16).astype(F32)
    return hi, mid, rest - mid


def either(lanes, even, odd):
    return jnp.where(lanes < 8, even, jnp.where(lanes < 16, odd, 0.0))


def slot_rows(kind):
    r = iota((TR, 1), 0)
    e = r >> 6
    j = r & 63
    c0 = j & 1
    tau = (j >> 1) & 3
    j3 = j >> 3
    low = c0 * 16 + j3 * 2 + e
    row = jnp.where(kind == 1, low * 4 + tau, tau * 32 + low)
    return hot(row == iota((TR, TR), 1))


def route_out_kernel(kind_ref, master_ref, out_ref):
    picked = slot_rows(kind_ref[pl.program_id(0)])
    rows = dot(picked, master_ref[0].astype(BF16), 1, 0).astype(BF16)
    out_ref[:, :PART] = rows[:NW]
    out_ref[:, PART:] = rows[NW:]


def route_out(kind, master):
    return call(
        route_out_kernel,
        (kind, master),
        [sds((NW, CAP * 2 * PART), BF16)],
        grid=(CAP,),
        specs={0: pl.BlockSpec((1, TR, PART), lambda s, k: (s, 0, 0))},
        out_specs={0: pl.BlockSpec((NW, 2 * PART), lambda s, k: (0, s))},
        prefetch=1,
        name="route_out",
    )[0]


def slot_code(rows, dim):
    shape = (rows, 1) if dim == 0 else (1, rows)
    m = iota(shape, dim)
    k = m & 63
    e = (m >> 6) & 1
    s = m >> 7
    return (k * CAP + s) * 2 + e


def pick_kernel(code_ref, moved_ref, first_ref, early_ref, late_ref):
    all_rows = jnp.concatenate([moved_ref[:, m * PART : (m + 1) * PART] for m in range(2 * CAP)], 0)
    picked = hot(code_ref[...] == slot_code(2 * CAP * NW, 1))
    rows = dot(picked, all_rows, 1, 0).astype(BF16)
    first_ref[...] = jnp.broadcast_to(rows[REST_ROWS:LAYER_ROWS][None], first_ref.shape)
    early_ref[:REST_ROWS] = rows[:REST_ROWS]
    early_ref[REST_ROWS:] = rows[LAYER_ROWS + FFN_ROWS :]
    late_ref[...] = rows[LAYER_ROWS : LAYER_ROWS + FFN_ROWS]


def pick(code_col, moved):
    return call(
        pick_kernel,
        (code_col, moved),
        [sds((32, 32, PART), BF16), sds((EARLY_ROWS, PART), BF16), sds((FFN_ROWS, PART), BF16)],
        name="pick",
    )


def route_back_kernel(code_ref, rows_ref, gains_ref, out_ref):
    placed = hot(slot_code(2 * CAP * NW, 0) == code_ref[...])
    rows = dot(placed, rows_ref[...].astype(BF16), 1, 0).astype(BF16)
    for m in range(2 * CAP):
        out_ref[:, m * PART : (m + 1) * PART] = rows[m * NW : (m + 1) * NW]
    base = 2 * CAP * PART
    for i in range(2 * LAYERS):
        row = jnp.broadcast_to(gains_ref[i : i + 1, :], (NW, D)).astype(BF16)
        out_ref[:, base + i * D : base + (i + 1) * D] = row


def route_back(code_row, rows, gains):
    return call(
        route_back_kernel,
        (code_row, rows, gains),
        [sds((NW, CAP * 2 * PART + 2 * LAYERS * D), BF16)],
        name="route_back",
    )[0]


def adam(grad, first, second, weights, rate):
    first_new = BETA_ONE * first + (1.0 - BETA_ONE) * grad
    second_new = BETA_TWO * second + (1.0 - BETA_TWO) * grad * grad
    step = (
        first_new
        / (1.0 - BETA_ONE**STEP)
        / (jnp.sqrt(second_new / (1.0 - BETA_TWO**STEP)) + EPSILON)
    )
    return first_new, second_new, weights - rate * (step + DECAY * weights)


def slots_kernel(kind_ref, moved_ref, m_ref, a_ref, b_ref, grad_ref, first_ref, second_ref, new_ref):
    placed = slot_rows(kind_ref[pl.program_id(0)])
    rows = jnp.concatenate([moved_ref[:, :PART], moved_ref[:, PART:]], 0)
    grad = dot(placed, rows, 0, 0)
    grad_ref[0] = grad
    first_ref[0], second_ref[0], new_ref[0] = adam(grad, a_ref[0], b_ref[0], m_ref[0], RATE_WEIGHT)


def slots_update(kind, moved, master, first, second):
    tile = pl.BlockSpec((1, TR, PART), lambda s, k: (s, 0, 0))
    return call(
        slots_kernel,
        (kind, moved, master, first, second),
        [sds((CAP, TR, PART), F32)] * 4,
        grid=(CAP,),
        specs={0: pl.BlockSpec((NW, 2 * PART), lambda s, k: (0, s)), 1: tile, 2: tile, 3: tile},
        out_specs={i: tile for i in range(4)},
        prefetch=1,
        name="slots_update",
    )


def inner_kernel(half_ref, *refs):
    count = len(refs) // 3
    n = half_ref[0]
    feature = feature_of(iota((1, D), 1))
    mine = hot(feature == iota((PART, 1), 0) + n * PART)
    theirs = hot(feature == iota((PART, 1), 0) + (1 - n) * PART)
    for i in range(count):
        own, other, out = refs[2 * i], refs[2 * i + 1], refs[2 * count + i]
        if own.dtype == BF16:
            out[...] = dot(own[...], mine, 1, 0) + dot(other[...], theirs, 1, 0)
        else:
            total = jnp.zeros(out.shape, F32)
            for a, b in zip(pieces(own[...]), pieces(other[...])):
                total = total + (dot(a.astype(BF16), mine, 1, 0) + dot(b.astype(BF16), theirs, 1, 0))
            out[...] = total


def inner(half, pairs, name):
    flat = [a for pair in pairs for a in pair]
    outs = [sds((own.shape[0], D), F32) for own, _ in pairs]
    return call(inner_kernel, (half, *flat), outs, prefetch=1, name=name)


def outer_kernel(count, half_ref, *refs):
    n = half_ref[0]
    feature = feature_of(iota((1, D), 1))
    back = hot(feature == iota((PART, 1), 0) + n * PART)
    for i in range(count):
        total = jnp.zeros(refs[count + i].shape, F32)
        for part in pieces(refs[i][...]):
            total = total + dot(part.astype(BF16), back, 1, 1)
        refs[count + i][...] = total


def outer(half, arrays, name):
    outs = [sds((a.shape[0], PART), F32) for a in arrays]
    return call(
        functools.partial(outer_kernel, len(arrays)), (half, *arrays), outs, prefetch=1, name=name
    )


def attn_spec(index):
    return pl.BlockSpec((32, 16, PART), lambda *_: (0, index, 0))


def attn_specs(args, places):
    specs = {}
    for at in places:
        specs[at - 1] = attn_spec(args[at][1])
        args[at] = args[at][0]
    return specs


def project_kernel(pending, core_ref, *refs):
    if pending:
        x_ref, own_ref, other_ref, *rest = refs
        x = x_ref[...] + (own_ref[...] + other_ref[...].astype(F32))
    else:
        x_ref, *rest = refs
        x = x_ref[...]
    gain_ref, q_own, q_other, v_own, v_other, rank_ref, x_out, hn_out, send_out = rest
    core = core_ref[0]
    x_out[...] = x
    xhat, _ = norm_parts(x)
    hn = xhat * gain_ref[...]
    hn_out[0] = hn[:, :PART].astype(BF16)
    hn_out[1] = hn[:, PART:].astype(BF16)
    q = into(core, hn, (flat(q_own), flat(q_other))).astype(BF16)
    v = into(core, hn, (flat(v_own), flat(v_other))).astype(BF16)
    qv = jnp.concatenate([m[:, h * DH : (h + 1) * DH] for h in range(HN) for m in (q, v)], 1)
    for r in range(ROUNDS):
        moved = dot(send_hots(rank_ref[r : r + 1, :]), qv, 1, 0)
        even, odd = moved[:NW].astype(BF16), moved[NW : 2 * NW].astype(BF16)
        lent_q, lent_v = moved[2 * NW : 3 * NW], moved[3 * NW :]
        for h in range(HN):
            rows = slice((r * HN + h) * NW, (r * HN + h + 1) * NW)
            at = h * 2 * DH
            send_out[rows, : 2 * DH] = even[:, at : at + 2 * DH]
            send_out[rows, 2 * DH : 4 * DH] = odd[:, at : at + 2 * DH]
            send_out[rows, 4 * DH :] = (
                lent_q[:, at : at + DH] + lent_v[:, at + DH : at + 2 * DH]
            ).astype(BF16)


def project(core, x, pending, gain, wq, wv, rank_row):
    args = [core, x, *(pending or ()), gain, *wq, *wv, rank_row]
    at = len(args) - 5
    specs = attn_specs(args, range(at, at + 4))
    return call(
        functools.partial(project_kernel, pending is not None),
        args,
        [sds((TOK, D), F32), sds((2, TOK, PART), BF16), sds((ROWS, QV_LANES), BF16)],
        specs=specs,
        prefetch=1,
        name="project",
    )


def scores_of(rows):
    keys = rows[:, :DH].astype(F32)
    inv = lax.rsqrt(jnp.sum(keys * keys, axis=-1, keepdims=True) + 1e-06)
    unit = (keys * inv).astype(BF16)
    scores = jnp.concatenate(
        [
            dot(
                rows[(c + 1) * SPAN : (c + 2) * SPAN, :DH],
                unit[c * SPAN : (c + 2) * SPAN],
                1,
                1,
            )
            for c in range(16)
        ],
        0,
    )
    own = iota((1024, TOK), 1) == (iota((1024, TOK), 0) & (SPAN - 1)) + SPAN
    scores = jnp.where(own, MASK_FILL, scores)
    peak = jnp.max(scores, axis=-1, keepdims=True)
    total = peak + jnp.log(jnp.sum(jnp.exp(scores - peak), axis=-1, keepdims=True))
    exact = jnp.exp(scores - total)
    return keys, inv, unit, own, total, exact


def arrive(place_row_ref, j, rows):
    count = 1024 if j < 2 else SPAN
    return dot(hot(iota((count, 1), 0) == place_row_ref[j : j + 1, :]), rows, 1, 0)


def leave(place_col_ref, j, rows):
    return dot(hot(place_col_ref[:, j : j + 1] == iota((1, rows.shape[0]), 1)), rows, 1, 0)


def attend_kernel(moved_ref, place_row_ref, place_col_ref, sorted_out, send_out):
    q_lent = arrive(place_row_ref, 2, moved_ref[:, 4 * DH :])
    v_lent = arrive(place_row_ref, 3, moved_ref[:, 4 * DH :])
    main = arrive(place_row_ref, 0, moved_ref[:, : 2 * DH]) + arrive(
        place_row_ref, 1, moved_ref[:, 2 * DH : 4 * DH]
    )
    rows = jnp.concatenate([jnp.concatenate([q_lent, v_lent], 1), main], 0).astype(BF16)
    sorted_out[...] = rows
    _, _, _, _, total, exact = scores_of(rows)
    probs = exact.astype(BF16)
    outs = jnp.concatenate(
        [
            dot(probs[c * SPAN : (c + 1) * SPAN], rows[c * SPAN : (c + 2) * SPAN, DH:], 1, 0)
            for c in range(16)
        ],
        0,
    )
    aux = spread(total, iota((1024, TOK), 1))
    both = jnp.concatenate([outs, aux], 1).astype(BF16)
    even = leave(place_col_ref, 0, both)
    odd = leave(place_col_ref, 1, both)
    send_out[:, :DH] = even[:, :DH].astype(BF16)
    send_out[:, DH : 2 * DH] = odd[:, :DH].astype(BF16)
    lanes = iota((ROWS, TOK), 1)
    send_out[:, 2 * DH :] = either(lanes, even[:, DH:], odd[:, DH:]).astype(BF16)


def attend(moved, place_row, place_col):
    return call(
        attend_kernel,
        (moved, place_row, place_col),
        [sds((1088, 2 * DH), BF16), sds((ROWS, O_LANES), BF16)],
        name="attend",
    )


def by_head(ref, r, cols):
    return jnp.concatenate(
        [ref[(r * HN + h) * NW : (r * HN + h + 1) * NW, cols] for h in range(HN)], 1
    )


def merge_kernel(
    core_ref, moved_ref, rank_col_ref, w_own, w_other, part_out, send_out, o_out, share_out, merged_out
):
    lanes = iota((TOK, TOK), 1)
    outs, logs = [], []
    for r in range(ROUNDS):
        hots = return_hots(rank_col_ref[:, r : r + 1], 2)
        aux = by_head(moved_ref, r, slice(2 * DH, 3 * DH))
        even = dot(
            hots[:, :NW], jnp.concatenate([by_head(moved_ref, r, slice(0, DH)), aux], 1), 1, 0
        )
        odd = dot(
            hots[:, NW:], jnp.concatenate([by_head(moved_ref, r, slice(DH, 2 * DH)), aux], 1), 1, 0
        )
        outs.append(even[:, :PART] + odd[:, :PART])
        o_out[r] = outs[r].astype(BF16)
        logs.append(
            [
                jnp.sum(
                    either(
                        lanes,
                        even[:, PART + h * DH : PART + (h + 1) * DH],
                        odd[:, PART + h * DH : PART + (h + 1) * DH],
                    ),
                    axis=-1,
                    keepdims=True,
                )
                for h in range(HN)
            ]
        )
    merged = []
    share_all = jnp.zeros((TOK, TOK), F32)
    for h in range(HN):
        top = jnp.maximum(logs[0][h], logs[1][h])
        e0 = jnp.exp(logs[0][h] - top)
        e1 = jnp.exp(logs[1][h] - top)
        total = e0 + e1
        cols = slice(h * DH, (h + 1) * DH)
        s0, s1 = e0 / total, e1 / total
        merged.append(s0 * outs[0][:, cols] + s1 * outs[1][:, cols])
        share_all = jnp.where(lanes == h, s0, jnp.where(lanes == HN + h, s1, share_all))
    share_out[...] = share_all
    merged = jnp.concatenate(merged, 1).astype(BF16)
    merged_out[...] = merged
    put_halves(out_of(core_ref[0], merged, (flat(w_own), flat(w_other))), part_out, send_out)


def put_halves(pair, part_out, send_out):
    for i in range(2):
        cols = slice(i * PART, (i + 1) * PART)
        part_out[:, cols] = pair[i]
        send_out[:, cols] = pair[i].astype(BF16)


def merge(core, moved, rank_col, wo):
    args = [core, moved, rank_col, *wo]
    specs = attn_specs(args, (3, 4))
    return call(
        merge_kernel,
        args,
        [
            sds((TOK, D), F32),
            sds((TOK, D), BF16),
            sds((ROUNDS, TOK, PART), BF16),
            sds((TOK, TOK), F32),
            sds((TOK, PART), BF16),
        ],
        specs=specs,
        prefetch=1,
        name="merge",
    )


def ffn_spec(index):
    return pl.BlockSpec((8, 1, 64, PART), lambda c, _: (0, c, index, 0))


def ffn_kernel(
    core_ref, x_ref, own_ref, other_ref, gain_ref, up_own, up_other, down_own, down_other,
    y_out, hf_out, pre_out, act_out, part_out, send_out, hf_ref, acc_ref
):
    c = pl.program_id(0)
    core = core_ref[0]

    @pl.when(c == 0)
    def _():
        y = x_ref[...] + (own_ref[...] + other_ref[...].astype(F32))
        y_out[...] = y
        xhat, _ = norm_parts(y)
        hf = xhat * gain_ref[...]
        first, second = hf[:, :PART], hf[:, PART:]
        hf_out[0] = first.astype(BF16)
        hf_out[1] = second.astype(BF16)
        own, other = halves(core, first, second)
        hf_ref[0] = own.astype(BF16)
        hf_ref[1] = other.astype(BF16)
        acc_ref[...] = jnp.zeros_like(acc_ref)

    pre = dot(hf_ref[0], flat(up_own), 1, 0) + dot(hf_ref[1], flat(up_other), 1, 0)
    pre_out[...] = pre
    act = (0.5 * pre * (1.0 + lax.erf(pre * (0.5**0.5)))).astype(BF16)
    act_out[...] = act
    acc_ref[0] += dot(act, flat(down_own), 1, 1)
    acc_ref[1] += dot(act, flat(down_other), 1, 1)

    @pl.when(c == QUAD - 1)
    def _():
        put_halves(halves(core, acc_ref[0], acc_ref[1]), part_out, send_out)


def ffn(core, x, own, other, gain, w):
    cols = pl.BlockSpec((TOK, PART), lambda c, _: (0, c))
    return call(
        ffn_kernel,
        (core, x, own, other, gain, w[0], w[1], w[0], w[1]),
        [
            sds((TOK, D), F32),
            sds((2, TOK, PART), BF16),
            sds((TOK, QUAD * PART), F32),
            sds((TOK, QUAD * PART), BF16),
            sds((TOK, D), F32),
            sds((TOK, D), BF16),
        ],
        grid=(QUAD,),
        specs={4: ffn_spec(UP), 5: ffn_spec(UP), 6: ffn_spec(DOWN), 7: ffn_spec(DOWN)},
        out_specs={2: cols, 3: cols},
        scratch=[pltpu.VMEM((2, TOK, PART), BF16), pltpu.VMEM((2, TOK, PART), F32)],
        prefetch=1,
        name="ffn",
    )


def ffn_back_kernel(pending, core_ref, *refs):
    if pending:
        g_ref, own_ref, other_ref, x_ref, gain_ref, *rest = refs
    else:
        g_ref, *rest = refs
    pre_ref, up_own, up_other, down_own, down_other, *rest = rest
    g_out, back_out, da_out, part_out, send_out, dgain_out, back_ref, acc_ref = rest
    c = pl.program_id(0)
    core = core_ref[0]

    @pl.when(c == 0)
    def _():
        g = g_ref[...]
        if pending:
            xhat, rstd = norm_parts(x_ref[...])
            add, dgain = norm_back(
                own_ref[...] + other_ref[...].astype(F32), gain_ref[...], xhat, rstd
            )
            g = g + add
            dgain_out[...] = dgain
        else:
            dgain_out[...] = jnp.zeros_like(dgain_out)
        g_out[...] = g
        first, second = g[:, :PART], g[:, PART:]
        back_out[0] = first.astype(BF16)
        back_out[1] = second.astype(BF16)
        own, other = halves(core, first, second)
        back_ref[0] = own.astype(BF16)
        back_ref[1] = other.astype(BF16)
        acc_ref[...] = jnp.zeros_like(acc_ref)

    d_act = dot(back_ref[0], flat(down_own), 1, 0) + dot(back_ref[1], flat(down_other), 1, 0)
    pre = pre_ref[...]
    slope = 0.5 * (1.0 + lax.erf(pre * (0.5**0.5))) + pre * (
        jnp.exp(-0.5 * pre * pre) * np.float32(1.0 / np.sqrt(2.0 * np.pi))
    )
    d_pre = (d_act * slope).astype(BF16)
    da_out[...] = d_pre
    acc_ref[0] += dot(d_pre, flat(up_own), 1, 1)
    acc_ref[1] += dot(d_pre, flat(up_other), 1, 1)

    @pl.when(c == QUAD - 1)
    def _():
        put_halves(halves(core, acc_ref[0], acc_ref[1]), part_out, send_out)


def ffn_back(core, g, pending, pre, w):
    cols = pl.BlockSpec((TOK, PART), lambda c, _: (0, c))
    args = [core, g, *(pending or ()), pre, w[0], w[1], w[0], w[1]]
    at = len(args) - 6
    specs = {at: cols}
    for i, index in enumerate((UP, UP, DOWN, DOWN)):
        specs[at + 1 + i] = ffn_spec(index)
    return call(
        functools.partial(ffn_back_kernel, pending is not None),
        args,
        [
            sds((TOK, D), F32),
            sds((2, TOK, PART), BF16),
            sds((TOK, QUAD * PART), BF16),
            sds((TOK, D), F32),
            sds((TOK, D), BF16),
            sds((1, D), F32),
        ],
        grid=(QUAD,),
        specs=specs,
        out_specs={2: cols},
        scratch=[pltpu.VMEM((2, TOK, PART), BF16), pltpu.VMEM((2, TOK, PART), F32)],
        prefetch=1,
        name="ffn_back",
    )


def merge_back_kernel(
    core_ref, g_ref, own_ref, other_ref, y_ref, gain_ref, w_own, w_other, o_ref, share_ref, rank_row_ref,
    g_out, back_out, send_out, dgain_out
):
    xhat, rstd = norm_parts(y_ref[...])
    add, dgain = norm_back(own_ref[...] + other_ref[...].astype(F32), gain_ref[...], xhat, rstd)
    dgain_out[...] = dgain
    g = g_ref[...] + add
    g_out[...] = g
    back_out[0] = g[:, :PART].astype(BF16)
    back_out[1] = g[:, PART:].astype(BF16)
    dout = into(core_ref[0], g, (flat(w_own), flat(w_other)))
    share = share_ref[...]
    o0 = o_ref[0].astype(F32)
    o1 = o_ref[1].astype(F32)
    lanes = iota((TOK, TOK), 1)
    parts = [[], []]
    logs = [[], []]
    for h in range(HN):
        cols = slice(h * DH, (h + 1) * DH)
        s0 = share[:, h : h + 1]
        s1 = share[:, HN + h : HN + h + 1]
        dh = dout[:, cols]
        t0 = jnp.sum(dh * o0[:, cols], axis=-1, keepdims=True)
        t1 = jnp.sum(dh * o1[:, cols], axis=-1, keepdims=True)
        mean = s0 * t0 + s1 * t1
        parts[0].append(s0 * dh)
        parts[1].append(s1 * dh)
        logs[0].append(spread(s0 * (t0 - mean), lanes))
        logs[1].append(spread(s1 * (t1 - mean), lanes))
    lanes = iota((NW, TOK), 1)
    for r in range(ROUNDS):
        moved = dot(
            send_hots(rank_row_ref[r : r + 1, :], 2),
            jnp.concatenate(parts[r] + logs[r], 1).astype(BF16),
            1,
            0,
        )
        even, odd = moved[:NW], moved[NW:]
        for h in range(HN):
            rows = slice((r * HN + h) * NW, (r * HN + h + 1) * NW)
            cols = slice(h * DH, (h + 1) * DH)
            aux = slice(PART + h * DH, PART + (h + 1) * DH)
            send_out[rows, :DH] = even[:, cols].astype(BF16)
            send_out[rows, DH : 2 * DH] = odd[:, cols].astype(BF16)
            send_out[rows, 2 * DH :] = either(lanes, even[:, aux], odd[:, aux]).astype(BF16)


def merge_back(core, g, own, other, y, gain, wo, o, share, rank_row):
    args = [core, g, own, other, y, gain, *wo, o, share, rank_row]
    specs = attn_specs(args, (6, 7))
    return call(
        merge_back_kernel,
        args,
        [
            sds((TOK, D), F32),
            sds((2, TOK, PART), BF16),
            sds((ROWS, O_LANES), BF16),
            sds((1, D), F32),
        ],
        specs=specs,
        prefetch=1,
        name="merge_back",
    )


def attend_back_kernel(moved_ref, sorted_ref, place_row_ref, place_col_ref, send_out):
    lanes = iota((ROWS, TOK), 1)
    aux = moved_ref[:, 2 * DH :].astype(F32)
    got = jnp.zeros((1024, 2 * DH), F32)
    for j in range(2):
        here = jnp.where(lanes >> 3 == j, aux, 0.0).astype(BF16)
        pair = jnp.concatenate([moved_ref[:, j * DH : (j + 1) * DH], here], 1)
        got = got + arrive(place_row_ref, j, pair)
    d_out = got[:, :DH].astype(BF16)
    d_log = jnp.sum(got[:, DH:], axis=-1, keepdims=True)
    rows = sorted_ref[...]
    keys, inv, unit, own, _, exact = scores_of(rows)
    probs = exact.astype(BF16)
    g_probs = jnp.concatenate(
        [
            dot(d_out[c * SPAN : (c + 1) * SPAN], rows[c * SPAN : (c + 2) * SPAN, DH:], 1, 1)
            for c in range(16)
        ],
        0,
    )
    inner_sum = jnp.sum(g_probs * exact, axis=-1, keepdims=True)
    g_scores = exact * (g_probs - inner_sum + d_log)
    g_scores = jnp.where(own, 0.0, g_scores).astype(BF16)
    d_query, d_unit, d_value = [], [], []
    for c in range(16):
        here = slice(c * SPAN, (c + 1) * SPAN)
        both = slice(c * SPAN, (c + 2) * SPAN)
        after = slice((c + 1) * SPAN, (c + 2) * SPAN)
        d_query.append(dot(g_scores[here], unit[both], 1, 0))
        d_unit.append(dot(g_scores[here], rows[after, :DH], 0, 0))
        d_value.append(dot(probs[here], d_out[here], 0, 0))

    def overlap(parts):
        out = [parts[0][:SPAN]]
        for c in range(15):
            out.append(parts[c][SPAN:] + parts[c + 1][:SPAN])
        out.append(parts[15][SPAN:])
        return jnp.concatenate(out, 0)

    g_unit = overlap(d_unit)
    along = jnp.sum(g_unit * keys, axis=-1, keepdims=True)
    g_keys = inv * g_unit - keys * (inv * inv * inv) * along
    g_query = jnp.concatenate([jnp.zeros((SPAN, DH), F32)] + d_query, 0) + g_keys
    grads = jnp.concatenate([g_query, overlap(d_value)], 1).astype(BF16)
    for j in range(2):
        cols = slice(j * 2 * DH, (j + 1) * 2 * DH)
        send_out[:, cols] = leave(place_col_ref, j, grads[SPAN:]).astype(BF16)
    lent = leave(place_col_ref, 2, grads[:SPAN, :DH]) + leave(place_col_ref, 3, grads[:SPAN, DH:])
    send_out[:, 4 * DH :] = lent.astype(BF16)


def attend_back(moved, rows, place_row, place_col):
    return call(
        attend_back_kernel,
        (moved, rows, place_row, place_col),
        [sds((ROWS, QV_LANES), BF16)],
        name="attend_back",
    )[0]


def project_back_kernel(
    core_ref, moved_ref, rank_col_ref, q_own, q_other, v_own, v_other, part_out, send_out, dq_out, dv_out
):
    total = jnp.zeros((TOK, HN * 2 * DH), F32)
    lent_q = jnp.zeros((TOK, PART), F32)
    lent_v = jnp.zeros((TOK, PART), F32)
    for r in range(ROUNDS):
        hots = return_hots(rank_col_ref[:, r : r + 1])
        total = total + dot(hots[:, :NW], by_head(moved_ref, r, slice(0, 2 * DH)), 1, 0)
        total = total + dot(hots[:, NW : 2 * NW], by_head(moved_ref, r, slice(2 * DH, 4 * DH)), 1, 0)
        lent = by_head(moved_ref, r, slice(4 * DH, 5 * DH))
        lent_q = lent_q + dot(hots[:, 2 * NW : 3 * NW], lent, 1, 0)
        lent_v = lent_v + dot(hots[:, 3 * NW :], lent, 1, 0)
    d_q = jnp.concatenate([total[:, h * 2 * DH : h * 2 * DH + DH] for h in range(HN)], 1)
    d_v = jnp.concatenate([total[:, h * 2 * DH + DH : (h + 1) * 2 * DH] for h in range(HN)], 1)
    d_q = (d_q + lent_q).astype(BF16)
    d_v = (d_v + lent_v).astype(BF16)
    dq_out[...] = d_q
    dv_out[...] = d_v
    core = core_ref[0]
    from_q = out_of(core, d_q, (flat(q_own), flat(q_other)))
    from_v = out_of(core, d_v, (flat(v_own), flat(v_other)))
    put_halves([a + b for a, b in zip(from_q, from_v)], part_out, send_out)


def project_back(core, moved, rank_col, wq, wv):
    args = [core, moved, rank_col, *wq, *wv]
    specs = attn_specs(args, range(3, 7))
    return call(
        project_back_kernel,
        args,
        [
            sds((TOK, D), F32),
            sds((TOK, D), BF16),
            sds((TOK, PART), BF16),
            sds((TOK, PART), BF16),
        ],
        specs=specs,
        prefetch=1,
        name="project_back",
    )


def last_kernel(g_ref, own_ref, other_ref, x_ref, gain_ref, g_out, dgain_out):
    xhat, rstd = norm_parts(x_ref[...])
    add, dgain = norm_back(own_ref[...] + other_ref[...].astype(F32), gain_ref[...], xhat, rstd)
    g_out[...] = g_ref[...] + add
    dgain_out[...] = dgain


def last(g, own, other, x, gain):
    return call(
        last_kernel, (g, own, other, x, gain), [sds((TOK, D), F32), sds((1, D), F32)], name="last"
    )


def pair_dot(left_a, left_b, right_a, right_b):
    left = jnp.concatenate([left_a, left_b], 0)
    right = jnp.concatenate([right_a, right_b], 0)
    return dot(left, right, 0, 0).astype(BF16)


def ffn_grad_kernel(core_ref, hf_a, hf_b, back_a, back_b, da_a, da_b, u_a, u_b, out_ref):
    up = pair_dot(hf_a[0], hf_b[0], da_a[...], da_b[...])
    down = pair_dot(back_a[0], back_b[0], u_a[...], u_b[...])
    out_ref[0, :, :64] = up.reshape(8, 64, PART)
    out_ref[0, :, 64:] = down.reshape(8, 64, PART)


def ffn_grad(core, hf, back, da, act):
    half = pl.BlockSpec((1, TOK, PART), lambda c, core: (core[0], 0, 0))
    cols = pl.BlockSpec((TOK, PART), lambda c, core: (0, c))
    return call(
        ffn_grad_kernel,
        (core, *hf, *back, *da, *act),
        [sds((QUAD, 8, 128, PART), BF16)],
        grid=(QUAD,),
        specs={0: half, 1: half, 2: half, 3: half, 4: cols, 5: cols, 6: cols, 7: cols},
        out_specs={0: pl.BlockSpec((1, 8, 128, PART), lambda c, core: (c, 0, 0, 0))},
        prefetch=1,
        name="ffn_grad",
    )[0]


def attn_grad_kernel(count, split, core_ref, *refs):
    out_ref = refs[-1]
    for i in range(count):
        la, lb, ra, rb = refs[4 * i : 4 * i + 4]
        got = pair_dot(la[0], lb[0], ra[...], rb[...])
        if split:
            got = got.reshape(8, QUAD, 16, PART)
            for tau in range(QUAD):
                out_ref[tau, :, i * 16 : (i + 1) * 16] = got[:, tau]
        else:
            out_ref[:, i * 16 : (i + 1) * 16] = got.reshape(32, 16, PART)


def attn_grad(core, pairs, split):
    half = pl.BlockSpec((1, TOK, PART), lambda i, core: (core[0], 0, 0))
    args = [a for left, right in pairs for a in (*left, *right)]
    specs = {4 * i + j: half for i in range(len(pairs)) for j in range(2)}
    return call(
        functools.partial(attn_grad_kernel, len(pairs), split),
        (core, *args),
        [sds(((QUAD, 8) if split else (32,)) + (16 * len(pairs), PART), BF16)],
        specs=specs,
        prefetch=1,
        name="attn_grad",
    )[0]


def swap_narrow(values):
    return lax.ppermute(values, "narrow", [(0, 1), (1, 0)])


def with_core(values):
    other = lax.ppermute(values, "wide", [(i, i ^ 1) for i in range(NW)])
    return values, other


def to_all(values):
    return lax.all_to_all(values, "wide", split_axis=0, concat_axis=0, tiled=True)


SAME_CORE = [[2 * k + c for k in range(NW // 2)] for c in range(2)]


def summed(values):
    return jnp.sum(to_same_core(values).astype(F32), axis=0).astype(BF16)


ALONG_X = [[hi * 8 + x * 2 + c for x in range(4)] for hi in range(8) for c in range(2)]
ACROSS_X = [[hi * 8 + x * 2 + c for hi in range(8)] for x in range(4) for c in range(2)]


def summed_along_x(values):
    return lax.psum_scatter(
        values, "wide", scatter_dimension=0, tiled=True, axis_index_groups=ALONG_X
    ).reshape(values.shape[1:])


def summed_across_x(values):
    moved = lax.all_to_all(
        values, "wide", split_axis=0, concat_axis=0, tiled=True, axis_index_groups=ACROSS_X
    )
    return jnp.sum(moved.astype(F32), axis=0).astype(BF16)


def to_same_core(values):
    return lax.all_to_all(
        values, "wide", split_axis=0, concat_axis=0, tiled=True, axis_index_groups=SAME_CORE
    )


def after(values, *others):
    return lax.optimization_barrier((values, others))[0]


def same_core_gather(rows):
    got = lax.all_gather(rows, "wide", axis=0, tiled=True, axis_index_groups=SAME_CORE)
    return got.reshape(NW // 2, rows.shape[0], PART)


def moved_rows(rows):
    return to_all(rows.reshape(NW, 8, -1)).reshape(ROWS, -1)


def on_device(
    x_first,
    x_second,
    grad_first,
    grad_second,
    sort_target,
    owner,
    master,
    moment_first,
    moment_second,
    gains,
    gain_first,
    gain_second,
):
    me = lax.axis_index("wide").astype(I32)
    half = lax.axis_index("narrow").astype(I32).reshape(1)
    core = (me & 1).reshape(1)

    tiles, parity = tile_rows()
    tile_of_row = np.concatenate([tiles, tiles + 88])
    code = owner[tile_of_row] * 2 + np.concatenate([parity, parity])
    code_col = code.reshape(-1, 1)
    code_row = code.reshape(1, -1)
    is_ffn = (np.arange(176) % 88 >= 24)[None, :]
    slots = me * CAP + jnp.arange(CAP, dtype=I32)
    kind = jnp.any((owner[None, :] == slots[:, None]) & is_ffn, axis=1).astype(I32)
    mine = lax.dynamic_slice_in_dim(sort_target, me * TOK, TOK, axis=2)
    ranks = jnp.sum((mine[:, :, None, :] < mine[:, :, :, None]).astype(I32), axis=3)
    rank_rows = [ranks[l] for l in range(LAYERS)]
    rank_cols = [ranks[l].T for l in range(LAYERS)]
    rnd, group = me >> 5, me & 7
    by_source = lax.dynamic_slice_in_dim(sort_target, rnd, 1, axis=1).reshape(LAYERS, NW, 1, TOK)
    blocks = jnp.concatenate([group * 8 + jnp.arange(8, dtype=I32), ((group * 8 - 1) & 63).reshape(1)])
    inside = (by_source >> 7) == blocks[None, None, :, None]
    low = jnp.min(jnp.where(inside, by_source & 127, TOK), axis=3)
    high = jnp.max(jnp.where(inside, by_source & 127, -1), axis=3)
    base = TOK * np.arange(8, dtype=np.int32)
    b = np.arange(8)[None, None, :]
    low9, high9 = low[:, :, 8:] - SPAN, high[:, :, 8:] - SPAN
    columns = (
        low[:, :, :8] + base,
        high[:, :, :8] + base,
        jnp.where(b == 0, low9, jnp.where(b == 2, high9, -1)),
        jnp.where(b == 1, low9, jnp.where(b == 3, high9, -1)),
    )
    place_rows = jnp.stack([c.reshape(LAYERS, ROWS) for c in columns], 1)
    place_cols = jnp.transpose(place_rows, (0, 2, 1))

    moved = to_all(route_out(kind, master))
    first_rows, early_rows, late_rows = pick(code_col, moved)
    first_w = with_core(to_same_core(first_rows))
    early_own = same_core_gather(early_rows)
    late_own = same_core_gather(late_rows)

    def rows_at(w, *indices):
        return tuple(tuple((a, index) for a in w) for index in indices)

    flat_gains = gains.reshape(LAYERS * 2, PART)
    x_two, gain_rows = inner(
        half, [(x_second, swap_narrow(x_second)), (flat_gains, swap_narrow(flat_gains))], "inner_a"
    )
    x_one, g_one, g_two = inner(
        half, [(a, swap_narrow(a)) for a in (x_first, grad_first, grad_second)], "inner_b"
    )
    x_two = after(x_two, x_one, g_one, g_two)
    gain = [[gain_rows[2 * l + i].reshape(1, D) for i in range(2)] for l in range(LAYERS)]

    saved = []
    pending = None
    w_qk, w_value = rows_at(first_w, 0, 1)
    for l in range(LAYERS):
        x_two, hn, send = project(core, x_two, pending, gain[l][0], w_qk, w_value, rank_rows[l])
        rows, send = attend(moved_rows(send), place_rows[l], place_cols[l])
        if l == 0:
            early_w = with_core(after(early_own, send))
            w_out, next_out, next_qk, next_value = rows_at(early_w, 8, 9, 10, 11)
            w_ffn = [a.reshape(8, QUAD, EARLY_ROWS, PART) for a in early_w]
        else:
            late_w = with_core(after(late_own, send))
            w_ffn = [a.reshape(8, QUAD, FFN_ROWS, PART) for a in late_w]
        own, send, o, share, merged = merge(core, moved_rows(send), rank_cols[l], w_out)
        x_one, hf, pre, act, own_f, send_f = ffn(
            core, x_one, own, swap_narrow(send), gain[l][1], w_ffn
        )
        pending = (own_f, swap_narrow(send_f))
        saved.append(
            (x_two, x_one, hn, rows, o, share, merged, hf, pre, act, w_qk, w_value, w_out, w_ffn)
        )
        w_qk, w_value, w_out = next_qk, next_value, next_out
    y_two = x_two + (pending[0] + pending[1].astype(F32))
    y_first, y_second = outer(half, (x_one, y_two), "outer_y")

    pending = None
    reduced = [None] * LAYERS
    dgains = [[None, None], [None, None]]
    for l in reversed(range(LAYERS)):
        x_in, y_mid, hn, rows, o, share, merged, hf, pre, act, w_qk, w_value, w_out, w_ffn = saved[l]
        g_two, back, da, own, send, dgain = ffn_back(core, g_two, pending, pre, w_ffn)
        if l == 0:
            dgains[1][0] = dgain
        other = swap_narrow(send)
        ffn_part = ffn_grad(core, with_core(hf), with_core(back), with_core(da), with_core(act))
        other = after(other, ffn_part)
        ffn_part = summed_along_x(ffn_part)
        if l == 0:
            other = after(other, ffn_rows)
        g_one, back, send, dgains[l][1] = merge_back(
            core, g_one, own, other, y_mid, gain[l][1], w_out, o, share, rank_rows[l]
        )
        send = attend_back(moved_rows(send), rows, place_rows[l], place_cols[l])
        arrived = moved_rows(send)
        own, send, dq, dv = project_back(core, arrived, rank_cols[l], w_qk, w_value)
        other = swap_narrow(send)
        hn2 = with_core(hn)
        pairs = [(with_core(back), with_core(merged)), (hn2, with_core(dq)), (hn2, with_core(dv))]
        attn_part = attn_grad(core, pairs, l > 0)
        if l > 0:
            other = after(other, attn_part)
            ffn_rows = summed_across_x(after(ffn_part, send))
            attn_part = summed_along_x(attn_part)
            attn_before = attn_part
        else:
            both = jnp.concatenate([after(ffn_part, arrived), after(attn_before, arrived)], 1)
            both = summed_across_x(both)
            attn_rows = summed(attn_part)
        pending = (own, other, x_in, gain[l][0])
    reduced = (both[:FFN_ROWS], attn_rows, ffn_rows, both[FFN_ROWS:])
    g_two, dgains[0][0] = last(g_two, *pending)
    dx_first, dx_second = outer(half, (g_one, g_two), "outer_dx")

    back_rows = to_all(
        route_back(
            code_row,
            jnp.concatenate(reduced, 0),
            jnp.concatenate([d for pair in dgains for d in pair], 0),
        )
    )
    slot_grad, slot_first, slot_second, slot_new = slots_update(
        kind, back_rows, master, moment_first, moment_second
    )
    gain_sum = jnp.sum(back_rows[:, CAP * 2 * PART :].astype(F32), axis=0).reshape(2 * LAYERS, D)
    gain_grad = outer(half, (gain_sum,), "outer_gain")[0].reshape(LAYERS, 2, PART)
    gain_first_new, gain_second_new, gain_new = adam(
        gain_grad, gain_first, gain_second, gains, RATE_GAIN
    )
    return (
        y_first,
        y_second,
        dx_first,
        dx_second,
        slot_grad,
        slot_first,
        slot_second,
        slot_new,
        gain_grad,
        gain_first_new,
        gain_second_new,
        gain_new,
    )


def solution(mesh):
    rows = P("wide", "narrow")
    tiles = P("wide", None, "narrow")
    gains = P(None, None, "narrow")
    return jax.shard_map(
        on_device,
        mesh=mesh,
        in_specs=(rows,) * 4 + (P(), P()) + (tiles,) * 3 + (gains,) * 3,
        out_specs=(rows,) * 4 + (tiles,) * 4 + (gains,) * 4,
        check_vma=False,
    )
```

time: 1050 us -> 612 us (0.58)
  the two profiles are of different devices: /device:TPU:1 before, /device:TPU:13 now
where the time goes in v2:
time: 612 us; the launch traced here: 601 us
  waiting for transfers between devices  212 us (35%)
  Pallas kernels  134 us (22%)
  starting transfers between devices  98.2 us (16%)
  blocking collectives  79.1 us (13%)
  local copies, waits for them, and re-layouts  44.2 us (7%)
  other arithmetic  17.9 us (3%)
  between operations  15 us (2%)
    pallas_call x30, Pallas kernels, call(): pl.pallas_call(kernel, out_shape=outs, grid_spec=pltpu.PrefetchScalarGrid...  134 us
    ppermute x13, waiting for transfers between devices, swap_narrow(): return lax.ppermute(values, 'narrow', [(0, 1), (1, 0)])  91.9 us
    all_to_all x4, blocking collectives, to_all(): lax.all_to_all(values, 'wide', split_axis=0, concat_axis=0, tiled=True)  79.1 us
    all_to_all x6, waiting for transfers between devices, to_all(): lax.all_to_all(values, 'wide', split_axis=0, concat_axis=0, tiled=True)  62.1 us
    all_to_all x6, starting transfers between devices, to_all(): lax.all_to_all(values, 'wide', split_axis=0, concat_axis=0, tiled=True)  52.6 us
    all_gather x2, waiting for transfers between devices, same_core_gather(): lax.all_gather(rows, 'wide', axis=0, tiled=True, axis_index_groups=SAME_C...  29.4 us
    unnamed x160, local copies, waits for them, and re-layouts  27 us
    all_to_all x2, starting transfers between devices, to_same_core(): lax.all_to_all(values, 'wide', split_axis=0, concat_axis=0, tiled=True, a...  14.6 us
  transfers between devices with their start and end apart: 49, of which 26 were waited for; matrix products, arithmetic and copies ran while one was open for 4% of the time, Pallas kernels for 16%

profile of v2, /device:TPU:13, one launch (start us, length us, event | category | flops | bytes accessed | tf_op | source)
XLA Modules:
  0.0 600.8 jit_solution(1765979275499262716)
XLA Ops:
  8.7 4.8 route_out.1
  17.5 11.0 %all-to-all-start = ((bf16[64,2,2560]{2,1,0:T(2,128)(2,1)}), bf16[64,2,2560]{2,1,0:T(2,128)(2,1)S(1)}, u32[]{:S(2)}, u32[]{:S(2)}) async-start(bf16[64,2,2560]{2,1,0:T(2,128)(2,1)} %reshape.333), calls=%async_computation | async-start | bytes 1310720 | tf_op jit(solution)/shard_map/all_to_all | solution.py:922
  32.8 8.9 %all-to-all-done = bf16[64,2,2560]{2,1,0:T(2,128)(2,1)S(1)} async-done(((bf16[64,2,2560]{2,1,0:T(2,128)(2,1)}), bf16[64,2,2560]{2,1,0:T(2,128)(2,1)S(1)}, u32[]{:S(2)}, u32[]{:S(2)}) %all-to-all-start) | async-done | bytes 655392 | tf_op jit(solution)/shard_map/all_to_all | solution.py:922
  49.3 5.7 all-to-all-start.1
  58.9 14.4 %all-to-all-done.1.refs_2_.refs_4_.q_own.v_own = bf16[32,32,512]{2,1,0:T(8,128)(2,1)S(1)} async-done(((bf16[32,32,512]{2,1,0:T(8,128)(2,1)}), bf16[32,32,512]{2,1,0:T(8,128)(2,1)S(1)}, u32[]{:S(2)}, u32[]{:S(2)}) %all-to-all-start.1) | async-done | bytes 1048608 | tf_op jit(solution)/shard_map/all_to_all | solution.py:950
  95.6 7.9 %all-to-all-start.2 = ((bf16[64,8,640]{2,1,0:T(8,128)(2,1)}), bf16[64,8,640]{2,1,0:T(8,128)(2,1)S(1)}, u32[]{:S(2)}, u32[]{:S(2)}) async-start(bf16[64,8,640]{2,1,0:T(8,128)(2,1)} %bitcast.105), calls=%async_computation.2 | async-start | bytes 1310720 | tf_op jit(solution)/shard_map/all_to_all | solution.py:922
  106.0 14.1 %all-to-all-done.2 = bf16[64,8,640]{2,1,0:T(8,128)(2,1)S(1)} async-done(((bf16[64,8,640]{2,1,0:T(8,128)(2,1)}), bf16[64,8,640]{2,1,0:T(8,128)(2,1)S(1)}, u32[]{:S(2)}, u32[]{:S(2)}) %all-to-all-start.2) | async-done | bytes 655392 | tf_op jit(solution)/shard_map/all_to_all | solution.py:922
  121.0 4.5 attend.2
  125.5 21.4 %all-gather.3.cloned.1.call-done = bf16[6144,512]{1,0:T(8,128)(2,1)} async-done(((bf16[192,512]{1,0:T(8,128)(2,1)}), bf16[6144,512]{1,0:T(8,128)(2,1)}) %all-gather.3.cloned.1.call-update) | async-done | bytes 6291472 | tf_op jit(solution)/shard_map/all_gather | solution.py:960
  147.7 16.6 %all_to_all.82 = bf16[64,8,384]{2,1,0:T(8,128)(2,1)} all-to-all(bf16[64,8,384]{2,1,0:T(8,128)(2,1)} %bitcast.108), channel_id=1, replica_groups=mesh['wide'=64,'narrow'=2] {'wide'}, dimensions={0} | all-to-all | bytes 786432 | tf_op jit(solution)/shard_map/all_to_all | solution.py:922
  171.2 6.3 %collective-permute-done.7.other_ref = bf16[128,1024]{1,0:T(8,128)(2,1)S(1)} collective-permute-done((bf16[128,1024]{1,0:T(8,128)(2,1)}, bf16[128,1024]{1,0:T(8,128)(2,1)S(1)}, u32[]{:S(2)}, u32[]{:S(2)}) %collective-permute-start.7) | collective-permute-done | bytes 262176 | tf_op jit(solution)/shard_map/ppermute | solution.py:913
  178.2 7.7 %ffn.2 = (f32[128,1024]{1,0:T(8,128)}, bf16[2,128,512]{2,1,0:T(8,128)(2,1)}, f32[128,2048]{1,0:T(8,128)}, bf16[128,2048]{1,0:T(8,128)(2,1)}, f32[128,1024]{1,0:T(8,128)}, /*index=5*/bf16[128,1024]{1,0:T(8,128)(2,1)}) custom-call(s32[1]{0:T(128)} %bitcast.1.core_ref, f32[128,1024]{1,0:T(8,128)} %get-tuple-element.99.x_ref, ...), custom_call_target="tpu_custom_call" | custom-call | tf_op jit(solution)/shard_map/ffn/pallas_call | solution.py:94
  187.7 4.8 collective-permute-done.8.refs_2_
  193.2 3.8 project.3
  197.0 9.1 %all-to-all-start.4 = ((bf16[64,8,640]{2,1,0:T(8,128)(2,1)}), bf16[64,8,640]{2,1,0:T(8,128)(2,1)S(1)}, u32[]{:S(2)}, u32[]{:S(2)}) async-start(bf16[64,8,640]{2,1,0:T(8,128)(2,1)} %bitcast.106), calls=%async_computation.4 | async-start | bytes 1310720 | tf_op jit(solution)/shard_map/all_to_all | solution.py:922
  206.8 14.0 %all-to-all-done.4 = bf16[64,8,640]{2,1,0:T(8,128)(2,1)S(1)} async-done(((bf16[64,8,640]{2,1,0:T(8,128)(2,1)}), bf16[64,8,640]{2,1,0:T(8,128)(2,1)S(1)}, u32[]{:S(2)}, u32[]{:S(2)}) %all-to-all-start.4) | async-done | bytes 655392 | tf_op jit(solution)/shard_map/all_to_all | solution.py:922
  221.6 4.5 attend.3
  226.1 7.9 %all-gather.5.cloned.1.call-done = bf16[4096,512]{1,0:T(8,128)(2,1)} async-done(((bf16[128,512]{1,0:T(8,128)(2,1)}), bf16[4096,512]{1,0:T(8,128)(2,1)}) %all-gather.5.cloned.1.call-update) | async-done | bytes 4194320 | tf_op jit(solution)/shard_map/all_gather | solution.py:960
  235.1 17.4 %all_to_all.83 = bf16[64,8,384]{2,1,0:T(8,128)(2,1)} all-to-all(bf16[64,8,384]{2,1,0:T(8,128)(2,1)} %bitcast.109), channel_id=1, replica_groups=mesh['wide'=64,'narrow'=2] {'wide'}, dimensions={0} | all-to-all | bytes 786432 | tf_op jit(solution)/shard_map/all_to_all | solution.py:922
  256.2 6.9 %collective-permute-done.9.other_ref = bf16[128,1024]{1,0:T(8,128)(2,1)S(1)} collective-permute-done((bf16[128,1024]{1,0:T(8,128)(2,1)}, bf16[128,1024]{1,0:T(8,128)(2,1)S(1)}, u32[]{:S(2)}, u32[]{:S(2)}) %collective-permute-start.9) | collective-permute-done | bytes 262176 | tf_op jit(solution)/shard_map/ppermute | solution.py:913
  265.2 7.6 %ffn.3 = (f32[128,1024]{1,0:T(8,128)}, bf16[2,128,512]{2,1,0:T(8,128)(2,1)}, f32[128,2048]{1,0:T(8,128)}, bf16[128,2048]{1,0:T(8,128)(2,1)}, f32[128,1024]{1,0:T(8,128)}, /*index=5*/bf16[128,1024]{1,0:T(8,128)(2,1)}) custom-call(s32[1]{0:T(128)} %bitcast.1.core_ref, f32[128,1024]{1,0:T(8,128)} %get-tuple-element.112.x_ref.y_ref, ...), custom_call_target="tpu_custom_call" | custom-call | tf_op jit(solution)/shard_map/ffn/pallas_call | solution.py:94
  272.8 7.2 %ffn_back.2 = (f32[128,1024]{1,0:T(8,128)}, bf16[2,128,512]{2,1,0:T(8,128)(2,1)}, bf16[128,2048]{1,0:T(8,128)(2,1)}, f32[128,1024]{1,0:T(8,128)}, bf16[128,1024]{1,0:T(8,128)(2,1)}, /*index=5*/f32[1,1024]{1,0:T(1,128)}) custom-call(s32[1]{0:T(128)} %bitcast.1.core_ref, f32[128,1024]{1,0:T(8,128)} %get-tuple-element.102.refs_0_, ...), custom_call_target="tpu_custom_call" | custom-call | tf_op jit(solution)/shard_map/ffn_back/pallas_call | solution.py:94
  286.6 5.6 ffn_grad.2
  293.4 7.3 %collective-permute-done.12.other_ref = bf16[128,1024]{1,0:T(8,128)(2,1)S(1)} collective-permute-done((bf16[128,1024]{1,0:T(8,128)(2,1)S(1)}, bf16[128,1024]{1,0:T(8,128)(2,1)S(1)}, u32[]{:S(2)}, u32[]{:S(2)}) %collective-permute-start.12) | collective-permute-done | bytes 262176 | tf_op jit(solution)/shard_map/ppermute | solution.py:913
  301.5 4.2 merge_back.2
  305.6 22.8 %all_to_all.84 = bf16[64,8,384]{2,1,0:T(8,128)(2,1)} all-to-all(bf16[64,8,384]{2,1,0:T(8,128)(2,1)} %bitcast.110), channel_id=1, replica_groups=mesh['wide'=64,'narrow'=2] {'wide'}, dimensions={0} | all-to-all | bytes 786432 | tf_op jit(solution)/shard_map/all_to_all | solution.py:922
  328.4 5.1 attend_back.2
  333.5 6.9 %all-to-all-start.7 = ((bf16[64,8,640]{2,1,0:T(8,128)(2,1)}), bf16[64,8,640]{2,1,0:T(8,128)(2,1)S(1)}, u32[]{:S(2)}, u32[]{:S(2)}) async-start(bf16[64,8,640]{2,1,0:T(8,128)(2,1)} %bitcast.87), calls=%async_computation.7 | async-start | bytes 1310720 | tf_op jit(solution)/shard_map/all_to_all | solution.py:922
  341.6 12.0 %all-to-all-done.7 = bf16[64,8,640]{2,1,0:T(8,128)(2,1)S(1)} async-done(((bf16[64,8,640]{2,1,0:T(8,128)(2,1)}), bf16[64,8,640]{2,1,0:T(8,128)(2,1)S(1)}, u32[]{:S(2)}, u32[]{:S(2)}) %all-to-all-start.7) | async-done | bytes 655392 | tf_op jit(solution)/shard_map/all_to_all | solution.py:922
  354.4 4.0 project_back.2
  366.9 6.7 %collective-permute-done.17.refs_2_ = bf16[128,1024]{1,0:T(8,128)(2,1)S(1)} collective-permute-done((bf16[128,1024]{1,0:T(8,128)(2,1)S(1)}, bf16[128,1024]{1,0:T(8,128)(2,1)S(1)}, u32[]{:S(2)}, u32[]{:S(2)}) %collective-permute-start.17) | collective-permute-done | bytes 262176 | tf_op jit(solution)/shard_map/ppermute | solution.py:913
  374.3 8.0 %ffn_back.3 = (f32[128,1024]{1,0:T(8,128)}, bf16[2,128,512]{2,1,0:T(8,128)(2,1)}, bf16[128,2048]{1,0:T(8,128)(2,1)}, f32[128,1024]{1,0:T(8,128)}, bf16[128,1024]{1,0:T(8,128)(2,1)}, /*index=5*/f32[1,1024]{1,0:T(1,128)}) custom-call(s32[1]{0:T(128)} %bitcast.1.core_ref, f32[128,1024]{1,0:T(8,128)} %get-tuple-element.139.refs_0_, ...), custom_call_target="tpu_custom_call" | custom-call | tf_op jit(solution)/shard_map/ffn_back/pallas_call | solution.py:94
  387.5 5.6 ffn_grad.3
  397.3 17.8 %collective-permute-done.23.other_ref = bf16[128,1024]{1,0:T(8,128)(2,1)S(1)} collective-permute-done((bf16[128,1024]{1,0:T(8,128)(2,1)S(1)}, bf16[128,1024]{1,0:T(8,128)(2,1)S(1)}, u32[]{:S(2)}, u32[]{:S(2)}) %collective-permute-start.23) | collective-permute-done | bytes 262176 | tf_op jit(solution)/shard_map/ppermute | solution.py:913
  415.8 4.3 merge_back.3
  420.1 22.3 %all_to_all.85 = bf16[64,8,384]{2,1,0:T(8,128)(2,1)} all-to-all(bf16[64,8,384]{2,1,0:T(8,128)(2,1)} %bitcast.107), channel_id=1, replica_groups=mesh['wide'=64,'narrow'=2] {'wide'}, dimensions={0} | all-to-all | bytes 786432 | tf_op jit(solution)/shard_map/all_to_all | solution.py:922
  442.4 5.0 attend_back.3
  447.4 7.3 %all-to-all-start.10 = ((bf16[64,8,640]{2,1,0:T(8,128)(2,1)}), bf16[64,8,640]{2,1,0:T(8,128)(2,1)S(1)}, u32[]{:S(2)}, u32[]{:S(2)}) async-start(bf16[64,8,640]{2,1,0:T(8,128)(2,1)} %bitcast.88), calls=%async_computation.11 | async-start | bytes 1310720 | tf_op jit(solution)/shard_map/all_to_all | solution.py:922
  454.7 13.0 %all-to-all-done.10 = bf16[64,8,640]{2,1,0:T(8,128)(2,1)S(1)} async-done(((bf16[64,8,640]{2,1,0:T(8,128)(2,1)}), bf16[64,8,640]{2,1,0:T(8,128)(2,1)S(1)}, u32[]{:S(2)}, u32[]{:S(2)}) %all-to-all-start.10) | async-done | bytes 655392 | tf_op jit(solution)/shard_map/all_to_all | solution.py:922
  475.8 4.0 project_back.3
  486.0 6.8 %all-to-all-done.11 = bf16[8,176,512]{2,1,0:T(8,128)(2,1)S(1)} async-done(((bf16[8,176,512]{2,1,0:T(8,128)(2,1)}), bf16[8,176,512]{2,1,0:T(8,128)(2,1)S(1)}, u32[]{:S(2)}, u32[]{:S(2)}) %all-to-all-start.11) | async-done | bytes 1441824 | tf_op jit(solution)/shard_map/all_to_all | solution.py:943
  492.8 8.9 %all-to-all-start.12 = ((bf16[32,48,512]{2,1,0:T(8,128)(2,1)}), bf16[32,48,512]{2,1,0:T(8,128)(2,1)S(1)}, u32[]{:S(2)}, u32[]{:S(2)}) async-start(bf16[32,48,512]{2,1,0:T(8,128)(2,1)} %attn_grad.3), calls=%async_computation.15 | async-start | bytes 3145728 | tf_op jit(solution)/shard_map/all_to_all | solution.py:950
  503.2 22.4 %collective-permute-done.28.other_ref = bf16[128,1024]{1,0:T(8,128)(2,1)S(1)} collective-permute-done((bf16[128,1024]{1,0:T(8,128)(2,1)}, bf16[128,1024]{1,0:T(8,128)(2,1)S(1)}, u32[]{:S(2)}, u32[]{:S(2)}) %collective-permute-start.28) | collective-permute-done | bytes 262176 | tf_op jit(solution)/shard_map/ppermute | solution.py:913
  538.6 10.5 %all-to-all-start.13 = ((bf16[64,2,4608]{2,1,0:T(2,128)(2,1)}), bf16[64,2,4608]{2,1,0:T(2,128)(2,1)S(1)}, u32[]{:S(2)}, u32[]{:S(2)}) async-start(bf16[64,2,4608]{2,1,0:T(2,128)(2,1)} %reshape.335), calls=%async_computation.16 | async-start | bytes 2359296 | tf_op jit(solution)/shard_map/all_to_all | solution.py:922
  551.6 19.5 %collective-permute-done.11 = bf16[128,1024]{1,0:T(8,128)(2,1)S(1)} collective-permute-done((bf16[128,1024]{1,0:T(8,128)(2,1)S(1)}, bf16[128,1024]{1,0:T(8,128)(2,1)S(1)}, u32[]{:S(2)}, u32[]{:S(2)}) %collective-permute-start.11) | collective-permute-done | bytes 262176 | tf_op jit(solution)/shard_map/ppermute | solution.py:913
  572.0 4.1 outer_y.1
  576.1 4.1 outer_dx.1
  585.4 7.8 %slots_update.1 = (f32[5,128,512]{2,1,0:T(8,128)}, f32[5,128,512]{2,1,0:T(8,128)}, f32[5,128,512]{2,1,0:T(8,128)}, f32[5,128,512]{2,1,0:T(8,128)}) custom-call(s32[5]{0:T(128)} %convert_element_type.8.kind_ref, bf16[64,9216]{1,0:T(8,128)(2,1)} %bitcast.83, f32[5,128,512]{2,1,0:T(8,128)} %m_ref.1, f32[5,128,512]{2,1,0:T(8,128)} %a_ref.1, f32[5,128,512]{2,1,0:T(8,128)} %b_ref.1), custom_call_target="tpu_custom_call" | custom-call | tf_op jit(solution)/shard_map/slots_update/pallas_call | solution.py:94
  (310 shorter events, 133.3 us)
Async XLA Ops:
  17.5 24.2 %all-to-all-start = ((bf16[64,2,2560]{2,1,0:T(2,128)(2,1)}), bf16[64,2,2560]{2,1,0:T(2,128)(2,1)S(1)}, u32[]{:S(2)}, u32[]{:S(2)}) async-start(bf16[64,2,2560]{2,1,0:T(2,128)(2,1)} %reshape.333), calls=%async_computation | async-start | bytes 1310720 | tf_op jit(solution)/shard_map/all_to_all | solution.py:922
  28.5 118.3 %all-gather.3.cloned.1.call-start = ((), (), s32[]{:S(2)}) async-start(), calls=%async_computation.17 | async-start | bytes 6488064 | tf_op jit(solution)/shard_map/all_gather | solution.py:960
  46.2 40.3 %collective-permute-start = (bf16[128,512]{1,0:T(8,128)(2,1)}, bf16[128,512]{1,0:T(8,128)(2,1)}, u32[]{:S(2)}, u32[]{:S(2)}) collective-permute-start(bf16[128,512]{1,0:T(8,128)(2,1)} %refs_0_.2), channel_id=1, source_target_pairs={{0,1},{1,0},{2,3},{3,2},{4,5},{5,4},{6,7},{7,6},{8,9},{9,8},{10,11... | collective-permute-start | bytes 393224 | tf_op jit(solution)/shard_map/ppermute | solution.py:913
  47.3 39.2 %collective-permute-start.1 = (bf16[128,512]{1,0:T(8,128)(2,1)}, bf16[128,512]{1,0:T(8,128)(2,1)}, u32[]{:S(2)}, u32[]{:S(2)}) collective-permute-start(bf16[128,512]{1,0:T(8,128)(2,1)} %refs_2_.1), channel_id=1, source_target_pairs={{0,1},{1,0},{2,3},{3,2},{4,5},{5,4},{6,7},{7,6},{8,9},{9,8},{10,11... | collective-permute-start | bytes 393224 | tf_op jit(solution)/shard_map/ppermute | solution.py:913
  47.7 38.8 %collective-permute-start.2 = (bf16[128,512]{1,0:T(8,128)(2,1)}, bf16[128,512]{1,0:T(8,128)(2,1)}, u32[]{:S(2)}, u32[]{:S(2)}) collective-permute-start(bf16[128,512]{1,0:T(8,128)(2,1)} %refs_4_.1), channel_id=1, source_target_pairs={{0,1},{1,0},{2,3},{3,2},{4,5},{5,4},{6,7},{7,6},{8,9},{9,8},{10,11... | collective-permute-start | bytes 393224 | tf_op jit(solution)/shard_map/ppermute | solution.py:913
  48.8 29.0 %collective-permute-start.4 = (f32[4,512]{1,0:T(4,128)S(1)}, f32[4,512]{1,0:T(4,128)S(1)}, u32[]{:S(2)}, u32[]{:S(2)}) collective-permute-start(f32[4,512]{1,0:T(4,128)S(1)} %reshape.293.refs_2_), channel_id=1, source_target_pairs={{0,1},{1,0},{2,3},{3,2},{4,5},{5,4},{6,7},{7,6},{8,9},{9,8},{10,11... | collective-permute-start | bytes 24584 | tf_op jit(solution)/shard_map/ppermute | solution.py:913
  49.3 24.0 %all-to-all-start.1 = ((bf16[32,32,512]{2,1,0:T(8,128)(2,1)}), bf16[32,32,512]{2,1,0:T(8,128)(2,1)S(1)}, u32[]{:S(2)}, u32[]{:S(2)}) async-start(bf16[32,32,512]{2,1,0:T(8,128)(2,1)} %get-tuple-element.105), calls=%async_computation.1 | async-start | bytes 2097152 | tf_op jit(solution)/shard_map/all_to_all | solution.py:950
  55.0 179.0 %all-gather.5.cloned.1.call-start = ((), (), s32[]{:S(2)}) async-start(), calls=%async_computation.18 | async-start | bytes 4325376 | tf_op jit(solution)/shard_map/all_gather | solution.py:960
  73.4 17.7 %collective-permute-start.5 = (bf16[32,32,512]{2,1,0:T(8,128)(2,1)S(1)}, bf16[32,32,512]{2,1,0:T(8,128)(2,1)S(1)}, u32[]{:S(2)}, u32[]{:S(2)}) collective-permute-start(bf16[32,32,512]{2,1,0:T(8,128)(2,1)S(1)} %all-to-all-done.1.refs_2_.refs_4_.q_own.v_own), channel_id=1, source_target_pairs={{0,2},{2,0},{4,6},{6,4},{8,10},{10,8},{12,14},{14,12},{16,18},{18,... | collective-permute-start | bytes 3145736 | tf_op jit(solution)/shard_map/ppermute | solution.py:917
  77.8 5.1 collective-permute-start.3
  95.6 24.6 %all-to-all-start.2 = ((bf16[64,8,640]{2,1,0:T(8,128)(2,1)}), bf16[64,8,640]{2,1,0:T(8,128)(2,1)S(1)}, u32[]{:S(2)}, u32[]{:S(2)}) async-start(bf16[64,8,640]{2,1,0:T(8,128)(2,1)} %bitcast.105), calls=%async_computation.2 | async-start | bytes 1310720 | tf_op jit(solution)/shard_map/all_to_all | solution.py:922
  146.9 17.4 %collective-permute-start.6 = (bf16[32,192,512]{2,1,0:T(8,128)(2,1)}, bf16[32,192,512]{2,1,0:T(8,128)(2,1)S(1)}, u32[]{:S(2)}, u32[]{:S(2)}) collective-permute-start(bf16[32,192,512]{2,1,0:T(8,128)(2,1)} %bitcast.56), channel_id=1, source_target_pairs={{0,2},{2,0},{4,6},{6,4},{8,10},{10,8},{12,14},{14,12},{16,18},{18,... | collective-permute-start | bytes 18874376 | tf_op jit(solution)/shard_map/ppermute | solution.py:917
  170.3 7.2 %collective-permute-start.7 = (bf16[128,1024]{1,0:T(8,128)(2,1)}, bf16[128,1024]{1,0:T(8,128)(2,1)S(1)}, u32[]{:S(2)}, u32[]{:S(2)}) collective-permute-start(bf16[128,1024]{1,0:T(8,128)(2,1)} %get-tuple-element.111), channel_id=1, source_target_pairs={{0,1},{1,0},{2,3},{3,2},{4,5},{5,4},{6,7},{7,6},{8,9},{9,8},{10,11... | collective-permute-start | bytes 786440 | tf_op jit(solution)/shard_map/ppermute | solution.py:913
  185.9 6.6 %collective-permute-start.8 = (bf16[128,1024]{1,0:T(8,128)(2,1)}, bf16[128,1024]{1,0:T(8,128)(2,1)S(1)}, u32[]{:S(2)}, u32[]{:S(2)}) collective-permute-start(bf16[128,1024]{1,0:T(8,128)(2,1)} %get-tuple-element.115), channel_id=1, source_target_pairs={{0,1},{1,0},{2,3},{3,2},{4,5},{5,4},{6,7},{7,6},{8,9},{9,8},{10,11... | collective-permute-start | bytes 786440 | tf_op jit(solution)/shard_map/ppermute | solution.py:913
  197.0 23.8 %all-to-all-start.4 = ((bf16[64,8,640]{2,1,0:T(8,128)(2,1)}), bf16[64,8,640]{2,1,0:T(8,128)(2,1)S(1)}, u32[]{:S(2)}, u32[]{:S(2)}) async-start(bf16[64,8,640]{2,1,0:T(8,128)(2,1)} %bitcast.106), calls=%async_computation.4 | async-start | bytes 1310720 | tf_op jit(solution)/shard_map/all_to_all | solution.py:922
  206.0 187.1 %reduce-scatter.4.cloned.1.call-start = ((), (), s32[]{:S(2)}) async-start(), calls=%async_computation.19 | async-start | bytes 5242880 | tf_op jit(solution)/shard_map/reduce_scatter | solution.py:937
  234.1 29.0 %collective-permute-start.10 = (bf16[32,128,512]{2,1,0:T(8,128)(2,1)}, bf16[32,128,512]{2,1,0:T(8,128)(2,1)S(1)}, u32[]{:S(2)}, u32[]{:S(2)}) collective-permute-start(bf16[32,128,512]{2,1,0:T(8,128)(2,1)} %bitcast.73), channel_id=1, source_target_pairs={{0,2},{2,0},{4,6},{6,4},{8,10},{10,8},{12,14},{14,12},{16,18},{18,... | collective-permute-start | bytes 12582920 | tf_op jit(solution)/shard_map/ppermute | solution.py:917
  255.9 7.2 %collective-permute-start.9 = (bf16[128,1024]{1,0:T(8,128)(2,1)}, bf16[128,1024]{1,0:T(8,128)(2,1)S(1)}, u32[]{:S(2)}, u32[]{:S(2)}) collective-permute-start(bf16[128,1024]{1,0:T(8,128)(2,1)} %get-tuple-element.119), channel_id=1, source_target_pairs={{0,1},{1,0},{2,3},{3,2},{4,5},{5,4},{6,7},{7,6},{8,9},{9,8},{10,11... | collective-permute-start | bytes 786440 | tf_op jit(solution)/shard_map/ppermute | solution.py:913
  280.0 5.0 collective-permute-start.15
  281.8 3.1 collective-permute-start.16
  281.9 2.9 collective-permute-start.13
  282.3 2.6 collective-permute-start.14
  293.1 7.6 %collective-permute-start.12 = (bf16[128,1024]{1,0:T(8,128)(2,1)S(1)}, bf16[128,1024]{1,0:T(8,128)(2,1)S(1)}, u32[]{:S(2)}, u32[]{:S(2)}) collective-permute-start(bf16[128,1024]{1,0:T(8,128)(2,1)S(1)} %copy-done.74), channel_id=1, source_target_pairs={{0,1},{1,0},{2,3},{3,2},{4,5},{5,4},{6,7},{7,6},{8,9},{9,8},{10,11... | collective-permute-start | bytes 786440 | tf_op jit(solution)/shard_map/ppermute | solution.py:913
  333.5 20.1 %all-to-all-start.7 = ((bf16[64,8,640]{2,1,0:T(8,128)(2,1)}), bf16[64,8,640]{2,1,0:T(8,128)(2,1)S(1)}, u32[]{:S(2)}, u32[]{:S(2)}) async-start(bf16[64,8,640]{2,1,0:T(8,128)(2,1)} %bitcast.87), calls=%async_computation.7 | async-start | bytes 1310720 | tf_op jit(solution)/shard_map/all_to_all | solution.py:922
  340.4 114.3 %reduce-scatter.8.cloned.1.call-start = ((), (), s32[]{:S(2)}) async-start(), calls=%async_computation.21 | async-start | bytes 1966080 | tf_op jit(solution)/shard_map/reduce_scatter | solution.py:937
  340.4 19.0 %collective-permute-start.20 = (bf16[2,128,512]{2,1,0:T(8,128)(2,1)S(1)}, bf16[2,128,512]{2,1,0:T(8,128)(2,1)S(1)}, u32[]{:S(2)}, u32[]{:S(2)}) collective-permute-start(bf16[2,128,512]{2,1,0:T(8,128)(2,1)S(1)} %copy-done.16), channel_id=1, source_target_pairs={{0,2},{2,0},{4,6},{6,4},{8,10},{10,8},{12,14},{14,12},{16,18},{18,... | collective-permute-start | bytes 786440 | tf_op jit(solution)/shard_map/ppermute | solution.py:917
  340.9 18.5 %collective-permute-start.18 = (bf16[2,128,512]{2,1,0:T(8,128)(2,1)S(1)}, bf16[2,128,512]{2,1,0:T(8,128)(2,1)S(1)}, u32[]{:S(2)}, u32[]{:S(2)}) collective-permute-start(bf16[2,128,512]{2,1,0:T(8,128)(2,1)S(1)} %copy-done.33), channel_id=1, source_target_pairs={{0,2},{2,0},{4,6},{6,4},{8,10},{10,8},{12,14},{14,12},{16,18},{18,... | collective-permute-start | bytes 786440 | tf_op jit(solution)/shard_map/ppermute | solution.py:917
  341.0 18.4 %collective-permute-start.19 = (bf16[128,512]{1,0:T(8,128)(2,1)S(1)}, bf16[128,512]{1,0:T(8,128)(2,1)S(1)}, u32[]{:S(2)}, u32[]{:S(2)}) collective-permute-start(bf16[128,512]{1,0:T(8,128)(2,1)S(1)} %copy-done.44), channel_id=1, source_target_pairs={{0,2},{2,0},{4,6},{6,4},{8,10},{10,8},{12,14},{14,12},{16,18},{18,... | collective-permute-start | bytes 393224 | tf_op jit(solution)/shard_map/ppermute | solution.py:917
  358.4 2.1 collective-permute-start.21
  365.1 102.7 %reduce-scatter.6.cloned.1.call-start = ((), (), s32[]{:S(2)}) async-start(), calls=%async_computation.20 | async-start | bytes 5242880 | tf_op jit(solution)/shard_map/reduce_scatter | solution.py:937
  366.0 7.6 %collective-permute-start.17 = (bf16[128,1024]{1,0:T(8,128)(2,1)S(1)}, bf16[128,1024]{1,0:T(8,128)(2,1)S(1)}, u32[]{:S(2)}, u32[]{:S(2)}) collective-permute-start(bf16[128,1024]{1,0:T(8,128)(2,1)S(1)} %copy-done.75), channel_id=1, source_target_pairs={{0,1},{1,0},{2,3},{3,2},{4,5},{5,4},{6,7},{7,6},{8,9},{9,8},{10,11... | collective-permute-start | bytes 786440 | tf_op jit(solution)/shard_map/ppermute | solution.py:913
  366.3 19.5 %collective-permute-start.27 = (bf16[128,2048]{1,0:T(8,128)(2,1)S(1)}, bf16[128,2048]{1,0:T(8,128)(2,1)S(1)}, u32[]{:S(2)}, u32[]{:S(2)}) collective-permute-start(bf16[128,2048]{1,0:T(8,128)(2,1)S(1)} %copy-done.20), channel_id=1, source_target_pairs={{0,2},{2,0},{4,6},{6,4},{8,10},{10,8},{12,14},{14,12},{16,18},{18,... | collective-permute-start | bytes 1572872 | tf_op jit(solution)/shard_map/ppermute | solution.py:917
  382.3 3.7 collective-permute-start.26
  383.5 2.3 collective-permute-start.24
  383.6 2.4 collective-permute-start.25
  393.2 21.9 %all-to-all-start.8 = ((bf16[8,128,512]{2,1,0:T(8,128)(2,1)}), bf16[8,128,512]{2,1,0:T(8,128)(2,1)S(1)}, u32[]{:S(2)}, u32[]{:S(2)}) async-start(bf16[8,128,512]{2,1,0:T(8,128)(2,1)} %bitcast.103), calls=%async_computation.9 | async-start | bytes 2097152 | tf_op jit(solution)/shard_map/all_to_all | solution.py:943
  396.9 18.2 %collective-permute-start.23 = (bf16[128,1024]{1,0:T(8,128)(2,1)S(1)}, bf16[128,1024]{1,0:T(8,128)(2,1)S(1)}, u32[]{:S(2)}, u32[]{:S(2)}) collective-permute-start(bf16[128,1024]{1,0:T(8,128)(2,1)S(1)} %copy-done.73), channel_id=1, source_target_pairs={{0,1},{1,0},{2,3},{3,2},{4,5},{5,4},{6,7},{7,6},{8,9},{9,8},{10,11... | collective-permute-start | bytes 786440 | tf_op jit(solution)/shard_map/ppermute | solution.py:913
  447.4 20.3 %all-to-all-start.10 = ((bf16[64,8,640]{2,1,0:T(8,128)(2,1)}), bf16[64,8,640]{2,1,0:T(8,128)(2,1)S(1)}, u32[]{:S(2)}, u32[]{:S(2)}) async-start(bf16[64,8,640]{2,1,0:T(8,128)(2,1)} %bitcast.88), calls=%async_computation.11 | async-start | bytes 1310720 | tf_op jit(solution)/shard_map/all_to_all | solution.py:922
  470.6 22.2 %all-to-all-start.11 = ((bf16[8,176,512]{2,1,0:T(8,128)(2,1)}), bf16[8,176,512]{2,1,0:T(8,128)(2,1)S(1)}, u32[]{:S(2)}, u32[]{:S(2)}) async-start(bf16[8,176,512]{2,1,0:T(8,128)(2,1)} %pad_maximum_fusion), calls=%async_computation.14 | async-start | bytes 2883584 | tf_op jit(solution)/shard_map/all_to_all | solution.py:943
  474.3 6.1 %collective-permute-start.31 = (bf16[2,128,512]{2,1,0:T(8,128)(2,1)S(1)}, bf16[2,128,512]{2,1,0:T(8,128)(2,1)S(1)}, u32[]{:S(2)}, u32[]{:S(2)}) collective-permute-start(bf16[2,128,512]{2,1,0:T(8,128)(2,1)S(1)} %copy-done.15), channel_id=1, source_target_pairs={{0,2},{2,0},{4,6},{6,4},{8,10},{10,8},{12,14},{14,12},{16,18},{18,... | collective-permute-start | bytes 786440 | tf_op jit(solution)/shard_map/ppermute | solution.py:917
  475.3 5.1 collective-permute-start.29
  475.4 5.0 collective-permute-start.30
  479.9 1.6 collective-permute-start.32
  480.0 1.7 collective-permute-start.33
  492.8 37.8 %all-to-all-start.12 = ((bf16[32,48,512]{2,1,0:T(8,128)(2,1)}), bf16[32,48,512]{2,1,0:T(8,128)(2,1)S(1)}, u32[]{:S(2)}, u32[]{:S(2)}) async-start(bf16[32,48,512]{2,1,0:T(8,128)(2,1)} %attn_grad.3), calls=%async_computation.15 | async-start | bytes 3145728 | tf_op jit(solution)/shard_map/all_to_all | solution.py:950
  501.7 24.0 %collective-permute-start.28 = (bf16[128,1024]{1,0:T(8,128)(2,1)}, bf16[128,1024]{1,0:T(8,128)(2,1)S(1)}, u32[]{:S(2)}, u32[]{:S(2)}) collective-permute-start(bf16[128,1024]{1,0:T(8,128)(2,1)} %get-tuple-element.167), channel_id=1, source_target_pairs={{0,1},{1,0},{2,3},{3,2},{4,5},{5,4},{6,7},{7,6},{8,9},{9,8},{10,11... | collective-permute-start | bytes 786440 | tf_op jit(solution)/shard_map/ppermute | solution.py:913
  538.6 41.6 %all-to-all-start.13 = ((bf16[64,2,4608]{2,1,0:T(2,128)(2,1)}), bf16[64,2,4608]{2,1,0:T(2,128)(2,1)S(1)}, u32[]{:S(2)}, u32[]{:S(2)}) async-start(bf16[64,2,4608]{2,1,0:T(2,128)(2,1)} %reshape.335), calls=%async_computation.16 | async-start | bytes 2359296 | tf_op jit(solution)/shard_map/all_to_all | solution.py:922
  549.1 22.0 %collective-permute-start.11 = (bf16[128,1024]{1,0:T(8,128)(2,1)S(1)}, bf16[128,1024]{1,0:T(8,128)(2,1)S(1)}, u32[]{:S(2)}, u32[]{:S(2)}) collective-permute-start(bf16[128,1024]{1,0:T(8,128)(2,1)S(1)} %copy-done.72), channel_id=1, source_target_pairs={{0,1},{1,0},{2,3},{3,2},{4,5},{5,4},{6,7},{7,6},{8,9},{9,8},{10,11... | collective-permute-start | bytes 786440 | tf_op jit(solution)/shard_map/ppermute | solution.py:913
  (77 other events, 507.4 us)
Sparse Core Ops, SparseCore 0:
  46.3 100.5 all-gather.2
  150.0 84.0 all-gather.4
  292.3 47.0 reduce-scatter.3
  365.2 20.3 reduce-scatter.7
  393.2 45.4 reduce-scatter.5

commit v3 on v2

v3 whole, which is shorter than its diff:
```python
import functools

import jax
import jax.numpy as jnp
import numpy as np
from jax import lax
from jax.experimental import pallas as pl
from jax.experimental.pallas import tpu as pltpu
from jax.sharding import PartitionSpec as P

D = 1024
PART = 512
DH = 128
HN = 4
SPAN = 64
TR = 128
CAP = 5
TILES = 176
TOK = 128
NW = 64
LAYERS = 2
ROUNDS = 2
STEP = 5
GROUPS = 8
QV_LANES = 5 * DH
O_LANES = 3 * DH
ROWS = NW * 8
PACK = 16
QUAD = 4
UP, DOWN = 0, 1
LAYER_ROWS = 176
ATTN_ROWS = 48
FFN_ROWS = 128
EARLY_ROWS = 192

MASK_FILL = -1000000000.0
NORM_EPS = 1e-05
BETA_ONE = 0.5
BETA_TWO = 0.5
RATE_WEIGHT = 0.05
RATE_GAIN = 0.2
DECAY = 0.01
EPSILON = 1e-08

F32 = jnp.float32
BF16 = jnp.bfloat16
I32 = jnp.int32
VMEM_BYTES = 20 * 1024 * 1024


def feature_of(p):
    c0 = p >> 9
    z = (p >> 7) & 3
    tau = (p >> 5) & 3
    y = (p >> 4) & 1
    t = (p >> 1) & 7
    e = p & 1
    return t * 128 + tau * 32 + c0 * 16 + (y * 4 + z) * 2 + e


def iota(shape, dim):
    return lax.broadcasted_iota(I32, shape, dim)


def hot(mask):
    return jnp.where(mask, 1.0, 0.0).astype(BF16)


def dot(a, b, ca, cb):
    return lax.dot_general(a, b, (((ca,), (cb,)), ((), ())), preferred_element_type=F32)


def in_hbm(array):
    return pltpu.with_memory_space_constraint(array, pltpu.MemorySpace.HBM)


def call(
    kernel, args, outs, grid=(1,), specs=None, out_specs=None, scratch=(), prefetch=0, in_place=(), name=None
):
    specs = specs or {}
    out_specs = out_specs or {}
    def whole(shape):
        zeros = (0,) * len(shape)
        return pl.BlockSpec(shape, lambda *_: zeros)
    in_list = [specs.get(i, whole(a.shape)) for i, a in enumerate(args[prefetch:])]
    args = [in_hbm(a) if i - prefetch in in_place else a for i, a in enumerate(args)]
    out_list = [out_specs.get(i, whole(o.shape)) for i, o in enumerate(outs)]
    return pl.pallas_call(
        kernel,
        out_shape=outs,
        grid_spec=pltpu.PrefetchScalarGridSpec(
            num_scalar_prefetch=prefetch,
            grid=grid,
            in_specs=in_list,
            out_specs=out_list,
            scratch_shapes=list(scratch),
        ),
        compiler_params=pltpu.CompilerParams(vmem_limit_bytes=VMEM_BYTES),
        name=name,
    )(*args)


def sds(shape, dtype):
    return jax.ShapeDtypeStruct(shape, dtype)


def kept(shape, dtype):
    return pltpu.MemorySpace.HBM(shape, dtype)


def norm_parts(values):
    mean = jnp.mean(values, axis=-1, keepdims=True)
    var = jnp.mean(values * values, axis=-1, keepdims=True) - mean * mean
    rstd = lax.rsqrt(var + NORM_EPS)
    return (values - mean) * rstd, rstd


def norm_back(upstream, gain, xhat, rstd):
    gh = upstream * gain
    m1 = jnp.mean(gh, axis=-1, keepdims=True)
    m2 = jnp.mean(gh * xhat, axis=-1, keepdims=True)
    return rstd * (gh - m1 - xhat * m2), jnp.sum(upstream * xhat, axis=0, keepdims=True)


def flat(ref):
    return ref[...].reshape(PART, PART)


def halves(core, first, second):
    mine = core == 0
    return jnp.where(mine, first, second), jnp.where(mine, second, first)


class Weight:
    def __init__(self, index, *arrays):
        self.index = index
        self.arrays = arrays

    def parts(self):
        index = self.index
        if len(self.arrays) == 2:
            return [
                (a, pl.BlockSpec((8, 16, PART), lambda *_, z=z: (z, index, 0)))
                for a in self.arrays
                for z in range(4)
            ]
        return [
            (self.arrays[0], pl.BlockSpec((1, QUAD, 2, 32, PART), lambda *_, z=z: (z, 0, 0, index, 0)))
            for z in range(4)
        ]


def rows_of(refs):
    return jnp.concatenate([r[...].reshape(-1, PART) for r in refs], 0)


def weight_halves(core, refs):
    if len(refs) == 4:
        return [
            jnp.concatenate([r[0, :, c0].reshape(-1, PART) for r in refs], 0) for c0 in range(2)
        ]
    return rows_of(refs[:4]), rows_of(refs[4:])


def into(core, full, refs):
    first, second = full[:, :PART], full[:, PART:]
    if len(refs) == 8:
        first, second = halves(core, first, second)
    w = weight_halves(core, refs)
    return dot(first.astype(BF16), w[0], 1, 0) + dot(second.astype(BF16), w[1], 1, 0)


def out_of(core, part, refs):
    w = weight_halves(core, refs)
    pair = dot(part, w[0], 1, 1), dot(part, w[1], 1, 1)
    return pair if len(refs) == 4 else halves(core, *pair)


def unpacked(args, prefetch):
    out, specs = [], {}
    for a in args:
        if isinstance(a, Weight):
            for array, spec in a.parts():
                specs[len(out) - prefetch] = spec
                out.append(array)
        else:
            out.append(a)
    return out, specs


def wanted(shape, dim):
    m = iota(shape, dim)
    g16 = (m >> 3) * 16
    b = m & 7
    before = (g16 - 2) & 127
    lent = before + (b >> 1)
    return (
        g16 + 2 * b,
        g16 + 2 * b + 1,
        jnp.where((b == 0) | (b == 2), lent, -1),
        jnp.where((b == 1) | (b == 3), lent, -1),
    )


def send_hots(rank_row, count=4):
    return hot(jnp.concatenate(wanted((NW, 1), 0)[:count], 0) == rank_row)


def return_hots(rank_col, count=4):
    return hot(rank_col == jnp.concatenate(wanted((1, NW), 1)[:count], 1))


def spread(col, lanes):
    hi, mid, lo = pieces(col)
    k = lanes & 7
    return jnp.where(k == 0, hi, jnp.where(k == 1, mid, jnp.where(k == 2, lo, 0.0)))


def pieces(col):
    hi = col.astype(BF16).astype(F32)
    rest = col - hi
    mid = rest.astype(BF16).astype(F32)
    return hi, mid, rest - mid


def either(lanes, even, odd):
    return jnp.where(lanes < 8, even, jnp.where(lanes < 16, odd, 0.0))


def slot_kinds(owner_ref, me):
    lane = iota((1, TILES), 1)
    ffn = jnp.where(lane >= TILES // LAYERS, lane - TILES // LAYERS, lane) >= 24
    return [
        jnp.max(
            jnp.where((owner_ref[...] == me * CAP + s) & ffn, 1, 0), axis=1, keepdims=True
        )
        for s in range(CAP)
    ]


def row_of_slots(kinds):
    r = iota((1, TR), 1)
    attn = (((r >> 1) & 7) * 8 + (r >> 5) * 2 + ((r >> 4) & 1)) * PACK + (r & 1)
    low = r >> 2
    ffn = (((low >> 1) & 7) * 8 + (r & 3) * 2 + (low >> 4)) * PACK + (low & 1)
    return jnp.concatenate([jnp.where(k == 1, ffn, attn) + 2 * s for s, k in enumerate(kinds)], 1)


def slot_of_row(kinds):
    r = iota((1, NW * PACK), 1)
    d, m = r >> 4, r & (PACK - 1)
    s, e = m >> 1, m & 1
    tau = (d >> 1) & 3
    low = (d & 1) * 16 + (d >> 3) * 2 + e
    out = jnp.full((1, NW * PACK), -1, I32)
    for i, k in enumerate(kinds):
        out = jnp.where(s == i, i * TR + jnp.where(k == 1, low * 4 + tau, tau * 32 + low), out)
    return out


def route_out_kernel(me_ref, owner_ref, master_ref, out_ref):
    tiles = master_ref[...].reshape(CAP * TR, PART).astype(BF16)
    place = row_of_slots(slot_kinds(owner_ref, me_ref[0]))
    out_ref[...] = dot(hot(iota((NW * PACK, 1), 0) == place), tiles, 1, 0).astype(BF16)


def route_out(me, owner_row, master):
    return call(
        route_out_kernel,
        (me, owner_row, master),
        [kept((NW * PACK, PART), BF16)],
        prefetch=1,
        in_place=(1,),
        name="route_out",
    )[0]


def pick_kernel(code_ref, moved_ref, first_ref, early_ref, late_ref):
    picked = hot(code_ref[...] == iota((1, NW * PACK), 1))
    rows = dot(picked, moved_ref[...], 1, 0).astype(BF16)
    late_ref[...] = rows[LAYER_ROWS : LAYER_ROWS + FFN_ROWS]
    early_ref[: FFN_ROWS + 16] = rows[: FFN_ROWS + 16]
    early_ref[FFN_ROWS + 16 :] = rows[LAYER_ROWS + FFN_ROWS :]
    first_ref[...] = jnp.broadcast_to(rows[FFN_ROWS + 16 : LAYER_ROWS][None], first_ref.shape)


def pick(code_col, moved):
    return call(
        pick_kernel,
        (code_col, moved),
        [kept((32, 32, PART), BF16), kept((EARLY_ROWS, PART), BF16), kept((FFN_ROWS, PART), BF16)],
        name="pick",
    )


def route_back_kernel(code_ref, *refs):
    *parts, gain_a, gain_b, gain_c, out_ref = refs
    rows = jnp.concatenate([p[...] for p in parts], 0)
    place = iota((NW * PACK, 1), 0)
    out = dot(hot(place == code_ref[...]), rows, 1, 0)
    gains = jnp.concatenate(
        [
            half
            for g in (gain_a, gain_b, gain_c)
            for half in (g[:, :PART], g[:, PART:])
        ]
        + [jnp.zeros((2, PART), F32)],
        0,
    ).astype(BF16)
    spare = hot((place & (PACK - 1)) - 2 * CAP == iota((1, 8), 1))
    out_ref[...] = (out + dot(spare, gains, 1, 0)).astype(BF16)


def route_back(code_row, parts, gains):
    return call(
        route_back_kernel,
        (code_row, *parts, *gains),
        [kept((NW * PACK, PART), BF16)],
        name="route_back",
    )[0]


def adam(grad, first, second, weights, rate):
    first_new = BETA_ONE * first + (1.0 - BETA_ONE) * grad
    second_new = BETA_TWO * second + (1.0 - BETA_TWO) * grad * grad
    step = (
        first_new
        / (1.0 - BETA_ONE**STEP)
        / (jnp.sqrt(second_new / (1.0 - BETA_TWO**STEP)) + EPSILON)
    )
    return first_new, second_new, weights - rate * (step + DECAY * weights)


def slots_kernel(
    half_ref, me_ref, owner_ref, moved_ref, ready_ref, m_ref, a_ref, b_ref, gains_ref, ga_ref, gb_ref,
    grad_ref, first_ref, second_ref, new_ref, gg_ref, gf_ref, gs_ref, gn_ref, all_ref
):
    s = pl.program_id(0)

    @pl.when(s == 0)
    def _():
        placed = hot(iota((CAP * TR, 1), 0) == slot_of_row(slot_kinds(owner_ref, me_ref[0])))
        all_ref[...] = dot(placed, moved_ref[...], 1, 0).reshape(CAP, TR, PART)
        spare = hot((iota((1, NW * PACK), 1) & (PACK - 1)) - 2 * CAP == iota((8, 1), 0))
        sums = dot(spare, moved_ref[...], 1, 0)
        gains = [jnp.concatenate([sums[q : q + 1], sums[q + 1 : q + 2]], 1) for q in (4, 2, 0)]
        inner_sum = jnp.concatenate(gains + [ready_ref[...]], 0)
        back = hot(feature_of(iota((1, D), 1)) == iota((PART, 1), 0) + half_ref[0] * PART)
        parts = dot(jnp.concatenate(pieces(inner_sum), 0).astype(BF16), back, 1, 1)
        n = 2 * LAYERS
        total = parts[:n] + parts[n : 2 * n] + parts[2 * n :]
        for l in range(LAYERS):
            gain_grad = total[2 * l : 2 * l + 2]
            gg_ref[l] = gain_grad
            gf_ref[l], gs_ref[l], gn_ref[l] = adam(
                gain_grad, ga_ref[l], gb_ref[l], gains_ref[l], RATE_GAIN
            )

    grad = all_ref[s]
    grad_ref[0] = grad
    first_ref[0], second_ref[0], new_ref[0] = adam(grad, a_ref[0], b_ref[0], m_ref[0], RATE_WEIGHT)


def slots_update(half, me, owner_row, moved, ready, master, first, second, gains, gain_first, gain_second):
    tile = pl.BlockSpec((1, TR, PART), lambda s, *_: (s, 0, 0))
    return call(
        slots_kernel,
        (half, me, owner_row, moved, ready, master, first, second, gains, gain_first, gain_second),
        [sds((CAP, TR, PART), F32)] * 4 + [sds((LAYERS, 2, PART), F32)] * 4,
        grid=(CAP,),
        specs={3: tile, 4: tile, 5: tile},
        out_specs={i: tile for i in range(4)},
        scratch=[pltpu.VMEM((CAP, TR, PART), F32)],
        prefetch=2,
        in_place=(3, 4, 5),
        name="slots_update",
    )


def turned(col):
    same = iota((TOK, TOK), 0) == iota((TOK, TOK), 1)
    return jnp.sum(jnp.where(same, col, 0), axis=0, keepdims=True)


def plan_kernel(group_ref, mine_ref, source_ref, *outs):
    same = iota((TOK, TOK), 0) == iota((TOK, TOK), 1)
    b = iota((ROWS, 1), 0) & 7
    block = group_ref[0] * 8 + b
    before = (group_ref[0] * 8 - 1) & 63
    lanes = iota((ROWS, TOK), 1)
    for l in range(LAYERS):
        rank_row, rank_col, place_row, place_col = outs[4 * l : 4 * l + 4]
        cols = jnp.zeros((TOK, TOK), I32)
        for r in range(ROUNDS):
            row = mine_ref[l * ROUNDS + r : l * ROUNDS + r + 1, :]
            col = jnp.sum(jnp.where(same, row, 0), axis=1, keepdims=True)
            rank_row[r : r + 1, :] = jnp.sum(jnp.where(col < row, 1, 0), axis=0, keepdims=True)
            rank = jnp.sum(jnp.where(row < col, 1, 0), axis=1, keepdims=True)
            cols = jnp.where(lanes[:TOK] == r, rank, cols)
        rank_col[...] = cols
        source = source_ref[l]
        target = jnp.broadcast_to(source[:, None, :], (NW, 8, TOK)).reshape(ROWS, TOK)
        place = target & (TOK - 1)
        got = []
        for want in (block, before):
            inside = (target >> 7) == want
            got.append(jnp.min(jnp.where(inside, place, TOK), axis=1, keepdims=True))
            got.append(jnp.max(jnp.where(inside, place, -1), axis=1, keepdims=True))
        low, high, low_lent, high_lent = got
        columns = (
            low + TOK * b,
            high + TOK * b,
            jnp.where(b == 0, low_lent - SPAN, jnp.where(b == 2, high_lent - SPAN, -1)),
            jnp.where(b == 1, low_lent - SPAN, jnp.where(b == 3, high_lent - SPAN, -1)),
        )
        cols = jnp.zeros((ROWS, TOK), I32)
        for j, column in enumerate(columns):
            cols = jnp.where(lanes == j, column, cols)
            for q in range(4):
                at = slice(q * TOK, (q + 1) * TOK)
                place_row[j : j + 1, at] = turned(column[at])
        place_col[...] = cols


def plan(group, mine, source):
    layer = [kept((ROUNDS, TOK), I32), kept((TOK, TOK), I32), kept((4, ROWS), I32), kept((ROWS, TOK), I32)]
    return call(plan_kernel, (group, mine, source), layer * LAYERS, prefetch=1, name="plan")


def inner_kernel(half_ref, *refs):
    count = len(refs) // 3
    n = half_ref[0]
    feature = feature_of(iota((1, D), 1))
    mine = hot(feature == iota((PART, 1), 0) + n * PART)
    theirs = hot(feature == iota((PART, 1), 0) + (1 - n) * PART)
    for i in range(count):
        own, other, out = refs[2 * i], refs[2 * i + 1], refs[2 * count + i]
        if own.dtype == BF16:
            out[...] = dot(own[...], mine, 1, 0) + dot(other[...], theirs, 1, 0)
        else:
            total = jnp.zeros(out.shape, F32)
            for a, b in zip(pieces(own[...]), pieces(other[...])):
                total = total + (dot(a.astype(BF16), mine, 1, 0) + dot(b.astype(BF16), theirs, 1, 0))
            out[...] = total


def inner(half, pairs, name):
    flat = [a for pair in pairs for a in pair]
    outs = [sds((own.shape[0], D), F32) for own, _ in pairs]
    return call(inner_kernel, (half, *flat), outs, prefetch=1, name=name)


def outer_kernel(count, half_ref, *refs):
    n = half_ref[0]
    feature = feature_of(iota((1, D), 1))
    back = hot(feature == iota((PART, 1), 0) + n * PART)
    for i in range(count):
        total = jnp.zeros(refs[count + i].shape, F32)
        for part in pieces(refs[i][...]):
            total = total + dot(part.astype(BF16), back, 1, 1)
        refs[count + i][...] = total


def outer(half, arrays, name):
    outs = [sds((a.shape[0], PART), F32) for a in arrays]
    return call(
        functools.partial(outer_kernel, len(arrays)), (half, *arrays), outs, prefetch=1, name=name
    )


def project_kernel(pending, count, core_ref, *refs):
    if pending:
        x_ref, own_ref, other_ref, *rest = refs
        x = x_ref[...] + (own_ref[...] + other_ref[...].astype(F32))
    else:
        x_ref, *rest = refs
        x = x_ref[...]
    gain_ref, *rest = rest
    q_refs, v_refs = rest[:count], rest[count : 2 * count]
    rank_ref, x_out, hn_out, send_out = rest[2 * count :]
    core = core_ref[0]
    x_out[...] = x
    xhat, _ = norm_parts(x)
    hn = xhat * gain_ref[...]
    hn_out[0] = hn[:, :PART].astype(BF16)
    hn_out[1] = hn[:, PART:].astype(BF16)
    q = into(core, hn, q_refs).astype(BF16)
    v = into(core, hn, v_refs).astype(BF16)
    qv = jnp.concatenate([m[:, h * DH : (h + 1) * DH] for h in range(HN) for m in (q, v)], 1)
    for r in range(ROUNDS):
        moved = dot(send_hots(rank_ref[r : r + 1, :]), qv, 1, 0)
        even, odd = moved[:NW].astype(BF16), moved[NW : 2 * NW].astype(BF16)
        lent_q, lent_v = moved[2 * NW : 3 * NW], moved[3 * NW :]
        for h in range(HN):
            rows = slice((r * HN + h) * NW, (r * HN + h + 1) * NW)
            at = h * 2 * DH
            send_out[rows, : 2 * DH] = even[:, at : at + 2 * DH]
            send_out[rows, 2 * DH : 4 * DH] = odd[:, at : at + 2 * DH]
            send_out[rows, 4 * DH :] = (
                lent_q[:, at : at + DH] + lent_v[:, at + DH : at + 2 * DH]
            ).astype(BF16)


def project(core, x, pending, gain, wq, wv, rank_row):
    args, specs = unpacked([core, x, *(pending or ()), gain, wq, wv, rank_row], 1)
    return call(
        functools.partial(project_kernel, pending is not None, len(wq.parts())),
        args,
        [kept((TOK, D), F32), kept((2, TOK, PART), BF16), kept((ROWS, QV_LANES), BF16)],
        specs=specs,
        in_place=(0, *(tuple(specs) if len(wq.parts()) == 4 else ())),
        prefetch=1,
        name="project",
    )


def scores_of(rows):
    keys = rows[:, :DH].astype(F32)
    inv = lax.rsqrt(jnp.sum(keys * keys, axis=-1, keepdims=True) + 1e-06)
    unit = (keys * inv).astype(BF16)
    scores = jnp.concatenate(
        [
            dot(
                rows[(c + 1) * SPAN : (c + 2) * SPAN, :DH],
                unit[c * SPAN : (c + 2) * SPAN],
                1,
                1,
            )
            for c in range(16)
        ],
        0,
    )
    own = iota((1024, TOK), 1) == (iota((1024, TOK), 0) & (SPAN - 1)) + SPAN
    scores = jnp.where(own, MASK_FILL, scores)
    peak = jnp.max(scores, axis=-1, keepdims=True)
    total = peak + jnp.log(jnp.sum(jnp.exp(scores - peak), axis=-1, keepdims=True))
    exact = jnp.exp(scores - total)
    return keys, inv, unit, own, total, exact


def arrive(place_row_ref, j, rows):
    count = 1024 if j < 2 else SPAN
    return dot(hot(iota((count, 1), 0) == place_row_ref[j : j + 1, :]), rows, 1, 0)


def leave(place_col_ref, j, rows):
    return dot(hot(place_col_ref[:, j : j + 1] == iota((1, rows.shape[0]), 1)), rows, 1, 0)


def attend_kernel(moved_ref, place_row_ref, place_col_ref, sorted_out, send_out):
    q_lent = arrive(place_row_ref, 2, moved_ref[:, 4 * DH :])
    v_lent = arrive(place_row_ref, 3, moved_ref[:, 4 * DH :])
    main = arrive(place_row_ref, 0, moved_ref[:, : 2 * DH]) + arrive(
        place_row_ref, 1, moved_ref[:, 2 * DH : 4 * DH]
    )
    rows = jnp.concatenate([jnp.concatenate([q_lent, v_lent], 1), main], 0).astype(BF16)
    sorted_out[...] = rows
    _, _, _, _, total, exact = scores_of(rows)
    probs = exact.astype(BF16)
    outs = jnp.concatenate(
        [
            dot(probs[c * SPAN : (c + 1) * SPAN], rows[c * SPAN : (c + 2) * SPAN, DH:], 1, 0)
            for c in range(16)
        ],
        0,
    )
    aux = spread(total, iota((1024, TOK), 1))
    both = jnp.concatenate([outs, aux], 1).astype(BF16)
    even = leave(place_col_ref, 0, both)
    odd = leave(place_col_ref, 1, both)
    send_out[:, :DH] = even[:, :DH].astype(BF16)
    send_out[:, DH : 2 * DH] = odd[:, :DH].astype(BF16)
    lanes = iota((ROWS, TOK), 1)
    send_out[:, 2 * DH :] = either(lanes, even[:, DH:], odd[:, DH:]).astype(BF16)


def attend(moved, place_row, place_col):
    return call(
        attend_kernel,
        (moved, place_row, place_col),
        [kept((1088, 2 * DH), BF16), kept((ROWS, O_LANES), BF16)],
        in_place=(1, 2),
        name="attend",
    )


def by_head(ref, r, cols):
    return jnp.concatenate(
        [ref[(r * HN + h) * NW : (r * HN + h + 1) * NW, cols] for h in range(HN)], 1
    )


def merge_kernel(count, core_ref, moved_ref, rank_col_ref, *refs):
    w_refs, refs = refs[:count], refs[count:]
    part_out, send_out, o_out, share_out, merged_out = refs
    lanes = iota((TOK, TOK), 1)
    outs, logs = [], []
    for r in range(ROUNDS):
        hots = return_hots(rank_col_ref[:, r : r + 1], 2)
        aux = by_head(moved_ref, r, slice(2 * DH, 3 * DH))
        even = dot(
            hots[:, :NW], jnp.concatenate([by_head(moved_ref, r, slice(0, DH)), aux], 1), 1, 0
        )
        odd = dot(
            hots[:, NW:], jnp.concatenate([by_head(moved_ref, r, slice(DH, 2 * DH)), aux], 1), 1, 0
        )
        outs.append(even[:, :PART] + odd[:, :PART])
        o_out[r] = outs[r].astype(BF16)
        logs.append(
            [
                jnp.sum(
                    either(
                        lanes,
                        even[:, PART + h * DH : PART + (h + 1) * DH],
                        odd[:, PART + h * DH : PART + (h + 1) * DH],
                    ),
                    axis=-1,
                    keepdims=True,
                )
                for h in range(HN)
            ]
        )
    merged = []
    share_all = jnp.zeros((TOK, TOK), F32)
    for h in range(HN):
        top = jnp.maximum(logs[0][h], logs[1][h])
        e0 = jnp.exp(logs[0][h] - top)
        e1 = jnp.exp(logs[1][h] - top)
        total = e0 + e1
        cols = slice(h * DH, (h + 1) * DH)
        s0, s1 = e0 / total, e1 / total
        merged.append(s0 * outs[0][:, cols] + s1 * outs[1][:, cols])
        share_all = jnp.where(lanes == h, s0, jnp.where(lanes == HN + h, s1, share_all))
    share_out[...] = share_all
    merged = jnp.concatenate(merged, 1).astype(BF16)
    merged_out[...] = merged
    put_halves(out_of(core_ref[0], merged, w_refs), part_out, send_out)


def put_halves(pair, part_out, send_out):
    for i in range(2):
        cols = slice(i * PART, (i + 1) * PART)
        part_out[:, cols] = pair[i]
        send_out[:, cols] = pair[i].astype(BF16)


def merge(core, moved, rank_col, wo):
    args, specs = unpacked([core, moved, rank_col, wo], 1)
    return call(
        functools.partial(merge_kernel, len(wo.parts())),
        args,
        [
            sds((TOK, D), F32),
            kept((TOK, D), BF16),
            kept((ROUNDS, TOK, PART), BF16),
            kept((TOK, TOK), F32),
            kept((TOK, PART), BF16),
        ],
        specs=specs,
        in_place=(1, *specs),
        prefetch=1,
        name="merge",
    )


def ffn_specs(at, index):
    return {
        at + z: pl.BlockSpec((1, 1, 2, FFN_ROWS, PART), lambda c, z=z: (z, c, 0, index, 0))
        for z in range(4)
    }


def ffn_half(refs, c0):
    return jnp.concatenate([r[0, 0, c0] for r in refs], 0)


def ffn_kernel(
    x_ref, own_ref, other_ref, gain_ref, *refs
):
    up_ref, down_ref = refs[:4], refs[4:8]
    y_out, hf_out, pre_out, act_out, part_out, send_out, hf_ref, acc_ref = refs[8:]
    c = pl.program_id(0)

    @pl.when(c == 0)
    def _():
        y = x_ref[...] + (own_ref[...] + other_ref[...].astype(F32))
        y_out[...] = y
        xhat, _ = norm_parts(y)
        hf = (xhat * gain_ref[...]).astype(BF16)
        for c0 in range(2):
            hf_ref[c0] = hf[:, c0 * PART : (c0 + 1) * PART]
        hf_out[...] = hf_ref[...]
        acc_ref[...] = jnp.zeros_like(acc_ref)

    pre = dot(hf_ref[0], ffn_half(up_ref, 0), 1, 0) + dot(hf_ref[1], ffn_half(up_ref, 1), 1, 0)
    pre_out[...] = pre
    act = (0.5 * pre * (1.0 + lax.erf(pre * (0.5**0.5)))).astype(BF16)
    act_out[...] = act
    for c0 in range(2):
        acc_ref[c0] += dot(act, ffn_half(down_ref, c0), 1, 1)

    @pl.when(c == QUAD - 1)
    def _():
        put_halves((acc_ref[0], acc_ref[1]), part_out, send_out)


def ffn(x, own, other, gain, w):
    cols = pl.BlockSpec((TOK, PART), lambda c: (0, c))
    return call(
        ffn_kernel,
        (x, own, other, gain, *[w] * 8),
        [
            kept((TOK, D), F32),
            kept((2, TOK, PART), BF16),
            kept((TOK, QUAD * PART), F32),
            kept((TOK, QUAD * PART), BF16),
            sds((TOK, D), F32),
            kept((TOK, D), BF16),
        ],
        grid=(QUAD,),
        specs={**ffn_specs(4, UP), **ffn_specs(8, DOWN)},
        in_place=(0, *range(4, 12)),
        out_specs={2: cols, 3: cols},
        scratch=[pltpu.VMEM((2, TOK, PART), BF16), pltpu.VMEM((2, TOK, PART), F32)],
        name="ffn",
    )


def put_pieces(out_ref, at, row, rows, grad):
    for piece in range(32):
        z, tau, y = piece >> 3, (piece >> 1) & 3, piece & 1
        got = grad[piece * 16 : (piece + 1) * 16]
        if rows == 16:
            out_ref[2 * tau + at, z * 2 + y, row : row + 16] = got
        else:
            out_ref[at, z * 2 + y, row + tau * 16 : row + (tau + 1) * 16] = got


def ffn_back_kernel(pending, *refs):
    if pending:
        g_ref, own_ref, other_ref, x_ref, gain_ref, *rest = refs
    else:
        g_ref, *rest = refs
    pre_ref, hf_ref, act_ref, *rest = rest
    up_ref, down_ref, rest = rest[:4], rest[4:8], rest[8:]
    g_out, part_out, send_out, dgain_out, grad_out, back_ref, acc_ref = rest
    c = pl.program_id(0)

    @pl.when(c == 0)
    def _():
        g = g_ref[...]
        if pending:
            xhat, rstd = norm_parts(x_ref[...])
            add, dgain = norm_back(
                own_ref[...] + other_ref[...].astype(F32), gain_ref[...], xhat, rstd
            )
            g = g + add
            dgain_out[...] = dgain
        else:
            dgain_out[...] = jnp.zeros_like(dgain_out)
        g_out[...] = g
        back = g.astype(BF16)
        for c0 in range(2):
            back_ref[c0] = back[:, c0 * PART : (c0 + 1) * PART]
        acc_ref[...] = jnp.zeros_like(acc_ref)

    d_act = dot(back_ref[0], ffn_half(down_ref, 0), 1, 0) + dot(
        back_ref[1], ffn_half(down_ref, 1), 1, 0
    )
    pre = pre_ref[...]
    slope = 0.5 * (1.0 + lax.erf(pre * (0.5**0.5))) + pre * (
        jnp.exp(-0.5 * pre * pre) * np.float32(1.0 / np.sqrt(2.0 * np.pi))
    )
    d_pre = (d_act * slope).astype(BF16)
    for c0 in range(2):
        acc_ref[c0] += dot(d_pre, ffn_half(up_ref, c0), 1, 1)
        put_pieces(grad_out, c0, 0, 64, dot(hf_ref[c0], d_pre, 0, 0).astype(BF16))
        put_pieces(grad_out, c0, 64, 64, dot(back_ref[c0], act_ref[...], 0, 0).astype(BF16))

    @pl.when(c == QUAD - 1)
    def _():
        put_halves((acc_ref[0], acc_ref[1]), part_out, send_out)


def ffn_back(g, pending, pre, hf, act, w):
    cols = pl.BlockSpec((TOK, PART), lambda c: (0, c))
    args = [g, *(pending or ()), pre, hf, act, *[w] * 8]
    at = len(args) - 11
    specs = {at: cols, at + 2: cols, **ffn_specs(at + 3, UP), **ffn_specs(at + 7, DOWN)}
    in_place = (0, *((3,) if pending else ()), *range(at, at + 11))
    return call(
        functools.partial(ffn_back_kernel, pending is not None),
        args,
        [
            kept((TOK, D), F32),
            sds((TOK, D), F32),
            kept((TOK, D), BF16),
            sds((1, D), F32),
            kept((2 * QUAD, 8, FFN_ROWS, PART), BF16),
        ],
        grid=(QUAD,),
        specs=specs,
        in_place=in_place,
        out_specs={4: pl.BlockSpec((2, 8, FFN_ROWS, PART), lambda c: (c, 0, 0, 0))},
        scratch=[pltpu.VMEM((2, TOK, PART), BF16), pltpu.VMEM((2, TOK, PART), F32)],
        name="ffn_back",
    )


def merge_back_kernel(count, core_ref, g_ref, own_ref, other_ref, y_ref, gain_ref, *refs):
    w_refs, refs = refs[:count], refs[count:]
    o_ref, share_ref, rank_row_ref, g_out, back_out, send_out, dgain_out = refs
    xhat, rstd = norm_parts(y_ref[...])
    add, dgain = norm_back(own_ref[...] + other_ref[...].astype(F32), gain_ref[...], xhat, rstd)
    dgain_out[...] = dgain
    g = g_ref[...] + add
    g_out[...] = g
    back_out[0] = g[:, :PART].astype(BF16)
    back_out[1] = g[:, PART:].astype(BF16)
    dout = into(core_ref[0], g, w_refs)
    share = share_ref[...]
    o0 = o_ref[0].astype(F32)
    o1 = o_ref[1].astype(F32)
    lanes = iota((TOK, TOK), 1)
    parts = [[], []]
    logs = [[], []]
    for h in range(HN):
        cols = slice(h * DH, (h + 1) * DH)
        s0 = share[:, h : h + 1]
        s1 = share[:, HN + h : HN + h + 1]
        dh = dout[:, cols]
        t0 = jnp.sum(dh * o0[:, cols], axis=-1, keepdims=True)
        t1 = jnp.sum(dh * o1[:, cols], axis=-1, keepdims=True)
        mean = s0 * t0 + s1 * t1
        parts[0].append(s0 * dh)
        parts[1].append(s1 * dh)
        logs[0].append(spread(s0 * (t0 - mean), lanes))
        logs[1].append(spread(s1 * (t1 - mean), lanes))
    lanes = iota((NW, TOK), 1)
    for r in range(ROUNDS):
        moved = dot(
            send_hots(rank_row_ref[r : r + 1, :], 2),
            jnp.concatenate(parts[r] + logs[r], 1).astype(BF16),
            1,
            0,
        )
        even, odd = moved[:NW], moved[NW:]
        for h in range(HN):
            rows = slice((r * HN + h) * NW, (r * HN + h + 1) * NW)
            cols = slice(h * DH, (h + 1) * DH)
            aux = slice(PART + h * DH, PART + (h + 1) * DH)
            send_out[rows, :DH] = even[:, cols].astype(BF16)
            send_out[rows, DH : 2 * DH] = odd[:, cols].astype(BF16)
            send_out[rows, 2 * DH :] = either(lanes, even[:, aux], odd[:, aux]).astype(BF16)


def merge_back(core, g, own, other, y, gain, wo, o, share, rank_row):
    args, specs = unpacked([core, g, own, other, y, gain, wo, o, share, rank_row], 1)
    return call(
        functools.partial(merge_back_kernel, len(wo.parts())),
        args,
        [
            kept((TOK, D), F32),
            kept((2, TOK, PART), BF16),
            kept((ROWS, O_LANES), BF16),
            sds((1, D), F32),
        ],
        specs=specs,
        in_place=(0, 3, *specs, *range(len(args) - 4, len(args) - 1)),
        prefetch=1,
        name="merge_back",
    )


def attend_back_kernel(moved_ref, sorted_ref, place_row_ref, place_col_ref, gain_ref, send_out):
    lanes = iota((ROWS, TOK), 1)
    aux = moved_ref[:, 2 * DH :].astype(F32)
    got = jnp.zeros((1024, 2 * DH), F32)
    for j in range(2):
        here = jnp.where(lanes >> 3 == j, aux, 0.0).astype(BF16)
        pair = jnp.concatenate([moved_ref[:, j * DH : (j + 1) * DH], here], 1)
        got = got + arrive(place_row_ref, j, pair)
    d_out = got[:, :DH].astype(BF16)
    d_log = jnp.sum(got[:, DH:], axis=-1, keepdims=True)
    rows = sorted_ref[...]
    keys, inv, unit, own, _, exact = scores_of(rows)
    probs = exact.astype(BF16)
    g_probs = jnp.concatenate(
        [
            dot(d_out[c * SPAN : (c + 1) * SPAN], rows[c * SPAN : (c + 2) * SPAN, DH:], 1, 1)
            for c in range(16)
        ],
        0,
    )
    inner_sum = jnp.sum(g_probs * exact, axis=-1, keepdims=True)
    g_scores = exact * (g_probs - inner_sum + d_log)
    g_scores = jnp.where(own, 0.0, g_scores).astype(BF16)
    d_query, d_unit, d_value = [], [], []
    for c in range(16):
        here = slice(c * SPAN, (c + 1) * SPAN)
        both = slice(c * SPAN, (c + 2) * SPAN)
        after = slice((c + 1) * SPAN, (c + 2) * SPAN)
        d_query.append(dot(g_scores[here], unit[both], 1, 0))
        d_unit.append(dot(g_scores[here], rows[after, :DH], 0, 0))
        d_value.append(dot(probs[here], d_out[here], 0, 0))

    def overlap(parts):
        out = [parts[0][:SPAN]]
        for c in range(15):
            out.append(parts[c][SPAN:] + parts[c + 1][:SPAN])
        out.append(parts[15][SPAN:])
        return jnp.concatenate(out, 0)

    g_unit = overlap(d_unit)
    along = jnp.sum(g_unit * keys, axis=-1, keepdims=True)
    g_keys = inv * g_unit - keys * (inv * inv * inv) * along
    g_query = jnp.concatenate([jnp.zeros((SPAN, DH), F32)] + d_query, 0) + g_keys
    grads = jnp.concatenate([g_query, overlap(d_value)], 1).astype(BF16)
    for j in range(2):
        cols = slice(j * 2 * DH, (j + 1) * 2 * DH)
        send_out[:, cols] = leave(place_col_ref, j, grads[SPAN:]).astype(BF16)
    lent = leave(place_col_ref, 2, grads[:SPAN, :DH]) + leave(place_col_ref, 3, grads[:SPAN, DH:])
    b = iota((ROWS, 1), 0) & 7
    for q in range(4):
        lent = jnp.where(b == 4 + q, gain_ref[:, q * DH : (q + 1) * DH], lent)
    send_out[:, 4 * DH :] = lent.astype(BF16)


def attend_back(moved, rows, place_row, place_col, gain):
    return call(
        attend_back_kernel,
        (moved, rows, place_row, place_col, gain),
        [kept((ROWS, QV_LANES), BF16)],
        in_place=(1, 2, 3),
        name="attend_back",
    )[0]


def project_back_kernel(count, grads, core_ref, moved_ref, rank_col_ref, *refs):
    q_refs, v_refs = refs[:count], refs[count : 2 * count]
    refs = refs[2 * count :]
    if grads:
        back_ref, merged_ref, hn_ref, *refs = refs
        part_out, send_out, grad_out, gain_out = refs
    else:
        part_out, send_out, dq_out, dv_out, gain_out = refs
    gain_out[...] = dot(
        hot(iota((8, 1), 0) == (iota((1, ROWS), 1) & 7)), moved_ref[:, 4 * DH :], 1, 0
    )
    total = jnp.zeros((TOK, HN * 2 * DH), F32)
    lent_q = jnp.zeros((TOK, PART), F32)
    lent_v = jnp.zeros((TOK, PART), F32)
    for r in range(ROUNDS):
        hots = return_hots(rank_col_ref[:, r : r + 1])
        total = total + dot(hots[:, :NW], by_head(moved_ref, r, slice(0, 2 * DH)), 1, 0)
        total = total + dot(hots[:, NW : 2 * NW], by_head(moved_ref, r, slice(2 * DH, 4 * DH)), 1, 0)
        lent = by_head(moved_ref, r, slice(4 * DH, 5 * DH))
        lent_q = lent_q + dot(hots[:, 2 * NW : 3 * NW], lent, 1, 0)
        lent_v = lent_v + dot(hots[:, 3 * NW :], lent, 1, 0)
    d_q = jnp.concatenate([total[:, h * 2 * DH : h * 2 * DH + DH] for h in range(HN)], 1)
    d_v = jnp.concatenate([total[:, h * 2 * DH + DH : (h + 1) * 2 * DH] for h in range(HN)], 1)
    d_q = (d_q + lent_q).astype(BF16)
    d_v = (d_v + lent_v).astype(BF16)
    if grads:
        for c0 in range(2):
            for i, (left, right) in enumerate(
                ((back_ref, merged_ref[...]), (hn_ref, d_q), (hn_ref, d_v))
            ):
                put_pieces(grad_out, c0, i * 16, 16, dot(left[c0], right, 0, 0).astype(BF16))
    else:
        dq_out[...] = d_q
        dv_out[...] = d_v
    core = core_ref[0]
    from_q = out_of(core, d_q, q_refs)
    from_v = out_of(core, d_v, v_refs)
    put_halves([a + b for a, b in zip(from_q, from_v)], part_out, send_out)


def project_back(core, moved, rank_col, wq, wv, lefts=None):
    args, specs = unpacked([core, moved, rank_col, wq, wv, *(lefts or ())], 1)
    if lefts:
        outs = [kept((2 * QUAD, 8, ATTN_ROWS, PART), BF16)]
    else:
        outs = [kept((TOK, PART), BF16)] * 2
    return call(
        functools.partial(project_back_kernel, len(wq.parts()), lefts is not None),
        args,
        [sds((TOK, D), F32), kept((TOK, D), BF16), *outs, sds((8, DH), F32)],
        specs=specs,
        in_place=range(1, len(args) - 1),
        prefetch=1,
        name="project_back",
    )


def last_kernel(g_ref, own_ref, other_ref, x_ref, gain_ref, g_out, dgain_out):
    xhat, rstd = norm_parts(x_ref[...])
    add, dgain = norm_back(own_ref[...] + other_ref[...].astype(F32), gain_ref[...], xhat, rstd)
    g_out[...] = g_ref[...] + add
    dgain_out[...] = dgain


def last(g, own, other, x, gain):
    return call(
        last_kernel,
        (g, own, other, x, gain),
        [kept((TOK, D), F32), sds((1, D), F32)],
        in_place=(0, 3),
        name="last",
    )


def pair_dot(left_a, left_b, right_a, right_b):
    left = jnp.concatenate([left_a, left_b], 0)
    right = jnp.concatenate([right_a, right_b], 0)
    return dot(left, right, 0, 0).astype(BF16)


def attn_grad_kernel(count, core_ref, *refs):
    out_ref = refs[-1]
    for i in range(count):
        la, lb, ra, rb = refs[4 * i : 4 * i + 4]
        got = pair_dot(la[0], lb[0], ra[...], rb[...])
        out_ref[:, i * 16 : (i + 1) * 16] = got.reshape(32, 16, PART)


def attn_grad(core, pairs):
    half = pl.BlockSpec((1, TOK, PART), lambda i, core: (core[0], 0, 0))
    args = [a for left, right in pairs for a in (*left, *right)]
    specs = {4 * i + j: half for i in range(len(pairs)) for j in range(2)}
    return call(
        functools.partial(attn_grad_kernel, len(pairs)),
        (core, *args),
        [kept((32, 16 * len(pairs), PART), BF16)],
        specs=specs,
        prefetch=1,
        in_place=range(0, len(args), 2),
        name="attn_grad",
    )[0]


def join_kernel(*refs):
    at = 0
    for ref in refs[:-1]:
        refs[-1][:, at : at + ref.shape[1]] = ref[...]
        at += ref.shape[1]


def join(arrays):
    rows = sum(a.shape[1] for a in arrays)
    return call(
        join_kernel,
        arrays,
        [kept((8, rows, PART), BF16)],
        grid=(4,),
        specs={
            i: pl.BlockSpec((2, a.shape[1], PART), lambda g: (g, 0, 0)) for i, a in enumerate(arrays)
        },
        out_specs={0: pl.BlockSpec((2, rows, PART), lambda g: (g, 0, 0))},
        in_place=range(len(arrays)),
        name="join",
    )[0]


def swap_narrow(values):
    return lax.ppermute(values, "narrow", [(0, 1), (1, 0)])


def with_core(values):
    other = lax.ppermute(values, "wide", [(i, i ^ 1) for i in range(NW)])
    return values, other


def to_all(values):
    return lax.all_to_all(values, "wide", split_axis=0, concat_axis=0, tiled=True)


SAME_CORE = [
    [y * 32 + z * 8 + x * 2 + c for z in range(4) for x in range(4) for y in range(2)]
    for c in range(2)
]
LAYER_OF_Y = [[y * 32 + i for i in range(NW // 2)] for y in range(2)]


def summed(values):
    return jnp.sum(to_same_core(values).astype(F32), axis=0).astype(BF16)


ALONG_X_AND_CORE = [[hi * 8 + i for i in range(8)] for hi in range(8)]
ALONG_Z_AND_Y = [
    [y * 32 + z * 8 + i for z in range(4) for y in range(2)] for i in range(8)
]
ALONG_Z = [
    [y * 32 + z * 8 + x * 2 + c for z in range(4)] for y in range(2) for x in range(4) for c in range(2)
]


def summed_along_x(values):
    return lax.psum_scatter(
        values, "wide", scatter_dimension=0, tiled=True, axis_index_groups=ALONG_X_AND_CORE
    ).reshape(values.shape[1:])


def summed_across_x(values):
    moved = lax.all_to_all(
        values, "wide", split_axis=0, concat_axis=0, tiled=True, axis_index_groups=ALONG_Z_AND_Y
    )
    return jnp.sum(moved.astype(F32), axis=0).astype(BF16)


def summed_along_z(values):
    return lax.psum_scatter(
        values, "wide", scatter_dimension=0, tiled=True, axis_index_groups=ALONG_Z
    )


def summed_along_y(values):
    y = lax.axis_index("wide") >> 5
    mine = lax.dynamic_index_in_dim(values, y, keepdims=False)
    theirs = lax.dynamic_index_in_dim(values, 1 - y, keepdims=False)
    got = lax.ppermute(theirs, "wide", [(i, i ^ 32) for i in range(NW)])
    return (mine.astype(F32) + got.astype(F32)).astype(BF16)


def to_same_core(values):
    return lax.all_to_all(
        values, "wide", split_axis=0, concat_axis=0, tiled=True, axis_index_groups=SAME_CORE
    )


def after(values, *others):
    return lax.optimization_barrier((values, others))[0]


def gathered(rows):
    other = lax.ppermute(rows, "wide", [(i, i ^ 32) for i in range(NW)])
    low = lax.axis_index("wide") < 32
    both = jnp.stack(
        [
            jnp.where(low, a, b).reshape(-1, 16, PART) for a, b in ((rows, other), (other, rows))
        ],
        1,
    ).reshape(-1, PART)
    got = lax.all_gather(both, "wide", axis=0, tiled=True, axis_index_groups=LAYER_OF_Y)
    return got.reshape(QUAD, QUAD, 2, both.shape[0], PART)


def moved_rows(rows):
    return to_all(rows.reshape(NW, rows.shape[0] // NW, -1)).reshape(rows.shape)


def on_device(
    x_first,
    x_second,
    grad_first,
    grad_second,
    sort_target,
    owner,
    master,
    moment_first,
    moment_second,
    gains,
    gain_first,
    gain_second,
):
    me = lax.axis_index("wide").astype(I32)
    half = lax.axis_index("narrow").astype(I32).reshape(1)
    core = (me & 1).reshape(1)
    owner_row = owner.reshape(1, TILES)

    routed = route_out(me.reshape(1), owner_row, master)
    sort_target, held = after((sort_target, owner), routed)
    moved = moved_rows(routed)
    held_by = []
    for l in range(LAYERS):
        of = held[l * 88 : (l + 1) * 88]
        held_by += [of[at : at + 32].reshape(8, 4).T.reshape(32) for at in (24, 56)]
        held_by += [of[16:24], of[:16]]
    held_by = jnp.repeat(jnp.concatenate(held_by), 2)
    code = (held_by // CAP) * PACK + (held_by % CAP) * 2 + np.arange(2 * TILES, dtype=np.int32) % 2
    code_col = code.reshape(-1, 1)
    code_row = code.reshape(1, -1)
    mine = lax.dynamic_slice_in_dim(sort_target, me * TOK, TOK, axis=2).reshape(-1, TOK)
    by_source = lax.dynamic_index_in_dim(sort_target, me >> 5, 1, keepdims=False)
    plans = plan((me & 7).reshape(1), mine, by_source.reshape(LAYERS, NW, TOK))
    rank_rows, rank_cols, place_rows, place_cols = [plans[i::4] for i in range(4)]
    flat_gains = gains.reshape(LAYERS * 2, PART)
    x_two, gain_rows = inner(
        half, [(x_second, swap_narrow(x_second)), (flat_gains, swap_narrow(flat_gains))], "inner_a"
    )
    moved = after(moved, code_col, code_row, plans, x_two, gain_rows)
    first_rows, early_rows, late_rows = pick(code_col, moved)
    x_first, grad_first, grad_second = after((x_first, grad_first, grad_second), x_two)
    pairs = [(a, swap_narrow(a)) for a in (x_first, grad_first, grad_second)]
    first_w = with_core(after(to_same_core(first_rows), pairs))
    early = gathered(early_rows)
    late = gathered(after(late_rows, first_w))
    x_one, g_one, g_two = inner(half, pairs, "inner_b")
    w_ffn = [early, late]
    w_attn = [
        [Weight(8, early), Weight(0, *first_w), Weight(1, *first_w)],
        [Weight(9, early), Weight(10, early), Weight(11, early)],
    ]
    gain = [[gain_rows[2 * l + i].reshape(1, D) for i in range(2)] for l in range(LAYERS)]

    saved = []
    pending = None
    for l in range(LAYERS):
        w_out, w_qk, w_value = w_attn[l]
        x_two, hn, send = project(core, x_two, pending, gain[l][0], w_qk, w_value, rank_rows[l])
        moved = moved_rows(send)
        if l == 0:
            moved = after(moved, x_one, g_one, g_two)
        rows, send = attend(moved, place_rows[l], place_cols[l])
        moved = moved_rows(send)
        own, send, o, share, merged = merge(core, moved, rank_cols[l], w_out)
        x_one, hf, pre, act, own_f, send_f = ffn(
            x_one, own, swap_narrow(send), gain[l][1], w_ffn[l]
        )
        pending = (own_f, swap_narrow(send_f))
        saved.append((x_two, x_one, hn, rows, o, share, merged, hf, pre, act))
    y_two = x_two + (pending[0] + pending[1].astype(F32))
    y_first, y_second = outer(half, (x_one, y_two), "outer_y")

    pending = None
    dgains = [[None, None], [None, None]]
    gain_sums = []
    for l in reversed(range(LAYERS)):
        x_in, y_mid, hn, rows, o, share, merged, hf, pre, act = saved[l]
        w_out, w_qk, w_value = w_attn[l]
        g_two, own, send, dgain, ffn_part = ffn_back(g_two, pending, pre, hf, act, w_ffn[l])
        if l == 0:
            dgains[1][0] = dgain
        other = swap_narrow(send)
        ffn_part = summed_along_x(ffn_part)
        g_one, back, send, dgains[l][1] = merge_back(
            core, g_one, own, other, y_mid, gain[l][1], w_out, o, share, rank_rows[l]
        )
        moved = moved_rows(send)
        if l > 0:
            moved = after(moved, y_first, y_second)
            half_gain = dgains[1][1][:, :PART]
        else:
            dx_first = outer(half, (g_one,), "outer_dx_first")[0]
            joined = join([ffn_before, attn_before])
            moved = after(moved, dx_first, joined)
            half_gain = dgains[1][1][:, PART:]
        send = attend_back(moved, rows, place_rows[l], place_cols[l], half_gain)
        moved = moved_rows(send)
        if l > 0:
            moved = after(moved, ffn_part)
        if l > 0:
            own, send, attn_part, gain_sum = project_back(
                core, moved, rank_cols[l], w_qk, w_value, (back, merged, hn)
            )
            attn_before = summed_along_x(attn_part)
            ffn_before = ffn_part
        else:
            own, send, dq, dv, gain_sum = project_back(core, moved, rank_cols[l], w_qk, w_value)
            hn2 = with_core(hn)
            pairs = [(with_core(back), with_core(merged)), (hn2, with_core(dq)), (hn2, with_core(dv))]
            attn_part = attn_grad(core, pairs)
            attn_rows = summed(attn_part)
            ffn_rows = summed_across_x(after(ffn_part, attn_part))
            reduced = summed_along_y(after(summed_along_z(joined), attn_part))
        other = swap_narrow(send)
        gain_sums.append(gain_sum[4:].reshape(1, PART))
        pending = (own, other, x_in, gain[l][0])
    g_two, dgains[0][0] = last(g_two, *pending)
    dx_second = outer(half, (g_two,), "outer_dx_second")[0]
    parts = (ffn_rows, attn_rows, reduced)
    back_rows = moved_rows(
        route_back(code_row, parts, (dgains[1][0], dgains[0][1], dgains[0][0]))
    )
    back_rows = after(back_rows, dx_second)
    slot_grad, slot_first, slot_second, slot_new, *gain_news = slots_update(
        half,
        me.reshape(1),
        owner_row,
        back_rows,
        jnp.concatenate(gain_sums, 1),
        master,
        moment_first,
        moment_second,
        gains,
        gain_first,
        gain_second,
    )
    gain_grad, gain_first_new, gain_second_new, gain_new = gain_news
    return (
        y_first,
        y_second,
        dx_first,
        dx_second,
        slot_grad,
        slot_first,
        slot_second,
        slot_new,
        gain_grad,
        gain_first_new,
        gain_second_new,
        gain_new,
    )


def solution(mesh):
    rows = P("wide", "narrow")
    tiles = P("wide", None, "narrow")
    gains = P(None, None, "narrow")
    return jax.shard_map(
        on_device,
        mesh=mesh,
        in_specs=(rows,) * 4 + (P(), P()) + (tiles,) * 3 + (gains,) * 3,
        out_specs=(rows,) * 4 + (tiles,) * 4 + (gains,) * 4,
        check_vma=False,
    )
```

time: 612 us -> 520 us (0.85)
  the two profiles are of different devices: /device:TPU:13 before, /device:TPU:1 now
where the time goes in v3:
time: 520 us; the launch traced here: 510 us
  waiting for transfers between devices  195 us (38%)
  Pallas kernels  119 us (23%)
  starting transfers between devices  84.5 us (16%)
  blocking collectives  79.9 us (15%)
  between operations  15.2 us (3%)
  local copies, waits for them, and re-layouts  13.1 us (3%)
    pallas_call x29, Pallas kernels, call(): pl.pallas_call(kernel, out_shape=outs, grid_spec=pltpu.PrefetchScalarGrid...  119 us
    all_to_all x6, waiting for transfers between devices, to_all(): lax.all_to_all(values, 'wide', split_axis=0, concat_axis=0, tiled=True)  81.1 us
    all_to_all x4, blocking collectives, to_all(): lax.all_to_all(values, 'wide', split_axis=0, concat_axis=0, tiled=True)  79.9 us
    ppermute x13, waiting for transfers between devices, swap_narrow(): return lax.ppermute(values, 'narrow', [(0, 1), (1, 0)])  62.8 us
    all_to_all x6, starting transfers between devices, to_all(): lax.all_to_all(values, 'wide', split_axis=0, concat_axis=0, tiled=True)  51.5 us
    all_to_all x2, waiting for transfers between devices, to_same_core(): lax.all_to_all(values, 'wide', split_axis=0, concat_axis=0, tiled=True, a...  27.5 us
    ppermute x2, waiting for transfers between devices, gathered(): other = lax.ppermute(rows, 'wide', [(i, i ^ 32) for i in range(NW)])  13.6 us
  transfers between devices with their start and end apart: 37, of which 25 were waited for; matrix products, arithmetic and copies ran while one was open for 1% of the time, Pallas kernels for 17%

profile of v3, /device:TPU:1, one launch (start us, length us, event | category | flops | bytes accessed | tf_op | source)
XLA Modules:
  0.0 509.8 jit_solution(1999018318961255729)
XLA Ops:
  14.3 12.5 %all-to-all-start = ((bf16[64,16,512]{2,1,0:T(8,128)(2,1)}), bf16[64,16,512]{2,1,0:T(8,128)(2,1)S(1)}, u32[]{:S(2)}, u32[]{:S(2)}) async-start(bf16[64,16,512]{2,1,0:T(8,128)(2,1)} %bitcast.127), calls=%async_computation | async-start | bytes 2097152 | tf_op jit(solution)/shard_map/all_to_all | solution.py:1075
  34.0 11.5 %all-to-all-done = bf16[64,16,512]{2,1,0:T(8,128)(2,1)S(1)} async-done(((bf16[64,16,512]{2,1,0:T(8,128)(2,1)}), bf16[64,16,512]{2,1,0:T(8,128)(2,1)S(1)}, u32[]{:S(2)}, u32[]{:S(2)}) %all-to-all-start) | async-done | bytes 1048608 | tf_op jit(solution)/shard_map/all_to_all | solution.py:1075
  47.9 7.4 %collective-permute-done.6 = bf16[192,512]{1,0:T(8,128)(2,1)S(1)} collective-permute-done((bf16[192,512]{1,0:T(8,128)(2,1)}, bf16[192,512]{1,0:T(8,128)(2,1)S(1)}, u32[]{:S(2)}, u32[]{:S(2)}) %collective-permute-start.6) | collective-permute-done | bytes 196640 | tf_op jit(solution)/shard_map/ppermute | solution.py:1136
  57.1 4.1 all-to-all-start.1
  63.2 6.5 %collective-permute-done.2.refs_1_ = bf16[128,512]{1,0:T(8,128)(2,1)S(1)} collective-permute-done((bf16[128,512]{1,0:T(8,128)(2,1)S(1)}, bf16[128,512]{1,0:T(8,128)(2,1)S(1)}, u32[]{:S(2)}, u32[]{:S(2)}) %collective-permute-start.2) | collective-permute-done | bytes 131104 | tf_op jit(solution)/shard_map/ppermute | solution.py:1066
  69.7 6.0 %collective-permute-done.3.refs_3_ = bf16[128,512]{1,0:T(8,128)(2,1)S(1)} collective-permute-done((bf16[128,512]{1,0:T(8,128)(2,1)S(1)}, bf16[128,512]{1,0:T(8,128)(2,1)S(1)}, u32[]{:S(2)}, u32[]{:S(2)}) %collective-permute-start.3) | collective-permute-done | bytes 131104 | tf_op jit(solution)/shard_map/ppermute | solution.py:1066
  75.7 5.3 %collective-permute-done.4.refs_5_ = bf16[128,512]{1,0:T(8,128)(2,1)S(1)} collective-permute-done((bf16[128,512]{1,0:T(8,128)(2,1)S(1)}, bf16[128,512]{1,0:T(8,128)(2,1)S(1)}, u32[]{:S(2)}, u32[]{:S(2)}) %collective-permute-start.4) | collective-permute-done | bytes 131104 | tf_op jit(solution)/shard_map/ppermute | solution.py:1066
  89.2 6.2 %collective-permute-done.10 = bf16[128,512]{1,0:T(8,128)(2,1)S(1)} collective-permute-done((bf16[128,512]{1,0:T(8,128)(2,1)S(1)}, bf16[128,512]{1,0:T(8,128)(2,1)S(1)}, u32[]{:S(2)}, u32[]{:S(2)}) %collective-permute-start.10) | collective-permute-done | bytes 131104 | tf_op jit(solution)/shard_map/ppermute | solution.py:1136
  99.1 7.6 %all-to-all-start.2 = ((bf16[64,8,640]{2,1,0:T(8,128)(2,1)}), bf16[64,8,640]{2,1,0:T(8,128)(2,1)S(1)}, u32[]{:S(2)}, u32[]{:S(2)}) async-start(bf16[64,8,640]{2,1,0:T(8,128)(2,1)} %bitcast.137), calls=%async_computation.2 | async-start | bytes 1310720 | tf_op jit(solution)/shard_map/all_to_all | solution.py:1075
  110.6 17.3 %all-to-all-done.2 = bf16[64,8,640]{2,1,0:T(8,128)(2,1)S(1)} async-done(((bf16[64,8,640]{2,1,0:T(8,128)(2,1)}), bf16[64,8,640]{2,1,0:T(8,128)(2,1)S(1)}, u32[]{:S(2)}, u32[]{:S(2)}) %all-to-all-start.2) | async-done | bytes 655392 | tf_op jit(solution)/shard_map/all_to_all | solution.py:1075
  128.0 4.3 attend.2
  132.2 18.1 %all_to_all.65 = bf16[64,8,384]{2,1,0:T(8,128)(2,1)S(1)} all-to-all(bf16[64,8,384]{2,1,0:T(8,128)(2,1)} %bitcast.143), channel_id=1, replica_groups=mesh['wide'=64,'narrow'=2] {'wide'}, dimensions={0} | all-to-all | bytes 786432 | tf_op jit(solution)/shard_map/all_to_all | solution.py:1075
  153.3 7.7 %collective-permute-done.7.other_ref = bf16[128,1024]{1,0:T(8,128)(2,1)S(1)} collective-permute-done((bf16[128,1024]{1,0:T(8,128)(2,1)}, bf16[128,1024]{1,0:T(8,128)(2,1)S(1)}, u32[]{:S(2)}, u32[]{:S(2)}) %collective-permute-start.7) | collective-permute-done | bytes 262176 | tf_op jit(solution)/shard_map/ppermute | solution.py:1066
  161.0 7.1 %ffn.2 = (f32[128,1024]{1,0:T(8,128)}, bf16[2,128,512]{2,1,0:T(8,128)(2,1)}, f32[128,2048]{1,0:T(8,128)}, bf16[128,2048]{1,0:T(8,128)(2,1)}, f32[128,1024]{1,0:T(8,128)S(1)}, /*index=5*/bf16[128,1024]{1,0:T(8,128)(2,1)}) custom-call(f32[128,1024]{1,0:T(8,128)} %copy-done.7, f32[128,1024]{1,0:T(8,128)S(1)} %get-tuple-element.138.own_ref, ...), custom_call_target="tpu_custom_call" | custom-call | tf_op jit(solution)/shard_map/ffn/pallas_call | solution.py:88
  168.6 6.1 %collective-permute-done.8.refs_2_ = bf16[128,1024]{1,0:T(8,128)(2,1)S(1)} collective-permute-done((bf16[128,1024]{1,0:T(8,128)(2,1)}, bf16[128,1024]{1,0:T(8,128)(2,1)S(1)}, u32[]{:S(2)}, u32[]{:S(2)}) %collective-permute-start.8) | collective-permute-done | bytes 262176 | tf_op jit(solution)/shard_map/ppermute | solution.py:1066
  174.7 3.7 project.3
  178.4 21.7 %all_to_all.66 = bf16[64,8,640]{2,1,0:T(8,128)(2,1)S(1)} all-to-all(bf16[64,8,640]{2,1,0:T(8,128)(2,1)} %bitcast.138), channel_id=1, replica_groups=mesh['wide'=64,'narrow'=2] {'wide'}, dimensions={0} | all-to-all | bytes 1310720 | tf_op jit(solution)/shard_map/all_to_all | solution.py:1075
  200.1 4.3 attend.3
  204.4 17.1 %all_to_all.67 = bf16[64,8,384]{2,1,0:T(8,128)(2,1)S(1)} all-to-all(bf16[64,8,384]{2,1,0:T(8,128)(2,1)} %bitcast.144), channel_id=1, replica_groups=mesh['wide'=64,'narrow'=2] {'wide'}, dimensions={0} | all-to-all | bytes 786432 | tf_op jit(solution)/shard_map/all_to_all | solution.py:1075
  224.8 7.4 %collective-permute-done.9.other_ref = bf16[128,1024]{1,0:T(8,128)(2,1)S(1)} collective-permute-done((bf16[128,1024]{1,0:T(8,128)(2,1)}, bf16[128,1024]{1,0:T(8,128)(2,1)S(1)}, u32[]{:S(2)}, u32[]{:S(2)}) %collective-permute-start.9) | collective-permute-done | bytes 262176 | tf_op jit(solution)/shard_map/ppermute | solution.py:1066
  232.2 7.1 %ffn.3 = (f32[128,1024]{1,0:T(8,128)}, bf16[2,128,512]{2,1,0:T(8,128)(2,1)}, f32[128,2048]{1,0:T(8,128)}, bf16[128,2048]{1,0:T(8,128)(2,1)}, f32[128,1024]{1,0:T(8,128)S(1)}, /*index=5*/bf16[128,1024]{1,0:T(8,128)(2,1)}) custom-call(f32[128,1024]{1,0:T(8,128)} %get-tuple-element.140.x_ref.y_ref, f32[128,1024]{1,0:T(8,128)S(1)} %get-tuple-element.146.own_ref, ...), custom_call_target="tpu_custom_call" | custom-call | tf_op jit(solution)/shard_map/ffn/pallas_call | solution.py:88
  239.4 10.3 %ffn_back.2 = (f32[128,1024]{1,0:T(8,128)}, f32[128,1024]{1,0:T(8,128)S(1)}, bf16[128,1024]{1,0:T(8,128)(2,1)}, f32[1,1024]{1,0:T(1,128)}, bf16[8,8,128,512]{3,2,1,0:T(8,128)(2,1)}) custom-call(f32[128,1024]{1,0:T(8,128)} %copy-done.6, f32[128,2048]{1,0:T(8,128)} %get-tuple-element.156.refs_1_, bf16[2,128,512]{2,1,0:T(8,128)(2,1)} %get-tuple-element.157.refs_2_, ...), custom_call_target="tpu_custom_call" | custom-call | tf_op jit(solution)/shard_map/ffn_back/pallas_call | solution.py:88
  252.2 5.1 %collective-permute-done.12.other_ref = bf16[128,1024]{1,0:T(8,128)(2,1)S(1)} collective-permute-done((bf16[128,1024]{1,0:T(8,128)(2,1)S(1)}, bf16[128,1024]{1,0:T(8,128)(2,1)S(1)}, u32[]{:S(2)}, u32[]{:S(2)}) %collective-permute-start.12) | collective-permute-done | bytes 262176 | tf_op jit(solution)/shard_map/ppermute | solution.py:1066
  257.3 4.0 merge_back.2
  261.3 8.2 %all-to-all-start.6 = ((bf16[64,8,384]{2,1,0:T(8,128)(2,1)}), bf16[64,8,384]{2,1,0:T(8,128)(2,1)S(1)}, u32[]{:S(2)}, u32[]{:S(2)}) async-start(bf16[64,8,384]{2,1,0:T(8,128)(2,1)} %bitcast.142), calls=%async_computation.6 | async-start | bytes 786432 | tf_op jit(solution)/shard_map/all_to_all | solution.py:1075
  272.5 11.6 %all-to-all-done.6 = bf16[64,8,384]{2,1,0:T(8,128)(2,1)S(1)} async-done(((bf16[64,8,384]{2,1,0:T(8,128)(2,1)}), bf16[64,8,384]{2,1,0:T(8,128)(2,1)S(1)}, u32[]{:S(2)}, u32[]{:S(2)}) %all-to-all-start.6) | async-done | bytes 393248 | tf_op jit(solution)/shard_map/all_to_all | solution.py:1075
  284.1 5.1 %attend_back.2 = bf16[512,640]{1,0:T(8,128)(2,1)} custom-call(bf16[512,384]{1,0:T(8,128)(2,1)S(1)} %bitcast.58, bf16[1088,256]{1,0:T(8,128)(2,1)} %get-tuple-element.167.sorted_ref, s32[4,512]{1,0:T(4,128)} %get-tuple-element.127.place_row_ref, s32[512,128]{1,0:T(8,128)} %get-tuple-element.128.place_col_ref, f32[1,512]{1,0:T(1,128)S(1)} %get-tuple-element.223.gain_ref), custom_call_target="tpu_custom_call" | custom-call | tf_op jit(solution)/shard_map/attend_back/pallas_call | solution.py:88
  289.2 23.0 %all_to_all.68 = bf16[64,8,640]{2,1,0:T(8,128)(2,1)S(1)} all-to-all(bf16[64,8,640]{2,1,0:T(8,128)(2,1)} %bitcast.130), channel_id=1, replica_groups=mesh['wide'=64,'narrow'=2] {'wide'}, dimensions={0} | all-to-all | bytes 1310720 | tf_op jit(solution)/shard_map/all_to_all | solution.py:1075
  312.2 5.0 project_back.2
  318.5 7.7 %collective-permute-done.13.refs_2_ = bf16[128,1024]{1,0:T(8,128)(2,1)S(1)} collective-permute-done((bf16[128,1024]{1,0:T(8,128)(2,1)S(1)}, bf16[128,1024]{1,0:T(8,128)(2,1)S(1)}, u32[]{:S(2)}, u32[]{:S(2)}) %collective-permute-start.13) | collective-permute-done | bytes 262176 | tf_op jit(solution)/shard_map/ppermute | solution.py:1066
  326.2 11.0 %ffn_back.3 = (f32[128,1024]{1,0:T(8,128)}, f32[128,1024]{1,0:T(8,128)S(1)}, bf16[128,1024]{1,0:T(8,128)(2,1)}, f32[1,1024]{1,0:T(1,128)S(1)}, bf16[8,8,128,512]{3,2,1,0:T(8,128)(2,1)}) custom-call(f32[128,1024]{1,0:T(8,128)} %get-tuple-element.164.refs_0_, f32[128,1024]{1,0:T(8,128)S(1)} %get-tuple-element.174.refs_1_, ...), custom_call_target="tpu_custom_call" | custom-call | tf_op jit(solution)/shard_map/ffn_back/pallas_call | solution.py:88
  338.4 6.8 %collective-permute-done.14.other_ref = bf16[128,1024]{1,0:T(8,128)(2,1)S(1)} collective-permute-done((bf16[128,1024]{1,0:T(8,128)(2,1)S(1)}, bf16[128,1024]{1,0:T(8,128)(2,1)S(1)}, u32[]{:S(2)}, u32[]{:S(2)}) %collective-permute-start.14) | collective-permute-done | bytes 262176 | tf_op jit(solution)/shard_map/ppermute | solution.py:1066
  345.1 4.0 merge_back.3
  349.1 8.0 %all-to-all-start.8 = ((bf16[64,8,384]{2,1,0:T(8,128)(2,1)}), bf16[64,8,384]{2,1,0:T(8,128)(2,1)S(1)}, u32[]{:S(2)}, u32[]{:S(2)}) async-start(bf16[64,8,384]{2,1,0:T(8,128)(2,1)} %bitcast.141), calls=%async_computation.9 | async-start | bytes 786432 | tf_op jit(solution)/shard_map/all_to_all | solution.py:1075
  357.2 3.6 join.1
  363.7 6.8 %all-to-all-done.8 = bf16[64,8,384]{2,1,0:T(8,128)(2,1)S(1)} async-done(((bf16[64,8,384]{2,1,0:T(8,128)(2,1)}), bf16[64,8,384]{2,1,0:T(8,128)(2,1)S(1)}, u32[]{:S(2)}, u32[]{:S(2)}) %all-to-all-start.8) | async-done | bytes 393248 | tf_op jit(solution)/shard_map/all_to_all | solution.py:1075
  370.6 5.2 %attend_back.3 = bf16[512,640]{1,0:T(8,128)(2,1)} custom-call(bf16[512,384]{1,0:T(8,128)(2,1)S(1)} %bitcast.57, bf16[1088,256]{1,0:T(8,128)(2,1)} %get-tuple-element.188.sorted_ref, s32[4,512]{1,0:T(4,128)} %get-tuple-element.123.place_row_ref, s32[512,128]{1,0:T(8,128)} %get-tuple-element.124.place_col_ref, f32[1,512]{1,0:T(1,128)S(1)} %get-tuple-element.222.gain_ref), custom_call_target="tpu_custom_call" | custom-call | tf_op jit(solution)/shard_map/attend_back/pallas_call | solution.py:88
  375.7 4.5 all-to-all-start.9
  381.6 16.9 %all-to-all-done.9 = bf16[64,8,640]{2,1,0:T(8,128)(2,1)S(1)} async-done(((bf16[64,8,640]{2,1,0:T(8,128)(2,1)}), bf16[64,8,640]{2,1,0:T(8,128)(2,1)S(1)}, u32[]{:S(2)}, u32[]{:S(2)}) %all-to-all-start.9) | async-done | bytes 655392 | tf_op jit(solution)/shard_map/all_to_all | solution.py:1075
  398.5 3.8 project_back.3
  407.1 4.7 all-to-all-start.11
  411.8 24.9 %all-to-all-done.11 = bf16[32,48,512]{2,1,0:T(8,128)(2,1)} async-done(((bf16[32,48,512]{2,1,0:T(8,128)(2,1)}), bf16[32,48,512]{2,1,0:T(8,128)(2,1)}, u32[]{:S(2)}, u32[]{:S(2)}) %all-to-all-start.11) | async-done | bytes 1572896 | tf_op jit(solution)/shard_map/all_to_all | solution.py:1126
  440.7 4.6 reduce-scatter.11.cloned.1.call-done
  446.2 6.6 %collective-permute-start.21 = (bf16[176,512]{1,0:T(8,128)(2,1)S(1)}, bf16[176,512]{1,0:T(8,128)(2,1)S(1)}, u32[]{:S(2)}, u32[]{:S(2)}) collective-permute-start(bf16[176,512]{1,0:T(8,128)(2,1)S(1)} %dynamic-slice_bitcast_fusion), channel_id=1, source_target_pairs={{0,64},{2,66},{4,68},{6,70},{8,72},{10,74},{12,76},{14,78},{16,80}... | collective-permute-start | bytes 540680 | tf_op jit(solution)/shard_map/ppermute | solution.py:1121
  452.8 4.3 collective-permute-done.15.other_ref
  465.1 10.9 %all-to-all-start.12 = ((bf16[64,16,512]{2,1,0:T(8,128)(2,1)}), bf16[64,16,512]{2,1,0:T(8,128)(2,1)S(1)}, u32[]{:S(2)}, u32[]{:S(2)}) async-start(bf16[64,16,512]{2,1,0:T(8,128)(2,1)} %bitcast.128), calls=%async_computation.16 | async-start | bytes 2097152 | tf_op jit(solution)/shard_map/all_to_all | solution.py:1075
  478.0 16.9 %all-to-all-done.12 = bf16[64,16,512]{2,1,0:T(8,128)(2,1)S(1)} async-done(((bf16[64,16,512]{2,1,0:T(8,128)(2,1)}), bf16[64,16,512]{2,1,0:T(8,128)(2,1)S(1)}, u32[]{:S(2)}, u32[]{:S(2)}) %all-to-all-start.12) | async-done | bytes 1048608 | tf_op jit(solution)/shard_map/all_to_all | solution.py:1075
  494.8 7.7 %slots_update.1 = (f32[5,128,512]{2,1,0:T(8,128)}, f32[5,128,512]{2,1,0:T(8,128)}, f32[5,128,512]{2,1,0:T(8,128)}, f32[5,128,512]{2,1,0:T(8,128)}, f32[2,2,512]{...) custom-call(s32[1]{0:T(128)} %bitcast.half_ref, s32[1]{0:T(128)} %bitcast.2.me_ref, ...), custom_call_target="tpu_custom_call" | custom-call | tf_op jit(solution)/shard_map/slots_update/pallas_call | solution.py:88
  (186 shorter events, 74.8 us)
Async XLA Ops:
  7.2 21.7 %copy-start = (s32[2,2,8192]{2,1,0:T(2,128)S(1)}, s32[2,2,8192]{2,1,0:T(2,128)}, u32[]{:S(2)}) copy-start(s32[2,2,8192]{2,1,0:T(2,128)} %param.17) | copy-start | bytes 393220
  7.2 24.7 %collective-permute-start = (bf16[128,512]{1,0:T(8,128)(2,1)}, bf16[128,512]{1,0:T(8,128)(2,1)S(1)}, u32[]{:S(2)}, u32[]{:S(2)}) collective-permute-start(bf16[128,512]{1,0:T(8,128)(2,1)} %refs_0_.1), channel_id=1, source_target_pairs={{0,1},{1,0},{2,3},{3,2},{4,5},{5,4},{6,7},{7,6},{8,9},{9,8},{10,11... | collective-permute-start | bytes 393224 | tf_op jit(solution)/shard_map/ppermute | solution.py:1066
  10.1 21.8 %collective-permute-start.1 = (f32[4,512]{1,0:T(4,128)S(1)}, f32[4,512]{1,0:T(4,128)S(1)}, u32[]{:S(2)}, u32[]{:S(2)}) collective-permute-start(f32[4,512]{1,0:T(4,128)S(1)} %reshape.210.refs_2_), channel_id=1, source_target_pairs={{0,1},{1,0},{2,3},{3,2},{4,5},{5,4},{6,7},{7,6},{8,9},{9,8},{10,11... | collective-permute-start | bytes 24584 | tf_op jit(solution)/shard_map/ppermute | solution.py:1066
  14.3 17.6 %copy-start.11 = (bf16[128,512]{1,0:T(8,128)(2,1)S(1)}, bf16[128,512]{1,0:T(8,128)(2,1)}, u32[]{:S(2)}) copy-start(bf16[128,512]{1,0:T(8,128)(2,1)} %refs_0_.1) | copy-start | bytes 393220
  14.3 31.3 %all-to-all-start = ((bf16[64,16,512]{2,1,0:T(8,128)(2,1)}), bf16[64,16,512]{2,1,0:T(8,128)(2,1)S(1)}, u32[]{:S(2)}, u32[]{:S(2)}) async-start(bf16[64,16,512]{2,1,0:T(8,128)(2,1)} %bitcast.127), calls=%async_computation | async-start | bytes 2097152 | tf_op jit(solution)/shard_map/all_to_all | solution.py:1075
  26.8 123.6 %all-gather.3.cloned.1.call-start = ((), (), s32[]{:S(2)}) async-start(), calls=%async_computation.17 | async-start | bytes 12976128 | tf_op jit(solution)/shard_map/all_gather | solution.py:1144
  47.3 7.9 %collective-permute-start.6 = (bf16[192,512]{1,0:T(8,128)(2,1)}, bf16[192,512]{1,0:T(8,128)(2,1)S(1)}, u32[]{:S(2)}, u32[]{:S(2)}) collective-permute-start(bf16[192,512]{1,0:T(8,128)(2,1)} %get-tuple-element.137), channel_id=1, source_target_pairs={{0,64},{2,66},{4,68},{6,70},{8,72},{10,74},{12,76},{14,78},{16,80}... | collective-permute-start | bytes 589832 | tf_op jit(solution)/shard_map/ppermute | solution.py:1136
  57.1 32.1 %copy-start.30 = (bf16[128,512]{1,0:T(8,128)(2,1)S(1)}, bf16[128,512]{1,0:T(8,128)(2,1)}, u32[]{:S(2)}) copy-start(bf16[128,512]{1,0:T(8,128)(2,1)} %get-tuple-element.149) | copy-start | bytes 393220
  57.1 26.5 %all-to-all-start.1 = ((bf16[32,32,512]{2,1,0:T(8,128)(2,1)}), bf16[32,32,512]{2,1,0:T(8,128)(2,1)S(1)}, u32[]{:S(2)}, u32[]{:S(2)}) async-start(bf16[32,32,512]{2,1,0:T(8,128)(2,1)} %get-tuple-element.130), calls=%async_computation.1 | async-start | bytes 2097152 | tf_op jit(solution)/shard_map/all_to_all | solution.py:1126
  61.2 35.1 %copy-start.23 = (s32[2,128]{1,0:T(2,128)S(1)}, s32[2,128]{1,0:T(2,128)}, u32[]{:S(2)}) copy-start(s32[2,128]{1,0:T(2,128)} %get-tuple-element.121.refs_18_.refs_6_) | copy-start | bytes 3076
  61.2 163.6 %all-gather.5.cloned.1.call-start = ((), (), s32[]{:S(2)}) async-start(), calls=%async_computation.18 | async-start | bytes 8650752 | tf_op jit(solution)/shard_map/all_gather | solution.py:1144
  61.2 8.4 %collective-permute-start.2 = (bf16[128,512]{1,0:T(8,128)(2,1)S(1)}, bf16[128,512]{1,0:T(8,128)(2,1)S(1)}, u32[]{:S(2)}, u32[]{:S(2)}) collective-permute-start(bf16[128,512]{1,0:T(8,128)(2,1)S(1)} %copy-done.12), channel_id=1, source_target_pairs={{0,1},{1,0},{2,3},{3,2},{4,5},{5,4},{6,7},{7,6},{8,9},{9,8},{10,11... | collective-permute-start | bytes 393224 | tf_op jit(solution)/shard_map/ppermute | solution.py:1066
  61.7 13.9 %collective-permute-start.3 = (bf16[128,512]{1,0:T(8,128)(2,1)S(1)}, bf16[128,512]{1,0:T(8,128)(2,1)S(1)}, u32[]{:S(2)}, u32[]{:S(2)}) collective-permute-start(bf16[128,512]{1,0:T(8,128)(2,1)S(1)} %copy-done.13), channel_id=1, source_target_pairs={{0,1},{1,0},{2,3},{3,2},{4,5},{5,4},{6,7},{7,6},{8,9},{9,8},{10,11... | collective-permute-start | bytes 393224 | tf_op jit(solution)/shard_map/ppermute | solution.py:1066
  62.8 18.1 %collective-permute-start.4 = (bf16[128,512]{1,0:T(8,128)(2,1)S(1)}, bf16[128,512]{1,0:T(8,128)(2,1)S(1)}, u32[]{:S(2)}, u32[]{:S(2)}) collective-permute-start(bf16[128,512]{1,0:T(8,128)(2,1)S(1)} %copy-done.14), channel_id=1, source_target_pairs={{0,1},{1,0},{2,3},{3,2},{4,5},{5,4},{6,7},{7,6},{8,9},{9,8},{10,11... | collective-permute-start | bytes 393224 | tf_op jit(solution)/shard_map/ppermute | solution.py:1066
  83.6 15.5 %copy-start.2 = (bf16[32,32,512]{2,1,0:T(8,128)(2,1)}, bf16[32,32,512]{2,1,0:T(8,128)(2,1)S(1)}, u32[]{:S(2)}) copy-start(bf16[32,32,512]{2,1,0:T(8,128)(2,1)S(1)} %all-to-all-done.1.refs_2_.refs_3_.refs_4_.refs_5_.refs_10_.refs_11_.refs_12_.refs_13_.refs_0_.refs_1_.refs_8_.refs_9_) | copy-start | bytes 3145732
  83.6 5.6 %collective-permute-start.5 = (bf16[32,32,512]{2,1,0:T(8,128)(2,1)S(1)}, bf16[32,32,512]{2,1,0:T(8,128)(2,1)S(1)}, u32[]{:S(2)}, u32[]{:S(2)}) collective-permute-start(bf16[32,32,512]{2,1,0:T(8,128)(2,1)S(1)} %all-to-all-done.1.refs_2_.refs_3_.refs_4_.refs_5_.refs_10_.refs_11_.refs_12_.refs_13_.refs_0_.refs_, ...), channel_id=1, source_target_pairs={{0,2},{2,0},{4,6},{6,4},{8,10},{10,8},{12,14},{14,12},{16,18},{18,... | collective-permute-start | bytes 3145736 | tf_op jit(solution)/shard_map/ppermute | solution.py:1070
  89.2 6.2 %collective-permute-start.10 = (bf16[128,512]{1,0:T(8,128)(2,1)S(1)}, bf16[128,512]{1,0:T(8,128)(2,1)S(1)}, u32[]{:S(2)}, u32[]{:S(2)}) collective-permute-start(bf16[128,512]{1,0:T(8,128)(2,1)S(1)} %copy-done.30), channel_id=1, source_target_pairs={{0,64},{2,66},{4,68},{6,70},{8,72},{10,74},{12,76},{14,78},{16,80}... | collective-permute-start | bytes 393224 | tf_op jit(solution)/shard_map/ppermute | solution.py:1136
  99.1 28.8 %all-to-all-start.2 = ((bf16[64,8,640]{2,1,0:T(8,128)(2,1)}), bf16[64,8,640]{2,1,0:T(8,128)(2,1)S(1)}, u32[]{:S(2)}, u32[]{:S(2)}) async-start(bf16[64,8,640]{2,1,0:T(8,128)(2,1)} %bitcast.137), calls=%async_computation.2 | async-start | bytes 1310720 | tf_op jit(solution)/shard_map/all_to_all | solution.py:1075
  106.7 205.5 %reduce-scatter.5.cloned.1.call-start = ((), (), s32[]{:S(2)}) async-start(), calls=%async_computation.19 | async-start | bytes 9437184 | tf_op jit(solution)/shard_map/reduce_scatter | solution.py:1099
  153.2 7.7 %collective-permute-start.7 = (bf16[128,1024]{1,0:T(8,128)(2,1)}, bf16[128,1024]{1,0:T(8,128)(2,1)S(1)}, u32[]{:S(2)}, u32[]{:S(2)}) collective-permute-start(bf16[128,1024]{1,0:T(8,128)(2,1)} %get-tuple-element.139), channel_id=1, source_target_pairs={{0,1},{1,0},{2,3},{3,2},{4,5},{5,4},{6,7},{7,6},{8,9},{9,8},{10,11... | collective-permute-start | bytes 786440 | tf_op jit(solution)/shard_map/ppermute | solution.py:1066
  168.1 6.6 %collective-permute-start.8 = (bf16[128,1024]{1,0:T(8,128)(2,1)}, bf16[128,1024]{1,0:T(8,128)(2,1)S(1)}, u32[]{:S(2)}, u32[]{:S(2)}) collective-permute-start(bf16[128,1024]{1,0:T(8,128)(2,1)} %get-tuple-element.143), channel_id=1, source_target_pairs={{0,1},{1,0},{2,3},{3,2},{4,5},{5,4},{6,7},{7,6},{8,9},{9,8},{10,11... | collective-permute-start | bytes 786440 | tf_op jit(solution)/shard_map/ppermute | solution.py:1066
  224.4 7.9 %collective-permute-start.9 = (bf16[128,1024]{1,0:T(8,128)(2,1)}, bf16[128,1024]{1,0:T(8,128)(2,1)S(1)}, u32[]{:S(2)}, u32[]{:S(2)}) collective-permute-start(bf16[128,1024]{1,0:T(8,128)(2,1)} %get-tuple-element.147), channel_id=1, source_target_pairs={{0,1},{1,0},{2,3},{3,2},{4,5},{5,4},{6,7},{7,6},{8,9},{9,8},{10,11... | collective-permute-start | bytes 786440 | tf_op jit(solution)/shard_map/ppermute | solution.py:1066
  250.7 6.6 %collective-permute-start.12 = (bf16[128,1024]{1,0:T(8,128)(2,1)S(1)}, bf16[128,1024]{1,0:T(8,128)(2,1)S(1)}, u32[]{:S(2)}, u32[]{:S(2)}) collective-permute-start(bf16[128,1024]{1,0:T(8,128)(2,1)S(1)} %copy-done.34), channel_id=1, source_target_pairs={{0,1},{1,0},{2,3},{3,2},{4,5},{5,4},{6,7},{7,6},{8,9},{9,8},{10,11... | collective-permute-start | bytes 786440 | tf_op jit(solution)/shard_map/ppermute | solution.py:1066
  251.0 18.5 %collective-permute-start.11 = (bf16[128,1024]{1,0:T(8,128)(2,1)S(1)}, bf16[128,1024]{1,0:T(8,128)(2,1)S(1)}, u32[]{:S(2)}, u32[]{:S(2)}) collective-permute-start(bf16[128,1024]{1,0:T(8,128)(2,1)S(1)} %copy-done.33), channel_id=1, source_target_pairs={{0,1},{1,0},{2,3},{3,2},{4,5},{5,4},{6,7},{7,6},{8,9},{9,8},{10,11... | collective-permute-start | bytes 786440 | tf_op jit(solution)/shard_map/ppermute | solution.py:1066
  261.3 22.8 %all-to-all-start.6 = ((bf16[64,8,384]{2,1,0:T(8,128)(2,1)}), bf16[64,8,384]{2,1,0:T(8,128)(2,1)S(1)}, u32[]{:S(2)}, u32[]{:S(2)}) async-start(bf16[64,8,384]{2,1,0:T(8,128)(2,1)} %bitcast.142), calls=%async_computation.6 | async-start | bytes 786432 | tf_op jit(solution)/shard_map/all_to_all | solution.py:1075
  269.4 87.8 %reduce-scatter.7.cloned.1.call-start = ((), (), s32[]{:S(2)}) async-start(), calls=%async_computation.20 | async-start | bytes 3538944 | tf_op jit(solution)/shard_map/reduce_scatter | solution.py:1099
  317.3 94.6 %reduce-scatter.9.cloned.1.call-start = ((), (), s32[]{:S(2)}) async-start(), calls=%async_computation.21 | async-start | bytes 9437184 | tf_op jit(solution)/shard_map/reduce_scatter | solution.py:1099
  318.2 8.0 %collective-permute-start.13 = (bf16[128,1024]{1,0:T(8,128)(2,1)S(1)}, bf16[128,1024]{1,0:T(8,128)(2,1)S(1)}, u32[]{:S(2)}, u32[]{:S(2)}) collective-permute-start(bf16[128,1024]{1,0:T(8,128)(2,1)S(1)} %copy-done.36), channel_id=1, source_target_pairs={{0,1},{1,0},{2,3},{3,2},{4,5},{5,4},{6,7},{7,6},{8,9},{9,8},{10,11... | collective-permute-start | bytes 786440 | tf_op jit(solution)/shard_map/ppermute | solution.py:1066
  338.1 7.0 %collective-permute-start.14 = (bf16[128,1024]{1,0:T(8,128)(2,1)S(1)}, bf16[128,1024]{1,0:T(8,128)(2,1)S(1)}, u32[]{:S(2)}, u32[]{:S(2)}) collective-permute-start(bf16[128,1024]{1,0:T(8,128)(2,1)S(1)} %copy-done.35), channel_id=1, source_target_pairs={{0,1},{1,0},{2,3},{3,2},{4,5},{5,4},{6,7},{7,6},{8,9},{9,8},{10,11... | collective-permute-start | bytes 786440 | tf_op jit(solution)/shard_map/ppermute | solution.py:1066
  349.1 21.4 %all-to-all-start.8 = ((bf16[64,8,384]{2,1,0:T(8,128)(2,1)}), bf16[64,8,384]{2,1,0:T(8,128)(2,1)S(1)}, u32[]{:S(2)}, u32[]{:S(2)}) async-start(bf16[64,8,384]{2,1,0:T(8,128)(2,1)} %bitcast.141), calls=%async_computation.9 | async-start | bytes 786432 | tf_op jit(solution)/shard_map/all_to_all | solution.py:1075
  357.1 88.2 %reduce-scatter.11.cloned.1.call-start = ((), (), s32[]{:S(2)}) async-start(), calls=%async_computation.22 | async-start | bytes 1802240 | tf_op jit(solution)/shard_map/reduce_scatter | solution.py:1112
  375.7 22.8 %all-to-all-start.9 = ((bf16[64,8,640]{2,1,0:T(8,128)(2,1)}), bf16[64,8,640]{2,1,0:T(8,128)(2,1)S(1)}, u32[]{:S(2)}, u32[]{:S(2)}) async-start(bf16[64,8,640]{2,1,0:T(8,128)(2,1)} %bitcast.129), calls=%async_computation.11 | async-start | bytes 1310720 | tf_op jit(solution)/shard_map/all_to_all | solution.py:1075
  380.2 22.6 %collective-permute-start.18 = (bf16[2,128,512]{2,1,0:T(8,128)(2,1)S(1)}, bf16[2,128,512]{2,1,0:T(8,128)(2,1)S(1)}, u32[]{:S(2)}, u32[]{:S(2)}) collective-permute-start(bf16[2,128,512]{2,1,0:T(8,128)(2,1)S(1)} %copy-done.26), channel_id=1, source_target_pairs={{0,2},{2,0},{4,6},{6,4},{8,10},{10,8},{12,14},{14,12},{16,18},{18,... | collective-permute-start | bytes 786440 | tf_op jit(solution)/shard_map/ppermute | solution.py:1070
  380.9 22.0 %collective-permute-start.16 = (bf16[2,128,512]{2,1,0:T(8,128)(2,1)S(1)}, bf16[2,128,512]{2,1,0:T(8,128)(2,1)S(1)}, u32[]{:S(2)}, u32[]{:S(2)}) collective-permute-start(bf16[2,128,512]{2,1,0:T(8,128)(2,1)S(1)} %copy-done.28), channel_id=1, source_target_pairs={{0,2},{2,0},{4,6},{6,4},{8,10},{10,8},{12,14},{14,12},{16,18},{18,... | collective-permute-start | bytes 786440 | tf_op jit(solution)/shard_map/ppermute | solution.py:1070
  381.0 21.9 %collective-permute-start.17 = (bf16[128,512]{1,0:T(8,128)(2,1)S(1)}, bf16[128,512]{1,0:T(8,128)(2,1)S(1)}, u32[]{:S(2)}, u32[]{:S(2)}) collective-permute-start(bf16[128,512]{1,0:T(8,128)(2,1)S(1)} %copy-done.29), channel_id=1, source_target_pairs={{0,2},{2,0},{4,6},{6,4},{8,10},{10,8},{12,14},{14,12},{16,18},{18,... | collective-permute-start | bytes 393224 | tf_op jit(solution)/shard_map/ppermute | solution.py:1070
  402.3 1.6 collective-permute-start.19
  402.4 1.7 collective-permute-start.20
  407.1 29.6 %all-to-all-start.11 = ((bf16[32,48,512]{2,1,0:T(8,128)(2,1)}), bf16[32,48,512]{2,1,0:T(8,128)(2,1)}, u32[]{:S(2)}, u32[]{:S(2)}) async-start(bf16[32,48,512]{2,1,0:T(8,128)(2,1)} %attn_grad.1), calls=%async_computation.14 | async-start | bytes 3145728 | tf_op jit(solution)/shard_map/all_to_all | solution.py:1126
  411.8 28.5 %copy-start.32 = (bf16[128,1024]{1,0:T(8,128)(2,1)S(1)}, bf16[128,1024]{1,0:T(8,128)(2,1)}, u32[]{:S(2)}) copy-start(bf16[128,1024]{1,0:T(8,128)(2,1)} %get-tuple-element.190) | copy-start | bytes 786436
  411.8 45.3 %copy-start.16 = (f32[1,1024]{1,0:T(1,128)S(1)}, f32[1,1024]{1,0:T(1,128)}, u32[]{:S(2)}) copy-start(f32[1,1024]{1,0:T(1,128)} %copy-done.15) | copy-start | bytes 12292
  436.7 26.3 %all-to-all-start.10 = ((bf16[8,128,512]{2,1,0:T(8,128)(2,1)}), bf16[8,128,512]{2,1,0:T(8,128)(2,1)S(1)}, u32[]{:S(2)}, u32[]{:S(2)}) async-start(bf16[8,128,512]{2,1,0:T(8,128)(2,1)} %bitcast.132), calls=%async_computation.13 | async-start | bytes 2097152 | tf_op jit(solution)/shard_map/all_to_all | solution.py:1105
  440.3 16.8 %collective-permute-start.15 = (bf16[128,1024]{1,0:T(8,128)(2,1)S(1)}, bf16[128,1024]{1,0:T(8,128)(2,1)S(1)}, u32[]{:S(2)}, u32[]{:S(2)}) collective-permute-start(bf16[128,1024]{1,0:T(8,128)(2,1)S(1)} %copy-done.32), channel_id=1, source_target_pairs={{0,1},{1,0},{2,3},{3,2},{4,5},{5,4},{6,7},{7,6},{8,9},{9,8},{10,11... | collective-permute-start | bytes 786440 | tf_op jit(solution)/shard_map/ppermute | solution.py:1066
  446.2 16.7 %collective-permute-start.21 = (bf16[176,512]{1,0:T(8,128)(2,1)S(1)}, bf16[176,512]{1,0:T(8,128)(2,1)S(1)}, u32[]{:S(2)}, u32[]{:S(2)}) collective-permute-start(bf16[176,512]{1,0:T(8,128)(2,1)S(1)} %dynamic-slice_bitcast_fusion), channel_id=1, source_target_pairs={{0,64},{2,66},{4,68},{6,70},{8,72},{10,74},{12,76},{14,78},{16,80}... | collective-permute-start | bytes 540680 | tf_op jit(solution)/shard_map/ppermute | solution.py:1121
  465.1 29.7 %copy-start.19 = (s32[176]{0:T(256)S(1)}, s32[176]{0:T(256)}, u32[]{:S(2)}) copy-start(s32[176]{0:T(256)} %param.18) | copy-start | bytes 2116
  465.1 29.7 %copy-start.20 = (f32[2,2,512]{2,1,0:T(2,128)S(1)}, f32[2,2,512]{2,1,0:T(2,128)}, u32[]{:S(2)}) copy-start(f32[2,2,512]{2,1,0:T(2,128)} %gains_ref.1) | copy-start | bytes 24580
  465.1 29.7 %copy-start.21 = (f32[2,2,512]{2,1,0:T(2,128)S(1)}, f32[2,2,512]{2,1,0:T(2,128)}, u32[]{:S(2)}) copy-start(f32[2,2,512]{2,1,0:T(2,128)} %ga_ref.1) | copy-start | bytes 24580
  465.1 29.7 %copy-start.22 = (f32[2,2,512]{2,1,0:T(2,128)S(1)}, f32[2,2,512]{2,1,0:T(2,128)}, u32[]{:S(2)}) copy-start(f32[2,2,512]{2,1,0:T(2,128)} %gb_ref.1) | copy-start | bytes 24580
  465.1 29.7 %all-to-all-start.12 = ((bf16[64,16,512]{2,1,0:T(8,128)(2,1)}), bf16[64,16,512]{2,1,0:T(8,128)(2,1)S(1)}, u32[]{:S(2)}, u32[]{:S(2)}) async-start(bf16[64,16,512]{2,1,0:T(8,128)(2,1)} %bitcast.128), calls=%async_computation.16 | async-start | bytes 2097152 | tf_op jit(solution)/shard_map/all_to_all | solution.py:1075
  (26 other events, 154.9 us)
Sparse Core Ops, SparseCore 0:
  57.2 73.0 all-gather.2
  132.6 52.5 all-gather.4
  249.9 58.8 reduce-scatter.4
  317.4 29.4 reduce-scatter.6
  349.1 62.3 reduce-scatter.8
  413.8 31.4 reduce-scatter.10

commit v4 on v3

--- a/solution.py
+++ b/solution.py
@@ -26,12 +26,14 @@
 O_LANES = 3 * DH
 ROWS = NW * 8
 PACK = 16
+WIDE_PACK = 24
+PAIR_ROWS = WIDE_PACK * (NW // 2)
 QUAD = 4
 UP, DOWN = 0, 1
 LAYER_ROWS = 176
 ATTN_ROWS = 48
 FFN_ROWS = 128
-EARLY_ROWS = 192
+EARLY_ROWS = 384
 
 MASK_FILL = -1000000000.0
 NORM_EPS = 1e-05
@@ -46,6 +48,7 @@
 BF16 = jnp.bfloat16
 I32 = jnp.int32
 VMEM_BYTES = 20 * 1024 * 1024
+BIG_VMEM_BYTES = 32 * 1024 * 1024
 
 
 def feature_of(p):
@@ -131,6 +134,176 @@
     return jnp.where(mine, first, second), jnp.where(mine, second, first)
 
 
+class Far:
+    def __init__(self, array):
+        self.operands = [in_hbm(array)]
+        self.scratch = [pltpu.VMEM(array.shape, array.dtype), pltpu.SemaphoreType.DMA((1,))]
+
+    def fetch(self, refs, buffer, sems):
+        return [pltpu.make_async_copy(refs[0], buffer, sems.at[0])]
+
+
+class FfnWeight(Far):
+    def __init__(self, array):
+        self.operands = [in_hbm(array)]
+        self.scratch = [
+            pltpu.VMEM((2, QUAD, 2, QUAD, FFN_ROWS, PART), BF16),
+            pltpu.SemaphoreType.DMA((16,)),
+        ]
+
+    def fetch(self, refs, buffer, sems):
+        copies = []
+        for c in range(QUAD):
+            for part in range(2):
+                for c0 in range(2):
+                    source = refs[0].at[:, c, c0, pl.ds(part * FFN_ROWS, FFN_ROWS), :]
+                    copies.append(
+                        pltpu.make_async_copy(source, buffer.at[part, c, c0], sems.at[len(copies)])
+                    )
+        return copies
+
+
+class Direct(Far):
+    def __init__(self, array):
+        self.operands = [in_hbm(array)]
+        self.scratch = []
+
+
+class FarSlots(Far):
+    def __init__(self, array):
+        self.operands = [in_hbm(array)]
+        self.scratch = [pltpu.VMEM(array.shape, array.dtype), pltpu.SemaphoreType.DMA((CAP,))]
+
+    def fetch(self, refs, buffer, sems):
+        return [
+            pltpu.make_async_copy(refs[0].at[s], buffer.at[s], sems.at[s]) for s in range(CAP)
+        ]
+
+
+class Fetched:
+    def __init__(self, copies, buffer):
+        self.copies = list(copies)
+        self.buffer = buffer
+        for copy in self.copies:
+            copy.start()
+
+    def wait(self, count=None):
+        count = len(self.copies) if count is None else count
+        for copy in self.copies[:count]:
+            copy.wait()
+        self.copies = self.copies[count:]
+
+    def __getitem__(self, index):
+        self.wait()
+        return self.buffer[index]
+
+    def halves(self):
+        self.wait()
+        return [self.buffer[i].reshape(PART, PART) for i in range(2)]
+
+    def block(self, part, c, c0):
+        return self.buffer[part, c, c0].reshape(PART, PART)
+
+
+class Sent:
+    def __init__(self, shape, dtype, pieces=1):
+        self.shape, self.dtype, self.pieces = shape, dtype, pieces
+
+
+class Sending:
+    def __init__(self, target, buffer, sems, pieces):
+        self.target, self.buffer, self.sems, self.pieces = target, buffer, sems, pieces
+        self.copies = []
+
+    def __setitem__(self, index, value):
+        self.buffer[index] = value
+
+    def flush(self):
+        k = len(self.copies)
+        size = self.target.shape[0] // self.pieces
+        rows = pl.ds(k * size, size)
+        source, target = self.buffer.at[rows], self.target.at[rows]
+        if source.shape != target.shape:
+            target = target.at[:, :, pl.ds(0, self.buffer.shape[2]), :]
+        copy = pltpu.make_async_copy(source, target, self.sems.at[k])
+        copy.start()
+        self.copies.append(copy)
+
+    def flush_all(self):
+        while len(self.copies) < self.pieces:
+            self.flush()
+
+    def wait(self):
+        for copy in self.copies:
+            copy.wait()
+
+
+def run(kernel, args, outs, prefetch=0, name=None, vmem=None, partial=None, temps=(), aliases=None):
+    operands, in_specs, scratch = [], [], []
+    for i, a in enumerate(args):
+        if isinstance(a, Far):
+            operands += a.operands
+            in_specs += [pl.BlockSpec(memory_space=pl.ANY)] * len(a.operands)
+            scratch += a.scratch
+        else:
+            operands.append(a)
+            if i >= prefetch:
+                zeros = (0,) * a.ndim
+                in_specs.append(pl.BlockSpec(a.shape, lambda *_, zeros=zeros: zeros))
+    out_shapes, out_specs = [], []
+    for i, o in enumerate(outs):
+        if isinstance(o, Sent):
+            out_shapes.append(kept(o.shape, o.dtype))
+            out_specs.append(pl.BlockSpec(memory_space=pl.ANY))
+            shape = (partial or {}).get(i, o.shape)
+            scratch += [pltpu.VMEM(shape, o.dtype), pltpu.SemaphoreType.DMA((o.pieces,))]
+        else:
+            zeros = (0,) * len(o.shape)
+            out_shapes.append(o)
+            out_specs.append(pl.BlockSpec(o.shape, lambda *_, zeros=zeros: zeros))
+
+    def body(*refs):
+        ins, rest = list(refs[: len(operands)]), list(refs[len(operands) :])
+        out_refs, temps = rest[: len(outs)], rest[len(outs) :]
+        seen = []
+        for a in args:
+            if isinstance(a, Far):
+                mine = [ins.pop(0) for _ in a.operands]
+                if a.scratch:
+                    buffer, sems = temps.pop(0), temps.pop(0)
+                    seen.append(Fetched(a.fetch(mine, buffer, sems), buffer))
+                else:
+                    seen.append(mine[0])
+            else:
+                seen.append(ins.pop(0))
+        sending = []
+        for o, ref in zip(outs, out_refs):
+            if isinstance(o, Sent):
+                ref = Sending(ref, temps.pop(0), temps.pop(0), o.pieces)
+                sending.append(ref)
+            seen.append(ref)
+        kernel(*seen, *temps)
+        for ref in sending:
+            ref.flush_all()
+        for ref in sending:
+            ref.wait()
+
+    return pl.pallas_call(
+        body,
+        out_shape=out_shapes,
+        grid_spec=pltpu.PrefetchScalarGridSpec(
+            num_scalar_prefetch=prefetch,
+            grid=(1,),
+            in_specs=in_specs,
+            out_specs=out_specs,
+            scratch_shapes=[*scratch, *temps],
+        ),
+        compiler_params=pltpu.CompilerParams(vmem_limit_bytes=vmem or VMEM_BYTES),
+        input_output_aliases=aliases or {},
+        name=name,
+    )(*operands)
+
+
 class Weight:
     def __init__(self, index, *arrays):
         self.index = index
@@ -240,10 +413,15 @@
 
 def row_of_slots(kinds):
     r = iota((1, TR), 1)
-    attn = (((r >> 1) & 7) * 8 + (r >> 5) * 2 + ((r >> 4) & 1)) * PACK + (r & 1)
-    low = r >> 2
-    ffn = (((low >> 1) & 7) * 8 + (r & 3) * 2 + (low >> 4)) * PACK + (low & 1)
-    return jnp.concatenate([jnp.where(k == 1, ffn, attn) + 2 * s for s, k in enumerate(kinds)], 1)
+
+    def place(low, x):
+        j3 = (low >> 1) & 7
+        device = (j3 & 3) * 8 + x * 2 + (low >> 4)
+        return device * WIDE_PACK + (j3 >> 2) * 2 + (low & 1)
+
+    attn = place(r & 31, r >> 5)
+    ffn = place(r >> 2, r & 3)
+    return jnp.concatenate([jnp.where(k == 1, ffn, attn) + 4 * s for s, k in enumerate(kinds)], 1)
 
 
 def slot_of_row(kinds):
@@ -261,14 +439,16 @@
 def route_out_kernel(me_ref, owner_ref, master_ref, out_ref):
     tiles = master_ref[...].reshape(CAP * TR, PART).astype(BF16)
     place = row_of_slots(slot_kinds(owner_ref, me_ref[0]))
-    out_ref[...] = dot(hot(iota((NW * PACK, 1), 0) == place), tiles, 1, 0).astype(BF16)
+    rows = dot(hot(iota((PAIR_ROWS, 1), 0) == place), tiles, 1, 0).astype(BF16)
+    out_ref[:PAIR_ROWS] = rows
+    out_ref[PAIR_ROWS:] = rows
 
 
 def route_out(me, owner_row, master):
     return call(
         route_out_kernel,
         (me, owner_row, master),
-        [kept((NW * PACK, PART), BF16)],
+        [kept((2 * PAIR_ROWS, PART), BF16)],
         prefetch=1,
         in_place=(1,),
         name="route_out",
@@ -276,19 +456,23 @@
 
 
 def pick_kernel(code_ref, moved_ref, first_ref, early_ref, late_ref):
-    picked = hot(code_ref[...] == iota((1, NW * PACK), 1))
+    picked = hot(code_ref[...] == iota((1, 2 * PAIR_ROWS), 1))
     rows = dot(picked, moved_ref[...], 1, 0).astype(BF16)
-    late_ref[...] = rows[LAYER_ROWS : LAYER_ROWS + FFN_ROWS]
-    early_ref[: FFN_ROWS + 16] = rows[: FFN_ROWS + 16]
-    early_ref[FFN_ROWS + 16 :] = rows[LAYER_ROWS + FFN_ROWS :]
-    first_ref[...] = jnp.broadcast_to(rows[FFN_ROWS + 16 : LAYER_ROWS][None], first_ref.shape)
+    early_ref[...] = rows[:EARLY_ROWS]
+    late_ref[...] = rows[EARLY_ROWS : EARLY_ROWS + 2 * FFN_ROWS]
+    first = rows[EARLY_ROWS + 2 * FFN_ROWS :]
+    first_ref[...] = jnp.broadcast_to(first[None], first_ref.shape)
 
 
 def pick(code_col, moved):
     return call(
         pick_kernel,
         (code_col, moved),
-        [kept((32, 32, PART), BF16), kept((EARLY_ROWS, PART), BF16), kept((FFN_ROWS, PART), BF16)],
+        [
+            kept((32, 32, PART), BF16),
+            kept((EARLY_ROWS, PART), BF16),
+            kept((2 * FFN_ROWS, PART), BF16),
+        ],
         name="pick",
     )
 
@@ -333,46 +517,47 @@
 
 def slots_kernel(
     half_ref, me_ref, owner_ref, moved_ref, ready_ref, m_ref, a_ref, b_ref, gains_ref, ga_ref, gb_ref,
-    grad_ref, first_ref, second_ref, new_ref, gg_ref, gf_ref, gs_ref, gn_ref, all_ref
+    grad_out, first_out, second_out, new_out, gg_out, gf_out, gs_out, gn_out
 ):
-    s = pl.program_id(0)
-
-    @pl.when(s == 0)
-    def _():
-        placed = hot(iota((CAP * TR, 1), 0) == slot_of_row(slot_kinds(owner_ref, me_ref[0])))
-        all_ref[...] = dot(placed, moved_ref[...], 1, 0).reshape(CAP, TR, PART)
-        spare = hot((iota((1, NW * PACK), 1) & (PACK - 1)) - 2 * CAP == iota((8, 1), 0))
-        sums = dot(spare, moved_ref[...], 1, 0)
-        gains = [jnp.concatenate([sums[q : q + 1], sums[q + 1 : q + 2]], 1) for q in (4, 2, 0)]
-        inner_sum = jnp.concatenate(gains + [ready_ref[...]], 0)
-        back = hot(feature_of(iota((1, D), 1)) == iota((PART, 1), 0) + half_ref[0] * PART)
-        parts = dot(jnp.concatenate(pieces(inner_sum), 0).astype(BF16), back, 1, 1)
-        n = 2 * LAYERS
-        total = parts[:n] + parts[n : 2 * n] + parts[2 * n :]
-        for l in range(LAYERS):
-            gain_grad = total[2 * l : 2 * l + 2]
-            gg_ref[l] = gain_grad
-            gf_ref[l], gs_ref[l], gn_ref[l] = adam(
-                gain_grad, ga_ref[l], gb_ref[l], gains_ref[l], RATE_GAIN
-            )
-
-    grad = all_ref[s]
-    grad_ref[0] = grad
-    first_ref[0], second_ref[0], new_ref[0] = adam(grad, a_ref[0], b_ref[0], m_ref[0], RATE_WEIGHT)
+    rows = moved_ref[...]
+    placed = hot(iota((CAP * TR, 1), 0) == slot_of_row(slot_kinds(owner_ref, me_ref[0])))
+    grads = dot(placed, rows, 1, 0)
+    for s in range(CAP):
+        for ref in (m_ref, a_ref, b_ref):
+            ref.wait(1)
+        grad = grads[s * TR : (s + 1) * TR]
+        grad_out[s] = grad
+        first_out[s], second_out[s], new_out[s] = adam(
+            grad, a_ref.buffer[s], b_ref.buffer[s], m_ref.buffer[s], RATE_WEIGHT
+        )
+        for out in (grad_out, first_out, second_out, new_out):
+            out.flush()
+    spare = hot((iota((1, NW * PACK), 1) & (PACK - 1)) - 2 * CAP == iota((8, 1), 0))
+    sums = dot(spare, rows, 1, 0)
+    gains = [jnp.concatenate([sums[q : q + 1], sums[q + 1 : q + 2]], 1) for q in (4, 2, 0)]
+    inner_sum = jnp.concatenate(gains + [ready_ref[...]], 0)
+    back = hot(feature_of(iota((1, D), 1)) == iota((PART, 1), 0) + half_ref[0] * PART)
+    parts = dot(jnp.concatenate(pieces(inner_sum), 0).astype(BF16), back, 1, 1)
+    n = 2 * LAYERS
+    total = parts[:n] + parts[n : 2 * n] + parts[2 * n :]
+    for l in range(LAYERS):
+        gain_grad = total[2 * l : 2 * l + 2]
+        gg_out[l] = gain_grad
+        gf_out[l], gs_out[l], gn_out[l] = adam(
+            gain_grad, ga_ref[l], gb_ref[l], gains_ref[l], RATE_GAIN
+        )
 
 
 def slots_update(half, me, owner_row, moved, ready, master, first, second, gains, gain_first, gain_second):
-    tile = pl.BlockSpec((1, TR, PART), lambda s, *_: (s, 0, 0))
-    return call(
+    return run(
         slots_kernel,
-        (half, me, owner_row, moved, ready, master, first, second, gains, gain_first, gain_second),
-        [sds((CAP, TR, PART), F32)] * 4 + [sds((LAYERS, 2, PART), F32)] * 4,
-        grid=(CAP,),
-        specs={3: tile, 4: tile, 5: tile},
-        out_specs={i: tile for i in range(4)},
-        scratch=[pltpu.VMEM((CAP, TR, PART), F32)],
+        [
+            half, me, owner_row, moved, ready,
+            FarSlots(master), FarSlots(first), FarSlots(second),
+            gains, gain_first, gain_second,
+        ],
+        [Sent((CAP, TR, PART), F32, CAP)] * 4 + [sds((LAYERS, 2, PART), F32)] * 4,
         prefetch=2,
-        in_place=(3, 4, 5),
         name="slots_update",
     )
 
@@ -387,16 +572,16 @@
     b = iota((ROWS, 1), 0) & 7
     block = group_ref[0] * 8 + b
     before = (group_ref[0] * 8 - 1) & 63
-    lanes = iota((ROWS, TOK), 1)
+    lanes = iota((TOK, TOK), 1)
     for l in range(LAYERS):
-        rank_row, rank_col, place_row, place_col = outs[4 * l : 4 * l + 4]
+        rank_row, rank_col, place_row = outs[3 * l : 3 * l + 3]
         cols = jnp.zeros((TOK, TOK), I32)
         for r in range(ROUNDS):
             row = mine_ref[l * ROUNDS + r : l * ROUNDS + r + 1, :]
             col = jnp.sum(jnp.where(same, row, 0), axis=1, keepdims=True)
             rank_row[r : r + 1, :] = jnp.sum(jnp.where(col < row, 1, 0), axis=0, keepdims=True)
             rank = jnp.sum(jnp.where(row < col, 1, 0), axis=1, keepdims=True)
-            cols = jnp.where(lanes[:TOK] == r, rank, cols)
+            cols = jnp.where(lanes == r, rank, cols)
         rank_col[...] = cols
         source = source_ref[l]
         target = jnp.broadcast_to(source[:, None, :], (NW, 8, TOK)).reshape(ROWS, TOK)
@@ -413,17 +598,14 @@
             jnp.where(b == 0, low_lent - SPAN, jnp.where(b == 2, high_lent - SPAN, -1)),
             jnp.where(b == 1, low_lent - SPAN, jnp.where(b == 3, high_lent - SPAN, -1)),
         )
-        cols = jnp.zeros((ROWS, TOK), I32)
         for j, column in enumerate(columns):
-            cols = jnp.where(lanes == j, column, cols)
             for q in range(4):
                 at = slice(q * TOK, (q + 1) * TOK)
                 place_row[j : j + 1, at] = turned(column[at])
-        place_col[...] = cols
 
 
 def plan(group, mine, source):
-    layer = [kept((ROUNDS, TOK), I32), kept((TOK, TOK), I32), kept((4, ROWS), I32), kept((ROWS, TOK), I32)]
+    layer = [kept((ROUNDS, TOK), I32), kept((TOK, TOK), I32), kept((4, ROWS), I32)]
     return call(plan_kernel, (group, mine, source), layer * LAYERS, prefetch=1, name="plan")
 
 
@@ -471,7 +653,7 @@
 def project_kernel(pending, count, core_ref, *refs):
     if pending:
         x_ref, own_ref, other_ref, *rest = refs
-        x = x_ref[...] + (own_ref[...] + other_ref[...].astype(F32))
+        x = x_ref[...] + (own_ref[...].astype(F32) + other_ref[...].astype(F32))
     else:
         x_ref, *rest = refs
         x = x_ref[...]
@@ -508,7 +690,7 @@
         args,
         [kept((TOK, D), F32), kept((2, TOK, PART), BF16), kept((ROWS, QV_LANES), BF16)],
         specs=specs,
-        in_place=(0, *(tuple(specs) if len(wq.parts()) == 4 else ())),
+        in_place=(0, *((1,) if pending else ()), *(tuple(specs) if len(wq.parts()) == 4 else ())),
         prefetch=1,
         name="project",
     )
@@ -543,11 +725,12 @@
     return dot(hot(iota((count, 1), 0) == place_row_ref[j : j + 1, :]), rows, 1, 0)
 
 
-def leave(place_col_ref, j, rows):
-    return dot(hot(place_col_ref[:, j : j + 1] == iota((1, rows.shape[0]), 1)), rows, 1, 0)
-
-
-def attend_kernel(moved_ref, place_row_ref, place_col_ref, sorted_out, send_out):
+def leave(place_row_ref, j, rows):
+    at = hot(iota((rows.shape[0], 1), 0) == place_row_ref[j : j + 1, :])
+    return dot(at, rows, 0, 0)
+
+
+def attend_kernel(moved_ref, place_row_ref, sorted_out, send_out):
     q_lent = arrive(place_row_ref, 2, moved_ref[:, 4 * DH :])
     v_lent = arrive(place_row_ref, 3, moved_ref[:, 4 * DH :])
     main = arrive(place_row_ref, 0, moved_ref[:, : 2 * DH]) + arrive(
@@ -566,20 +749,20 @@
     )
     aux = spread(total, iota((1024, TOK), 1))
     both = jnp.concatenate([outs, aux], 1).astype(BF16)
-    even = leave(place_col_ref, 0, both)
-    odd = leave(place_col_ref, 1, both)
+    even = leave(place_row_ref, 0, both)
+    odd = leave(place_row_ref, 1, both)
     send_out[:, :DH] = even[:, :DH].astype(BF16)
     send_out[:, DH : 2 * DH] = odd[:, :DH].astype(BF16)
     lanes = iota((ROWS, TOK), 1)
     send_out[:, 2 * DH :] = either(lanes, even[:, DH:], odd[:, DH:]).astype(BF16)
 
 
-def attend(moved, place_row, place_col):
+def attend(moved, place_row):
     return call(
         attend_kernel,
-        (moved, place_row, place_col),
+        (moved, place_row),
         [kept((1088, 2 * DH), BF16), kept((ROWS, O_LANES), BF16)],
-        in_place=(1, 2),
+        in_place=(1,),
         name="attend",
     )
 
@@ -592,7 +775,7 @@
 
 def merge_kernel(count, core_ref, moved_ref, rank_col_ref, *refs):
     w_refs, refs = refs[:count], refs[count:]
-    part_out, send_out, o_out, share_out, merged_out = refs
+    send_out, o_out, share_out, merged_out = refs
     lanes = iota((TOK, TOK), 1)
     outs, logs = [], []
     for r in range(ROUNDS):
@@ -634,14 +817,12 @@
     share_out[...] = share_all
     merged = jnp.concatenate(merged, 1).astype(BF16)
     merged_out[...] = merged
-    put_halves(out_of(core_ref[0], merged, w_refs), part_out, send_out)
-
-
-def put_halves(pair, part_out, send_out):
+    put_halves(out_of(core_ref[0], merged, w_refs), send_out)
+
+
+def put_halves(pair, send_out):
     for i in range(2):
-        cols = slice(i * PART, (i + 1) * PART)
-        part_out[:, cols] = pair[i]
-        send_out[:, cols] = pair[i].astype(BF16)
+        send_out[:, i * PART : (i + 1) * PART] = pair[i].astype(BF16)
 
 
 def merge(core, moved, rank_col, wo):
@@ -650,7 +831,6 @@
         functools.partial(merge_kernel, len(wo.parts())),
         args,
         [
-            sds((TOK, D), F32),
             kept((TOK, D), BF16),
             kept((ROUNDS, TOK, PART), BF16),
             kept((TOK, TOK), F32),
@@ -663,65 +843,58 @@
     )
 
 
-def ffn_specs(at, index):
-    return {
-        at + z: pl.BlockSpec((1, 1, 2, FFN_ROWS, PART), lambda c, z=z: (z, c, 0, index, 0))
-        for z in range(4)
-    }
-
-
-def ffn_half(refs, c0):
-    return jnp.concatenate([r[0, 0, c0] for r in refs], 0)
+def gelu_parts(pre):
+    half = 0.5 * (1.0 + lax.erf(pre * (0.5**0.5)))
+    slope = half + pre * (jnp.exp(-0.5 * pre * pre) * np.float32(1.0 / np.sqrt(2.0 * np.pi)))
+    return (pre * half).astype(BF16), slope.astype(BF16)
+
+
+def add_up(total, more):
+    return more if total is None else [a + b for a, b in zip(total, more)]
+
+
+def ffn_forward(x_ref, own_ref, other_ref, gain_ref, w_ref, y_out, hf_out, act_out, slope_out):
+    y = x_ref[...] + (own_ref[...].astype(F32) + other_ref[...].astype(F32))
+    y_out[...] = y
+    y_out.flush()
+    xhat, _ = norm_parts(y)
+    hf = (xhat * gain_ref[...]).astype(BF16)
+    hf_out[0], hf_out[1] = hf[:, :PART], hf[:, PART:]
+    total = None
+    for c in range(QUAD):
+        w_ref.wait(4)
+        pre = dot(hf[:, :PART], w_ref.block(UP, c, 0), 1, 0) + dot(
+            hf[:, PART:], w_ref.block(UP, c, 1), 1, 0
+        )
+        act, slope = gelu_parts(pre)
+        act_out[:, c * PART : (c + 1) * PART] = act
+        slope_out[:, c * PART : (c + 1) * PART] = slope
+        total = add_up(total, [dot(act, w_ref.block(DOWN, c, c0), 1, 1) for c0 in range(2)])
+    return total
 
 
 def ffn_kernel(
-    x_ref, own_ref, other_ref, gain_ref, *refs
+    x_ref, own_ref, other_ref, gain_ref, w_ref, y_out, hf_out, act_out, slope_out, send_out
 ):
-    up_ref, down_ref = refs[:4], refs[4:8]
-    y_out, hf_out, pre_out, act_out, part_out, send_out, hf_ref, acc_ref = refs[8:]
-    c = pl.program_id(0)
-
-    @pl.when(c == 0)
-    def _():
-        y = x_ref[...] + (own_ref[...] + other_ref[...].astype(F32))
-        y_out[...] = y
-        xhat, _ = norm_parts(y)
-        hf = (xhat * gain_ref[...]).astype(BF16)
-        for c0 in range(2):
-            hf_ref[c0] = hf[:, c0 * PART : (c0 + 1) * PART]
-        hf_out[...] = hf_ref[...]
-        acc_ref[...] = jnp.zeros_like(acc_ref)
-
-    pre = dot(hf_ref[0], ffn_half(up_ref, 0), 1, 0) + dot(hf_ref[1], ffn_half(up_ref, 1), 1, 0)
-    pre_out[...] = pre
-    act = (0.5 * pre * (1.0 + lax.erf(pre * (0.5**0.5)))).astype(BF16)
-    act_out[...] = act
-    for c0 in range(2):
-        acc_ref[c0] += dot(act, ffn_half(down_ref, c0), 1, 1)
-
-    @pl.when(c == QUAD - 1)
-    def _():
-        put_halves((acc_ref[0], acc_ref[1]), part_out, send_out)
+    put_halves(
+        ffn_forward(
+            x_ref, own_ref, other_ref, gain_ref, w_ref, y_out, hf_out, act_out, slope_out
+        ),
+        send_out,
+    )
 
 
 def ffn(x, own, other, gain, w):
-    cols = pl.BlockSpec((TOK, PART), lambda c: (0, c))
-    return call(
+    return run(
         ffn_kernel,
-        (x, own, other, gain, *[w] * 8),
+        [Far(x), Far(own), other, Far(gain), FfnWeight(w)],
         [
-            kept((TOK, D), F32),
-            kept((2, TOK, PART), BF16),
-            kept((TOK, QUAD * PART), F32),
-            kept((TOK, QUAD * PART), BF16),
-            sds((TOK, D), F32),
-            kept((TOK, D), BF16),
+            Sent((TOK, D), F32),
+            Sent((2, TOK, PART), BF16),
+            Sent((TOK, QUAD * PART), BF16),
+            Sent((TOK, QUAD * PART), BF16),
+            Sent((TOK, D), BF16),
         ],
-        grid=(QUAD,),
-        specs={**ffn_specs(4, UP), **ffn_specs(8, DOWN)},
-        in_place=(0, *range(4, 12)),
-        out_specs={2: cols, 3: cols},
-        scratch=[pltpu.VMEM((2, TOK, PART), BF16), pltpu.VMEM((2, TOK, PART), F32)],
         name="ffn",
     )
 
@@ -736,74 +909,95 @@
             out_ref[at, z * 2 + y, row + tau * 16 : row + (tau + 1) * 16] = got
 
 
-def ffn_back_kernel(pending, *refs):
-    if pending:
-        g_ref, own_ref, other_ref, x_ref, gain_ref, *rest = refs
-    else:
-        g_ref, *rest = refs
-    pre_ref, hf_ref, act_ref, *rest = rest
-    up_ref, down_ref, rest = rest[:4], rest[4:8], rest[8:]
-    g_out, part_out, send_out, dgain_out, grad_out, back_ref, acc_ref = rest
-    c = pl.program_id(0)
-
-    @pl.when(c == 0)
-    def _():
-        g = g_ref[...]
-        if pending:
-            xhat, rstd = norm_parts(x_ref[...])
-            add, dgain = norm_back(
-                own_ref[...] + other_ref[...].astype(F32), gain_ref[...], xhat, rstd
-            )
-            g = g + add
-            dgain_out[...] = dgain
-        else:
-            dgain_out[...] = jnp.zeros_like(dgain_out)
-        g_out[...] = g
-        back = g.astype(BF16)
+def ffn_backward(back, waits, w_ref, hf_ref, act_ref, slope_ref, send_out, grad_out):
+    total = None
+    for c in range(QUAD):
+        if waits:
+            w_ref.wait(4)
+        cols = slice(c * PART, (c + 1) * PART)
+        d_act = dot(back[0], w_ref.block(DOWN, c, 0), 1, 0) + dot(
+            back[1], w_ref.block(DOWN, c, 1), 1, 0
+        )
+        d_pre = (d_act * slope_ref[:, cols].astype(F32)).astype(BF16)
+        total = add_up(total, [dot(d_pre, w_ref.block(UP, c, c0), 1, 1) for c0 in range(2)])
+        act = act_ref[:, cols]
         for c0 in range(2):
-            back_ref[c0] = back[:, c0 * PART : (c0 + 1) * PART]
-        acc_ref[...] = jnp.zeros_like(acc_ref)
-
-    d_act = dot(back_ref[0], ffn_half(down_ref, 0), 1, 0) + dot(
-        back_ref[1], ffn_half(down_ref, 1), 1, 0
-    )
-    pre = pre_ref[...]
-    slope = 0.5 * (1.0 + lax.erf(pre * (0.5**0.5))) + pre * (
-        jnp.exp(-0.5 * pre * pre) * np.float32(1.0 / np.sqrt(2.0 * np.pi))
-    )
-    d_pre = (d_act * slope).astype(BF16)
-    for c0 in range(2):
-        acc_ref[c0] += dot(d_pre, ffn_half(up_ref, c0), 1, 1)
-        put_pieces(grad_out, c0, 0, 64, dot(hf_ref[c0], d_pre, 0, 0).astype(BF16))
-        put_pieces(grad_out, c0, 64, 64, dot(back_ref[c0], act_ref[...], 0, 0).astype(BF16))
-
-    @pl.when(c == QUAD - 1)
-    def _():
-        put_halves((acc_ref[0], acc_ref[1]), part_out, send_out)
-
-
-def ffn_back(g, pending, pre, hf, act, w):
-    cols = pl.BlockSpec((TOK, PART), lambda c: (0, c))
-    args = [g, *(pending or ()), pre, hf, act, *[w] * 8]
-    at = len(args) - 11
-    specs = {at: cols, at + 2: cols, **ffn_specs(at + 3, UP), **ffn_specs(at + 7, DOWN)}
-    in_place = (0, *((3,) if pending else ()), *range(at, at + 11))
-    return call(
-        functools.partial(ffn_back_kernel, pending is not None),
-        args,
+            put_pieces(grad_out, 2 * c + c0, 0, 64, dot(hf_ref[c0], d_pre, 0, 0).astype(BF16))
+            put_pieces(grad_out, 2 * c + c0, 64, 64, dot(back[c0], act, 0, 0).astype(BF16))
+        grad_out.flush()
+    put_halves(total, send_out)
+
+
+def turn_kernel(
+    x_ref, own_ref, other_ref, gain_ref, g_ref, w_ref,
+    y_out, forth_out, send_out, grad_out, hf_ref, act_ref, slope_ref
+):
+    put_halves(
+        ffn_forward(
+            x_ref, own_ref, other_ref, gain_ref, w_ref, y_out, hf_ref, act_ref, slope_ref
+        ),
+        forth_out,
+    )
+    forth_out.flush()
+    back = g_ref[...].astype(BF16)
+    back = [back[:, :PART], back[:, PART:]]
+    ffn_backward(back, False, w_ref, hf_ref, act_ref, slope_ref, send_out, grad_out)
+
+
+def turn(x, own, other, gain, g, w):
+    return run(
+        turn_kernel,
+        [Far(x), Far(own), other, Far(gain), Far(g), FfnWeight(w)],
         [
-            kept((TOK, D), F32),
-            sds((TOK, D), F32),
-            kept((TOK, D), BF16),
+            Sent((TOK, D), F32),
+            Sent((TOK, D), BF16),
+            Sent((TOK, D), BF16),
+            Sent((2 * QUAD, 8, FFN_ROWS, PART), BF16, QUAD),
+        ],
+        temps=[
+            pltpu.VMEM((2, TOK, PART), BF16),
+            pltpu.VMEM((TOK, QUAD * PART), BF16),
+            pltpu.VMEM((TOK, QUAD * PART), BF16),
+        ],
+        name="turn",
+        vmem=BIG_VMEM_BYTES,
+    )
+
+
+def ffn_back_kernel(
+    g_ref, own_ref, other_ref, x_ref, gain_ref, hf_ref, act_ref, slope_ref, w_ref, unused_ref,
+    g_out, send_out, grad_out, dgain_out
+):
+    xhat, rstd = norm_parts(x_ref[...])
+    add, dgain = norm_back(
+        own_ref[...].astype(F32) + other_ref[...].astype(F32), gain_ref[...], xhat, rstd
+    )
+    dgain_out[...] = dgain
+    g = g_ref[...] + add
+    g_out[...] = g
+    g_out.flush()
+    back = g.astype(BF16)
+    back = [back[:, :PART], back[:, PART:]]
+    ffn_backward(back, True, w_ref, hf_ref, act_ref, slope_ref, send_out, grad_out)
+
+
+def ffn_back(g, own, other, x, gain, more, hf, act, slope, w):
+    return run(
+        ffn_back_kernel,
+        [
+            Far(g), Far(own), other, Far(x), Far(gain),
+            Far(hf), Far(act), Far(slope), FfnWeight(w), Direct(more),
+        ],
+        [
+            Sent((TOK, D), F32),
+            Sent((TOK, D), BF16),
+            Sent((2 * QUAD, 8, FFN_ROWS + ATTN_ROWS, PART), BF16, QUAD),
             sds((1, D), F32),
-            kept((2 * QUAD, 8, FFN_ROWS, PART), BF16),
         ],
-        grid=(QUAD,),
-        specs=specs,
-        in_place=in_place,
-        out_specs={4: pl.BlockSpec((2, 8, FFN_ROWS, PART), lambda c: (c, 0, 0, 0))},
-        scratch=[pltpu.VMEM((2, TOK, PART), BF16), pltpu.VMEM((2, TOK, PART), F32)],
+        partial={2: (2 * QUAD, 8, FFN_ROWS, PART)},
+        aliases={9: 2},
         name="ffn_back",
+        vmem=BIG_VMEM_BYTES,
     )
 
 
@@ -811,7 +1005,7 @@
     w_refs, refs = refs[:count], refs[count:]
     o_ref, share_ref, rank_row_ref, g_out, back_out, send_out, dgain_out = refs
     xhat, rstd = norm_parts(y_ref[...])
-    add, dgain = norm_back(own_ref[...] + other_ref[...].astype(F32), gain_ref[...], xhat, rstd)
+    add, dgain = norm_back(own_ref[...].astype(F32) + other_ref[...].astype(F32), gain_ref[...], xhat, rstd)
     dgain_out[...] = dgain
     g = g_ref[...] + add
     g_out[...] = g
@@ -866,13 +1060,13 @@
             sds((1, D), F32),
         ],
         specs=specs,
-        in_place=(0, 3, *specs, *range(len(args) - 4, len(args) - 1)),
+        in_place=(0, 1, 3, *specs, *range(len(args) - 4, len(args) - 1)),
         prefetch=1,
         name="merge_back",
     )
 
 
-def attend_back_kernel(moved_ref, sorted_ref, place_row_ref, place_col_ref, gain_ref, send_out):
+def attend_back_kernel(moved_ref, sorted_ref, place_row_ref, gain_ref, send_out):
     lanes = iota((ROWS, TOK), 1)
     aux = moved_ref[:, 2 * DH :].astype(F32)
     got = jnp.zeros((1024, 2 * DH), F32)
@@ -918,20 +1112,20 @@
     grads = jnp.concatenate([g_query, overlap(d_value)], 1).astype(BF16)
     for j in range(2):
         cols = slice(j * 2 * DH, (j + 1) * 2 * DH)
-        send_out[:, cols] = leave(place_col_ref, j, grads[SPAN:]).astype(BF16)
-    lent = leave(place_col_ref, 2, grads[:SPAN, :DH]) + leave(place_col_ref, 3, grads[:SPAN, DH:])
+        send_out[:, cols] = leave(place_row_ref, j, grads[SPAN:]).astype(BF16)
+    lent = leave(place_row_ref, 2, grads[:SPAN, :DH]) + leave(place_row_ref, 3, grads[:SPAN, DH:])
     b = iota((ROWS, 1), 0) & 7
     for q in range(4):
         lent = jnp.where(b == 4 + q, gain_ref[:, q * DH : (q + 1) * DH], lent)
     send_out[:, 4 * DH :] = lent.astype(BF16)
 
 
-def attend_back(moved, rows, place_row, place_col, gain):
+def attend_back(moved, rows, place_row, gain):
     return call(
         attend_back_kernel,
-        (moved, rows, place_row, place_col, gain),
+        (moved, rows, place_row, gain),
         [kept((ROWS, QV_LANES), BF16)],
-        in_place=(1, 2, 3),
+        in_place=(1, 2),
         name="attend_back",
     )[0]
 
@@ -941,9 +1135,9 @@
     refs = refs[2 * count :]
     if grads:
         back_ref, merged_ref, hn_ref, *refs = refs
-        part_out, send_out, grad_out, gain_out = refs
+        send_out, grad_out, gain_out, grad_ref, sems = refs
     else:
-        part_out, send_out, dq_out, dv_out, gain_out = refs
+        send_out, dq_out, dv_out, gain_out = refs
     gain_out[...] = dot(
         hot(iota((8, 1), 0) == (iota((1, ROWS), 1) & 7)), moved_ref[:, 4 * DH :], 1, 0
     )
@@ -966,27 +1160,40 @@
             for i, (left, right) in enumerate(
                 ((back_ref, merged_ref[...]), (hn_ref, d_q), (hn_ref, d_v))
             ):
-                put_pieces(grad_out, c0, i * 16, 16, dot(left[c0], right, 0, 0).astype(BF16))
+                put_pieces(grad_ref, c0, i * 16, 16, dot(left[c0], right, 0, 0).astype(BF16))
+        sending = pltpu.make_async_copy(
+            grad_ref, grad_out.at[:, :, pl.ds(FFN_ROWS, ATTN_ROWS), :], sems.at[0]
+        )
+        sending.start()
     else:
         dq_out[...] = d_q
         dv_out[...] = d_v
     core = core_ref[0]
     from_q = out_of(core, d_q, q_refs)
     from_v = out_of(core, d_v, v_refs)
-    put_halves([a + b for a, b in zip(from_q, from_v)], part_out, send_out)
+    put_halves([a + b for a, b in zip(from_q, from_v)], send_out)
+    if grads:
+        sending.wait()
 
 
 def project_back(core, moved, rank_col, wq, wv, lefts=None):
     args, specs = unpacked([core, moved, rank_col, wq, wv, *(lefts or ())], 1)
+    out_specs = {}
     if lefts:
-        outs = [kept((2 * QUAD, 8, ATTN_ROWS, PART), BF16)]
+        rows = FFN_ROWS + ATTN_ROWS
+        outs = [kept((2 * QUAD, 8, rows, PART), BF16)]
+        out_specs = {1: pl.BlockSpec(memory_space=pl.ANY)}
+        temps = [pltpu.VMEM((2 * QUAD, 8, ATTN_ROWS, PART), BF16), pltpu.SemaphoreType.DMA((1,))]
     else:
         outs = [kept((TOK, PART), BF16)] * 2
+        temps = []
     return call(
         functools.partial(project_back_kernel, len(wq.parts()), lefts is not None),
         args,
-        [sds((TOK, D), F32), kept((TOK, D), BF16), *outs, sds((8, DH), F32)],
+        [kept((TOK, D), BF16), *outs, sds((8, DH), F32)],
         specs=specs,
+        out_specs=out_specs,
+        scratch=temps,
         in_place=range(1, len(args) - 1),
         prefetch=1,
         name="project_back",
@@ -995,7 +1202,7 @@
 
 def last_kernel(g_ref, own_ref, other_ref, x_ref, gain_ref, g_out, dgain_out):
     xhat, rstd = norm_parts(x_ref[...])
-    add, dgain = norm_back(own_ref[...] + other_ref[...].astype(F32), gain_ref[...], xhat, rstd)
+    add, dgain = norm_back(own_ref[...].astype(F32) + other_ref[...].astype(F32), gain_ref[...], xhat, rstd)
     g_out[...] = g_ref[...] + add
     dgain_out[...] = dgain
 
@@ -1005,7 +1212,7 @@
         last_kernel,
         (g, own, other, x, gain),
         [kept((TOK, D), F32), sds((1, D), F32)],
-        in_place=(0, 3),
+        in_place=(0, 1, 3),
         name="last",
     )
 
@@ -1039,29 +1246,6 @@
     )[0]
 
 
-def join_kernel(*refs):
-    at = 0
-    for ref in refs[:-1]:
-        refs[-1][:, at : at + ref.shape[1]] = ref[...]
-        at += ref.shape[1]
-
-
-def join(arrays):
-    rows = sum(a.shape[1] for a in arrays)
-    return call(
-        join_kernel,
-        arrays,
-        [kept((8, rows, PART), BF16)],
-        grid=(4,),
-        specs={
-            i: pl.BlockSpec((2, a.shape[1], PART), lambda g: (g, 0, 0)) for i, a in enumerate(arrays)
-        },
-        out_specs={0: pl.BlockSpec((2, rows, PART), lambda g: (g, 0, 0))},
-        in_place=range(len(arrays)),
-        name="join",
-    )[0]
-
-
 def swap_narrow(values):
     return lax.ppermute(values, "narrow", [(0, 1), (1, 0)])
 
@@ -1133,16 +1317,8 @@
 
 
 def gathered(rows):
-    other = lax.ppermute(rows, "wide", [(i, i ^ 32) for i in range(NW)])
-    low = lax.axis_index("wide") < 32
-    both = jnp.stack(
-        [
-            jnp.where(low, a, b).reshape(-1, 16, PART) for a, b in ((rows, other), (other, rows))
-        ],
-        1,
-    ).reshape(-1, PART)
-    got = lax.all_gather(both, "wide", axis=0, tiled=True, axis_index_groups=LAYER_OF_Y)
-    return got.reshape(QUAD, QUAD, 2, both.shape[0], PART)
+    got = lax.all_gather(rows, "wide", axis=0, tiled=True, axis_index_groups=LAYER_OF_Y)
+    return got.reshape(QUAD, QUAD, 2, rows.shape[0], PART)
 
 
 def moved_rows(rows):
@@ -1171,19 +1347,29 @@
     routed = route_out(me.reshape(1), owner_row, master)
     sort_target, held = after((sort_target, owner), routed)
     moved = moved_rows(routed)
-    held_by = []
+    chunks = []
     for l in range(LAYERS):
         of = held[l * 88 : (l + 1) * 88]
-        held_by += [of[at : at + 32].reshape(8, 4).T.reshape(32) for at in (24, 56)]
-        held_by += [of[16:24], of[:16]]
-    held_by = jnp.repeat(jnp.concatenate(held_by), 2)
-    code = (held_by // CAP) * PACK + (held_by % CAP) * 2 + np.arange(2 * TILES, dtype=np.int32) % 2
-    code_col = code.reshape(-1, 1)
-    code_row = code.reshape(1, -1)
+        chunks += [of[at : at + 32].reshape(8, 4).T.reshape(4, 8) for at in (24, 56)]
+        chunks += [of[16:24].reshape(1, 8), of[:16].reshape(2, 8)]
+    holder = jnp.repeat(jnp.concatenate(chunks), 2, axis=1)
+    e = np.arange(16, dtype=np.int32)[None] & 1
+    code_row = ((holder // CAP) * PACK + (holder % CAP) * 2 + e).reshape(1, -1)
+    there = (holder // CAP) * WIDE_PACK + (holder % CAP) * 4 + e
+    both = jnp.stack([there, there + 2], 1)
+    mine_only = there + 2 * (me >> 5)
+    code_col = jnp.concatenate(
+        [
+            both[:9].reshape(-1),
+            both[19:].reshape(-1),
+            both[11:19].reshape(-1),
+            mine_only[9:11].reshape(-1),
+        ]
+    ).reshape(-1, 1)
     mine = lax.dynamic_slice_in_dim(sort_target, me * TOK, TOK, axis=2).reshape(-1, TOK)
     by_source = lax.dynamic_index_in_dim(sort_target, me >> 5, 1, keepdims=False)
     plans = plan((me & 7).reshape(1), mine, by_source.reshape(LAYERS, NW, TOK))
-    rank_rows, rank_cols, place_rows, place_cols = [plans[i::4] for i in range(4)]
+    rank_rows, rank_cols, place_rows = [plans[i::3] for i in range(3)]
     flat_gains = gains.reshape(LAYERS * 2, PART)
     x_two, gain_rows = inner(
         half, [(x_second, swap_narrow(x_second)), (flat_gains, swap_narrow(flat_gains))], "inner_a"
@@ -1194,7 +1380,7 @@
     pairs = [(a, swap_narrow(a)) for a in (x_first, grad_first, grad_second)]
     first_w = with_core(after(to_same_core(first_rows), pairs))
     early = gathered(early_rows)
-    late = gathered(after(late_rows, first_w))
+    late = gathered(late_rows)
     x_one, g_one, g_two = inner(half, pairs, "inner_b")
     w_ffn = [early, late]
     w_attn = [
@@ -1211,30 +1397,36 @@
         moved = moved_rows(send)
         if l == 0:
             moved = after(moved, x_one, g_one, g_two)
-        rows, send = attend(moved, place_rows[l], place_cols[l])
+        rows, send = attend(moved, place_rows[l])
         moved = moved_rows(send)
-        own, send, o, share, merged = merge(core, moved, rank_cols[l], w_out)
-        x_one, hf, pre, act, own_f, send_f = ffn(
-            x_one, own, swap_narrow(send), gain[l][1], w_ffn[l]
-        )
-        pending = (own_f, swap_narrow(send_f))
-        saved.append((x_two, x_one, hn, rows, o, share, merged, hf, pre, act))
-    y_two = x_two + (pending[0] + pending[1].astype(F32))
+        send, o, share, merged = merge(core, moved, rank_cols[l], w_out)
+        stream = (x_one, send, swap_narrow(send), gain[l][1])
+        if l < LAYERS - 1:
+            x_one, *for_ffn, send_f = ffn(*stream, w_ffn[l])
+        else:
+            x_one, send_f, send, ffn_part = turn(*stream, g_two, w_ffn[l])
+        pending = (send_f, swap_narrow(send_f))
+        saved.append((x_two, x_one, hn, rows, o, share, merged))
+    y_two = x_two + (pending[0].astype(F32) + pending[1].astype(F32))
     y_first, y_second = outer(half, (x_one, y_two), "outer_y")
 
     pending = None
     dgains = [[None, None], [None, None]]
     gain_sums = []
     for l in reversed(range(LAYERS)):
-        x_in, y_mid, hn, rows, o, share, merged, hf, pre, act = saved[l]
+        x_in, y_mid, hn, rows, o, share, merged = saved[l]
         w_out, w_qk, w_value = w_attn[l]
-        g_two, own, send, dgain, ffn_part = ffn_back(g_two, pending, pre, hf, act, w_ffn[l])
-        if l == 0:
-            dgains[1][0] = dgain
+        if l < LAYERS - 1:
+            g_two, send, ffn_part, dgains[l + 1][0] = ffn_back(
+                g_two, *pending, *for_ffn, w_ffn[l]
+            )
         other = swap_narrow(send)
         ffn_part = summed_along_x(ffn_part)
+        if l == 0:
+            other = after(other, ffn_rows)
+            ffn_rows = summed_along_y(ffn_rows)
         g_one, back, send, dgains[l][1] = merge_back(
-            core, g_one, own, other, y_mid, gain[l][1], w_out, o, share, rank_rows[l]
+            core, g_one, send, other, y_mid, gain[l][1], w_out, o, share, rank_rows[l]
         )
         moved = moved_rows(send)
         if l > 0:
@@ -1242,33 +1434,33 @@
             half_gain = dgains[1][1][:, :PART]
         else:
             dx_first = outer(half, (g_one,), "outer_dx_first")[0]
-            joined = join([ffn_before, attn_before])
-            moved = after(moved, dx_first, joined)
+            moved = after(moved, dx_first, ffn_rows)
             half_gain = dgains[1][1][:, PART:]
-        send = attend_back(moved, rows, place_rows[l], place_cols[l], half_gain)
+        send = attend_back(moved, rows, place_rows[l], half_gain)
         moved = moved_rows(send)
         if l > 0:
             moved = after(moved, ffn_part)
         if l > 0:
-            own, send, attn_part, gain_sum = project_back(
+            send, attn_part, gain_sum = project_back(
                 core, moved, rank_cols[l], w_qk, w_value, (back, merged, hn)
             )
-            attn_before = summed_along_x(attn_part)
-            ffn_before = ffn_part
+            ffn_rows = summed_along_z(after(ffn_part, moved))
         else:
-            own, send, dq, dv, gain_sum = project_back(core, moved, rank_cols[l], w_qk, w_value)
+            send, dq, dv, gain_sum = project_back(core, moved, rank_cols[l], w_qk, w_value)
             hn2 = with_core(hn)
             pairs = [(with_core(back), with_core(merged)), (hn2, with_core(dq)), (hn2, with_core(dv))]
             attn_part = attn_grad(core, pairs)
             attn_rows = summed(attn_part)
-            ffn_rows = summed_across_x(after(ffn_part, attn_part))
-            reduced = summed_along_y(after(summed_along_z(joined), attn_part))
         other = swap_narrow(send)
+        if l == 0:
+            ffn_part = after(ffn_part, attn_part)
+            last_rows = summed_along_y(summed_along_z(ffn_part[:, FFN_ROWS:]))
+            both_rows = summed_across_x(after(ffn_part[:, :FFN_ROWS], other))
         gain_sums.append(gain_sum[4:].reshape(1, PART))
-        pending = (own, other, x_in, gain[l][0])
-    g_two, dgains[0][0] = last(g_two, *pending)
+        pending = (send, other, x_in, gain[l][0], attn_part)
+    g_two, dgains[0][0] = last(g_two, *pending[:4])
     dx_second = outer(half, (g_two,), "outer_dx_second")[0]
-    parts = (ffn_rows, attn_rows, reduced)
+    parts = (both_rows, attn_rows, ffn_rows, last_rows)
     back_rows = moved_rows(
         route_back(code_row, parts, (dgains[1][0], dgains[0][1], dgains[0][0]))
     )

time: 520 us -> 502 us (0.965)
  waiting for transfers between devices: 195 us -> 182 us
  Pallas kernels: 119 us -> 111 us
    pallas_call x29 -> x23, Pallas kernels: 119 us -> 74.4 us  [call(): pl.pallas_call(kernel, out_shape=outs, grid_spec=pltpu.PrefetchScalarGrid...]
    pallas_call x0 -> x4, Pallas kernels: none -> 36.5 us  [run(): pl.pallas_call(body, out_shape=out_shapes, grid_spec=pltpu.PrefetchScalar...]
    all_to_all x2, waiting for transfers between devices: 27.5 us -> 4.58 us  [to_same_core(): lax.all_to_all(values, 'wide', split_axis=0, concat_axis=0, tiled=True, a...]
    ppermute x13, waiting for transfers between devices: 62.8 us -> 77 us  [swap_narrow(): return lax.ppermute(values, 'narrow', [(0, 1), (1, 0)])]
    ppermute x2 -> x0, waiting for transfers between devices: 13.6 us -> none  [gathered(): other = lax.ppermute(rows, 'wide', [(i, i ^ 32) for i in range(NW)])]
    ppermute x1 -> x2, waiting for transfers between devices: 1.8 us -> 10.6 us  [summed_along_y(): got = lax.ppermute(theirs, 'wide', [(i, i ^ 32) for i in range(NW)])]
  transfers between devices with their start and end apart: 37 -> 36, of which waited for: 25 -> 25; matrix products, arithmetic and copies ran while one was open for 1% -> 2% of each run, Pallas kernels for 17% -> 18%
where the time goes in v4:
time: 502 us; the launch traced here: 492 us
  waiting for transfers between devices  182 us (36%)
  Pallas kernels  111 us (22%)
  starting transfers between devices  85.3 us (17%)
  blocking collectives  82 us (16%)
  local copies, waits for them, and re-layouts  16.2 us (3%)
  between operations  15.1 us (3%)
    all_to_all x6, waiting for transfers between devices, to_all(): lax.all_to_all(values, 'wide', split_axis=0, concat_axis=0, tiled=True)  84.5 us
    all_to_all x4, blocking collectives, to_all(): lax.all_to_all(values, 'wide', split_axis=0, concat_axis=0, tiled=True)  82 us
    ppermute x13, waiting for transfers between devices, swap_narrow(): return lax.ppermute(values, 'narrow', [(0, 1), (1, 0)])  77 us
    pallas_call x23, Pallas kernels, call(): pl.pallas_call(kernel, out_shape=outs, grid_spec=pltpu.PrefetchScalarGrid...  74.4 us
    all_to_all x6, starting transfers between devices, to_all(): lax.all_to_all(values, 'wide', split_axis=0, concat_axis=0, tiled=True)  50.5 us
    pallas_call x4, Pallas kernels, run(): pl.pallas_call(body, out_shape=out_shapes, grid_spec=pltpu.PrefetchScalar...  36.5 us
    ppermute x2, waiting for transfers between devices, summed_along_y(): got = lax.ppermute(theirs, 'wide', [(i, i ^ 32) for i in range(NW)])  10.6 us
  transfers between devices with their start and end apart: 36, of which 25 were waited for; matrix products, arithmetic and copies ran while one was open for 2% of the time, Pallas kernels for 18%

profile of v4, /device:TPU:1, one launch (start us, length us, event | category | flops | bytes accessed | tf_op | source)
XLA Modules:
  0.0 492.3 jit_solution(6783632817690007464)
XLA Ops:
  10.9 3.4 route_out.1
  14.3 12.4 %all-to-all-start = ((bf16[64,24,512]{2,1,0:T(8,128)(2,1)}), bf16[64,24,512]{2,1,0:T(8,128)(2,1)S(1)}, u32[]{:S(2)}, u32[]{:S(2)}) async-start(bf16[64,24,512]{2,1,0:T(8,128)(2,1)} %bitcast.144), calls=%async_computation | async-start | bytes 3145728 | tf_op jit(solution)/shard_map/all_to_all | solution.py:1259
  35.1 15.6 %all-to-all-done = bf16[64,24,512]{2,1,0:T(8,128)(2,1)S(1)} async-done(((bf16[64,24,512]{2,1,0:T(8,128)(2,1)}), bf16[64,24,512]{2,1,0:T(8,128)(2,1)S(1)}, u32[]{:S(2)}, u32[]{:S(2)}) %all-to-all-start) | async-done | bytes 1572896 | tf_op jit(solution)/shard_map/all_to_all | solution.py:1259
  53.8 4.4 all-to-all-start.1
  60.2 7.1 %collective-permute-done.2.refs_1_ = bf16[128,512]{1,0:T(8,128)(2,1)S(1)} collective-permute-done((bf16[128,512]{1,0:T(8,128)(2,1)S(1)}, bf16[128,512]{1,0:T(8,128)(2,1)S(1)}, u32[]{:S(2)}, u32[]{:S(2)}) %collective-permute-start.2) | collective-permute-done | bytes 131104 | tf_op jit(solution)/shard_map/ppermute | solution.py:1250
  67.4 5.7 %collective-permute-done.3.refs_3_ = bf16[128,512]{1,0:T(8,128)(2,1)S(1)} collective-permute-done((bf16[128,512]{1,0:T(8,128)(2,1)S(1)}, bf16[128,512]{1,0:T(8,128)(2,1)S(1)}, u32[]{:S(2)}, u32[]{:S(2)}) %collective-permute-start.3) | collective-permute-done | bytes 131104 | tf_op jit(solution)/shard_map/ppermute | solution.py:1250
  73.0 5.6 %collective-permute-done.4.refs_5_ = bf16[128,512]{1,0:T(8,128)(2,1)S(1)} collective-permute-done((bf16[128,512]{1,0:T(8,128)(2,1)S(1)}, bf16[128,512]{1,0:T(8,128)(2,1)S(1)}, u32[]{:S(2)}, u32[]{:S(2)}) %collective-permute-start.4) | collective-permute-done | bytes 131104 | tf_op jit(solution)/shard_map/ppermute | solution.py:1250
  78.6 3.3 all-to-all-done.1.refs_2_.refs_3_.refs_4_.refs_5_.refs_10_.refs_11_.refs_12_.refs_13_.refs_0_.refs_1_.refs_8_.refs_9_
  86.8 3.2 project.2
  90.0 6.3 %all-to-all-start.2 = ((bf16[64,8,640]{2,1,0:T(8,128)(2,1)}), bf16[64,8,640]{2,1,0:T(8,128)(2,1)S(1)}, u32[]{:S(2)}, u32[]{:S(2)}) async-start(bf16[64,8,640]{2,1,0:T(8,128)(2,1)} %bitcast.151), calls=%async_computation.2 | async-start | bytes 1310720 | tf_op jit(solution)/shard_map/all_to_all | solution.py:1259
  100.0 17.6 %all-to-all-done.2 = bf16[64,8,640]{2,1,0:T(8,128)(2,1)S(1)} async-done(((bf16[64,8,640]{2,1,0:T(8,128)(2,1)}), bf16[64,8,640]{2,1,0:T(8,128)(2,1)S(1)}, u32[]{:S(2)}, u32[]{:S(2)}) %all-to-all-start.2) | async-done | bytes 655392 | tf_op jit(solution)/shard_map/all_to_all | solution.py:1259
  117.6 4.0 attend.2
  121.5 18.1 %all_to_all.65 = bf16[64,8,384]{2,1,0:T(8,128)(2,1)S(1)} all-to-all(bf16[64,8,384]{2,1,0:T(8,128)(2,1)} %bitcast.155), channel_id=1, replica_groups=mesh['wide'=64,'narrow'=2] {'wide'}, dimensions={0} | all-to-all | bytes 786432 | tf_op jit(solution)/shard_map/all_to_all | solution.py:1259
  142.7 7.8 %collective-permute-done.6.refs_2_ = bf16[128,1024]{1,0:T(8,128)(2,1)S(1)} collective-permute-done((bf16[128,1024]{1,0:T(8,128)(2,1)}, bf16[128,1024]{1,0:T(8,128)(2,1)S(1)}, u32[]{:S(2)}, u32[]{:S(2)}) %collective-permute-start.6) | collective-permute-done | bytes 262176 | tf_op jit(solution)/shard_map/ppermute | solution.py:1250
  150.4 7.4 %ffn.1 = (f32[128,1024]{1,0:T(8,128)}, bf16[2,128,512]{2,1,0:T(8,128)(2,1)}, bf16[128,2048]{1,0:T(8,128)(2,1)}, bf16[128,2048]{1,0:T(8,128)(2,1)}, bf16[128,1024]{1,0:T(8,128)(2,1)}) custom-call(f32[128,1024]{1,0:T(8,128)} %copy-done.8, bf16[128,1024]{1,0:T(8,128)(2,1)} %get-tuple-element.123.refs_1_, bf16[128,1024]{1,0:T(8,128)(2,1)S(1)} %collective-permute-done.6.refs_2_, ...), custom_call_target="tpu_custom_call" | custom-call | tf_op jit(solution)/shard_map/ffn/pallas_call | solution.py:291
  158.3 6.6 %collective-permute-done.7.refs_2_ = bf16[128,1024]{1,0:T(8,128)(2,1)S(1)} collective-permute-done((bf16[128,1024]{1,0:T(8,128)(2,1)}, bf16[128,1024]{1,0:T(8,128)(2,1)S(1)}, u32[]{:S(2)}, u32[]{:S(2)}) %collective-permute-start.7) | collective-permute-done | bytes 262176 | tf_op jit(solution)/shard_map/ppermute | solution.py:1250
  164.9 3.7 project.3
  168.6 23.2 %all_to_all.66 = bf16[64,8,640]{2,1,0:T(8,128)(2,1)S(1)} all-to-all(bf16[64,8,640]{2,1,0:T(8,128)(2,1)} %bitcast.152), channel_id=1, replica_groups=mesh['wide'=64,'narrow'=2] {'wide'}, dimensions={0} | all-to-all | bytes 1310720 | tf_op jit(solution)/shard_map/all_to_all | solution.py:1259
  191.8 4.0 attend.3
  195.8 17.9 %all_to_all.67 = bf16[64,8,384]{2,1,0:T(8,128)(2,1)S(1)} all-to-all(bf16[64,8,384]{2,1,0:T(8,128)(2,1)} %bitcast.156), channel_id=1, replica_groups=mesh['wide'=64,'narrow'=2] {'wide'}, dimensions={0} | all-to-all | bytes 786432 | tf_op jit(solution)/shard_map/all_to_all | solution.py:1259
  217.4 6.9 %collective-permute-done.8.refs_2_ = bf16[128,1024]{1,0:T(8,128)(2,1)S(1)} collective-permute-done((bf16[128,1024]{1,0:T(8,128)(2,1)}, bf16[128,1024]{1,0:T(8,128)(2,1)S(1)}, u32[]{:S(2)}, u32[]{:S(2)}) %collective-permute-start.8) | collective-permute-done | bytes 262176 | tf_op jit(solution)/shard_map/ppermute | solution.py:1250
  224.3 12.6 %turn.1 = (f32[128,1024]{1,0:T(8,128)}, bf16[128,1024]{1,0:T(8,128)(2,1)}, bf16[128,1024]{1,0:T(8,128)(2,1)}, bf16[8,8,128,512]{3,2,1,0:T(8,128)(2,1)}) custom-call(f32[128,1024]{1,0:T(8,128)} %get-tuple-element.124.refs_0_.y_ref, bf16[128,1024]{1,0:T(8,128)(2,1)} %get-tuple-element.129.refs_1_, bf16[128,1024]{1,0:T(8,128)(2,1)S(1)} %collective-permute-done.8.refs_2_, ...), custom_call_target="tpu_custom_call" | custom-call | tf_op jit(solution)/shard_map/turn/pallas_call | solution.py:291
  239.4 5.1 %collective-permute-done.10.other_ref = bf16[128,1024]{1,0:T(8,128)(2,1)S(1)} collective-permute-done((bf16[128,1024]{1,0:T(8,128)(2,1)S(1)}, bf16[128,1024]{1,0:T(8,128)(2,1)S(1)}, u32[]{:S(2)}, u32[]{:S(2)}) %collective-permute-start.10) | collective-permute-done | bytes 262176 | tf_op jit(solution)/shard_map/ppermute | solution.py:1250
  244.5 4.1 merge_back.2
  248.6 8.1 %all-to-all-start.6 = ((bf16[64,8,384]{2,1,0:T(8,128)(2,1)}), bf16[64,8,384]{2,1,0:T(8,128)(2,1)S(1)}, u32[]{:S(2)}, u32[]{:S(2)}) async-start(bf16[64,8,384]{2,1,0:T(8,128)(2,1)} %bitcast.153), calls=%async_computation.6 | async-start | bytes 786432 | tf_op jit(solution)/shard_map/all_to_all | solution.py:1259
  259.9 11.4 %all-to-all-done.6 = bf16[64,8,384]{2,1,0:T(8,128)(2,1)S(1)} async-done(((bf16[64,8,384]{2,1,0:T(8,128)(2,1)}), bf16[64,8,384]{2,1,0:T(8,128)(2,1)S(1)}, u32[]{:S(2)}, u32[]{:S(2)}) %all-to-all-start.6) | async-done | bytes 393248 | tf_op jit(solution)/shard_map/all_to_all | solution.py:1259
  271.4 5.3 %attend_back.2 = bf16[512,640]{1,0:T(8,128)(2,1)} custom-call(bf16[512,384]{1,0:T(8,128)(2,1)S(1)} %bitcast.103, bf16[1088,256]{1,0:T(8,128)(2,1)} %get-tuple-element.142.sorted_ref, s32[4,512]{1,0:T(4,128)} %get-tuple-element.113.place_row_ref, f32[1,512]{1,0:T(1,128)S(1)} %get-tuple-element.197.gain_ref), custom_call_target="tpu_custom_call" | custom-call | tf_op jit(solution)/shard_map/attend_back/pallas_call | solution.py:91
  276.7 22.8 %all_to_all.68 = bf16[64,8,640]{2,1,0:T(8,128)(2,1)S(1)} all-to-all(bf16[64,8,640]{2,1,0:T(8,128)(2,1)} %bitcast.147), channel_id=1, replica_groups=mesh['wide'=64,'narrow'=2] {'wide'}, dimensions={0} | all-to-all | bytes 1310720 | tf_op jit(solution)/shard_map/all_to_all | solution.py:1259
  299.6 5.7 %project_back.2 = (bf16[128,1024]{1,0:T(8,128)(2,1)}, bf16[8,8,176,512]{3,2,1,0:T(8,128)(2,1)}, f32[8,128]{1,0:T(8,128)S(1)}) custom-call(s32[1]{0:T(128)} %bitcast.1.core_ref, bf16[512,640]{1,0:T(8,128)(2,1)S(1)} %bitcast.97, s32[128,128]{1,0:T(8,128)} %get-tuple-element.112.rank_col_ref, bf16[4,4,2,384,512]{4,3,2,1,0:T(8,128)(2,1)} %bitcast.130, ...), custom_call_target="tpu_custom_call" | custom-call | tf_op jit(solution)/shard_map/project_back/pallas_call | solution.py:91
  306.1 7.4 %collective-permute-done.11.refs_2_ = bf16[128,1024]{1,0:T(8,128)(2,1)S(1)} collective-permute-done((bf16[128,1024]{1,0:T(8,128)(2,1)}, bf16[128,1024]{1,0:T(8,128)(2,1)S(1)}, u32[]{:S(2)}, u32[]{:S(2)}) %collective-permute-start.11) | collective-permute-done | bytes 262176 | tf_op jit(solution)/shard_map/ppermute | solution.py:1250
  313.5 11.1 %ffn_back.1 = (f32[128,1024]{1,0:T(8,128)}, bf16[128,1024]{1,0:T(8,128)(2,1)}, bf16[8,8,176,512]{3,2,1,0:T(8,128)(2,1)}, f32[1,1024]{1,0:T(1,128)S(1)}) custom-call(f32[128,1024]{1,0:T(8,128)} %copy-done.5, bf16[128,1024]{1,0:T(8,128)(2,1)} %get-tuple-element.149.refs_1_, ...), custom_call_target="tpu_custom_call", output_to_operand_aliasing={{2}: (9, {})} | custom-call | tf_op jit(solution)/shard_map/ffn_back/pallas_call | solution.py:291
  326.5 6.5 %collective-permute-done.12.other_ref = bf16[128,1024]{1,0:T(8,128)(2,1)S(1)} collective-permute-done((bf16[128,1024]{1,0:T(8,128)(2,1)S(1)}, bf16[128,1024]{1,0:T(8,128)(2,1)S(1)}, u32[]{:S(2)}, u32[]{:S(2)}) %collective-permute-start.12) | collective-permute-done | bytes 262176 | tf_op jit(solution)/shard_map/ppermute | solution.py:1250
  333.0 4.6 merge_back.3
  337.6 7.5 %all-to-all-start.8 = ((bf16[64,8,384]{2,1,0:T(8,128)(2,1)}), bf16[64,8,384]{2,1,0:T(8,128)(2,1)S(1)}, u32[]{:S(2)}, u32[]{:S(2)}) async-start(bf16[64,8,384]{2,1,0:T(8,128)(2,1)} %bitcast.154), calls=%async_computation.10 | async-start | bytes 786432 | tf_op jit(solution)/shard_map/all_to_all | solution.py:1259
  345.1 3.1 collective-permute-start.13
  353.7 5.9 %all-to-all-done.8 = bf16[64,8,384]{2,1,0:T(8,128)(2,1)S(1)} async-done(((bf16[64,8,384]{2,1,0:T(8,128)(2,1)}), bf16[64,8,384]{2,1,0:T(8,128)(2,1)S(1)}, u32[]{:S(2)}, u32[]{:S(2)}) %all-to-all-start.8) | async-done | bytes 393248 | tf_op jit(solution)/shard_map/all_to_all | solution.py:1259
  359.6 5.3 %attend_back.3 = bf16[512,640]{1,0:T(8,128)(2,1)} custom-call(bf16[512,384]{1,0:T(8,128)(2,1)S(1)} %bitcast.104, bf16[1088,256]{1,0:T(8,128)(2,1)} %get-tuple-element.163.sorted_ref, s32[4,512]{1,0:T(4,128)} %get-tuple-element.110.place_row_ref, f32[1,512]{1,0:T(1,128)S(1)} %get-tuple-element.196.gain_ref), custom_call_target="tpu_custom_call" | custom-call | tf_op jit(solution)/shard_map/attend_back/pallas_call | solution.py:91
  364.9 4.9 %all-to-all-start.9 = ((bf16[64,8,640]{2,1,0:T(8,128)(2,1)}), bf16[64,8,640]{2,1,0:T(8,128)(2,1)S(1)}, u32[]{:S(2)}, u32[]{:S(2)}) async-start(bf16[64,8,640]{2,1,0:T(8,128)(2,1)} %bitcast.146), calls=%async_computation.11 | async-start | bytes 1310720 | tf_op jit(solution)/shard_map/all_to_all | solution.py:1259
  370.9 17.2 %all-to-all-done.9 = bf16[64,8,640]{2,1,0:T(8,128)(2,1)S(1)} async-done(((bf16[64,8,640]{2,1,0:T(8,128)(2,1)}), bf16[64,8,640]{2,1,0:T(8,128)(2,1)S(1)}, u32[]{:S(2)}, u32[]{:S(2)}) %all-to-all-start.9) | async-done | bytes 655392 | tf_op jit(solution)/shard_map/all_to_all | solution.py:1259
  388.1 3.8 project_back.3
  396.7 4.6 all-to-all-start.11
  406.6 18.3 %collective-permute-done.14.other_ref = bf16[128,1024]{1,0:T(8,128)(2,1)S(1)} collective-permute-done((bf16[128,1024]{1,0:T(8,128)(2,1)S(1)}, bf16[128,1024]{1,0:T(8,128)(2,1)S(1)}, u32[]{:S(2)}, u32[]{:S(2)}) %collective-permute-start.14) | collective-permute-done | bytes 262176 | tf_op jit(solution)/shard_map/ppermute | solution.py:1250
  426.2 5.7 %all-to-all-start.10 = ((bf16[8,128,512]{2,1,0:T(8,128)(2,1)}), bf16[8,128,512]{2,1,0:T(8,128)(2,1)S(1)}, u32[]{:S(2)}, u32[]{:S(2)}) async-start(bf16[8,128,512]{2,1,0:T(8,128)(2,1)} %slice.142), calls=%async_computation.13 | async-start | bytes 2097152 | tf_op jit(solution)/shard_map/all_to_all | solution.py:1289
  432.7 3.2 collective-permute-start.20
  438.6 8.0 %collective-permute-done.20 = bf16[48,512]{1,0:T(8,128)(2,1)S(1)} collective-permute-done((bf16[48,512]{1,0:T(8,128)(2,1)S(1)}, bf16[48,512]{1,0:T(8,128)(2,1)S(1)}, u32[]{:S(2)}, u32[]{:S(2)}) %collective-permute-start.20) | collective-permute-done | bytes 49184 | tf_op jit(solution)/shard_map/ppermute | solution.py:1305
  449.5 11.4 %all-to-all-start.12 = ((bf16[64,16,512]{2,1,0:T(8,128)(2,1)}), bf16[64,16,512]{2,1,0:T(8,128)(2,1)S(1)}, u32[]{:S(2)}, u32[]{:S(2)}) async-start(bf16[64,16,512]{2,1,0:T(8,128)(2,1)} %bitcast.145), calls=%async_computation.16 | async-start | bytes 2097152 | tf_op jit(solution)/shard_map/all_to_all | solution.py:1259
  462.8 16.9 %all-to-all-done.12 = bf16[64,16,512]{2,1,0:T(8,128)(2,1)S(1)} async-done(((bf16[64,16,512]{2,1,0:T(8,128)(2,1)}), bf16[64,16,512]{2,1,0:T(8,128)(2,1)S(1)}, u32[]{:S(2)}, u32[]{:S(2)}) %all-to-all-start.12) | async-done | bytes 1048608 | tf_op jit(solution)/shard_map/all_to_all | solution.py:1259
  479.6 5.3 %slots_update.1 = (f32[5,128,512]{2,1,0:T(8,128)}, f32[5,128,512]{2,1,0:T(8,128)}, f32[5,128,512]{2,1,0:T(8,128)}, f32[5,128,512]{2,1,0:T(8,128)}, f32[2,2,512]{...) custom-call(s32[1]{0:T(128)} %bitcast.half_ref.refs_0_, ...), custom_call_target="tpu_custom_call" | custom-call | tf_op jit(solution)/shard_map/slots_update/pallas_call | solution.py:291
  (202 shorter events, 67.2 us)
Async XLA Ops:
  7.2 22.9 %copy-start = (s32[2,2,8192]{2,1,0:T(2,128)S(1)}, s32[2,2,8192]{2,1,0:T(2,128)}, u32[]{:S(2)}) copy-start(s32[2,2,8192]{2,1,0:T(2,128)} %param.17) | copy-start | bytes 393220
  7.9 25.1 %collective-permute-start.1 = (f32[4,512]{1,0:T(4,128)S(1)}, f32[4,512]{1,0:T(4,128)S(1)}, u32[]{:S(2)}, u32[]{:S(2)}) collective-permute-start(f32[4,512]{1,0:T(4,128)S(1)} %reshape.447.refs_2_), channel_id=1, source_target_pairs={{0,1},{1,0},{2,3},{3,2},{4,5},{5,4},{6,7},{7,6},{8,9},{9,8},{10,11... | collective-permute-start | bytes 24584 | tf_op jit(solution)/shard_map/ppermute | solution.py:1250
  10.1 22.9 %collective-permute-start = (bf16[128,512]{1,0:T(8,128)(2,1)}, bf16[128,512]{1,0:T(8,128)(2,1)S(1)}, u32[]{:S(2)}, u32[]{:S(2)}) collective-permute-start(bf16[128,512]{1,0:T(8,128)(2,1)} %refs_0_.1), channel_id=1, source_target_pairs={{0,1},{1,0},{2,3},{3,2},{4,5},{5,4},{6,7},{7,6},{8,9},{9,8},{10,11... | collective-permute-start | bytes 393224 | tf_op jit(solution)/shard_map/ppermute | solution.py:1250
  14.3 13.7 %copy-start.36 = (s32[16]{0:T(128)S(1)}, s32[16]{0:T(128)}, u32[]{:S(2)}) copy-start(s32[16]{0:T(128)} %constant.78) | copy-start | bytes 196
  14.3 36.4 %all-to-all-start = ((bf16[64,24,512]{2,1,0:T(8,128)(2,1)}), bf16[64,24,512]{2,1,0:T(8,128)(2,1)S(1)}, u32[]{:S(2)}, u32[]{:S(2)}) async-start(bf16[64,24,512]{2,1,0:T(8,128)(2,1)} %bitcast.144), calls=%async_computation | async-start | bytes 3145728 | tf_op jit(solution)/shard_map/all_to_all | solution.py:1259
  26.7 113.0 %all-gather.3.cloned.1.call-start = ((), (), s32[]{:S(2)}) async-start(), calls=%async_computation.17 | async-start | bytes 12976128 | tf_op jit(solution)/shard_map/all_gather | solution.py:1320
  53.1 33.7 %copy-start.24 = (s32[2,128]{1,0:T(2,128)S(1)}, s32[2,128]{1,0:T(2,128)}, u32[]{:S(2)}) copy-start(s32[2,128]{1,0:T(2,128)} %get-tuple-element.108.refs_18_.refs_6_) | copy-start | bytes 3076
  53.1 164.4 %all-gather.5.cloned.1.call-start = ((), (), s32[]{:S(2)}) async-start(), calls=%async_computation.18 | async-start | bytes 8650752 | tf_op jit(solution)/shard_map/all_gather | solution.py:1320
  53.8 28.1 %all-to-all-start.1 = ((bf16[32,32,512]{2,1,0:T(8,128)(2,1)}), bf16[32,32,512]{2,1,0:T(8,128)(2,1)S(1)}, u32[]{:S(2)}, u32[]{:S(2)}) async-start(bf16[32,32,512]{2,1,0:T(8,128)(2,1)} %get-tuple-element.115), calls=%async_computation.1 | async-start | bytes 2097152 | tf_op jit(solution)/shard_map/all_to_all | solution.py:1310
  58.3 9.1 %collective-permute-start.2 = (bf16[128,512]{1,0:T(8,128)(2,1)S(1)}, bf16[128,512]{1,0:T(8,128)(2,1)S(1)}, u32[]{:S(2)}, u32[]{:S(2)}) collective-permute-start(bf16[128,512]{1,0:T(8,128)(2,1)S(1)} %copy-done.12), channel_id=1, source_target_pairs={{0,1},{1,0},{2,3},{3,2},{4,5},{5,4},{6,7},{7,6},{8,9},{9,8},{10,11... | collective-permute-start | bytes 393224 | tf_op jit(solution)/shard_map/ppermute | solution.py:1250
  58.7 14.3 %collective-permute-start.3 = (bf16[128,512]{1,0:T(8,128)(2,1)S(1)}, bf16[128,512]{1,0:T(8,128)(2,1)S(1)}, u32[]{:S(2)}, u32[]{:S(2)}) collective-permute-start(bf16[128,512]{1,0:T(8,128)(2,1)S(1)} %copy-done.13), channel_id=1, source_target_pairs={{0,1},{1,0},{2,3},{3,2},{4,5},{5,4},{6,7},{7,6},{8,9},{9,8},{10,11... | collective-permute-start | bytes 393224 | tf_op jit(solution)/shard_map/ppermute | solution.py:1250
  59.8 18.8 %collective-permute-start.4 = (bf16[128,512]{1,0:T(8,128)(2,1)S(1)}, bf16[128,512]{1,0:T(8,128)(2,1)S(1)}, u32[]{:S(2)}, u32[]{:S(2)}) collective-permute-start(bf16[128,512]{1,0:T(8,128)(2,1)S(1)} %copy-done.14), channel_id=1, source_target_pairs={{0,1},{1,0},{2,3},{3,2},{4,5},{5,4},{6,7},{7,6},{8,9},{9,8},{10,11... | collective-permute-start | bytes 393224 | tf_op jit(solution)/shard_map/ppermute | solution.py:1250
  81.9 4.9 collective-permute-start.5
  85.1 79.8 %copy-start.20 = (f32[1,1024]{1,0:T(1,128)}, f32[1,1024]{1,0:T(1,128)S(1)}, u32[]{:S(2)}) copy-start(f32[1,1024]{1,0:T(1,128)S(1)} %get-tuple-element.191.refs_3_.refs_4_) | copy-start | bytes 12292
  90.0 27.6 %all-to-all-start.2 = ((bf16[64,8,640]{2,1,0:T(8,128)(2,1)}), bf16[64,8,640]{2,1,0:T(8,128)(2,1)S(1)}, u32[]{:S(2)}, u32[]{:S(2)}) async-start(bf16[64,8,640]{2,1,0:T(8,128)(2,1)} %bitcast.151), calls=%async_computation.2 | async-start | bytes 1310720 | tf_op jit(solution)/shard_map/all_to_all | solution.py:1259
  96.3 203.2 %reduce-scatter.5.cloned.1.call-start = ((), (), s32[]{:S(2)}) async-start(), calls=%async_computation.19 | async-start | bytes 9437184 | tf_op jit(solution)/shard_map/reduce_scatter | solution.py:1283
  142.6 7.8 %collective-permute-start.6 = (bf16[128,1024]{1,0:T(8,128)(2,1)}, bf16[128,1024]{1,0:T(8,128)(2,1)S(1)}, u32[]{:S(2)}, u32[]{:S(2)}) collective-permute-start(bf16[128,1024]{1,0:T(8,128)(2,1)} %get-tuple-element.123.refs_1_), channel_id=1, source_target_pairs={{0,1},{1,0},{2,3},{3,2},{4,5},{5,4},{6,7},{7,6},{8,9},{9,8},{10,11... | collective-permute-start | bytes 786440 | tf_op jit(solution)/shard_map/ppermute | solution.py:1250
  150.4 14.5 %copy-start.25 = (s32[2,128]{1,0:T(2,128)S(1)}, s32[2,128]{1,0:T(2,128)}, u32[]{:S(2)}) copy-start(s32[2,128]{1,0:T(2,128)} %get-tuple-element.111.refs_12_.refs_6_) | copy-start | bytes 3076
  157.8 7.0 %collective-permute-start.7 = (bf16[128,1024]{1,0:T(8,128)(2,1)}, bf16[128,1024]{1,0:T(8,128)(2,1)S(1)}, u32[]{:S(2)}, u32[]{:S(2)}) collective-permute-start(bf16[128,1024]{1,0:T(8,128)(2,1)} %get-tuple-element.126.refs_1_), channel_id=1, source_target_pairs={{0,1},{1,0},{2,3},{3,2},{4,5},{5,4},{6,7},{7,6},{8,9},{9,8},{10,11... | collective-permute-start | bytes 786440 | tf_op jit(solution)/shard_map/ppermute | solution.py:1250
  216.6 7.7 %collective-permute-start.8 = (bf16[128,1024]{1,0:T(8,128)(2,1)}, bf16[128,1024]{1,0:T(8,128)(2,1)S(1)}, u32[]{:S(2)}, u32[]{:S(2)}) collective-permute-start(bf16[128,1024]{1,0:T(8,128)(2,1)} %get-tuple-element.129.refs_1_), channel_id=1, source_target_pairs={{0,1},{1,0},{2,3},{3,2},{4,5},{5,4},{6,7},{7,6},{8,9},{9,8},{10,11... | collective-permute-start | bytes 786440 | tf_op jit(solution)/shard_map/ppermute | solution.py:1250
  237.9 6.6 %collective-permute-start.10 = (bf16[128,1024]{1,0:T(8,128)(2,1)S(1)}, bf16[128,1024]{1,0:T(8,128)(2,1)S(1)}, u32[]{:S(2)}, u32[]{:S(2)}) collective-permute-start(bf16[128,1024]{1,0:T(8,128)(2,1)S(1)} %copy-done.29), channel_id=1, source_target_pairs={{0,1},{1,0},{2,3},{3,2},{4,5},{5,4},{6,7},{7,6},{8,9},{9,8},{10,11... | collective-permute-start | bytes 786440 | tf_op jit(solution)/shard_map/ppermute | solution.py:1250
  238.7 18.2 %collective-permute-start.9 = (bf16[128,1024]{1,0:T(8,128)(2,1)S(1)}, bf16[128,1024]{1,0:T(8,128)(2,1)S(1)}, u32[]{:S(2)}, u32[]{:S(2)}) collective-permute-start(bf16[128,1024]{1,0:T(8,128)(2,1)S(1)} %copy-done.33), channel_id=1, source_target_pairs={{0,1},{1,0},{2,3},{3,2},{4,5},{5,4},{6,7},{7,6},{8,9},{9,8},{10,11... | collective-permute-start | bytes 786440 | tf_op jit(solution)/shard_map/ppermute | solution.py:1250
  248.6 22.8 %all-to-all-start.6 = ((bf16[64,8,384]{2,1,0:T(8,128)(2,1)}), bf16[64,8,384]{2,1,0:T(8,128)(2,1)S(1)}, u32[]{:S(2)}, u32[]{:S(2)}) async-start(bf16[64,8,384]{2,1,0:T(8,128)(2,1)} %bitcast.153), calls=%async_computation.6 | async-start | bytes 786432 | tf_op jit(solution)/shard_map/all_to_all | solution.py:1259
  256.7 76.3 %reduce-scatter.7.cloned.1.call-start = ((), (), s32[]{:S(2)}) async-start(), calls=%async_computation.20 | async-start | bytes 1310720 | tf_op jit(solution)/shard_map/reduce_scatter | solution.py:1296
  299.5 103.1 %reduce-scatter.9.cloned.1.call-start = ((), (), s32[]{:S(2)}) async-start(), calls=%async_computation.21 | async-start | bytes 12976128 | tf_op jit(solution)/shard_map/reduce_scatter | solution.py:1283
  305.3 8.3 %collective-permute-start.11 = (bf16[128,1024]{1,0:T(8,128)(2,1)}, bf16[128,1024]{1,0:T(8,128)(2,1)S(1)}, u32[]{:S(2)}, u32[]{:S(2)}) collective-permute-start(bf16[128,1024]{1,0:T(8,128)(2,1)} %get-tuple-element.149.refs_1_), channel_id=1, source_target_pairs={{0,1},{1,0},{2,3},{3,2},{4,5},{5,4},{6,7},{7,6},{8,9},{9,8},{10,11... | collective-permute-start | bytes 786440 | tf_op jit(solution)/shard_map/ppermute | solution.py:1250
  325.6 7.3 %collective-permute-start.12 = (bf16[128,1024]{1,0:T(8,128)(2,1)S(1)}, bf16[128,1024]{1,0:T(8,128)(2,1)S(1)}, u32[]{:S(2)}, u32[]{:S(2)}) collective-permute-start(bf16[128,1024]{1,0:T(8,128)(2,1)S(1)} %copy-done.28), channel_id=1, source_target_pairs={{0,1},{1,0},{2,3},{3,2},{4,5},{5,4},{6,7},{7,6},{8,9},{9,8},{10,11... | collective-permute-start | bytes 786440 | tf_op jit(solution)/shard_map/ppermute | solution.py:1250
  337.6 22.0 %all-to-all-start.8 = ((bf16[64,8,384]{2,1,0:T(8,128)(2,1)}), bf16[64,8,384]{2,1,0:T(8,128)(2,1)S(1)}, u32[]{:S(2)}, u32[]{:S(2)}) async-start(bf16[64,8,384]{2,1,0:T(8,128)(2,1)} %bitcast.154), calls=%async_computation.10 | async-start | bytes 786432 | tf_op jit(solution)/shard_map/all_to_all | solution.py:1259
  345.1 8.6 %collective-permute-start.13 = (bf16[128,512]{1,0:T(8,128)(2,1)S(1)}, bf16[128,512]{1,0:T(8,128)(2,1)S(1)}, u32[]{:S(2)}, u32[]{:S(2)}) collective-permute-start(bf16[128,512]{1,0:T(8,128)(2,1)S(1)} %dynamic-slice_bitcast_fusion), channel_id=1, source_target_pairs={{0,64},{2,66},{4,68},{6,70},{8,72},{10,74},{12,76},{14,78},{16,80}... | collective-permute-start | bytes 393224 | tf_op jit(solution)/shard_map/ppermute | solution.py:1305
  351.1 18.8 %copy-start.27 = (bf16[2,128,512]{2,1,0:T(8,128)(2,1)S(1)}, bf16[2,128,512]{2,1,0:T(8,128)(2,1)}, u32[]{:S(2)}) copy-start(bf16[2,128,512]{2,1,0:T(8,128)(2,1)} %get-tuple-element.169.refs_4_.refs_8_) | copy-start | bytes 786436
  351.1 19.3 %copy-start.30 = (bf16[2,128,512]{2,1,0:T(8,128)(2,1)S(1)}, bf16[2,128,512]{2,1,0:T(8,128)(2,1)}, u32[]{:S(2)}) copy-start(bf16[2,128,512]{2,1,0:T(8,128)(2,1)} %get-tuple-element.167.refs_0_) | copy-start | bytes 786436
  351.1 19.4 %copy-start.34 = (bf16[128,512]{1,0:T(8,128)(2,1)S(1)}, bf16[128,512]{1,0:T(8,128)(2,1)}, u32[]{:S(2)}) copy-start(bf16[128,512]{1,0:T(8,128)(2,1)} %get-tuple-element.168.refs_2_) | copy-start | bytes 393220
  364.9 23.2 %all-to-all-start.9 = ((bf16[64,8,640]{2,1,0:T(8,128)(2,1)}), bf16[64,8,640]{2,1,0:T(8,128)(2,1)S(1)}, u32[]{:S(2)}, u32[]{:S(2)}) async-start(bf16[64,8,640]{2,1,0:T(8,128)(2,1)} %bitcast.146), calls=%async_computation.11 | async-start | bytes 1310720 | tf_op jit(solution)/shard_map/all_to_all | solution.py:1259
  369.9 22.6 %collective-permute-start.17 = (bf16[2,128,512]{2,1,0:T(8,128)(2,1)S(1)}, bf16[2,128,512]{2,1,0:T(8,128)(2,1)S(1)}, u32[]{:S(2)}, u32[]{:S(2)}) collective-permute-start(bf16[2,128,512]{2,1,0:T(8,128)(2,1)S(1)} %copy-done.27), channel_id=1, source_target_pairs={{0,2},{2,0},{4,6},{6,4},{8,10},{10,8},{12,14},{14,12},{16,18},{18,... | collective-permute-start | bytes 786440 | tf_op jit(solution)/shard_map/ppermute | solution.py:1254
  370.4 22.1 %collective-permute-start.15 = (bf16[2,128,512]{2,1,0:T(8,128)(2,1)S(1)}, bf16[2,128,512]{2,1,0:T(8,128)(2,1)S(1)}, u32[]{:S(2)}, u32[]{:S(2)}) collective-permute-start(bf16[2,128,512]{2,1,0:T(8,128)(2,1)S(1)} %copy-done.30), channel_id=1, source_target_pairs={{0,2},{2,0},{4,6},{6,4},{8,10},{10,8},{12,14},{14,12},{16,18},{18,... | collective-permute-start | bytes 786440 | tf_op jit(solution)/shard_map/ppermute | solution.py:1254
  370.5 22.0 %collective-permute-start.16 = (bf16[128,512]{1,0:T(8,128)(2,1)S(1)}, bf16[128,512]{1,0:T(8,128)(2,1)S(1)}, u32[]{:S(2)}, u32[]{:S(2)}) collective-permute-start(bf16[128,512]{1,0:T(8,128)(2,1)S(1)} %copy-done.34), channel_id=1, source_target_pairs={{0,2},{2,0},{4,6},{6,4},{8,10},{10,8},{12,14},{14,12},{16,18},{18,... | collective-permute-start | bytes 393224 | tf_op jit(solution)/shard_map/ppermute | solution.py:1254
  392.0 1.6 collective-permute-start.18
  392.0 1.7 collective-permute-start.19
  396.7 29.5 %all-to-all-start.11 = ((bf16[32,48,512]{2,1,0:T(8,128)(2,1)}), bf16[32,48,512]{2,1,0:T(8,128)(2,1)S(1)}, u32[]{:S(2)}, u32[]{:S(2)}) async-start(bf16[32,48,512]{2,1,0:T(8,128)(2,1)} %attn_grad.1), calls=%async_computation.14 | async-start | bytes 3145728 | tf_op jit(solution)/shard_map/all_to_all | solution.py:1310
  401.3 30.5 %reduce-scatter.11.cloned.1.call-start = ((), (), s32[]{:S(2)}) async-start(), calls=%async_computation.22 | async-start | bytes 491520 | tf_op jit(solution)/shard_map/reduce_scatter | solution.py:1296
  401.4 23.5 %collective-permute-start.14 = (bf16[128,1024]{1,0:T(8,128)(2,1)S(1)}, bf16[128,1024]{1,0:T(8,128)(2,1)S(1)}, u32[]{:S(2)}, u32[]{:S(2)}) collective-permute-start(bf16[128,1024]{1,0:T(8,128)(2,1)S(1)} %copy-done.32), channel_id=1, source_target_pairs={{0,1},{1,0},{2,3},{3,2},{4,5},{5,4},{6,7},{7,6},{8,9},{9,8},{10,11... | collective-permute-start | bytes 786440 | tf_op jit(solution)/shard_map/ppermute | solution.py:1250
  426.2 21.1 %all-to-all-start.10 = ((bf16[8,128,512]{2,1,0:T(8,128)(2,1)}), bf16[8,128,512]{2,1,0:T(8,128)(2,1)S(1)}, u32[]{:S(2)}, u32[]{:S(2)}) async-start(bf16[8,128,512]{2,1,0:T(8,128)(2,1)} %slice.142), calls=%async_computation.13 | async-start | bytes 2097152 | tf_op jit(solution)/shard_map/all_to_all | solution.py:1289
  432.7 13.9 %collective-permute-start.20 = (bf16[48,512]{1,0:T(8,128)(2,1)S(1)}, bf16[48,512]{1,0:T(8,128)(2,1)S(1)}, u32[]{:S(2)}, u32[]{:S(2)}) collective-permute-start(bf16[48,512]{1,0:T(8,128)(2,1)S(1)} %dynamic-slice_bitcast_fusion.1), channel_id=1, source_target_pairs={{0,64},{2,66},{4,68},{6,70},{8,72},{10,74},{12,76},{14,78},{16,80}... | collective-permute-start | bytes 147464 | tf_op jit(solution)/shard_map/ppermute | solution.py:1305
  449.4 30.2 %copy-start.19 = (s32[176]{0:T(256)S(1)}, s32[176]{0:T(256)}, u32[]{:S(2)}) copy-start(s32[176]{0:T(256)} %param.18) | copy-start | bytes 2116
  449.4 30.2 %copy-start.21 = (f32[2,2,512]{2,1,0:T(2,128)S(1)}, f32[2,2,512]{2,1,0:T(2,128)}, u32[]{:S(2)}) copy-start(f32[2,2,512]{2,1,0:T(2,128)} %refs_8_.1) | copy-start | bytes 24580
  449.4 30.2 %copy-start.22 = (f32[2,2,512]{2,1,0:T(2,128)S(1)}, f32[2,2,512]{2,1,0:T(2,128)}, u32[]{:S(2)}) copy-start(f32[2,2,512]{2,1,0:T(2,128)} %refs_9_.1) | copy-start | bytes 24580
  449.4 30.2 %copy-start.23 = (f32[2,2,512]{2,1,0:T(2,128)S(1)}, f32[2,2,512]{2,1,0:T(2,128)}, u32[]{:S(2)}) copy-start(f32[2,2,512]{2,1,0:T(2,128)} %refs_10_.1) | copy-start | bytes 24580
  449.5 30.2 %all-to-all-start.12 = ((bf16[64,16,512]{2,1,0:T(8,128)(2,1)}), bf16[64,16,512]{2,1,0:T(8,128)(2,1)S(1)}, u32[]{:S(2)}, u32[]{:S(2)}) async-start(bf16[64,16,512]{2,1,0:T(8,128)(2,1)} %bitcast.145), calls=%async_computation.16 | async-start | bytes 2097152 | tf_op jit(solution)/shard_map/all_to_all | solution.py:1259
  (25 other events, 139.4 us)
Sparse Core Ops, SparseCore 0:
  53.2 74.2 all-gather.2
  130.3 57.8 all-gather.4
  237.1 59.1 reduce-scatter.4
  299.6 21.4 reduce-scatter.6
  324.9 77.6 reduce-scatter.8
  405.5 23.1 reduce-scatter.10

commit v5 on v4

--- a/solution.py
+++ b/solution.py
@@ -33,6 +33,7 @@
 LAYER_ROWS = 176
 ATTN_ROWS = 48
 FFN_ROWS = 128
+SPLIT = 96
 EARLY_ROWS = 384
 
 MASK_FILL = -1000000000.0
@@ -82,6 +83,16 @@
 ):
     specs = specs or {}
     out_specs = out_specs or {}
+    gains = {i: a.index for i, a in enumerate(args) if isinstance(a, Gain)}
+    args = [a.rows if isinstance(a, Gain) else a for a in args]
+    if gains:
+        inner_kernel_body = kernel
+
+        def kernel(*refs):
+            inner_kernel_body(
+                *[GainRow(r, gains[i]) if i in gains else r for i, r in enumerate(refs)]
+            )
+
     def whole(shape):
         zeros = (0,) * len(shape)
         return pl.BlockSpec(shape, lambda *_: zeros)
@@ -134,8 +145,24 @@
     return jnp.where(mine, first, second), jnp.where(mine, second, first)
 
 
+class Gain:
+    def __init__(self, rows, index):
+        self.rows, self.index = rows, index
+
+
+class GainRow:
+    def __init__(self, ref, index):
+        self.ref, self.index = ref, index
+
+    def __getitem__(self, index):
+        return self.ref[self.index : self.index + 1, :]
+
+
 class Far:
     def __init__(self, array):
+        self.row = None
+        if isinstance(array, Gain):
+            array, self.row = array.rows, array.index
         self.operands = [in_hbm(array)]
         self.scratch = [pltpu.VMEM(array.shape, array.dtype), pltpu.SemaphoreType.DMA((1,))]
 
@@ -271,7 +298,9 @@
                 mine = [ins.pop(0) for _ in a.operands]
                 if a.scratch:
                     buffer, sems = temps.pop(0), temps.pop(0)
-                    seen.append(Fetched(a.fetch(mine, buffer, sems), buffer))
+                    got = Fetched(a.fetch(mine, buffer, sems), buffer)
+                    row = getattr(a, "row", None)
+                    seen.append(got if row is None else GainRow(got, row))
                 else:
                     seen.append(mine[0])
             else:
@@ -478,8 +507,9 @@
 
 
 def route_back_kernel(code_ref, *refs):
-    *parts, gain_a, gain_b, gain_c, out_ref = refs
-    rows = jnp.concatenate([p[...] for p in parts], 0)
+    first, last_rows, attn, ffn, gain_a, gain_b, gain_c, out_ref = refs
+    at = FFN_ROWS - SPLIT
+    rows = jnp.concatenate([first[...], last_rows[:at], attn[...], ffn[...], last_rows[at:]], 0)
     place = iota((NW * PACK, 1), 0)
     out = dot(hot(place == code_ref[...]), rows, 1, 0)
     gains = jnp.concatenate(
@@ -1130,14 +1160,9 @@
     )[0]
 
 
-def project_back_kernel(count, grads, core_ref, moved_ref, rank_col_ref, *refs):
+def project_back_kernel(count, core_ref, moved_ref, rank_col_ref, *refs):
     q_refs, v_refs = refs[:count], refs[count : 2 * count]
-    refs = refs[2 * count :]
-    if grads:
-        back_ref, merged_ref, hn_ref, *refs = refs
-        send_out, grad_out, gain_out, grad_ref, sems = refs
-    else:
-        send_out, dq_out, dv_out, gain_out = refs
+    send_out, dq_out, dv_out, gain_out = refs[2 * count :]
     gain_out[...] = dot(
         hot(iota((8, 1), 0) == (iota((1, ROWS), 1) & 7)), moved_ref[:, 4 * DH :], 1, 0
     )
@@ -1155,49 +1180,50 @@
     d_v = jnp.concatenate([total[:, h * 2 * DH + DH : (h + 1) * 2 * DH] for h in range(HN)], 1)
     d_q = (d_q + lent_q).astype(BF16)
     d_v = (d_v + lent_v).astype(BF16)
-    if grads:
-        for c0 in range(2):
-            for i, (left, right) in enumerate(
-                ((back_ref, merged_ref[...]), (hn_ref, d_q), (hn_ref, d_v))
-            ):
-                put_pieces(grad_ref, c0, i * 16, 16, dot(left[c0], right, 0, 0).astype(BF16))
-        sending = pltpu.make_async_copy(
-            grad_ref, grad_out.at[:, :, pl.ds(FFN_ROWS, ATTN_ROWS), :], sems.at[0]
-        )
-        sending.start()
-    else:
-        dq_out[...] = d_q
-        dv_out[...] = d_v
+    dq_out[...] = d_q
+    dv_out[...] = d_v
     core = core_ref[0]
     from_q = out_of(core, d_q, q_refs)
     from_v = out_of(core, d_v, v_refs)
     put_halves([a + b for a, b in zip(from_q, from_v)], send_out)
-    if grads:
-        sending.wait()
-
-
-def project_back(core, moved, rank_col, wq, wv, lefts=None):
-    args, specs = unpacked([core, moved, rank_col, wq, wv, *(lefts or ())], 1)
-    out_specs = {}
-    if lefts:
-        rows = FFN_ROWS + ATTN_ROWS
-        outs = [kept((2 * QUAD, 8, rows, PART), BF16)]
-        out_specs = {1: pl.BlockSpec(memory_space=pl.ANY)}
-        temps = [pltpu.VMEM((2 * QUAD, 8, ATTN_ROWS, PART), BF16), pltpu.SemaphoreType.DMA((1,))]
-    else:
-        outs = [kept((TOK, PART), BF16)] * 2
-        temps = []
+
+
+def project_back(core, moved, rank_col, wq, wv):
+    args, specs = unpacked([core, moved, rank_col, wq, wv], 1)
     return call(
-        functools.partial(project_back_kernel, len(wq.parts()), lefts is not None),
+        functools.partial(project_back_kernel, len(wq.parts())),
         args,
-        [kept((TOK, D), BF16), *outs, sds((8, DH), F32)],
+        [kept((TOK, D), BF16), kept((TOK, PART), BF16), kept((TOK, PART), BF16), sds((8, DH), F32)],
         specs=specs,
-        out_specs=out_specs,
-        scratch=temps,
         in_place=range(1, len(args) - 1),
         prefetch=1,
         name="project_back",
     )
+
+
+def attn_part_kernel(back_ref, merged_ref, hn_ref, dq_ref, dv_ref, grad_out, buffer, sems):
+    for c0 in range(2):
+        for i, (left, right) in enumerate(
+            ((back_ref, merged_ref), (hn_ref, dq_ref), (hn_ref, dv_ref))
+        ):
+            put_pieces(buffer, c0, i * 16, 16, dot(left[c0], right[...], 0, 0).astype(BF16))
+    copy = pltpu.make_async_copy(
+        buffer, grad_out.at[:, :, pl.ds(FFN_ROWS, ATTN_ROWS), :], sems.at[0]
+    )
+    copy.start()
+    copy.wait()
+
+
+def attn_part_of(back, merged, hn, dq, dv):
+    return call(
+        attn_part_kernel,
+        (back, merged, hn, dq, dv),
+        [kept((2 * QUAD, 8, FFN_ROWS + ATTN_ROWS, PART), BF16)],
+        out_specs={0: pl.BlockSpec(memory_space=pl.ANY)},
+        scratch=[pltpu.VMEM((2 * QUAD, 8, ATTN_ROWS, PART), BF16), pltpu.SemaphoreType.DMA((1,))],
+        in_place=range(5),
+        name="attn_part",
+    )[0]
 
 
 def last_kernel(g_ref, own_ref, other_ref, x_ref, gain_ref, g_out, dgain_out):
@@ -1371,14 +1397,13 @@
     plans = plan((me & 7).reshape(1), mine, by_source.reshape(LAYERS, NW, TOK))
     rank_rows, rank_cols, place_rows = [plans[i::3] for i in range(3)]
     flat_gains = gains.reshape(LAYERS * 2, PART)
-    x_two, gain_rows = inner(
-        half, [(x_second, swap_narrow(x_second)), (flat_gains, swap_narrow(flat_gains))], "inner_a"
-    )
-    moved = after(moved, code_col, code_row, plans, x_two, gain_rows)
+    moved = after(moved, code_col, code_row, plans)
     first_rows, early_rows, late_rows = pick(code_col, moved)
-    x_first, grad_first, grad_second = after((x_first, grad_first, grad_second), x_two)
-    pairs = [(a, swap_narrow(a)) for a in (x_first, grad_first, grad_second)]
-    first_w = with_core(after(to_same_core(first_rows), pairs))
+    streams = (x_second, flat_gains, x_first, grad_first, grad_second)
+    pairs = [(a, swap_narrow(a)) for a in after(streams, moved)]
+    x_two, gain_rows = inner(half, pairs[:2], "inner_a")
+    pairs = pairs[2:]
+    first_w = with_core(after(to_same_core(first_rows), x_two, gain_rows, pairs))
     early = gathered(early_rows)
     late = gathered(late_rows)
     x_one, g_one, g_two = inner(half, pairs, "inner_b")
@@ -1387,7 +1412,7 @@
         [Weight(8, early), Weight(0, *first_w), Weight(1, *first_w)],
         [Weight(9, early), Weight(10, early), Weight(11, early)],
     ]
-    gain = [[gain_rows[2 * l + i].reshape(1, D) for i in range(2)] for l in range(LAYERS)]
+    gain = [[Gain(gain_rows, 2 * l + i) for i in range(2)] for l in range(LAYERS)]
 
     saved = []
     pending = None
@@ -1440,27 +1465,25 @@
         moved = moved_rows(send)
         if l > 0:
             moved = after(moved, ffn_part)
+        send, dq, dv, gain_sum = project_back(core, moved, rank_cols[l], w_qk, w_value)
+        other = swap_narrow(send)
         if l > 0:
-            send, attn_part, gain_sum = project_back(
-                core, moved, rank_cols[l], w_qk, w_value, (back, merged, hn)
-            )
+            attn_part = attn_part_of(back, merged, hn, dq, dv)
+            other = after(other, attn_part)
             ffn_rows = summed_along_z(after(ffn_part, moved))
         else:
-            send, dq, dv, gain_sum = project_back(core, moved, rank_cols[l], w_qk, w_value)
             hn2 = with_core(hn)
             pairs = [(with_core(back), with_core(merged)), (hn2, with_core(dq)), (hn2, with_core(dv))]
             attn_part = attn_grad(core, pairs)
             attn_rows = summed(attn_part)
-        other = swap_narrow(send)
-        if l == 0:
             ffn_part = after(ffn_part, attn_part)
-            last_rows = summed_along_y(summed_along_z(ffn_part[:, FFN_ROWS:]))
-            both_rows = summed_across_x(after(ffn_part[:, :FFN_ROWS], other))
+            last_rows = summed_along_y(summed_along_z(ffn_part[:, SPLIT:]))
+            both_rows = summed_across_x(after(ffn_part[:, :SPLIT], other))
         gain_sums.append(gain_sum[4:].reshape(1, PART))
         pending = (send, other, x_in, gain[l][0], attn_part)
     g_two, dgains[0][0] = last(g_two, *pending[:4])
     dx_second = outer(half, (g_two,), "outer_dx_second")[0]
-    parts = (both_rows, attn_rows, ffn_rows, last_rows)
+    parts = (both_rows, last_rows, attn_rows, ffn_rows)
     back_rows = moved_rows(
         route_back(code_row, parts, (dgains[1][0], dgains[0][1], dgains[0][0]))
     )

time: 502 us -> 497 us (0.990)
    ppermute x2, waiting for transfers between devices: 10.6 us -> 2.39 us  [summed_along_y(): got = lax.ppermute(theirs, 'wide', [(i, i ^ 32) for i in range(NW)])]
    all_to_all x6, starting transfers between devices: 50.5 us -> 56.3 us  [to_all(): lax.all_to_all(values, 'wide', split_axis=0, concat_axis=0, tiled=True)]
    all_to_all x1, waiting for transfers between devices: 0.74 us -> 6.19 us  [summed_across_x(): lax.all_to_all(values, 'wide', split_axis=0, concat_axis=0, tiled=True, a...]
    pallas_call x23 -> x24, Pallas kernels: 74.4 us -> 75.6 us  [call(): pl.pallas_call(kernel, out_shape=outs, grid_spec=pltpu.PrefetchScalarGrid...]
  transfers between devices with their start and end apart: 36 -> 36, of which waited for: 25 -> 21; matrix products, arithmetic and copies ran while one was open for 2% -> 2% of each run, Pallas kernels for 18% -> 18%
where the time goes in v5:
time: 497 us; the launch traced here: 488 us
  waiting for transfers between devices  177 us (36%)
  Pallas kernels  112 us (23%)
  starting transfers between devices  88.4 us (18%)
  blocking collectives  79.8 us (16%)
  between operations  15.3 us (3%)
  local copies, waits for them, and re-layouts  14 us (3%)
    all_to_all x6, waiting for transfers between devices, to_all(): lax.all_to_all(values, 'wide', split_axis=0, concat_axis=0, tiled=True)  86.4 us
    all_to_all x4, blocking collectives, to_all(): lax.all_to_all(values, 'wide', split_axis=0, concat_axis=0, tiled=True)  79.8 us
    pallas_call x24, Pallas kernels, call(): pl.pallas_call(kernel, out_shape=outs, grid_spec=pltpu.PrefetchScalarGrid...  75.6 us
    ppermute x13, waiting for transfers between devices, swap_narrow(): return lax.ppermute(values, 'narrow', [(0, 1), (1, 0)])  72.8 us
    all_to_all x6, starting transfers between devices, to_all(): lax.all_to_all(values, 'wide', split_axis=0, concat_axis=0, tiled=True)  56.3 us
    pallas_call x4, Pallas kernels, run(): pl.pallas_call(body, out_shape=out_shapes, grid_spec=pltpu.PrefetchScalar...  36.5 us
  transfers between devices with their start and end apart: 36, of which 21 were waited for; matrix products, arithmetic and copies ran while one was open for 2% of the time, Pallas kernels for 18%

profile of v5, /device:TPU:1, one launch (start us, length us, event | category | flops | bytes accessed | tf_op | source)
XLA Modules:
  0.0 487.5 jit_solution(9678164457851472756)
XLA Ops:
  7.9 3.4 route_out.1
  11.3 12.6 %all-to-all-start = ((bf16[64,24,512]{2,1,0:T(8,128)(2,1)}), bf16[64,24,512]{2,1,0:T(8,128)(2,1)S(1)}, u32[]{:S(2)}, u32[]{:S(2)}) async-start(bf16[64,24,512]{2,1,0:T(8,128)(2,1)} %bitcast.144), calls=%async_computation | async-start | bytes 3145728 | tf_op jit(solution)/shard_map/all_to_all | solution.py:1285
  30.2 17.6 %all-to-all-done = bf16[64,24,512]{2,1,0:T(8,128)(2,1)S(1)} async-done(((bf16[64,24,512]{2,1,0:T(8,128)(2,1)}), bf16[64,24,512]{2,1,0:T(8,128)(2,1)S(1)}, u32[]{:S(2)}, u32[]{:S(2)}) %all-to-all-start) | async-done | bytes 1572896 | tf_op jit(solution)/shard_map/all_to_all | solution.py:1285
  51.0 4.4 all-to-all-start.1
  58.9 19.9 %collective-permute-done.4.refs_3_ = f32[4,512]{1,0:T(4,128)S(1)} collective-permute-done((f32[4,512]{1,0:T(4,128)S(1)}, f32[4,512]{1,0:T(4,128)S(1)}, u32[]{:S(2)}, u32[]{:S(2)}) %collective-permute-start.4) | collective-permute-done | bytes 8224 | tf_op jit(solution)/shard_map/ppermute | solution.py:1276
  84.7 3.2 project.2
  87.9 10.8 %all-to-all-start.2 = ((bf16[64,8,640]{2,1,0:T(8,128)(2,1)}), bf16[64,8,640]{2,1,0:T(8,128)(2,1)S(1)}, u32[]{:S(2)}, u32[]{:S(2)}) async-start(bf16[64,8,640]{2,1,0:T(8,128)(2,1)} %bitcast.151), calls=%async_computation.2 | async-start | bytes 1310720 | tf_op jit(solution)/shard_map/all_to_all | solution.py:1285
  102.4 17.6 %all-to-all-done.2 = bf16[64,8,640]{2,1,0:T(8,128)(2,1)S(1)} async-done(((bf16[64,8,640]{2,1,0:T(8,128)(2,1)}), bf16[64,8,640]{2,1,0:T(8,128)(2,1)S(1)}, u32[]{:S(2)}, u32[]{:S(2)}) %all-to-all-start.2) | async-done | bytes 655392 | tf_op jit(solution)/shard_map/all_to_all | solution.py:1285
  120.0 4.0 attend.2
  124.0 18.1 %all_to_all.65 = bf16[64,8,384]{2,1,0:T(8,128)(2,1)S(1)} all-to-all(bf16[64,8,384]{2,1,0:T(8,128)(2,1)} %bitcast.155), channel_id=1, replica_groups=mesh['wide'=64,'narrow'=2] {'wide'}, dimensions={0} | all-to-all | bytes 786432 | tf_op jit(solution)/shard_map/all_to_all | solution.py:1285
  145.1 7.7 %collective-permute-done.6.refs_2_ = bf16[128,1024]{1,0:T(8,128)(2,1)S(1)} collective-permute-done((bf16[128,1024]{1,0:T(8,128)(2,1)}, bf16[128,1024]{1,0:T(8,128)(2,1)S(1)}, u32[]{:S(2)}, u32[]{:S(2)}) %collective-permute-start.6) | collective-permute-done | bytes 262176 | tf_op jit(solution)/shard_map/ppermute | solution.py:1276
  152.8 7.4 %ffn.1 = (f32[128,1024]{1,0:T(8,128)}, bf16[2,128,512]{2,1,0:T(8,128)(2,1)}, bf16[128,2048]{1,0:T(8,128)(2,1)}, bf16[128,2048]{1,0:T(8,128)(2,1)}, bf16[128,1024]{1,0:T(8,128)(2,1)}) custom-call(f32[128,1024]{1,0:T(8,128)} %copy-done.14, bf16[128,1024]{1,0:T(8,128)(2,1)} %get-tuple-element.129.refs_1_, bf16[128,1024]{1,0:T(8,128)(2,1)S(1)} %collective-permute-done.6.refs_2_, ...), custom_call_target="tpu_custom_call" | custom-call | tf_op jit(solution)/shard_map/ffn/pallas_call | solution.py:320
  160.5 6.6 %collective-permute-done.7.refs_3_ = bf16[128,1024]{1,0:T(8,128)(2,1)S(1)} collective-permute-done((bf16[128,1024]{1,0:T(8,128)(2,1)}, bf16[128,1024]{1,0:T(8,128)(2,1)S(1)}, u32[]{:S(2)}, u32[]{:S(2)}) %collective-permute-start.7) | collective-permute-done | bytes 262176 | tf_op jit(solution)/shard_map/ppermute | solution.py:1276
  167.1 3.8 project.3
  170.9 21.4 %all_to_all.66 = bf16[64,8,640]{2,1,0:T(8,128)(2,1)S(1)} all-to-all(bf16[64,8,640]{2,1,0:T(8,128)(2,1)} %bitcast.152), channel_id=1, replica_groups=mesh['wide'=64,'narrow'=2] {'wide'}, dimensions={0} | all-to-all | bytes 1310720 | tf_op jit(solution)/shard_map/all_to_all | solution.py:1285
  192.3 4.0 attend.3
  196.3 17.5 %all_to_all.67 = bf16[64,8,384]{2,1,0:T(8,128)(2,1)S(1)} all-to-all(bf16[64,8,384]{2,1,0:T(8,128)(2,1)} %bitcast.156), channel_id=1, replica_groups=mesh['wide'=64,'narrow'=2] {'wide'}, dimensions={0} | all-to-all | bytes 786432 | tf_op jit(solution)/shard_map/all_to_all | solution.py:1285
  216.9 7.5 %collective-permute-done.8.refs_2_ = bf16[128,1024]{1,0:T(8,128)(2,1)S(1)} collective-permute-done((bf16[128,1024]{1,0:T(8,128)(2,1)}, bf16[128,1024]{1,0:T(8,128)(2,1)S(1)}, u32[]{:S(2)}, u32[]{:S(2)}) %collective-permute-start.8) | collective-permute-done | bytes 262176 | tf_op jit(solution)/shard_map/ppermute | solution.py:1276
  224.4 12.6 %turn.1 = (f32[128,1024]{1,0:T(8,128)}, bf16[128,1024]{1,0:T(8,128)(2,1)}, bf16[128,1024]{1,0:T(8,128)(2,1)}, bf16[8,8,128,512]{3,2,1,0:T(8,128)(2,1)}) custom-call(f32[128,1024]{1,0:T(8,128)} %get-tuple-element.130.refs_0_.refs_4_, bf16[128,1024]{1,0:T(8,128)(2,1)} %get-tuple-element.135.refs_1_, bf16[128,1024]{1,0:T(8,128)(2,1)S(1)} %collective-permute-done.8.refs_2_, ...), custom_call_target="tpu_custom_call" | custom-call | tf_op jit(solution)/shard_map/turn/pallas_call | solution.py:320
  239.4 5.1 %collective-permute-done.10.refs_3_ = bf16[128,1024]{1,0:T(8,128)(2,1)S(1)} collective-permute-done((bf16[128,1024]{1,0:T(8,128)(2,1)S(1)}, bf16[128,1024]{1,0:T(8,128)(2,1)S(1)}, u32[]{:S(2)}, u32[]{:S(2)}) %collective-permute-start.10) | collective-permute-done | bytes 262176 | tf_op jit(solution)/shard_map/ppermute | solution.py:1276
  244.5 4.1 merge_back.2
  248.6 8.2 %all-to-all-start.6 = ((bf16[64,8,384]{2,1,0:T(8,128)(2,1)}), bf16[64,8,384]{2,1,0:T(8,128)(2,1)S(1)}, u32[]{:S(2)}, u32[]{:S(2)}) async-start(bf16[64,8,384]{2,1,0:T(8,128)(2,1)} %bitcast.153), calls=%async_computation.6 | async-start | bytes 786432 | tf_op jit(solution)/shard_map/all_to_all | solution.py:1285
  260.0 11.4 %all-to-all-done.6 = bf16[64,8,384]{2,1,0:T(8,128)(2,1)S(1)} async-done(((bf16[64,8,384]{2,1,0:T(8,128)(2,1)}), bf16[64,8,384]{2,1,0:T(8,128)(2,1)S(1)}, u32[]{:S(2)}, u32[]{:S(2)}) %all-to-all-start.6) | async-done | bytes 393248 | tf_op jit(solution)/shard_map/all_to_all | solution.py:1285
  271.4 5.3 %attend_back.2 = bf16[512,640]{1,0:T(8,128)(2,1)} custom-call(bf16[512,384]{1,0:T(8,128)(2,1)S(1)} %bitcast.103, bf16[1088,256]{1,0:T(8,128)(2,1)} %get-tuple-element.148.sorted_ref, s32[4,512]{1,0:T(4,128)} %get-tuple-element.111.place_row_ref, f32[1,512]{1,0:T(1,128)S(1)} %get-tuple-element.201.gain_ref), custom_call_target="tpu_custom_call" | custom-call | tf_op jit(solution)/shard_map/attend_back/pallas_call | solution.py:102
  276.8 22.8 %all_to_all.68 = bf16[64,8,640]{2,1,0:T(8,128)(2,1)S(1)} all-to-all(bf16[64,8,640]{2,1,0:T(8,128)(2,1)} %bitcast.147), channel_id=1, replica_groups=mesh['wide'=64,'narrow'=2] {'wide'}, dimensions={0} | all-to-all | bytes 1310720 | tf_op jit(solution)/shard_map/all_to_all | solution.py:1285
  299.7 3.7 project_back.2
  303.7 3.9 attn_part.1.refs_9_
  307.6 4.1 collective-permute-done.11.refs_2_
  311.7 11.1 %ffn_back.1 = (f32[128,1024]{1,0:T(8,128)}, bf16[128,1024]{1,0:T(8,128)(2,1)}, bf16[8,8,176,512]{3,2,1,0:T(8,128)(2,1)}, f32[1,1024]{1,0:T(1,128)S(1)}) custom-call(f32[128,1024]{1,0:T(8,128)} %copy-done.5, bf16[128,1024]{1,0:T(8,128)(2,1)} %get-tuple-element.152.refs_1_, ...), custom_call_target="tpu_custom_call", output_to_operand_aliasing={{2}: (9, {})} | custom-call | tf_op jit(solution)/shard_map/ffn_back/pallas_call | solution.py:320
  324.0 6.9 %collective-permute-done.12.refs_3_ = bf16[128,1024]{1,0:T(8,128)(2,1)S(1)} collective-permute-done((bf16[128,1024]{1,0:T(8,128)(2,1)S(1)}, bf16[128,1024]{1,0:T(8,128)(2,1)S(1)}, u32[]{:S(2)}, u32[]{:S(2)}) %collective-permute-start.12) | collective-permute-done | bytes 262176 | tf_op jit(solution)/shard_map/ppermute | solution.py:1276
  330.9 4.1 merge_back.3
  335.0 7.5 %all-to-all-start.8 = ((bf16[64,8,384]{2,1,0:T(8,128)(2,1)}), bf16[64,8,384]{2,1,0:T(8,128)(2,1)S(1)}, u32[]{:S(2)}, u32[]{:S(2)}) async-start(bf16[64,8,384]{2,1,0:T(8,128)(2,1)} %bitcast.154), calls=%async_computation.10 | async-start | bytes 786432 | tf_op jit(solution)/shard_map/all_to_all | solution.py:1285
  342.5 3.3 collective-permute-start.13
  351.2 5.8 %all-to-all-done.8 = bf16[64,8,384]{2,1,0:T(8,128)(2,1)S(1)} async-done(((bf16[64,8,384]{2,1,0:T(8,128)(2,1)}), bf16[64,8,384]{2,1,0:T(8,128)(2,1)S(1)}, u32[]{:S(2)}, u32[]{:S(2)}) %all-to-all-start.8) | async-done | bytes 393248 | tf_op jit(solution)/shard_map/all_to_all | solution.py:1285
  357.0 5.3 %attend_back.3 = bf16[512,640]{1,0:T(8,128)(2,1)} custom-call(bf16[512,384]{1,0:T(8,128)(2,1)S(1)} %bitcast.104, bf16[1088,256]{1,0:T(8,128)(2,1)} %get-tuple-element.171.sorted_ref, s32[4,512]{1,0:T(4,128)} %get-tuple-element.108.place_row_ref, f32[1,512]{1,0:T(1,128)S(1)} %get-tuple-element.200.gain_ref), custom_call_target="tpu_custom_call" | custom-call | tf_op jit(solution)/shard_map/attend_back/pallas_call | solution.py:102
  362.3 5.0 %all-to-all-start.9 = ((bf16[64,8,640]{2,1,0:T(8,128)(2,1)}), bf16[64,8,640]{2,1,0:T(8,128)(2,1)S(1)}, u32[]{:S(2)}, u32[]{:S(2)}) async-start(bf16[64,8,640]{2,1,0:T(8,128)(2,1)} %bitcast.146), calls=%async_computation.11 | async-start | bytes 1310720 | tf_op jit(solution)/shard_map/all_to_all | solution.py:1285
  368.4 17.2 %all-to-all-done.9 = bf16[64,8,640]{2,1,0:T(8,128)(2,1)S(1)} async-done(((bf16[64,8,640]{2,1,0:T(8,128)(2,1)}), bf16[64,8,640]{2,1,0:T(8,128)(2,1)S(1)}, u32[]{:S(2)}, u32[]{:S(2)}) %all-to-all-start.9) | async-done | bytes 655392 | tf_op jit(solution)/shard_map/all_to_all | solution.py:1285
  385.6 3.8 project_back.3
  391.1 3.0 attn_grad.1
  394.1 4.5 all-to-all-start.11
  398.6 3.6 reduce-scatter.9.cloned.1.call-done
  406.9 15.0 %collective-permute-done.14.refs_2_ = bf16[128,1024]{1,0:T(8,128)(2,1)S(1)} collective-permute-done((bf16[128,1024]{1,0:T(8,128)(2,1)}, bf16[128,1024]{1,0:T(8,128)(2,1)S(1)}, u32[]{:S(2)}, u32[]{:S(2)}) %collective-permute-start.14) | collective-permute-done | bytes 262176 | tf_op jit(solution)/shard_map/ppermute | solution.py:1276
  423.4 5.6 %all-to-all-start.10 = ((bf16[8,96,512]{2,1,0:T(8,128)(2,1)}), bf16[8,96,512]{2,1,0:T(8,128)(2,1)S(1)}, u32[]{:S(2)}, u32[]{:S(2)}) async-start(bf16[8,96,512]{2,1,0:T(8,128)(2,1)} %slice.126), calls=%async_computation.13 | async-start | bytes 1572864 | tf_op jit(solution)/shard_map/all_to_all | solution.py:1315
  430.0 2.9 collective-permute-start.20
  435.6 6.2 %all-to-all-done.10 = bf16[8,96,512]{2,1,0:T(8,128)(2,1)S(1)} async-done(((bf16[8,96,512]{2,1,0:T(8,128)(2,1)}), bf16[8,96,512]{2,1,0:T(8,128)(2,1)S(1)}, u32[]{:S(2)}, u32[]{:S(2)}) %all-to-all-start.10) | async-done | bytes 786464 | tf_op jit(solution)/shard_map/all_to_all | solution.py:1315
  443.9 12.2 %all-to-all-start.12 = ((bf16[64,16,512]{2,1,0:T(8,128)(2,1)}), bf16[64,16,512]{2,1,0:T(8,128)(2,1)S(1)}, u32[]{:S(2)}, u32[]{:S(2)}) async-start(bf16[64,16,512]{2,1,0:T(8,128)(2,1)} %bitcast.145), calls=%async_computation.16 | async-start | bytes 2097152 | tf_op jit(solution)/shard_map/all_to_all | solution.py:1285
  458.1 16.7 %all-to-all-done.12 = bf16[64,16,512]{2,1,0:T(8,128)(2,1)S(1)} async-done(((bf16[64,16,512]{2,1,0:T(8,128)(2,1)}), bf16[64,16,512]{2,1,0:T(8,128)(2,1)S(1)}, u32[]{:S(2)}, u32[]{:S(2)}) %all-to-all-start.12) | async-done | bytes 1048608 | tf_op jit(solution)/shard_map/all_to_all | solution.py:1285
  474.8 5.3 %slots_update.1 = (f32[5,128,512]{2,1,0:T(8,128)}, f32[5,128,512]{2,1,0:T(8,128)}, f32[5,128,512]{2,1,0:T(8,128)}, f32[5,128,512]{2,1,0:T(8,128)}, f32[2,2,512]{...) custom-call(s32[1]{0:T(128)} %bitcast.half_ref.refs_0_, ...), custom_call_target="tpu_custom_call" | custom-call | tf_op jit(solution)/shard_map/slots_update/pallas_call | solution.py:320
  (206 shorter events, 58.4 us)
Async XLA Ops:
  7.2 20.4 %copy-start = (s32[2,2,8192]{2,1,0:T(2,128)S(1)}, s32[2,2,8192]{2,1,0:T(2,128)}, u32[]{:S(2)}) copy-start(s32[2,2,8192]{2,1,0:T(2,128)} %param.17) | copy-start | bytes 393220
  11.3 36.6 %all-to-all-start = ((bf16[64,24,512]{2,1,0:T(8,128)(2,1)}), bf16[64,24,512]{2,1,0:T(8,128)(2,1)S(1)}, u32[]{:S(2)}, u32[]{:S(2)}) async-start(bf16[64,24,512]{2,1,0:T(8,128)(2,1)} %bitcast.144), calls=%async_computation | async-start | bytes 3145728 | tf_op jit(solution)/shard_map/all_to_all | solution.py:1285
  23.9 118.2 %all-gather.3.cloned.1.call-start = ((), (), s32[]{:S(2)}) async-start(), calls=%async_computation.17 | async-start | bytes 12976128 | tf_op jit(solution)/shard_map/all_gather | solution.py:1346
  50.3 34.4 %copy-start.26 = (s32[2,128]{1,0:T(2,128)S(1)}, s32[2,128]{1,0:T(2,128)}, u32[]{:S(2)}) copy-start(s32[2,128]{1,0:T(2,128)} %get-tuple-element.106.refs_19_.refs_12_) | copy-start | bytes 3076
  50.3 166.6 %all-gather.5.cloned.1.call-start = ((), (), s32[]{:S(2)}) async-start(), calls=%async_computation.18 | async-start | bytes 8650752 | tf_op jit(solution)/shard_map/all_gather | solution.py:1346
  51.0 29.9 %all-to-all-start.1 = ((bf16[32,32,512]{2,1,0:T(8,128)(2,1)}), bf16[32,32,512]{2,1,0:T(8,128)(2,1)S(1)}, u32[]{:S(2)}, u32[]{:S(2)}) async-start(bf16[32,32,512]{2,1,0:T(8,128)(2,1)} %get-tuple-element.121), calls=%async_computation.1 | async-start | bytes 2097152 | tf_op jit(solution)/shard_map/all_to_all | solution.py:1336
  55.5 23.3 %collective-permute-start.3 = (bf16[128,512]{1,0:T(8,128)(2,1)S(1)}, bf16[128,512]{1,0:T(8,128)(2,1)S(1)}, u32[]{:S(2)}, u32[]{:S(2)}) collective-permute-start(bf16[128,512]{1,0:T(8,128)(2,1)S(1)} %copy-done.15), channel_id=1, source_target_pairs={{0,1},{1,0},{2,3},{3,2},{4,5},{5,4},{6,7},{7,6},{8,9},{9,8},{10,11... | collective-permute-start | bytes 393224 | tf_op jit(solution)/shard_map/ppermute | solution.py:1276
  56.0 24.9 %collective-permute-start = (bf16[128,512]{1,0:T(8,128)(2,1)S(1)}, bf16[128,512]{1,0:T(8,128)(2,1)S(1)}, u32[]{:S(2)}, u32[]{:S(2)}) collective-permute-start(bf16[128,512]{1,0:T(8,128)(2,1)S(1)} %copy-done.16), channel_id=1, source_target_pairs={{0,1},{1,0},{2,3},{3,2},{4,5},{5,4},{6,7},{7,6},{8,9},{9,8},{10,11... | collective-permute-start | bytes 393224 | tf_op jit(solution)/shard_map/ppermute | solution.py:1276
  57.1 23.8 %collective-permute-start.1 = (bf16[128,512]{1,0:T(8,128)(2,1)S(1)}, bf16[128,512]{1,0:T(8,128)(2,1)S(1)}, u32[]{:S(2)}, u32[]{:S(2)}) collective-permute-start(bf16[128,512]{1,0:T(8,128)(2,1)S(1)} %copy-done.17), channel_id=1, source_target_pairs={{0,1},{1,0},{2,3},{3,2},{4,5},{5,4},{6,7},{7,6},{8,9},{9,8},{10,11... | collective-permute-start | bytes 393224 | tf_op jit(solution)/shard_map/ppermute | solution.py:1276
  57.5 23.5 %collective-permute-start.2 = (bf16[128,512]{1,0:T(8,128)(2,1)S(1)}, bf16[128,512]{1,0:T(8,128)(2,1)S(1)}, u32[]{:S(2)}, u32[]{:S(2)}) collective-permute-start(bf16[128,512]{1,0:T(8,128)(2,1)S(1)} %copy-done.18), channel_id=1, source_target_pairs={{0,1},{1,0},{2,3},{3,2},{4,5},{5,4},{6,7},{7,6},{8,9},{9,8},{10,11... | collective-permute-start | bytes 393224 | tf_op jit(solution)/shard_map/ppermute | solution.py:1276
  58.5 20.3 %collective-permute-start.4 = (f32[4,512]{1,0:T(4,128)S(1)}, f32[4,512]{1,0:T(4,128)S(1)}, u32[]{:S(2)}, u32[]{:S(2)}) collective-permute-start(f32[4,512]{1,0:T(4,128)S(1)} %reshape.447.refs_2_), channel_id=1, source_target_pairs={{0,1},{1,0},{2,3},{3,2},{4,5},{5,4},{6,7},{7,6},{8,9},{9,8},{10,11... | collective-permute-start | bytes 24584 | tf_op jit(solution)/shard_map/ppermute | solution.py:1276
  81.0 3.7 collective-permute-start.5
  87.9 32.1 %all-to-all-start.2 = ((bf16[64,8,640]{2,1,0:T(8,128)(2,1)}), bf16[64,8,640]{2,1,0:T(8,128)(2,1)S(1)}, u32[]{:S(2)}, u32[]{:S(2)}) async-start(bf16[64,8,640]{2,1,0:T(8,128)(2,1)} %bitcast.151), calls=%async_computation.2 | async-start | bytes 1310720 | tf_op jit(solution)/shard_map/all_to_all | solution.py:1285
  98.7 200.9 %reduce-scatter.5.cloned.1.call-start = ((), (), s32[]{:S(2)}) async-start(), calls=%async_computation.19 | async-start | bytes 9437184 | tf_op jit(solution)/shard_map/reduce_scatter | solution.py:1309
  145.0 22.1 %copy-start.7 = (f32[4,1024]{1,0:T(4,128)S(1)}, f32[4,1024]{1,0:T(4,128)}, u32[]{:S(2)}) copy-start(f32[4,1024]{1,0:T(4,128)} %copy-done.6) | copy-start | bytes 49156
  145.0 22.1 %copy-start.27 = (s32[2,128]{1,0:T(2,128)S(1)}, s32[2,128]{1,0:T(2,128)}, u32[]{:S(2)}) copy-start(s32[2,128]{1,0:T(2,128)} %get-tuple-element.109.refs_13_.refs_12_) | copy-start | bytes 3076
  145.0 7.8 %collective-permute-start.6 = (bf16[128,1024]{1,0:T(8,128)(2,1)}, bf16[128,1024]{1,0:T(8,128)(2,1)S(1)}, u32[]{:S(2)}, u32[]{:S(2)}) collective-permute-start(bf16[128,1024]{1,0:T(8,128)(2,1)} %get-tuple-element.129.refs_1_), channel_id=1, source_target_pairs={{0,1},{1,0},{2,3},{3,2},{4,5},{5,4},{6,7},{7,6},{8,9},{9,8},{10,11... | collective-permute-start | bytes 786440 | tf_op jit(solution)/shard_map/ppermute | solution.py:1276
  160.2 6.9 %collective-permute-start.7 = (bf16[128,1024]{1,0:T(8,128)(2,1)}, bf16[128,1024]{1,0:T(8,128)(2,1)S(1)}, u32[]{:S(2)}, u32[]{:S(2)}) collective-permute-start(bf16[128,1024]{1,0:T(8,128)(2,1)} %get-tuple-element.132.refs_2_), channel_id=1, source_target_pairs={{0,1},{1,0},{2,3},{3,2},{4,5},{5,4},{6,7},{7,6},{8,9},{9,8},{10,11... | collective-permute-start | bytes 786440 | tf_op jit(solution)/shard_map/ppermute | solution.py:1276
  216.7 7.7 %collective-permute-start.8 = (bf16[128,1024]{1,0:T(8,128)(2,1)}, bf16[128,1024]{1,0:T(8,128)(2,1)S(1)}, u32[]{:S(2)}, u32[]{:S(2)}) collective-permute-start(bf16[128,1024]{1,0:T(8,128)(2,1)} %get-tuple-element.135.refs_1_), channel_id=1, source_target_pairs={{0,1},{1,0},{2,3},{3,2},{4,5},{5,4},{6,7},{7,6},{8,9},{9,8},{10,11... | collective-permute-start | bytes 786440 | tf_op jit(solution)/shard_map/ppermute | solution.py:1276
  237.9 6.5 %collective-permute-start.10 = (bf16[128,1024]{1,0:T(8,128)(2,1)S(1)}, bf16[128,1024]{1,0:T(8,128)(2,1)S(1)}, u32[]{:S(2)}, u32[]{:S(2)}) collective-permute-start(bf16[128,1024]{1,0:T(8,128)(2,1)S(1)} %copy-done.32), channel_id=1, source_target_pairs={{0,1},{1,0},{2,3},{3,2},{4,5},{5,4},{6,7},{7,6},{8,9},{9,8},{10,11... | collective-permute-start | bytes 786440 | tf_op jit(solution)/shard_map/ppermute | solution.py:1276
  238.1 18.9 %collective-permute-start.9 = (bf16[128,1024]{1,0:T(8,128)(2,1)S(1)}, bf16[128,1024]{1,0:T(8,128)(2,1)S(1)}, u32[]{:S(2)}, u32[]{:S(2)}) collective-permute-start(bf16[128,1024]{1,0:T(8,128)(2,1)S(1)} %copy-done.35), channel_id=1, source_target_pairs={{0,1},{1,0},{2,3},{3,2},{4,5},{5,4},{6,7},{7,6},{8,9},{9,8},{10,11... | collective-permute-start | bytes 786440 | tf_op jit(solution)/shard_map/ppermute | solution.py:1276
  248.6 22.9 %all-to-all-start.6 = ((bf16[64,8,384]{2,1,0:T(8,128)(2,1)}), bf16[64,8,384]{2,1,0:T(8,128)(2,1)S(1)}, u32[]{:S(2)}, u32[]{:S(2)}) async-start(bf16[64,8,384]{2,1,0:T(8,128)(2,1)} %bitcast.153), calls=%async_computation.6 | async-start | bytes 786432 | tf_op jit(solution)/shard_map/all_to_all | solution.py:1285
  256.8 74.1 %reduce-scatter.7.cloned.1.call-start = ((), (), s32[]{:S(2)}) async-start(), calls=%async_computation.20 | async-start | bytes 1310720 | tf_op jit(solution)/shard_map/reduce_scatter | solution.py:1322
  299.6 102.6 %reduce-scatter.9.cloned.1.call-start = ((), (), s32[]{:S(2)}) async-start(), calls=%async_computation.21 | async-start | bytes 12976128 | tf_op jit(solution)/shard_map/reduce_scatter | solution.py:1309
  303.3 8.4 %collective-permute-start.11 = (bf16[128,1024]{1,0:T(8,128)(2,1)}, bf16[128,1024]{1,0:T(8,128)(2,1)S(1)}, u32[]{:S(2)}, u32[]{:S(2)}) collective-permute-start(bf16[128,1024]{1,0:T(8,128)(2,1)} %get-tuple-element.152.refs_1_), channel_id=1, source_target_pairs={{0,1},{1,0},{2,3},{3,2},{4,5},{5,4},{6,7},{7,6},{8,9},{9,8},{10,11... | collective-permute-start | bytes 786440 | tf_op jit(solution)/shard_map/ppermute | solution.py:1276
  323.8 7.1 %collective-permute-start.12 = (bf16[128,1024]{1,0:T(8,128)(2,1)S(1)}, bf16[128,1024]{1,0:T(8,128)(2,1)S(1)}, u32[]{:S(2)}, u32[]{:S(2)}) collective-permute-start(bf16[128,1024]{1,0:T(8,128)(2,1)S(1)} %copy-done.31), channel_id=1, source_target_pairs={{0,1},{1,0},{2,3},{3,2},{4,5},{5,4},{6,7},{7,6},{8,9},{9,8},{10,11... | collective-permute-start | bytes 786440 | tf_op jit(solution)/shard_map/ppermute | solution.py:1276
  335.0 22.0 %all-to-all-start.8 = ((bf16[64,8,384]{2,1,0:T(8,128)(2,1)}), bf16[64,8,384]{2,1,0:T(8,128)(2,1)S(1)}, u32[]{:S(2)}, u32[]{:S(2)}) async-start(bf16[64,8,384]{2,1,0:T(8,128)(2,1)} %bitcast.154), calls=%async_computation.10 | async-start | bytes 786432 | tf_op jit(solution)/shard_map/all_to_all | solution.py:1285
  342.5 8.6 %collective-permute-start.13 = (bf16[128,512]{1,0:T(8,128)(2,1)S(1)}, bf16[128,512]{1,0:T(8,128)(2,1)S(1)}, u32[]{:S(2)}, u32[]{:S(2)}) collective-permute-start(bf16[128,512]{1,0:T(8,128)(2,1)S(1)} %dynamic-slice_bitcast_fusion), channel_id=1, source_target_pairs={{0,64},{2,66},{4,68},{6,70},{8,72},{10,74},{12,76},{14,78},{16,80}... | collective-permute-start | bytes 393224 | tf_op jit(solution)/shard_map/ppermute | solution.py:1331
  348.7 18.6 %copy-start.30 = (bf16[2,128,512]{2,1,0:T(8,128)(2,1)S(1)}, bf16[2,128,512]{2,1,0:T(8,128)(2,1)}, u32[]{:S(2)}) copy-start(bf16[2,128,512]{2,1,0:T(8,128)(2,1)} %get-tuple-element.177.refs_4_.refs_8_) | copy-start | bytes 786436
  348.7 19.1 %copy-start.33 = (bf16[2,128,512]{2,1,0:T(8,128)(2,1)S(1)}, bf16[2,128,512]{2,1,0:T(8,128)(2,1)}, u32[]{:S(2)}) copy-start(bf16[2,128,512]{2,1,0:T(8,128)(2,1)} %get-tuple-element.175.refs_0_) | copy-start | bytes 786436
  348.7 19.2 %copy-start.37 = (bf16[128,512]{1,0:T(8,128)(2,1)S(1)}, bf16[128,512]{1,0:T(8,128)(2,1)}, u32[]{:S(2)}) copy-start(bf16[128,512]{1,0:T(8,128)(2,1)} %get-tuple-element.176.refs_2_) | copy-start | bytes 393220
  362.3 23.2 %all-to-all-start.9 = ((bf16[64,8,640]{2,1,0:T(8,128)(2,1)}), bf16[64,8,640]{2,1,0:T(8,128)(2,1)S(1)}, u32[]{:S(2)}, u32[]{:S(2)}) async-start(bf16[64,8,640]{2,1,0:T(8,128)(2,1)} %bitcast.146), calls=%async_computation.11 | async-start | bytes 1310720 | tf_op jit(solution)/shard_map/all_to_all | solution.py:1285
  367.3 22.6 %collective-permute-start.17 = (bf16[2,128,512]{2,1,0:T(8,128)(2,1)S(1)}, bf16[2,128,512]{2,1,0:T(8,128)(2,1)S(1)}, u32[]{:S(2)}, u32[]{:S(2)}) collective-permute-start(bf16[2,128,512]{2,1,0:T(8,128)(2,1)S(1)} %copy-done.30), channel_id=1, source_target_pairs={{0,2},{2,0},{4,6},{6,4},{8,10},{10,8},{12,14},{14,12},{16,18},{18,... | collective-permute-start | bytes 786440 | tf_op jit(solution)/shard_map/ppermute | solution.py:1280
  367.9 22.0 %collective-permute-start.15 = (bf16[2,128,512]{2,1,0:T(8,128)(2,1)S(1)}, bf16[2,128,512]{2,1,0:T(8,128)(2,1)S(1)}, u32[]{:S(2)}, u32[]{:S(2)}) collective-permute-start(bf16[2,128,512]{2,1,0:T(8,128)(2,1)S(1)} %copy-done.33), channel_id=1, source_target_pairs={{0,2},{2,0},{4,6},{6,4},{8,10},{10,8},{12,14},{14,12},{16,18},{18,... | collective-permute-start | bytes 786440 | tf_op jit(solution)/shard_map/ppermute | solution.py:1280
  368.0 21.9 %collective-permute-start.16 = (bf16[128,512]{1,0:T(8,128)(2,1)S(1)}, bf16[128,512]{1,0:T(8,128)(2,1)S(1)}, u32[]{:S(2)}, u32[]{:S(2)}) collective-permute-start(bf16[128,512]{1,0:T(8,128)(2,1)S(1)} %copy-done.37), channel_id=1, source_target_pairs={{0,2},{2,0},{4,6},{6,4},{8,10},{10,8},{12,14},{14,12},{16,18},{18,... | collective-permute-start | bytes 393224 | tf_op jit(solution)/shard_map/ppermute | solution.py:1280
  389.4 1.6 collective-permute-start.18
  389.4 1.7 collective-permute-start.19
  394.1 29.3 %all-to-all-start.11 = ((bf16[32,48,512]{2,1,0:T(8,128)(2,1)}), bf16[32,48,512]{2,1,0:T(8,128)(2,1)S(1)}, u32[]{:S(2)}, u32[]{:S(2)}) async-start(bf16[32,48,512]{2,1,0:T(8,128)(2,1)} %attn_grad.1), calls=%async_computation.15 | async-start | bytes 3145728 | tf_op jit(solution)/shard_map/all_to_all | solution.py:1336
  398.6 30.5 %reduce-scatter.11.cloned.1.call-start = ((), (), s32[]{:S(2)}) async-start(), calls=%async_computation.22 | async-start | bytes 819200 | tf_op jit(solution)/shard_map/reduce_scatter | solution.py:1322
  404.4 17.6 %collective-permute-start.14 = (bf16[128,1024]{1,0:T(8,128)(2,1)}, bf16[128,1024]{1,0:T(8,128)(2,1)S(1)}, u32[]{:S(2)}, u32[]{:S(2)}) collective-permute-start(bf16[128,1024]{1,0:T(8,128)(2,1)} %get-tuple-element.172.refs_1_), channel_id=1, source_target_pairs={{0,1},{1,0},{2,3},{3,2},{4,5},{5,4},{6,7},{7,6},{8,9},{9,8},{10,11... | collective-permute-start | bytes 786440 | tf_op jit(solution)/shard_map/ppermute | solution.py:1276
  423.4 18.4 %all-to-all-start.10 = ((bf16[8,96,512]{2,1,0:T(8,128)(2,1)}), bf16[8,96,512]{2,1,0:T(8,128)(2,1)S(1)}, u32[]{:S(2)}, u32[]{:S(2)}) async-start(bf16[8,96,512]{2,1,0:T(8,128)(2,1)} %slice.126), calls=%async_computation.13 | async-start | bytes 1572864 | tf_op jit(solution)/shard_map/all_to_all | solution.py:1315
  430.0 12.0 %collective-permute-start.20 = (bf16[80,512]{1,0:T(8,128)(2,1)S(1)}, bf16[80,512]{1,0:T(8,128)(2,1)S(1)}, u32[]{:S(2)}, u32[]{:S(2)}) collective-permute-start(bf16[80,512]{1,0:T(8,128)(2,1)S(1)} %dynamic-slice_bitcast_fusion.1), channel_id=1, source_target_pairs={{0,64},{2,66},{4,68},{6,70},{8,72},{10,74},{12,76},{14,78},{16,80}... | collective-permute-start | bytes 245768 | tf_op jit(solution)/shard_map/ppermute | solution.py:1331
  442.0 14.2 %copy-start.12 = (f32[128,1024]{1,0:T(8,128)S(1)}, f32[128,1024]{1,0:T(8,128)}, u32[]{:S(2)}) copy-start(f32[128,1024]{1,0:T(8,128)} %get-tuple-element.173.refs_0_) | copy-start | bytes 1572868
  443.9 30.9 %copy-start.21 = (s32[176]{0:T(256)S(1)}, s32[176]{0:T(256)}, u32[]{:S(2)}) copy-start(s32[176]{0:T(256)} %param.18) | copy-start | bytes 2116
  443.9 30.9 %copy-start.23 = (f32[2,2,512]{2,1,0:T(2,128)S(1)}, f32[2,2,512]{2,1,0:T(2,128)}, u32[]{:S(2)}) copy-start(f32[2,2,512]{2,1,0:T(2,128)} %refs_8_.1) | copy-start | bytes 24580
  443.9 30.9 %copy-start.24 = (f32[2,2,512]{2,1,0:T(2,128)S(1)}, f32[2,2,512]{2,1,0:T(2,128)}, u32[]{:S(2)}) copy-start(f32[2,2,512]{2,1,0:T(2,128)} %refs_9_.1) | copy-start | bytes 24580
  443.9 30.9 %copy-start.25 = (f32[2,2,512]{2,1,0:T(2,128)S(1)}, f32[2,2,512]{2,1,0:T(2,128)}, u32[]{:S(2)}) copy-start(f32[2,2,512]{2,1,0:T(2,128)} %refs_10_.1) | copy-start | bytes 24580
  443.9 30.9 %all-to-all-start.12 = ((bf16[64,16,512]{2,1,0:T(8,128)(2,1)}), bf16[64,16,512]{2,1,0:T(8,128)(2,1)S(1)}, u32[]{:S(2)}, u32[]{:S(2)}) async-start(bf16[64,16,512]{2,1,0:T(8,128)(2,1)} %bitcast.145), calls=%async_computation.16 | async-start | bytes 2097152 | tf_op jit(solution)/shard_map/all_to_all | solution.py:1285
  (27 other events, 145.9 us)
Sparse Core Ops, SparseCore 0:
  50.4 74.3 all-gather.2
  127.6 52.5 all-gather.4
  237.1 58.7 reduce-scatter.4
  299.7 20.7 reduce-scatter.6
  323.0 79.1 reduce-scatter.8
  405.2 22.4 reduce-scatter.10

commit v6 on v5

--- a/solution.py
+++ b/solution.py
@@ -33,7 +33,7 @@
 LAYER_ROWS = 176
 ATTN_ROWS = 48
 FFN_ROWS = 128
-SPLIT = 96
+SPLIT = 80
 EARLY_ROWS = 384
 
 MASK_FILL = -1000000000.0
@@ -79,7 +79,8 @@
 
 
 def call(
-    kernel, args, outs, grid=(1,), specs=None, out_specs=None, scratch=(), prefetch=0, in_place=(), name=None
+    kernel, args, outs, grid=(1,), specs=None, out_specs=None, scratch=(), prefetch=0, in_place=(), name=None,
+    aliases=None
 ):
     specs = specs or {}
     out_specs = out_specs or {}
@@ -110,6 +111,7 @@
             scratch_shapes=list(scratch),
         ),
         compiler_params=pltpu.CompilerParams(vmem_limit_bytes=VMEM_BYTES),
+        input_output_aliases=aliases or {},
         name=name,
     )(*args)
 
@@ -1162,7 +1164,7 @@
 
 def project_back_kernel(count, core_ref, moved_ref, rank_col_ref, *refs):
     q_refs, v_refs = refs[:count], refs[count : 2 * count]
-    send_out, dq_out, dv_out, gain_out = refs[2 * count :]
+    send_out, grad_out, gain_out = refs[2 * count :]
     gain_out[...] = dot(
         hot(iota((8, 1), 0) == (iota((1, ROWS), 1) & 7)), moved_ref[:, 4 * DH :], 1, 0
     )
@@ -1180,8 +1182,8 @@
     d_v = jnp.concatenate([total[:, h * 2 * DH + DH : (h + 1) * 2 * DH] for h in range(HN)], 1)
     d_q = (d_q + lent_q).astype(BF16)
     d_v = (d_v + lent_v).astype(BF16)
-    dq_out[...] = d_q
-    dv_out[...] = d_v
+    grad_out[0] = d_q
+    grad_out[1] = d_v
     core = core_ref[0]
     from_q = out_of(core, d_q, q_refs)
     from_v = out_of(core, d_v, v_refs)
@@ -1193,7 +1195,7 @@
     return call(
         functools.partial(project_back_kernel, len(wq.parts())),
         args,
-        [kept((TOK, D), BF16), kept((TOK, PART), BF16), kept((TOK, PART), BF16), sds((8, DH), F32)],
+        [kept((TOK, D), BF16), kept((2, TOK, PART), BF16), sds((8, DH), F32)],
         specs=specs,
         in_place=range(1, len(args) - 1),
         prefetch=1,
@@ -1201,12 +1203,12 @@
     )
 
 
-def attn_part_kernel(back_ref, merged_ref, hn_ref, dq_ref, dv_ref, grad_out, buffer, sems):
+def attn_part_kernel(back_ref, merged_ref, hn_ref, dqv_ref, grad_out, buffer, sems):
     for c0 in range(2):
         for i, (left, right) in enumerate(
-            ((back_ref, merged_ref), (hn_ref, dq_ref), (hn_ref, dv_ref))
+            ((back_ref, merged_ref[...]), (hn_ref, dqv_ref[0]), (hn_ref, dqv_ref[1]))
         ):
-            put_pieces(buffer, c0, i * 16, 16, dot(left[c0], right[...], 0, 0).astype(BF16))
+            put_pieces(buffer, c0, i * 16, 16, dot(left[c0], right, 0, 0).astype(BF16))
     copy = pltpu.make_async_copy(
         buffer, grad_out.at[:, :, pl.ds(FFN_ROWS, ATTN_ROWS), :], sems.at[0]
     )
@@ -1214,14 +1216,14 @@
     copy.wait()
 
 
-def attn_part_of(back, merged, hn, dq, dv):
+def attn_part_of(back, merged, hn, dqv):
     return call(
         attn_part_kernel,
-        (back, merged, hn, dq, dv),
+        (back, merged, hn, dqv),
         [kept((2 * QUAD, 8, FFN_ROWS + ATTN_ROWS, PART), BF16)],
         out_specs={0: pl.BlockSpec(memory_space=pl.ANY)},
         scratch=[pltpu.VMEM((2 * QUAD, 8, ATTN_ROWS, PART), BF16), pltpu.SemaphoreType.DMA((1,))],
-        in_place=range(5),
+        in_place=range(4),
         name="attn_part",
     )[0]
 
@@ -1249,26 +1251,36 @@
     return dot(left, right, 0, 0).astype(BF16)
 
 
-def attn_grad_kernel(count, core_ref, *refs):
-    out_ref = refs[-1]
-    for i in range(count):
-        la, lb, ra, rb = refs[4 * i : 4 * i + 4]
-        got = pair_dot(la[0], lb[0], ra[...], rb[...])
-        out_ref[:, i * 16 : (i + 1) * 16] = got.reshape(32, 16, PART)
-
-
-def attn_grad(core, pairs):
+def attn_grad_kernel(row, core_ref, la, lb, ra, rb, *refs):
+    out_ref, buffer, sems = refs[-3:]
+    for i in range(buffer.shape[1] // 16):
+        got = pair_dot(la[0], lb[0], ra[i], rb[i])
+        buffer[:, i * 16 : (i + 1) * 16] = got.reshape(32, 16, PART)
+    rows = pl.ds(row, buffer.shape[1])
+    copy = pltpu.make_async_copy(buffer, out_ref.at[:, rows, :], sems.at[0])
+    copy.start()
+    copy.wait()
+
+
+def attn_grad(core, left, right, before=None):
     half = pl.BlockSpec((1, TOK, PART), lambda i, core: (core[0], 0, 0))
-    args = [a for left, right in pairs for a in (*left, *right)]
-    specs = {4 * i + j: half for i in range(len(pairs)) for j in range(2)}
+    args, specs, row, aliases = [*left, *right], {0: half, 1: half}, 0, {}
+    if before is not None:
+        args.append(before)
+        specs[4] = pl.BlockSpec(memory_space=pl.ANY)
+        row, aliases = 16, {5: 0}
+    rows = 16 * right[0].shape[0]
     return call(
-        functools.partial(attn_grad_kernel, len(pairs)),
+        functools.partial(attn_grad_kernel, row),
         (core, *args),
-        [kept((32, 16 * len(pairs), PART), BF16)],
+        [kept((32, ATTN_ROWS, PART), BF16)],
         specs=specs,
+        out_specs={0: pl.BlockSpec(memory_space=pl.ANY)},
+        scratch=[pltpu.VMEM((32, rows, PART), BF16), pltpu.SemaphoreType.DMA((1,))],
         prefetch=1,
-        in_place=range(0, len(args), 2),
+        in_place=(0, 2, 4),
         name="attn_grad",
+        aliases=aliases,
     )[0]
 
 
@@ -1465,16 +1477,17 @@
         moved = moved_rows(send)
         if l > 0:
             moved = after(moved, ffn_part)
-        send, dq, dv, gain_sum = project_back(core, moved, rank_cols[l], w_qk, w_value)
+        if l == 0:
+            out_part = attn_grad(core, with_core(back), with_core(merged.reshape(1, TOK, PART)))
+            moved = after(moved, out_part)
+        send, dqv, gain_sum = project_back(core, moved, rank_cols[l], w_qk, w_value)
         other = swap_narrow(send)
         if l > 0:
-            attn_part = attn_part_of(back, merged, hn, dq, dv)
+            attn_part = attn_part_of(back, merged, hn, dqv)
             other = after(other, attn_part)
             ffn_rows = summed_along_z(after(ffn_part, moved))
         else:
-            hn2 = with_core(hn)
-            pairs = [(with_core(back), with_core(merged)), (hn2, with_core(dq)), (hn2, with_core(dv))]
-            attn_part = attn_grad(core, pairs)
+            attn_part = attn_grad(core, with_core(hn), with_core(dqv), out_part)
             attn_rows = summed(attn_part)
             ffn_part = after(ffn_part, attn_part)
             last_rows = summed_along_y(summed_along_z(ffn_part[:, SPLIT:]))

time: 497 us -> 496 us (level)
  waiting for transfers between devices: 177 us -> 172 us
    pallas_call x24 -> x25, Pallas kernels: 75.6 us -> 77.2 us  [call(): pl.pallas_call(kernel, out_shape=outs, grid_spec=pltpu.PrefetchScalarGrid...]
  transfers between devices with their start and end apart: 36 -> 35, of which waited for: 21 -> 22; matrix products, arithmetic and copies ran while one was open for 2% -> 2% of each run, Pallas kernels for 18% -> 18%
where the time goes in v6:
time: 496 us; the launch traced here: 486 us
  waiting for transfers between devices  172 us (35%)
  Pallas kernels  114 us (23%)
  starting transfers between devices  89 us (18%)
  blocking collectives  79.9 us (16%)
  between operations  15.3 us (3%)
  local copies, waits for them, and re-layouts  15 us (3%)
    all_to_all x6, waiting for transfers between devices, to_all(): lax.all_to_all(values, 'wide', split_axis=0, concat_axis=0, tiled=True)  83.3 us
    all_to_all x4, blocking collectives, to_all(): lax.all_to_all(values, 'wide', split_axis=0, concat_axis=0, tiled=True)  79.9 us
    pallas_call x25, Pallas kernels, call(): pl.pallas_call(kernel, out_shape=outs, grid_spec=pltpu.PrefetchScalarGrid...  77.2 us
    ppermute x13, waiting for transfers between devices, swap_narrow(): return lax.ppermute(values, 'narrow', [(0, 1), (1, 0)])  70.1 us
    all_to_all x6, starting transfers between devices, to_all(): lax.all_to_all(values, 'wide', split_axis=0, concat_axis=0, tiled=True)  56.8 us
    pallas_call x4, Pallas kernels, run(): pl.pallas_call(body, out_shape=out_shapes, grid_spec=pltpu.PrefetchScalar...  36.5 us
  transfers between devices with their start and end apart: 35, of which 22 were waited for; matrix products, arithmetic and copies ran while one was open for 2% of the time, Pallas kernels for 18%

profile of v6, /device:TPU:1, one launch (start us, length us, event | category | flops | bytes accessed | tf_op | source)
XLA Modules:
  0.0 485.8 jit_solution(14090967521633895735)
XLA Ops:
  7.9 3.4 route_out.1
  11.3 12.6 %all-to-all-start = ((bf16[64,24,512]{2,1,0:T(8,128)(2,1)}), bf16[64,24,512]{2,1,0:T(8,128)(2,1)S(1)}, u32[]{:S(2)}, u32[]{:S(2)}) async-start(bf16[64,24,512]{2,1,0:T(8,128)(2,1)} %bitcast.145), calls=%async_computation | async-start | bytes 3145728 | tf_op jit(solution)/shard_map/all_to_all | solution.py:1297
  30.2 17.6 %all-to-all-done = bf16[64,24,512]{2,1,0:T(8,128)(2,1)S(1)} async-done(((bf16[64,24,512]{2,1,0:T(8,128)(2,1)}), bf16[64,24,512]{2,1,0:T(8,128)(2,1)S(1)}, u32[]{:S(2)}, u32[]{:S(2)}) %all-to-all-start) | async-done | bytes 1572896 | tf_op jit(solution)/shard_map/all_to_all | solution.py:1297
  51.1 4.4 all-to-all-start.1
  58.9 19.9 %collective-permute-done.4.refs_3_ = f32[4,512]{1,0:T(4,128)S(1)} collective-permute-done((f32[4,512]{1,0:T(4,128)S(1)}, f32[4,512]{1,0:T(4,128)S(1)}, u32[]{:S(2)}, u32[]{:S(2)}) %collective-permute-start.4) | collective-permute-done | bytes 8224 | tf_op jit(solution)/shard_map/ppermute | solution.py:1288
  84.7 3.2 project.2
  87.9 10.8 %all-to-all-start.2 = ((bf16[64,8,640]{2,1,0:T(8,128)(2,1)}), bf16[64,8,640]{2,1,0:T(8,128)(2,1)S(1)}, u32[]{:S(2)}, u32[]{:S(2)}) async-start(bf16[64,8,640]{2,1,0:T(8,128)(2,1)} %bitcast.152), calls=%async_computation.2 | async-start | bytes 1310720 | tf_op jit(solution)/shard_map/all_to_all | solution.py:1297
  102.4 17.6 %all-to-all-done.2 = bf16[64,8,640]{2,1,0:T(8,128)(2,1)S(1)} async-done(((bf16[64,8,640]{2,1,0:T(8,128)(2,1)}), bf16[64,8,640]{2,1,0:T(8,128)(2,1)S(1)}, u32[]{:S(2)}, u32[]{:S(2)}) %all-to-all-start.2) | async-done | bytes 655392 | tf_op jit(solution)/shard_map/all_to_all | solution.py:1297
  120.0 4.0 attend.2
  124.0 18.1 %all_to_all.65 = bf16[64,8,384]{2,1,0:T(8,128)(2,1)S(1)} all-to-all(bf16[64,8,384]{2,1,0:T(8,128)(2,1)} %bitcast.156), channel_id=1, replica_groups=mesh['wide'=64,'narrow'=2] {'wide'}, dimensions={0} | all-to-all | bytes 786432 | tf_op jit(solution)/shard_map/all_to_all | solution.py:1297
  142.1 2.9 merge.2
  145.1 7.7 %collective-permute-done.6.refs_2_ = bf16[128,1024]{1,0:T(8,128)(2,1)S(1)} collective-permute-done((bf16[128,1024]{1,0:T(8,128)(2,1)}, bf16[128,1024]{1,0:T(8,128)(2,1)S(1)}, u32[]{:S(2)}, u32[]{:S(2)}) %collective-permute-start.6) | collective-permute-done | bytes 262176 | tf_op jit(solution)/shard_map/ppermute | solution.py:1288
  152.7 7.4 %ffn.1 = (f32[128,1024]{1,0:T(8,128)}, bf16[2,128,512]{2,1,0:T(8,128)(2,1)}, bf16[128,2048]{1,0:T(8,128)(2,1)}, bf16[128,2048]{1,0:T(8,128)(2,1)}, bf16[128,1024]{1,0:T(8,128)(2,1)}) custom-call(f32[128,1024]{1,0:T(8,128)} %copy-done.14, bf16[128,1024]{1,0:T(8,128)(2,1)} %get-tuple-element.128.refs_1_, bf16[128,1024]{1,0:T(8,128)(2,1)S(1)} %collective-permute-done.6.refs_2_, ...), custom_call_target="tpu_custom_call" | custom-call | tf_op jit(solution)/shard_map/ffn/pallas_call | solution.py:322
  160.5 6.6 %collective-permute-done.7.refs_3_ = bf16[128,1024]{1,0:T(8,128)(2,1)S(1)} collective-permute-done((bf16[128,1024]{1,0:T(8,128)(2,1)}, bf16[128,1024]{1,0:T(8,128)(2,1)S(1)}, u32[]{:S(2)}, u32[]{:S(2)}) %collective-permute-start.7) | collective-permute-done | bytes 262176 | tf_op jit(solution)/shard_map/ppermute | solution.py:1288
  167.1 3.7 project.3
  170.8 21.4 %all_to_all.66 = bf16[64,8,640]{2,1,0:T(8,128)(2,1)S(1)} all-to-all(bf16[64,8,640]{2,1,0:T(8,128)(2,1)} %bitcast.153), channel_id=1, replica_groups=mesh['wide'=64,'narrow'=2] {'wide'}, dimensions={0} | all-to-all | bytes 1310720 | tf_op jit(solution)/shard_map/all_to_all | solution.py:1297
  192.2 4.0 attend.3
  196.2 17.5 %all_to_all.67 = bf16[64,8,384]{2,1,0:T(8,128)(2,1)S(1)} all-to-all(bf16[64,8,384]{2,1,0:T(8,128)(2,1)} %bitcast.157), channel_id=1, replica_groups=mesh['wide'=64,'narrow'=2] {'wide'}, dimensions={0} | all-to-all | bytes 786432 | tf_op jit(solution)/shard_map/all_to_all | solution.py:1297
  216.8 7.5 %collective-permute-done.8.refs_2_ = bf16[128,1024]{1,0:T(8,128)(2,1)S(1)} collective-permute-done((bf16[128,1024]{1,0:T(8,128)(2,1)}, bf16[128,1024]{1,0:T(8,128)(2,1)S(1)}, u32[]{:S(2)}, u32[]{:S(2)}) %collective-permute-start.8) | collective-permute-done | bytes 262176 | tf_op jit(solution)/shard_map/ppermute | solution.py:1288
  224.3 12.6 %turn.1 = (f32[128,1024]{1,0:T(8,128)}, bf16[128,1024]{1,0:T(8,128)(2,1)}, bf16[128,1024]{1,0:T(8,128)(2,1)}, bf16[8,8,128,512]{3,2,1,0:T(8,128)(2,1)}) custom-call(f32[128,1024]{1,0:T(8,128)} %get-tuple-element.129.refs_0_.refs_4_, bf16[128,1024]{1,0:T(8,128)(2,1)} %get-tuple-element.134.refs_1_, bf16[128,1024]{1,0:T(8,128)(2,1)S(1)} %collective-permute-done.8.refs_2_, ...), custom_call_target="tpu_custom_call" | custom-call | tf_op jit(solution)/shard_map/turn/pallas_call | solution.py:322
  239.4 5.1 %collective-permute-done.10.refs_3_ = bf16[128,1024]{1,0:T(8,128)(2,1)S(1)} collective-permute-done((bf16[128,1024]{1,0:T(8,128)(2,1)S(1)}, bf16[128,1024]{1,0:T(8,128)(2,1)S(1)}, u32[]{:S(2)}, u32[]{:S(2)}) %collective-permute-start.10) | collective-permute-done | bytes 262176 | tf_op jit(solution)/shard_map/ppermute | solution.py:1288
  244.4 4.1 merge_back.2
  248.5 8.2 %all-to-all-start.6 = ((bf16[64,8,384]{2,1,0:T(8,128)(2,1)}), bf16[64,8,384]{2,1,0:T(8,128)(2,1)S(1)}, u32[]{:S(2)}, u32[]{:S(2)}) async-start(bf16[64,8,384]{2,1,0:T(8,128)(2,1)} %bitcast.154), calls=%async_computation.6 | async-start | bytes 786432 | tf_op jit(solution)/shard_map/all_to_all | solution.py:1297
  260.0 11.4 %all-to-all-done.6 = bf16[64,8,384]{2,1,0:T(8,128)(2,1)S(1)} async-done(((bf16[64,8,384]{2,1,0:T(8,128)(2,1)}), bf16[64,8,384]{2,1,0:T(8,128)(2,1)S(1)}, u32[]{:S(2)}, u32[]{:S(2)}) %all-to-all-start.6) | async-done | bytes 393248 | tf_op jit(solution)/shard_map/all_to_all | solution.py:1297
  271.4 5.3 %attend_back.2 = bf16[512,640]{1,0:T(8,128)(2,1)} custom-call(bf16[512,384]{1,0:T(8,128)(2,1)S(1)} %bitcast.104, bf16[1088,256]{1,0:T(8,128)(2,1)} %get-tuple-element.147.sorted_ref, s32[4,512]{1,0:T(4,128)} %get-tuple-element.110.place_row_ref, f32[1,512]{1,0:T(1,128)S(1)} %get-tuple-element.199.gain_ref), custom_call_target="tpu_custom_call" | custom-call | tf_op jit(solution)/shard_map/attend_back/pallas_call | solution.py:103
  276.8 22.8 %all_to_all.68 = bf16[64,8,640]{2,1,0:T(8,128)(2,1)S(1)} all-to-all(bf16[64,8,640]{2,1,0:T(8,128)(2,1)} %bitcast.148), channel_id=1, replica_groups=mesh['wide'=64,'narrow'=2] {'wide'}, dimensions={0} | all-to-all | bytes 1310720 | tf_op jit(solution)/shard_map/all_to_all | solution.py:1297
  299.7 3.7 project_back.2
  303.7 3.9 attn_part.1.refs_9_
  307.6 4.1 collective-permute-done.11.refs_2_
  311.7 11.1 %ffn_back.1 = (f32[128,1024]{1,0:T(8,128)}, bf16[128,1024]{1,0:T(8,128)(2,1)}, bf16[8,8,176,512]{3,2,1,0:T(8,128)(2,1)}, f32[1,1024]{1,0:T(1,128)S(1)}) custom-call(f32[128,1024]{1,0:T(8,128)} %copy-done.5, bf16[128,1024]{1,0:T(8,128)(2,1)} %get-tuple-element.151.refs_1_, ...), custom_call_target="tpu_custom_call", output_to_operand_aliasing={{2}: (9, {})} | custom-call | tf_op jit(solution)/shard_map/ffn_back/pallas_call | solution.py:322
  323.9 7.0 %collective-permute-done.12.refs_3_ = bf16[128,1024]{1,0:T(8,128)(2,1)S(1)} collective-permute-done((bf16[128,1024]{1,0:T(8,128)(2,1)S(1)}, bf16[128,1024]{1,0:T(8,128)(2,1)S(1)}, u32[]{:S(2)}, u32[]{:S(2)}) %collective-permute-start.12) | collective-permute-done | bytes 262176 | tf_op jit(solution)/shard_map/ppermute | solution.py:1288
  330.9 4.1 merge_back.3
  335.0 7.4 %all-to-all-start.8 = ((bf16[64,8,384]{2,1,0:T(8,128)(2,1)}), bf16[64,8,384]{2,1,0:T(8,128)(2,1)S(1)}, u32[]{:S(2)}, u32[]{:S(2)}) async-start(bf16[64,8,384]{2,1,0:T(8,128)(2,1)} %bitcast.155), calls=%async_computation.10 | async-start | bytes 786432 | tf_op jit(solution)/shard_map/all_to_all | solution.py:1297
  342.5 3.3 collective-permute-start.13
  351.1 5.8 %all-to-all-done.8 = bf16[64,8,384]{2,1,0:T(8,128)(2,1)S(1)} async-done(((bf16[64,8,384]{2,1,0:T(8,128)(2,1)}), bf16[64,8,384]{2,1,0:T(8,128)(2,1)S(1)}, u32[]{:S(2)}, u32[]{:S(2)}) %all-to-all-start.8) | async-done | bytes 393248 | tf_op jit(solution)/shard_map/all_to_all | solution.py:1297
  357.0 5.3 %attend_back.3 = bf16[512,640]{1,0:T(8,128)(2,1)} custom-call(bf16[512,384]{1,0:T(8,128)(2,1)S(1)} %bitcast.105, bf16[1088,256]{1,0:T(8,128)(2,1)} %get-tuple-element.169.sorted_ref, s32[4,512]{1,0:T(4,128)} %get-tuple-element.107.place_row_ref, f32[1,512]{1,0:T(1,128)S(1)} %get-tuple-element.198.gain_ref), custom_call_target="tpu_custom_call" | custom-call | tf_op jit(solution)/shard_map/attend_back/pallas_call | solution.py:103
  362.3 5.0 %all-to-all-start.9 = ((bf16[64,8,640]{2,1,0:T(8,128)(2,1)}), bf16[64,8,640]{2,1,0:T(8,128)(2,1)S(1)}, u32[]{:S(2)}, u32[]{:S(2)}) async-start(bf16[64,8,640]{2,1,0:T(8,128)(2,1)} %bitcast.147), calls=%async_computation.11 | async-start | bytes 1310720 | tf_op jit(solution)/shard_map/all_to_all | solution.py:1297
  371.5 14.0 %all-to-all-done.9 = bf16[64,8,640]{2,1,0:T(8,128)(2,1)S(1)} async-done(((bf16[64,8,640]{2,1,0:T(8,128)(2,1)}), bf16[64,8,640]{2,1,0:T(8,128)(2,1)S(1)}, u32[]{:S(2)}, u32[]{:S(2)}) %all-to-all-start.9) | async-done | bytes 655392 | tf_op jit(solution)/shard_map/all_to_all | solution.py:1297
  385.5 3.8 project_back.3
  393.6 4.3 all-to-all-start.11
  397.9 4.5 reduce-scatter.9.cloned.1.call-done
  409.1 12.2 %collective-permute-done.16.refs_2_ = bf16[128,1024]{1,0:T(8,128)(2,1)S(1)} collective-permute-done((bf16[128,1024]{1,0:T(8,128)(2,1)S(1)}, bf16[128,1024]{1,0:T(8,128)(2,1)S(1)}, u32[]{:S(2)}, u32[]{:S(2)}) %collective-permute-start.16) | collective-permute-done | bytes 262176 | tf_op jit(solution)/shard_map/ppermute | solution.py:1288
  422.5 5.6 %all-to-all-start.10 = ((bf16[8,80,512]{2,1,0:T(8,128)(2,1)}), bf16[8,80,512]{2,1,0:T(8,128)(2,1)S(1)}, u32[]{:S(2)}, u32[]{:S(2)}) async-start(bf16[8,80,512]{2,1,0:T(8,128)(2,1)} %slice.126), calls=%async_computation.13 | async-start | bytes 1310720 | tf_op jit(solution)/shard_map/all_to_all | solution.py:1327
  430.4 2.9 collective-permute-start.19
  436.1 3.4 all-to-all-done.10
  441.6 12.8 %all-to-all-start.12 = ((bf16[64,16,512]{2,1,0:T(8,128)(2,1)}), bf16[64,16,512]{2,1,0:T(8,128)(2,1)S(1)}, u32[]{:S(2)}, u32[]{:S(2)}) async-start(bf16[64,16,512]{2,1,0:T(8,128)(2,1)} %bitcast.146), calls=%async_computation.16 | async-start | bytes 2097152 | tf_op jit(solution)/shard_map/all_to_all | solution.py:1297
  456.3 16.8 %all-to-all-done.12 = bf16[64,16,512]{2,1,0:T(8,128)(2,1)S(1)} async-done(((bf16[64,16,512]{2,1,0:T(8,128)(2,1)}), bf16[64,16,512]{2,1,0:T(8,128)(2,1)S(1)}, u32[]{:S(2)}, u32[]{:S(2)}) %all-to-all-start.12) | async-done | bytes 1048608 | tf_op jit(solution)/shard_map/all_to_all | solution.py:1297
  473.1 5.3 %slots_update.1 = (f32[5,128,512]{2,1,0:T(8,128)}, f32[5,128,512]{2,1,0:T(8,128)}, f32[5,128,512]{2,1,0:T(8,128)}, f32[5,128,512]{2,1,0:T(8,128)}, f32[2,2,512]{...) custom-call(s32[1]{0:T(128)} %bitcast.half_ref.refs_0_, ...), custom_call_target="tpu_custom_call" | custom-call | tf_op jit(solution)/shard_map/slots_update/pallas_call | solution.py:322
  (205 shorter events, 64.2 us)
Async XLA Ops:
  7.2 20.4 %copy-start = (s32[2,2,8192]{2,1,0:T(2,128)S(1)}, s32[2,2,8192]{2,1,0:T(2,128)}, u32[]{:S(2)}) copy-start(s32[2,2,8192]{2,1,0:T(2,128)} %param.17) | copy-start | bytes 393220
  11.3 13.9 %copy-start.38 = (s32[16]{0:T(128)S(1)}, s32[16]{0:T(128)}, u32[]{:S(2)}) copy-start(s32[16]{0:T(128)} %constant.78) | copy-start | bytes 196
  11.3 36.6 %all-to-all-start = ((bf16[64,24,512]{2,1,0:T(8,128)(2,1)}), bf16[64,24,512]{2,1,0:T(8,128)(2,1)S(1)}, u32[]{:S(2)}, u32[]{:S(2)}) async-start(bf16[64,24,512]{2,1,0:T(8,128)(2,1)} %bitcast.145), calls=%async_computation | async-start | bytes 3145728 | tf_op jit(solution)/shard_map/all_to_all | solution.py:1297
  23.9 118.2 %all-gather.3.cloned.1.call-start = ((), (), s32[]{:S(2)}) async-start(), calls=%async_computation.17 | async-start | bytes 12976128 | tf_op jit(solution)/shard_map/all_gather | solution.py:1358
  50.3 34.4 %copy-start.26 = (s32[2,128]{1,0:T(2,128)S(1)}, s32[2,128]{1,0:T(2,128)}, u32[]{:S(2)}) copy-start(s32[2,128]{1,0:T(2,128)} %get-tuple-element.105.refs_19_.refs_12_) | copy-start | bytes 3076
  50.3 166.5 %all-gather.5.cloned.1.call-start = ((), (), s32[]{:S(2)}) async-start(), calls=%async_computation.18 | async-start | bytes 8650752 | tf_op jit(solution)/shard_map/all_gather | solution.py:1358
  51.1 29.9 %all-to-all-start.1 = ((bf16[32,32,512]{2,1,0:T(8,128)(2,1)}), bf16[32,32,512]{2,1,0:T(8,128)(2,1)S(1)}, u32[]{:S(2)}, u32[]{:S(2)}) async-start(bf16[32,32,512]{2,1,0:T(8,128)(2,1)} %get-tuple-element.120), calls=%async_computation.1 | async-start | bytes 2097152 | tf_op jit(solution)/shard_map/all_to_all | solution.py:1348
  55.5 23.3 %collective-permute-start.3 = (bf16[128,512]{1,0:T(8,128)(2,1)S(1)}, bf16[128,512]{1,0:T(8,128)(2,1)S(1)}, u32[]{:S(2)}, u32[]{:S(2)}) collective-permute-start(bf16[128,512]{1,0:T(8,128)(2,1)S(1)} %copy-done.15), channel_id=1, source_target_pairs={{0,1},{1,0},{2,3},{3,2},{4,5},{5,4},{6,7},{7,6},{8,9},{9,8},{10,11... | collective-permute-start | bytes 393224 | tf_op jit(solution)/shard_map/ppermute | solution.py:1288
  56.0 24.9 %collective-permute-start = (bf16[128,512]{1,0:T(8,128)(2,1)S(1)}, bf16[128,512]{1,0:T(8,128)(2,1)S(1)}, u32[]{:S(2)}, u32[]{:S(2)}) collective-permute-start(bf16[128,512]{1,0:T(8,128)(2,1)S(1)} %copy-done.16), channel_id=1, source_target_pairs={{0,1},{1,0},{2,3},{3,2},{4,5},{5,4},{6,7},{7,6},{8,9},{9,8},{10,11... | collective-permute-start | bytes 393224 | tf_op jit(solution)/shard_map/ppermute | solution.py:1288
  57.1 23.8 %collective-permute-start.1 = (bf16[128,512]{1,0:T(8,128)(2,1)S(1)}, bf16[128,512]{1,0:T(8,128)(2,1)S(1)}, u32[]{:S(2)}, u32[]{:S(2)}) collective-permute-start(bf16[128,512]{1,0:T(8,128)(2,1)S(1)} %copy-done.17), channel_id=1, source_target_pairs={{0,1},{1,0},{2,3},{3,2},{4,5},{5,4},{6,7},{7,6},{8,9},{9,8},{10,11... | collective-permute-start | bytes 393224 | tf_op jit(solution)/shard_map/ppermute | solution.py:1288
  57.5 23.4 %collective-permute-start.2 = (bf16[128,512]{1,0:T(8,128)(2,1)S(1)}, bf16[128,512]{1,0:T(8,128)(2,1)S(1)}, u32[]{:S(2)}, u32[]{:S(2)}) collective-permute-start(bf16[128,512]{1,0:T(8,128)(2,1)S(1)} %copy-done.18), channel_id=1, source_target_pairs={{0,1},{1,0},{2,3},{3,2},{4,5},{5,4},{6,7},{7,6},{8,9},{9,8},{10,11... | collective-permute-start | bytes 393224 | tf_op jit(solution)/shard_map/ppermute | solution.py:1288
  58.6 20.3 %collective-permute-start.4 = (f32[4,512]{1,0:T(4,128)S(1)}, f32[4,512]{1,0:T(4,128)S(1)}, u32[]{:S(2)}, u32[]{:S(2)}) collective-permute-start(f32[4,512]{1,0:T(4,128)S(1)} %reshape.450.refs_2_), channel_id=1, source_target_pairs={{0,1},{1,0},{2,3},{3,2},{4,5},{5,4},{6,7},{7,6},{8,9},{9,8},{10,11... | collective-permute-start | bytes 24584 | tf_op jit(solution)/shard_map/ppermute | solution.py:1288
  80.9 3.7 collective-permute-start.5
  87.9 32.1 %all-to-all-start.2 = ((bf16[64,8,640]{2,1,0:T(8,128)(2,1)}), bf16[64,8,640]{2,1,0:T(8,128)(2,1)S(1)}, u32[]{:S(2)}, u32[]{:S(2)}) async-start(bf16[64,8,640]{2,1,0:T(8,128)(2,1)} %bitcast.152), calls=%async_computation.2 | async-start | bytes 1310720 | tf_op jit(solution)/shard_map/all_to_all | solution.py:1297
  98.7 200.9 %reduce-scatter.5.cloned.1.call-start = ((), (), s32[]{:S(2)}) async-start(), calls=%async_computation.19 | async-start | bytes 9437184 | tf_op jit(solution)/shard_map/reduce_scatter | solution.py:1321
  145.0 22.1 %copy-start.7 = (f32[4,1024]{1,0:T(4,128)S(1)}, f32[4,1024]{1,0:T(4,128)}, u32[]{:S(2)}) copy-start(f32[4,1024]{1,0:T(4,128)} %copy-done.6) | copy-start | bytes 49156
  145.0 22.1 %copy-start.27 = (s32[2,128]{1,0:T(2,128)S(1)}, s32[2,128]{1,0:T(2,128)}, u32[]{:S(2)}) copy-start(s32[2,128]{1,0:T(2,128)} %get-tuple-element.108.refs_13_.refs_12_) | copy-start | bytes 3076
  145.0 7.7 %collective-permute-start.6 = (bf16[128,1024]{1,0:T(8,128)(2,1)}, bf16[128,1024]{1,0:T(8,128)(2,1)S(1)}, u32[]{:S(2)}, u32[]{:S(2)}) collective-permute-start(bf16[128,1024]{1,0:T(8,128)(2,1)} %get-tuple-element.128.refs_1_), channel_id=1, source_target_pairs={{0,1},{1,0},{2,3},{3,2},{4,5},{5,4},{6,7},{7,6},{8,9},{9,8},{10,11... | collective-permute-start | bytes 786440 | tf_op jit(solution)/shard_map/ppermute | solution.py:1288
  160.1 6.9 %collective-permute-start.7 = (bf16[128,1024]{1,0:T(8,128)(2,1)}, bf16[128,1024]{1,0:T(8,128)(2,1)S(1)}, u32[]{:S(2)}, u32[]{:S(2)}) collective-permute-start(bf16[128,1024]{1,0:T(8,128)(2,1)} %get-tuple-element.131.refs_2_), channel_id=1, source_target_pairs={{0,1},{1,0},{2,3},{3,2},{4,5},{5,4},{6,7},{7,6},{8,9},{9,8},{10,11... | collective-permute-start | bytes 786440 | tf_op jit(solution)/shard_map/ppermute | solution.py:1288
  216.6 7.7 %collective-permute-start.8 = (bf16[128,1024]{1,0:T(8,128)(2,1)}, bf16[128,1024]{1,0:T(8,128)(2,1)S(1)}, u32[]{:S(2)}, u32[]{:S(2)}) collective-permute-start(bf16[128,1024]{1,0:T(8,128)(2,1)} %get-tuple-element.134.refs_1_), channel_id=1, source_target_pairs={{0,1},{1,0},{2,3},{3,2},{4,5},{5,4},{6,7},{7,6},{8,9},{9,8},{10,11... | collective-permute-start | bytes 786440 | tf_op jit(solution)/shard_map/ppermute | solution.py:1288
  237.9 6.5 %collective-permute-start.10 = (bf16[128,1024]{1,0:T(8,128)(2,1)S(1)}, bf16[128,1024]{1,0:T(8,128)(2,1)S(1)}, u32[]{:S(2)}, u32[]{:S(2)}) collective-permute-start(bf16[128,1024]{1,0:T(8,128)(2,1)S(1)} %copy-done.30), channel_id=1, source_target_pairs={{0,1},{1,0},{2,3},{3,2},{4,5},{5,4},{6,7},{7,6},{8,9},{9,8},{10,11... | collective-permute-start | bytes 786440 | tf_op jit(solution)/shard_map/ppermute | solution.py:1288
  238.1 18.9 %collective-permute-start.9 = (bf16[128,1024]{1,0:T(8,128)(2,1)S(1)}, bf16[128,1024]{1,0:T(8,128)(2,1)S(1)}, u32[]{:S(2)}, u32[]{:S(2)}) collective-permute-start(bf16[128,1024]{1,0:T(8,128)(2,1)S(1)} %copy-done.35), channel_id=1, source_target_pairs={{0,1},{1,0},{2,3},{3,2},{4,5},{5,4},{6,7},{7,6},{8,9},{9,8},{10,11... | collective-permute-start | bytes 786440 | tf_op jit(solution)/shard_map/ppermute | solution.py:1288
  248.5 22.9 %all-to-all-start.6 = ((bf16[64,8,384]{2,1,0:T(8,128)(2,1)}), bf16[64,8,384]{2,1,0:T(8,128)(2,1)S(1)}, u32[]{:S(2)}, u32[]{:S(2)}) async-start(bf16[64,8,384]{2,1,0:T(8,128)(2,1)} %bitcast.154), calls=%async_computation.6 | async-start | bytes 786432 | tf_op jit(solution)/shard_map/all_to_all | solution.py:1297
  256.8 74.2 %reduce-scatter.7.cloned.1.call-start = ((), (), s32[]{:S(2)}) async-start(), calls=%async_computation.20 | async-start | bytes 1310720 | tf_op jit(solution)/shard_map/reduce_scatter | solution.py:1334
  299.6 102.8 %reduce-scatter.9.cloned.1.call-start = ((), (), s32[]{:S(2)}) async-start(), calls=%async_computation.21 | async-start | bytes 12976128 | tf_op jit(solution)/shard_map/reduce_scatter | solution.py:1321
  303.3 8.4 %collective-permute-start.11 = (bf16[128,1024]{1,0:T(8,128)(2,1)}, bf16[128,1024]{1,0:T(8,128)(2,1)S(1)}, u32[]{:S(2)}, u32[]{:S(2)}) collective-permute-start(bf16[128,1024]{1,0:T(8,128)(2,1)} %get-tuple-element.151.refs_1_), channel_id=1, source_target_pairs={{0,1},{1,0},{2,3},{3,2},{4,5},{5,4},{6,7},{7,6},{8,9},{9,8},{10,11... | collective-permute-start | bytes 786440 | tf_op jit(solution)/shard_map/ppermute | solution.py:1288
  323.8 7.1 %collective-permute-start.12 = (bf16[128,1024]{1,0:T(8,128)(2,1)S(1)}, bf16[128,1024]{1,0:T(8,128)(2,1)S(1)}, u32[]{:S(2)}, u32[]{:S(2)}) collective-permute-start(bf16[128,1024]{1,0:T(8,128)(2,1)S(1)} %copy-done.29), channel_id=1, source_target_pairs={{0,1},{1,0},{2,3},{3,2},{4,5},{5,4},{6,7},{7,6},{8,9},{9,8},{10,11... | collective-permute-start | bytes 786440 | tf_op jit(solution)/shard_map/ppermute | solution.py:1288
  335.0 22.0 %all-to-all-start.8 = ((bf16[64,8,384]{2,1,0:T(8,128)(2,1)}), bf16[64,8,384]{2,1,0:T(8,128)(2,1)S(1)}, u32[]{:S(2)}, u32[]{:S(2)}) async-start(bf16[64,8,384]{2,1,0:T(8,128)(2,1)} %bitcast.155), calls=%async_computation.10 | async-start | bytes 786432 | tf_op jit(solution)/shard_map/all_to_all | solution.py:1297
  342.5 8.6 %collective-permute-start.13 = (bf16[128,512]{1,0:T(8,128)(2,1)S(1)}, bf16[128,512]{1,0:T(8,128)(2,1)S(1)}, u32[]{:S(2)}, u32[]{:S(2)}) collective-permute-start(bf16[128,512]{1,0:T(8,128)(2,1)S(1)} %dynamic-slice_bitcast_fusion), channel_id=1, source_target_pairs={{0,64},{2,66},{4,68},{6,70},{8,72},{10,74},{12,76},{14,78},{16,80}... | collective-permute-start | bytes 393224 | tf_op jit(solution)/shard_map/ppermute | solution.py:1343
  348.7 18.6 %copy-start.33 = (bf16[2,128,512]{2,1,0:T(8,128)(2,1)S(1)}, bf16[2,128,512]{2,1,0:T(8,128)(2,1)}, u32[]{:S(2)}) copy-start(bf16[2,128,512]{2,1,0:T(8,128)(2,1)} %get-tuple-element.170.la) | copy-start | bytes 786436
  348.7 19.1 %copy-start.37 = (bf16[128,512]{1,0:T(8,128)(2,1)S(1)}, bf16[128,512]{1,0:T(8,128)(2,1)}, u32[]{:S(2)}) copy-start(bf16[128,512]{1,0:T(8,128)(2,1)} %get-tuple-element.171) | copy-start | bytes 393220
  348.7 19.2 %copy-start.31 = (bf16[2,128,512]{2,1,0:T(8,128)(2,1)S(1)}, bf16[2,128,512]{2,1,0:T(8,128)(2,1)}, u32[]{:S(2)}) copy-start(bf16[2,128,512]{2,1,0:T(8,128)(2,1)} %get-tuple-element.176.la) | copy-start | bytes 786436
  362.3 23.2 %all-to-all-start.9 = ((bf16[64,8,640]{2,1,0:T(8,128)(2,1)}), bf16[64,8,640]{2,1,0:T(8,128)(2,1)S(1)}, u32[]{:S(2)}, u32[]{:S(2)}) async-start(bf16[64,8,640]{2,1,0:T(8,128)(2,1)} %bitcast.147), calls=%async_computation.11 | async-start | bytes 1310720 | tf_op jit(solution)/shard_map/all_to_all | solution.py:1297
  367.3 2.1 collective-permute-start.14
  367.8 1.5 collective-permute-start.15
  367.9 21.4 %collective-permute-start.17 = (bf16[2,128,512]{2,1,0:T(8,128)(2,1)S(1)}, bf16[2,128,512]{2,1,0:T(8,128)(2,1)S(1)}, u32[]{:S(2)}, u32[]{:S(2)}) collective-permute-start(bf16[2,128,512]{2,1,0:T(8,128)(2,1)S(1)} %copy-done.31), channel_id=1, source_target_pairs={{0,2},{2,0},{4,6},{6,4},{8,10},{10,8},{12,14},{14,12},{16,18},{18,... | collective-permute-start | bytes 786440 | tf_op jit(solution)/shard_map/ppermute | solution.py:1292
  389.3 1.7 collective-permute-start.18
  393.6 29.0 %all-to-all-start.11 = ((bf16[32,48,512]{2,1,0:T(8,128)(2,1)}), bf16[32,48,512]{2,1,0:T(8,128)(2,1)S(1)}, u32[]{:S(2)}, u32[]{:S(2)}) async-start(bf16[32,48,512]{2,1,0:T(8,128)(2,1)} %attn_grad.3), calls=%async_computation.15 | async-start | bytes 3145728 | tf_op jit(solution)/shard_map/all_to_all | solution.py:1348
  397.9 31.7 %reduce-scatter.11.cloned.1.call-start = ((), (), s32[]{:S(2)}) async-start(), calls=%async_computation.22 | async-start | bytes 983040 | tf_op jit(solution)/shard_map/reduce_scatter | solution.py:1334
  404.5 16.8 %collective-permute-start.16 = (bf16[128,1024]{1,0:T(8,128)(2,1)S(1)}, bf16[128,1024]{1,0:T(8,128)(2,1)S(1)}, u32[]{:S(2)}, u32[]{:S(2)}) collective-permute-start(bf16[128,1024]{1,0:T(8,128)(2,1)S(1)} %copy-done.32), channel_id=1, source_target_pairs={{0,1},{1,0},{2,3},{3,2},{4,5},{5,4},{6,7},{7,6},{8,9},{9,8},{10,11... | collective-permute-start | bytes 786440 | tf_op jit(solution)/shard_map/ppermute | solution.py:1288
  422.5 16.9 %all-to-all-start.10 = ((bf16[8,80,512]{2,1,0:T(8,128)(2,1)}), bf16[8,80,512]{2,1,0:T(8,128)(2,1)S(1)}, u32[]{:S(2)}, u32[]{:S(2)}) async-start(bf16[8,80,512]{2,1,0:T(8,128)(2,1)} %slice.126), calls=%async_computation.13 | async-start | bytes 1310720 | tf_op jit(solution)/shard_map/all_to_all | solution.py:1327
  430.4 9.1 %collective-permute-start.19 = (bf16[96,512]{1,0:T(8,128)(2,1)S(1)}, bf16[96,512]{1,0:T(8,128)(2,1)S(1)}, u32[]{:S(2)}, u32[]{:S(2)}) collective-permute-start(bf16[96,512]{1,0:T(8,128)(2,1)S(1)} %dynamic-slice_bitcast_fusion.1), channel_id=1, source_target_pairs={{0,64},{2,66},{4,68},{6,70},{8,72},{10,74},{12,76},{14,78},{16,80}... | collective-permute-start | bytes 294920 | tf_op jit(solution)/shard_map/ppermute | solution.py:1343
  439.6 14.8 %copy-start.12 = (f32[128,1024]{1,0:T(8,128)S(1)}, f32[128,1024]{1,0:T(8,128)}, u32[]{:S(2)}) copy-start(f32[128,1024]{1,0:T(8,128)} %get-tuple-element.174.refs_0_) | copy-start | bytes 1572868
  441.6 31.5 %copy-start.21 = (s32[176]{0:T(256)S(1)}, s32[176]{0:T(256)}, u32[]{:S(2)}) copy-start(s32[176]{0:T(256)} %param.18) | copy-start | bytes 2116
  441.6 31.5 %copy-start.23 = (f32[2,2,512]{2,1,0:T(2,128)S(1)}, f32[2,2,512]{2,1,0:T(2,128)}, u32[]{:S(2)}) copy-start(f32[2,2,512]{2,1,0:T(2,128)} %refs_8_.1) | copy-start | bytes 24580
  441.6 31.5 %copy-start.24 = (f32[2,2,512]{2,1,0:T(2,128)S(1)}, f32[2,2,512]{2,1,0:T(2,128)}, u32[]{:S(2)}) copy-start(f32[2,2,512]{2,1,0:T(2,128)} %refs_9_.1) | copy-start | bytes 24580
  441.6 31.5 %copy-start.25 = (f32[2,2,512]{2,1,0:T(2,128)S(1)}, f32[2,2,512]{2,1,0:T(2,128)}, u32[]{:S(2)}) copy-start(f32[2,2,512]{2,1,0:T(2,128)} %refs_10_.1) | copy-start | bytes 24580
  441.6 31.5 %all-to-all-start.12 = ((bf16[64,16,512]{2,1,0:T(8,128)(2,1)}), bf16[64,16,512]{2,1,0:T(8,128)(2,1)S(1)}, u32[]{:S(2)}, u32[]{:S(2)}) async-start(bf16[64,16,512]{2,1,0:T(8,128)(2,1)} %bitcast.146), calls=%async_computation.16 | async-start | bytes 2097152 | tf_op jit(solution)/shard_map/all_to_all | solution.py:1297
  (26 other events, 132.1 us)
Sparse Core Ops, SparseCore 0:
  50.4 74.2 all-gather.2
  127.6 52.4 all-gather.4
  237.1 58.7 reduce-scatter.4
  299.7 20.6 reduce-scatter.6
  323.0 79.3 reduce-scatter.8
  405.4 24.0 reduce-scatter.10
